TPU v7x, 32 devices: a whole 2x2x4 slice. The times are simulated.
32 devices in a mesh: rep: 4 (over z), fsdp: 8 (over y, x, core).
Axes of the slice: x: 2, y: 2, z: 4, core: 2. Of those that a mesh axis runs over, the one named last changes fastest.
Arguments:
- tokens: bfloat16 [8192, 2048], P(('rep', 'fsdp')), may hold values from -6 to 6
- cotangent: bfloat16 [8192, 2048], P(('rep', 'fsdp')), may hold values from -6 to 6
- lengths: int32 [32], replicated, may hold values from 64 to 256, as said below
- slot_owner: int32 [32], replicated, may hold values from 0 to 31, each once
- gain_in: bfloat16 [2048], P('fsdp'), may hold values from 0.5 to 1.5
- w_proj: bfloat16 [2048, 12288], P('fsdp'), may hold values from -0.125 to 0.125
- w_decay: bfloat16 [2048, 32], P('fsdp'), may hold values from -0.125 to 0.125
- conv_weight: bfloat16 [4, 8192], P(None, 'fsdp'), may hold values from -3 to 3
- a_log: bfloat16 [16], P('fsdp'), may hold values from -5.5 to -2.5
- dt_bias: bfloat16 [16], P('fsdp'), may hold values from -1 to 1
- o_gain: bfloat16 [256], P('fsdp'), may hold values from 0.5 to 1.5
- w_out: bfloat16 [4096, 2048], P('fsdp'), may hold values from -0.1875 to 0.1875
- gain_mid: bfloat16 [2048], P('fsdp'), may hold values from 0.5 to 1.5
- w_gate_up: bfloat16 [2048, 11264], P('fsdp'), may hold values from -0.125 to 0.125
- w_down: bfloat16 [5632, 2048], P('fsdp'), may hold values from -0.078125 to 0.078125
Outputs:
- output: bfloat16 [8192, 2048], P(('rep', 'fsdp'))
- grad_tokens: float32 [8192, 2048], P(('rep', 'fsdp'))
- grad_gain_in: float32 [2048], P('fsdp')
- grad_w_proj: float32 [2048, 12288], P('fsdp')
- grad_w_decay: float32 [2048, 32], P('fsdp')
- grad_conv: float32 [4, 8192], P(None, 'fsdp')
- grad_a_log: float32 [16], P('fsdp')
- grad_dt_bias: float32 [16], P('fsdp')
- grad_o_gain: float32 [256], P('fsdp')
- grad_w_out: float32 [4096, 2048], P('fsdp')
- grad_gain_mid: float32 [2048], P('fsdp')
- grad_w_gate_up: float32 [2048, 11264], P('fsdp')
- grad_w_down: float32 [5632, 2048], P('fsdp')
Inputs may be any that keep to these rules, and one draw needn't show every extreme that they name: `lengths`: one slot holds 256 valid tokens in every draw. `slot_owner`: each device holds exactly one slot.
All inputs are finite; a program needn't handle non-finite values.
Results may differ from a plain program's by a relative error of at most 0.017.
Values may be sent and summed in bfloat16 or wider, within the bound.
No kernel may reach another device: no remote copies, remote signals or barrier semaphores. Data moves between devices by JAX's collectives and lax.ppermute only.
A program may use at most 704 MiB of HBM per device.

v0:
```python
from functools import partial

import jax
import jax.numpy as jnp
from jax import lax
from jax.sharding import PartitionSpec as P

H = 16
DK = 128
DV = 256
FF = 5632
KCONV = 4
BLOCK = 64
TOK_DEV = 256
CONV = 8192


eps_norm = 1e-05
eps_unit = 1e-06
highest_precision = lax.Precision.HIGHEST


def rms_scale(rows_in, gain):
    return (
        rows_in * lax.rsqrt(jnp.mean(rows_in * rows_in, axis=-1, keepdims=True) + eps_norm) * gain
    )


def mixer_inputs(mixed, decay_pre, conv_weight, a_log, dt_bias):
    row_count = mixed.shape[0]
    padded = jnp.pad(mixed, ((KCONV - 1, 0), (0, 0)))
    convolved = conv_weight[0] * padded[0:row_count]
    for offset in range(1, KCONV):
        convolved = convolved + conv_weight[offset] * padded[offset : offset + row_count]
    active = jax.nn.silu(convolved)
    query_rows = active[:, : H * DK].reshape(row_count, H, DK)
    key_matrix_rows = active[:, H * DK : 2 * H * DK].reshape(row_count, H, DK)
    values = active[:, 2 * H * DK :]
    query_rows = (
        query_rows
        * lax.rsqrt(jnp.sum(query_rows * query_rows, axis=-1, keepdims=True) + eps_unit)
        * DK ** (-0.5)
    )
    key_matrix_rows = key_matrix_rows * lax.rsqrt(
        jnp.sum(key_matrix_rows * key_matrix_rows, axis=-1, keepdims=True) + eps_unit
    )
    beta_gate = jax.nn.sigmoid(decay_pre[:, H:])
    log_decay = -jnp.exp(a_log) * jax.nn.softplus(decay_pre[:, :H] + dt_bias)
    return (
        query_rows.reshape(row_count, H * DK),
        key_matrix_rows.reshape(row_count, H * DK),
        values,
        beta_gate,
        log_decay,
    )


def gated_output(mixer_out, gate_pre, o_gain):
    row_count = mixer_out.shape[0]
    normed = (
        mixer_out
        * lax.rsqrt(jnp.mean(mixer_out * mixer_out, axis=-1, keepdims=True) + eps_norm)
        * o_gain
    )
    return (normed * jax.nn.silu(gate_pre.reshape(row_count, H, DV))).reshape(row_count, H * DV)


def swiglu(gate_up):
    return jax.nn.silu(gate_up[:, :FF]) * gate_up[:, FF:]


def delta_block(carried_state, query_rows, key_matrix_rows, values, beta_gate, log_decay):
    length = query_rows.shape[1]
    positions = jnp.arange(length)
    on_or_below = positions[:, None] >= positions[None, :]
    strict = positions[:, None] > positions[None, :]
    cumulative = jnp.cumsum(log_decay, axis=1)
    spread = cumulative[:, :, None] - cumulative[:, None, :]
    fading = jnp.where(on_or_below, jnp.exp(jnp.where(on_or_below, spread, 0.0)), 0.0)
    similar = jnp.einsum(
        "hck,hdk->hcd", key_matrix_rows, key_matrix_rows, precision=highest_precision
    )
    system = jnp.eye(length, dtype=jnp.float32) + jnp.where(
        strict, beta_gate[:, :, None] * fading * similar, 0.0
    )
    state_growth = jnp.exp(cumulative)
    recalled_value = jnp.einsum(
        "uiw,uwt->uit", key_matrix_rows, carried_state, precision=highest_precision
    )
    right_side = beta_gate[:, :, None] * (values - state_growth[:, :, None] * recalled_value)
    state_update = jax.scipy.linalg.solve_triangular(
        system, right_side, lower=True, unit_diagonal=True
    )
    scores = (
        jnp.einsum("hck,hdk->hcd", query_rows, key_matrix_rows, precision=highest_precision)
        * fading
    )
    output_rows = state_growth[:, :, None] * jnp.einsum(
        "uiw,uwt->uit", query_rows, carried_state, precision=highest_precision
    )
    output_rows = output_rows + jnp.einsum(
        "hcd,hdv->hcv", scores, state_update, precision=highest_precision
    )
    decay_to_finish = jnp.exp(cumulative[:, -1:] - cumulative)
    carried_state = state_growth[:, -1][:, None, None] * carried_state + jnp.einsum(
        "szj,szg->sjg",
        key_matrix_rows,
        decay_to_finish[:, :, None] * state_update,
        precision=highest_precision,
    )
    return (carried_state, output_rows)


def mixer_core(
    query_rows, key_matrix_rows, values, beta_gate, log_decay, gate_pre, o_gain, live_blocks
):
    row_count = query_rows.shape[0]
    blocks = row_count // BLOCK

    def arrange(source, width):
        return source.reshape(blocks, BLOCK, H, width).transpose(0, 2, 1, 3)

    def arrange_heads(source):
        return source.reshape(blocks, BLOCK, H).transpose(0, 2, 1)

    def advance(carried_state, items):
        number, block_q, block_k, block_v, block_b, block_g = items
        return delta_block(carried_state, block_q, block_k, block_v, block_b, block_g)

    items = (
        jnp.arange(blocks, dtype=jnp.int32),
        arrange(query_rows, DK),
        arrange(key_matrix_rows, DK),
        arrange(values, DV),
        arrange_heads(beta_gate),
        arrange_heads(log_decay),
    )
    final_state, output_rows = lax.scan(advance, jnp.zeros((H, DK, DV), jnp.float32), items)
    mixer_out = output_rows.transpose(0, 2, 1, 3).reshape(row_count, H, DV)
    return gated_output(mixer_out, gate_pre, o_gain)


def rounded(source):
    return lax.optimization_barrier(source.astype(jnp.bfloat16)).astype(jnp.float32)


def column_term(left, right):
    return lax.dot_general(
        left, right, (((0,), (0,)), ((), ())), preferred_element_type=jnp.float32
    )


def local(
    tokens,
    cotangent,
    lengths,
    slot_owner,
    gain_in,
    w_proj,
    w_decay,
    conv_weight,
    a_log,
    dt_bias,
    o_gain,
    w_out,
    gain_mid,
    w_gate_up,
    w_down,
):
    device = lax.axis_index(("rep", "fsdp"))
    held_length = jnp.sum(jnp.where(slot_owner == device, lengths, 0))
    live_rows = (jnp.arange(TOK_DEV, dtype=jnp.int32) < held_length).astype(jnp.float32)[:, None]
    live_blocks = (held_length + BLOCK - 1) // BLOCK
    mixer_set = (
        lax.all_gather(w_proj, "fsdp", axis=0, tiled=True),
        lax.all_gather(w_decay, "fsdp", axis=0, tiled=True),
        lax.all_gather(gain_in, "fsdp", axis=0, tiled=True),
        lax.all_gather(conv_weight, "fsdp", axis=1, tiled=True),
        lax.all_gather(a_log, "fsdp", axis=0, tiled=True),
        lax.all_gather(dt_bias, "fsdp", axis=0, tiled=True),
        lax.all_gather(o_gain, "fsdp", axis=0, tiled=True),
        lax.all_gather(w_out, "fsdp", axis=0, tiled=True),
    )
    proj_full, decay_full, gain_in_full, conv_full, alog_full, bias_full, ogain_full, out_full = (
        mixer_set
    )
    rows_f32 = tokens.astype(jnp.float32)
    normed32, pull_in = jax.vjp(rms_scale, rows_f32, gain_in_full.astype(jnp.float32))
    normed_in = normed32.astype(jnp.bfloat16)
    projected = jnp.dot(normed_in, proj_full, preferred_element_type=jnp.float32)
    decay_pre = jnp.dot(normed_in, decay_full, preferred_element_type=jnp.float32)
    inputs_out, pull_front = jax.vjp(
        mixer_inputs,
        projected[:, :CONV],
        decay_pre,
        conv_full.astype(jnp.float32),
        alog_full.astype(jnp.float32),
        bias_full.astype(jnp.float32),
    )
    query_rows, key_matrix_rows, values, beta_gate, log_decay = inputs_out
    gated32, pull_core = jax.vjp(
        partial(mixer_core, live_blocks=live_blocks),
        rounded(query_rows),
        rounded(key_matrix_rows),
        rounded(values),
        beta_gate,
        log_decay,
        projected[:, CONV:],
        ogain_full.astype(jnp.float32),
    )
    gated = gated32.astype(jnp.bfloat16)
    branch = jnp.dot(gated, out_full, preferred_element_type=jnp.float32)
    ffn_set = (
        lax.all_gather(gain_mid, "fsdp", axis=0, tiled=True),
        lax.all_gather(w_gate_up, "fsdp", axis=0, tiled=True),
        lax.all_gather(w_down, "fsdp", axis=0, tiled=True),
    )
    gain_mid_full, up_full, down_full = ffn_set

    def middle_part(branch_in, rows_in, gain):
        middle = rows_in + live_rows * branch_in
        return (middle, rms_scale(middle, gain))

    (middle, normed_mid32), pull_mid = jax.vjp(
        middle_part, branch, rows_f32, gain_mid_full.astype(jnp.float32)
    )
    normed_mid = normed_mid32.astype(jnp.bfloat16)
    gate_up = jnp.dot(normed_mid, up_full, preferred_element_type=jnp.float32)
    hidden32, pull_act = jax.vjp(swiglu, gate_up)
    hidden = hidden32.astype(jnp.bfloat16)
    ffn_branch = jnp.dot(hidden, down_full, preferred_element_type=jnp.float32)
    output = (middle + live_rows * ffn_branch).astype(jnp.bfloat16)
    ffn_back = (
        lax.all_gather(gain_mid, "fsdp", axis=0, tiled=True),
        lax.all_gather(w_gate_up, "fsdp", axis=0, tiled=True),
        lax.all_gather(w_down, "fsdp", axis=0, tiled=True),
    )
    up_back, down_back = (ffn_back[1], ffn_back[2])
    seeded = cotangent.astype(jnp.float32) * live_rows
    d_ffn = (live_rows * seeded).astype(jnp.bfloat16)
    grad_down = lax.psum_scatter(
        column_term(hidden, d_ffn).astype(jnp.bfloat16), "fsdp", scatter_dimension=0, tiled=True
    )
    d_hidden = jnp.dot(d_ffn, down_back.T, preferred_element_type=jnp.float32)
    d_gate_up = pull_act(d_hidden)[0].astype(jnp.bfloat16)
    grad_up = lax.psum_scatter(
        column_term(normed_mid, d_gate_up).astype(jnp.bfloat16),
        "fsdp",
        scatter_dimension=0,
        tiled=True,
    )
    d_normed_mid = jnp.dot(d_gate_up, up_back.T, preferred_element_type=jnp.float32)
    d_branch32, d_rows_mid, d_gain_mid = pull_mid((seeded, d_normed_mid))
    d_branch = d_branch32.astype(jnp.bfloat16)
    mixer_back = (
        lax.all_gather(w_proj, "fsdp", axis=0, tiled=True),
        lax.all_gather(w_decay, "fsdp", axis=0, tiled=True),
        lax.all_gather(w_out, "fsdp", axis=0, tiled=True),
    )
    proj_back, decay_back, out_back = mixer_back
    grad_out = lax.psum_scatter(
        column_term(gated, d_branch).astype(jnp.bfloat16), "fsdp", scatter_dimension=0, tiled=True
    )
    d_gated = jnp.dot(d_branch, out_back.T, preferred_element_type=jnp.float32)
    d_queries, d_keys, d_values, d_beta, d_decay, d_gate_pre, d_ogain = pull_core(d_gated)
    d_mixed, d_decay_pre32, d_conv, d_alog, d_bias = pull_front(
        (d_queries, d_keys, d_values, d_beta, d_decay)
    )
    d_projected = jnp.concatenate([d_mixed, d_gate_pre], axis=1).astype(jnp.bfloat16)
    d_decay_pre = d_decay_pre32.astype(jnp.bfloat16)
    grad_proj = lax.psum_scatter(
        column_term(normed_in, d_projected).astype(jnp.bfloat16),
        "fsdp",
        scatter_dimension=0,
        tiled=True,
    )
    decay_term = lax.dot_general(
        normed_in, d_decay_pre, (((0,), (0,)), ((), ())), preferred_element_type=jnp.float32
    )
    d_normed_in = jnp.dot(d_projected, proj_back.T, preferred_element_type=jnp.float32)
    d_normed_in = d_normed_in + jnp.dot(
        d_decay_pre, decay_back.T, preferred_element_type=jnp.float32
    )
    d_rows_in, d_gain_in = pull_in(d_normed_in)
    grad_tokens = d_rows_mid + d_rows_in
    small_set = (
        lax.psum_scatter(d_gain_in, "fsdp", scatter_dimension=0, tiled=True),
        lax.psum_scatter(decay_term, "fsdp", scatter_dimension=0, tiled=True),
        lax.psum_scatter(d_conv, "fsdp", scatter_dimension=1, tiled=True),
        lax.psum_scatter(d_alog, "fsdp", scatter_dimension=0, tiled=True),
        lax.psum_scatter(d_bias, "fsdp", scatter_dimension=0, tiled=True),
        lax.psum_scatter(d_ogain, "fsdp", scatter_dimension=0, tiled=True),
        lax.psum_scatter(d_gain_mid, "fsdp", scatter_dimension=0, tiled=True),
    )
    s_gain_in, s_decay, s_conv, s_alog, s_bias, s_ogain, s_gain_mid = small_set
    summed = (
        lax.psum(s_gain_in.astype(jnp.bfloat16), "rep").astype(jnp.float32),
        lax.psum(grad_proj, "rep").astype(jnp.float32),
        lax.psum(s_decay.astype(jnp.bfloat16), "rep").astype(jnp.float32),
        lax.psum(s_conv.astype(jnp.bfloat16), "rep").astype(jnp.float32),
        lax.psum(s_alog.astype(jnp.bfloat16), "rep").astype(jnp.float32),
        lax.psum(s_bias.astype(jnp.bfloat16), "rep").astype(jnp.float32),
        lax.psum(s_ogain.astype(jnp.bfloat16), "rep").astype(jnp.float32),
        lax.psum(grad_out, "rep").astype(jnp.float32),
        lax.psum(s_gain_mid.astype(jnp.bfloat16), "rep").astype(jnp.float32),
        lax.psum(grad_up, "rep").astype(jnp.float32),
        lax.psum(grad_down, "rep").astype(jnp.float32),
    )
    return (
        output,
        grad_tokens,
        summed[0],
        summed[1],
        summed[2],
        summed[3],
        summed[4],
        summed[5],
        summed[6],
        summed[7],
        summed[8],
        summed[9],
        summed[10],
    )


def solution(mesh):
    in_specs = (
        P(("rep", "fsdp"), None),
        P(("rep", "fsdp"), None),
        P(),
        P(),
        P("fsdp"),
        P("fsdp", None),
        P("fsdp", None),
        P(None, "fsdp"),
        P("fsdp"),
        P("fsdp"),
        P("fsdp"),
        P("fsdp", None),
        P("fsdp"),
        P("fsdp", None),
        P("fsdp", None),
    )
    out_specs = (
        P(("rep", "fsdp"), None),
        P(("rep", "fsdp"), None),
        P("fsdp"),
        P("fsdp", None),
        P("fsdp", None),
        P(None, "fsdp"),
        P("fsdp"),
        P("fsdp"),
        P("fsdp"),
        P("fsdp", None),
        P("fsdp"),
        P("fsdp", None),
        P("fsdp", None),
    )
    return jax.shard_map(local, mesh=mesh, in_specs=in_specs, out_specs=out_specs, check_vma=False)
```

profile of v0, /device:TPU:0, one launch (start us, length us, event | category | flops | bytes accessed | tf_op | source)
XLA Modules:
  0.0 2570.9 jit_solution(15023497366268604852)
XLA Ops:
  12.9 15.1 all-reduce.29
  28.1 7.9 all-gather
  36.1 10.3 all_gather.40
  48.0 7.9 all-gather.1
  56.0 9.3 all_gather.42
  66.7 178.8 %all-gather.7.cloned.1.call-done = bf16[2048,12288]{1,0:T(8,128)(2,1)} async-done(((bf16[256,12288]{1,0:T(8,128)(2,1)}), bf16[2048,12288]{1,0:T(8,128)(2,1)}) %all-gather.7.cloned.1.call-update) | async-done | bytes 50331664 | tf_op jit(solution)/shard_map/all_gather | solution.py:175
  245.5 26.7 %fusion.231 = f32[256,12288]{1,0:T(8,128)} fusion(bf16[2048,12288]{1,0:T(8,128)(2,1)} %all-gather.7.cloned.1.call-done, bf16[256,2048]{1,0:T(8,128)(2,1)S(1)} %copy-done.22, f32[2048]{0:T(1024)S(1)} %bitcast.565, f32[256]{0:T(256)S(1)} %fusion.217), kind=kOutput, calls=%fused_computation.382 | convolution fusion | flops 12886999040 | bytes 63972352 | tf_op jit(solution)/shard_map/dot_general | solution.py:190
  272.3 7.7 slice.119
  280.0 21.3 fusion.184
  316.6 4.4 copy.189
  340.0 433.5 %while.85 = (s32[]{:T(128)}, f32[16,128,256]{2,1,0:T(8,128)S(1)}, f32[4,16,64,256]{3,2,1,0:T(8,128)}, f32[4,16,64,64]{3,2,1,0:T(8,128)}, f32[4,16,64,64]{3,2,1,0...) while((s32[]{:T(128)}, f32[16,128,256]{2,1,0:T(8,128)S(1)}, ...), condition=%wide.region_6.7_spmd.clone.clone, body=%wide.region_4.6_spmd.clone.clone.sunk | while | flops 1819170816 | bytes 50434820 | solution.py:138
  345.9 5.2 bitcast_dynamic-update-slice_fusion.20
  354.7 79.4 %custom-call.43 = f32[16,1,64,64]{2,3,1,0:T(8,128)S(1)} custom-call(f32[16,1,64,64]{3,2,1,0:T(8,128)} %add_bitcast_fusion.4), custom_call_target="InvertDiagBlocksLowerTriangular" | custom-call | tf_op jit(solution)/shard_map/jvp()/while/body/eval_jaxpr/jit(_solve_triangular)/vmap()/triangular_solve | solution.py:91
  434.1 4.5 bitcast_dynamic-update-slice_fusion.21
  454.7 4.5 bitcast_dynamic-update-slice_fusion.20
  462.6 79.4 %custom-call.43 = f32[16,1,64,64]{2,3,1,0:T(8,128)S(1)} custom-call(f32[16,1,64,64]{3,2,1,0:T(8,128)} %add_bitcast_fusion.4), custom_call_target="InvertDiagBlocksLowerTriangular" | custom-call | tf_op jit(solution)/shard_map/jvp()/while/body/eval_jaxpr/jit(_solve_triangular)/vmap()/triangular_solve | solution.py:91
  542.0 4.5 bitcast_dynamic-update-slice_fusion.21
  549.3 3.9 bitcast_dynamic-update-slice_fusion.23
  562.6 4.9 bitcast_dynamic-update-slice_fusion.20
  571.2 79.4 %custom-call.43 = f32[16,1,64,64]{2,3,1,0:T(8,128)S(1)} custom-call(f32[16,1,64,64]{3,2,1,0:T(8,128)} %add_bitcast_fusion.4), custom_call_target="InvertDiagBlocksLowerTriangular" | custom-call | tf_op jit(solution)/shard_map/jvp()/while/body/eval_jaxpr/jit(_solve_triangular)/vmap()/triangular_solve | solution.py:91
  650.6 4.5 bitcast_dynamic-update-slice_fusion.21
  671.2 4.5 bitcast_dynamic-update-slice_fusion.20
  679.2 79.4 %custom-call.43 = f32[16,1,64,64]{2,3,1,0:T(8,128)S(1)} custom-call(f32[16,1,64,64]{3,2,1,0:T(8,128)} %add_bitcast_fusion.4), custom_call_target="InvertDiagBlocksLowerTriangular" | custom-call | tf_op jit(solution)/shard_map/jvp()/while/body/eval_jaxpr/jit(_solve_triangular)/vmap()/triangular_solve | solution.py:91
  758.6 4.5 bitcast_dynamic-update-slice_fusion.21
  766.0 3.9 bitcast_dynamic-update-slice_fusion.23
  773.6 4.6 copy.90
  778.3 5.8 copy.159
  792.0 4.0 multiply_convert_fusion.1
  796.0 10.6 multiply_reduce_fusion.11
  806.7 24.8 fusion.228
  831.4 27.4 %fusion.206 = (f32[256,5632]{1,0:T(8,128)}, f32[256,5632]{1,0:T(8,128)}, bf16[256,5632]{1,0:T(8,128)(2,1)}) fusion(f32[256,11264]{1,0:T(8,128)} %fusion.228, bf16[5632,2048]{1,0:T(8,128)(2,1)} %all-gather.13.cloned.1.call-done, bf16[256,2048]{1,0:T(8,128)(2,1)S(1)} %copy-done.37, f32[256]{0:T(256)S(1)} %compare_convert_fusion), kind=kOutput, calls=%fused_computation.322 | convolution fusion | flops 5927862272 | bytes 50070528 | tf_op jit(solution)/shard_map/dot_general | solution.py:244
  858.8 24.5 multiply_reduce_fusion.7
  886.2 10.6 convolution_convert_fusion.3
  898.7 16.2 convolution_convert_fusion.2
  916.9 25.3 convolution_convert_fusion.1
  942.6 13.5 fusion.227
  956.1 8.9 fusion.239
  969.5 6.0 multiply_reduce_fusion.4
  983.8 507.5 %while.86 = (s32[]{:T(128)}, f32[16,128,256]{2,1,0:T(8,128)S(1)}, f32[4,16,64,128]{3,1,2,0:T(8,128)}, f32[4,16,64,128]{3,1,2,0:T(8,128)}, f32[4,16,64,256]{3,2,1...) while((s32[]{:T(128)}, f32[16,128,256]{2,1,0:T(8,128)S(1)}, ...), condition=%wide.region_22.23_spmd.clone.clone, body=%wide.region_11.22_spmd.clone.clone.sunk | while | flops 3686482944 | bytes 151007488 | solution.py:138
  997.0 80.0 %custom-call.44 = f32[16,1,64,64]{2,3,1,0:T(8,128)} custom-call(f32[16,1,64,64]{3,2,1,0:T(8,128)} %add_bitcast_fusion.5), custom_call_target="InvertDiagBlocksLowerTriangular" | custom-call | tf_op jit(solution)/shard_map/transpose(jvp())/while/body/eval_jaxpr/jit(_solve_triangular)/vmap()/triangular_solve | solution.py:91
  1084.1 4.1 fusion.350
  1123.0 80.0 %custom-call.44 = f32[16,1,64,64]{2,3,1,0:T(8,128)} custom-call(f32[16,1,64,64]{3,2,1,0:T(8,128)} %add_bitcast_fusion.5), custom_call_target="InvertDiagBlocksLowerTriangular" | custom-call | tf_op jit(solution)/shard_map/transpose(jvp())/while/body/eval_jaxpr/jit(_solve_triangular)/vmap()/triangular_solve | solution.py:91
  1205.4 4.6 fusion.344
  1211.9 5.0 fusion.350
  1252.6 80.0 %custom-call.44 = f32[16,1,64,64]{2,3,1,0:T(8,128)} custom-call(f32[16,1,64,64]{3,2,1,0:T(8,128)} %add_bitcast_fusion.5), custom_call_target="InvertDiagBlocksLowerTriangular" | custom-call | tf_op jit(solution)/shard_map/transpose(jvp())/while/body/eval_jaxpr/jit(_solve_triangular)/vmap()/triangular_solve | solution.py:91
  1339.8 4.1 fusion.350
  1378.7 80.0 %custom-call.44 = f32[16,1,64,64]{2,3,1,0:T(8,128)} custom-call(f32[16,1,64,64]{3,2,1,0:T(8,128)} %add_bitcast_fusion.5), custom_call_target="InvertDiagBlocksLowerTriangular" | custom-call | tf_op jit(solution)/shard_map/transpose(jvp())/while/body/eval_jaxpr/jit(_solve_triangular)/vmap()/triangular_solve | solution.py:91
  1491.3 4.6 copy.97
  1495.9 5.9 copy.164
  1510.9 13.6 add_add_fusion.4
  1524.6 13.6 multiply_reduce_fusion.2
  1538.2 11.5 broadcast_multiply_fusion
  1549.8 12.4 fusion.183
  1562.2 22.6 convolution_convert_fusion
  1589.6 281.8 %reduce-scatter.21.cloned.1.call-done = bf16[256,12288]{1,0:T(8,128)(2,1)} async-done(((bf16[2048,12288]{1,0:T(8,128)(2,1)}), bf16[256,12288]{1,0:T(8,128)(2,1)}) %reduce-scatter.21.cloned.1.call-update) | async-done | bytes 6291472
  1873.4 23.7 fusion.192
  1897.2 4.2 fusion.198
  1901.3 23.8 all-reduce.28
  1929.3 12.0 fusion.194
  1942.5 21.8 reduce-scatter.13.cloned.1.call-done
  1965.1 22.2 all-reduce.30
  1991.2 550.6 %all-reduce.34.cloned.1.call-done = (bf16[256,12288]{1,0:T(8,128)(2,1)}, bf16[512,2048]{1,0:T(8,128)(2,1)}, bf16[256,11264]{1,0:T(8,128)(2,1)}, bf16[704,2048]{1,0:T(8,128)(2,1)}) async-done(((bf16[256,12288]{1,0:T(8,128)(2,1)}, bf16[512,2048]{1,0:T(8,128)(2,1)}, bf16[256,11264]{1,0:T(8,128)(2,1)}, bf16[704,2048]{1,0:T(8,128)(2,1)}), (bf16[256,12288]{1,0:T(8,128)(2,1)}, bf16[512,2048]{1,0:T(8,128)(2,1)}, ...) | async-done | bytes 17039376 | tf_op jit(solution)/shard_map/psum | solution.py:298
  2541.8 9.2 convert_element_type.171
  2555.1 5.8 convert_element_type.187
  (627 shorter events, 339.1 us)
Async XLA Ops:
  7.2 238.3 %all-gather.7.cloned.1.call-start = ((), (), s32[]{:S(2)}) async-start(), calls=%async_computation.6 | async-start | bytes 56623104 | tf_op jit(solution)/shard_map/all_gather | solution.py:175
  7.9 788.0 %all-gather.9.cloned.1.call-start = ((), (), s32[]{:S(2)}) async-start(), calls=%async_computation.7 | async-start | bytes 18874368 | tf_op jit(solution)/shard_map/all_gather | solution.py:182
  8.7 798.0 %all-gather.11.cloned.1.call-start = ((), (), s32[]{:S(2)}) async-start(), calls=%async_computation.8 | async-start | bytes 51904512 | tf_op jit(solution)/shard_map/all_gather | solution.py:215
  9.4 18.7 copy-start.90
  9.5 26.6 %copy-start.70 = (bf16[256,32]{0,1:T(8,128)(2,1)S(1)}, bf16[256,32]{0,1:T(8,128)(2,1)}, u32[]{:S(2)}) copy-start(bf16[256,32]{0,1:T(8,128)(2,1)} %param.25) | copy-start | bytes 49156
  9.5 36.9 %copy-start.22 = (bf16[256,2048]{1,0:T(8,128)(2,1)S(1)}, bf16[256,2048]{1,0:T(8,128)(2,1)}, u32[]{:S(2)}) copy-start(bf16[256,2048]{1,0:T(8,128)(2,1)} %param.19) | copy-start | bytes 3145732
  9.5 38.5 %copy-start.91 = (bf16[256]{0:T(256)(128)(2,1)S(1)}, bf16[256]{0:T(256)(128)(2,1)}, u32[]{:S(2)}) copy-start(bf16[256]{0:T(256)(128)(2,1)} %param.31) | copy-start | bytes 1540
  9.5 46.5 %copy-start.77 = (bf16[4,1024]{1,0:T(4,128)(2,1)S(1)}, bf16[4,1024]{1,0:T(4,128)(2,1)}, u32[]{:S(2)}) copy-start(bf16[4,1024]{1,0:T(4,128)(2,1)} %param.26) | copy-start | bytes 24580
  9.5 55.8 %copy-start.85 = (s32[32]{0:T(128)S(1)}, s32[32]{0:T(128)}, u32[]{:S(2)}) copy-start(s32[32]{0:T(128)} %param.21) | copy-start | bytes 388
  9.5 55.7 %copy-start.86 = (s32[32]{0:T(128)S(1)}, s32[32]{0:T(128)}, u32[]{:S(2)}) copy-start(s32[32]{0:T(128)} %param.22) | copy-start | bytes 388
  9.5 821.9 %all-gather.13.cloned.1.call-start = ((), (), s32[]{:S(2)}) async-start(), calls=%async_computation.9 | async-start | bytes 25952256 | tf_op jit(solution)/shard_map/all_gather | solution.py:216
  10.1 1579.4 %reduce-scatter.15.cloned.1.call-start = ((), (), s32[]{:S(2)}) async-start(), calls=%async_computation.11 | async-start | bytes 18874368 | tf_op jit(solution)/shard_map/reduce_scatter | solution.py:261
  28.1 18.7 copy-start.92
  28.1 18.7 copy-start.73
  36.1 236.2 %copy-start.46 = (f32[8,1,256]{2,1,0:T(1,128)}, f32[8,1,256]{2,1,0:T(1,128)S(1)}, u32[]{:S(2)}) copy-start(f32[8,1,256]{2,1,0:T(1,128)S(1)} %convert_element_type.190) | copy-start | bytes 24580
  36.1 236.2 %copy-start.80 = (f32[16]{0:T(128)}, f32[16]{0:T(128)S(1)}, u32[]{:S(2)}) copy-start(f32[16]{0:T(128)S(1)} %convert_element_type.152) | copy-start | bytes 196
  46.7 225.5 %copy-start.54 = (f32[256]{0:T(256)}, f32[256]{0:T(256)S(1)}, u32[]{:S(2)}) copy-start(f32[256]{0:T(256)S(1)} %fusion.217) | copy-start | bytes 3076
  47.7 18.8 copy-start.67
  66.5 876.0 %copy-start.71 = (f32[256]{0:T(256)}, f32[256]{0:T(256)S(1)}, u32[]{:S(2)}) copy-start(f32[256]{0:T(256)S(1)} %compare_convert_fusion) | copy-start | bytes 3076
  66.7 213.2 %copy-start.56 = (f32[1,8192]{1,0:T(1,128)}, f32[1,8192]{1,0:T(1,128)S(1)}, u32[]{:S(2)}) copy-start(f32[1,8192]{1,0:T(1,128)S(1)} %get-tuple-element.1894) | copy-start | bytes 98308
  66.7 213.2 %copy-start.58 = (f32[1,8192]{1,0:T(1,128)}, f32[1,8192]{1,0:T(1,128)S(1)}, u32[]{:S(2)}) copy-start(f32[1,8192]{1,0:T(1,128)S(1)} %get-tuple-element.1895) | copy-start | bytes 98308
  66.7 213.2 %copy-start.60 = (f32[1,8192]{1,0:T(1,128)}, f32[1,8192]{1,0:T(1,128)S(1)}, u32[]{:S(2)}) copy-start(f32[1,8192]{1,0:T(1,128)S(1)} %get-tuple-element.1896) | copy-start | bytes 98308
  66.7 213.2 %copy-start.62 = (f32[1,8192]{1,0:T(1,128)}, f32[1,8192]{1,0:T(1,128)S(1)}, u32[]{:S(2)}) copy-start(f32[1,8192]{1,0:T(1,128)S(1)} %get-tuple-element.1897) | copy-start | bytes 98308
  778.2 5.9 copy-start.3
  786.1 5.9 copy-start.9
  795.9 10.7 copy-start.27
  806.6 24.8 copy-start.37
  831.4 27.4 %copy-start.28 = (f32[256,2048]{1,0:T(8,128)S(1)}, f32[256,2048]{1,0:T(8,128)}, u32[]{:S(2)}) copy-start(f32[256,2048]{1,0:T(8,128)} %get-tuple-element.1905) | copy-start | bytes 6291460
  886.2 10.7 copy-start.12
  896.9 692.6 %reduce-scatter.17.cloned.1.call-start = ((), (), s32[]{:S(2)}) async-start(), calls=%async_computation.12 | async-start | bytes 25952256 | tf_op jit(solution)/shard_map/reduce_scatter | solution.py:241
  915.0 674.6 %reduce-scatter.23.cloned.1.call-start = ((), (), s32[]{:S(2)}) async-start(), calls=%async_computation.15 | async-start | bytes 51904512
  942.3 929.1 %reduce-scatter.21.cloned.1.call-start = ((), (), s32[]{:S(2)}) async-start(), calls=%async_computation.14 | async-start | bytes 56623104
  969.5 6.0 copy-start.65
  1083.0 6.0 copy-start.2
  1089.0 8.5 slice-start
  1205.4 5.5 copy-start.11
  1210.8 6.8 copy-start.2
  1217.7 6.0 copy-start.1
  1217.7 9.7 slice-start
  1338.8 6.0 copy-start.2
  1344.7 8.5 slice-start
  1464.4 5.6 copy-start.2
  1470.0 8.5 slice-start
  1495.9 5.9 copy-start.17
  1495.9 5.9 copy-start.21
  1505.2 5.8 copy-start.15
  1510.9 13.6 slice-start.2
  1510.9 13.6 slice-start.3
  1524.5 13.7 copy-start.57
  1524.5 13.7 copy-start.59
  1524.6 13.7 copy-start.61
  1524.6 13.7 copy-start.63
  1549.8 12.4 copy-start.24
  1549.8 12.4 copy-start.31
  1549.8 12.4 copy-start.47
  1549.8 12.4 copy-start.55
  1584.9 356.4 %reduce-scatter.19.cloned.1.call-start = ((), (), s32[]{:S(2)}) async-start(), calls=%async_computation.13 | async-start | bytes 4718592
  1588.2 376.1 %reduce-scatter.13.cloned.1.call-start = ((), (), s32[]{:S(2)}) async-start(), calls=%async_computation.10 | async-start | bytes 294912 | tf_op jit(solution)/shard_map/reduce_scatter | solution.py:288
  1589.4 952.3 %all-reduce.34.cloned.1.call-start = ((), (), s32[]{:S(2)}) async-start(), calls=%async_computation.16 | async-start | bytes 34078720 | tf_op jit(solution)/shard_map/psum | solution.py:298
  1873.4 23.8 copy-start.51
  1897.1 28.4 %copy-start.76 = (f32[256]{0:T(256)S(1)}, f32[256]{0:T(256)}, u32[]{:S(2)}) copy-start(f32[256]{0:T(256)} %copy-done.75) | copy-start | bytes 3076
  1897.1 28.4 %copy-start.13 = (f32[256,2048]{1,0:T(8,128)S(1)}, f32[256,2048]{1,0:T(8,128)}, u32[]{:S(2)}) copy-start(f32[256,2048]{1,0:T(8,128)} %copy-done.12) | copy-start | bytes 6291460
  2541.8 9.2 copy-start.41
  2555.1 5.8 copy-start.38
  (80 other events, 263.1 us)
Sparse Core Ops, SparseCore 0:
  9.9 235.5 all-gather.6
  247.4 89.8 all-gather.8
  339.2 214.8 all-gather.10
  555.9 116.7 all-gather.12
  897.0 115.8 reduce-scatter.14
  1016.4 146.0 reduce-scatter.16
  1166.2 264.5 reduce-scatter.22
  1585.0 286.3 reduce-scatter.20
  1875.3 51.5 reduce-scatter.18
  1930.6 33.6 reduce-scatter.12
  1967.3 574.4 all-reduce.33
where the time goes:
time: 2580 us; the launch traced here: 2570 us
  waiting for transfers between devices  1040 us (40%)
  other arithmetic  820 us (32%)
  matrix products  472 us (18%)
  local copies, waits for them, and re-layouts  125 us (5%)
  blocking collectives  96.5 us (4%)
    another operation x36, other arithmetic, delta_block(): jax.scipy.linalg.solve_triangular(system, right_side, lower=True, unit_di...  650 us
    psum x1, waiting for transfers between devices, local(): lax.psum(grad_proj, 'rep').astype(jnp.float32)  551 us
    unnamed x14, waiting for transfers between devices  285 us
    all_gather x1, waiting for transfers between devices, local(): lax.all_gather(w_proj, 'fsdp', axis=0, tiled=True)  179 us
    dot_general x4, matrix products, column_term(): lax.dot_general(left, right, (((0,), (0,)), ((), ())), preferred_element_...  74.8 us
  transfers between devices with their start and end apart: 11, of which 4 were waited for; matrix products, arithmetic and copies ran while one was open for 51% of the time, Pallas kernels for 0%

commit v1 on v0

v1 whole, which is shorter than its diff:
```python
from functools import partial

import jax
import jax.numpy as jnp
from jax import lax
from jax.experimental import pallas as pl
from jax.experimental.pallas import tpu as pltpu
from jax.sharding import PartitionSpec as P

H = 16
DK = 128
DV = 256
KCONV = 4
BLOCK = 64
TOK_DEV = 256
eps_norm = 1e-05
eps_unit = 1e-06
bf16 = jnp.bfloat16
f32 = jnp.float32


def mm(a, b):
    return lax.dot_general(
        a.astype(bf16), b.astype(bf16), (((1,), (0,)), ((), ())), preferred_element_type=f32
    )


def mm_nt(a, b):
    return lax.dot_general(
        a.astype(bf16), b.astype(bf16), (((1,), (1,)), ((), ())), preferred_element_type=f32
    )


def mm_tn(a, b):
    return lax.dot_general(
        a.astype(bf16), b.astype(bf16), (((0,), (0,)), ((), ())), preferred_element_type=f32
    )


def mm_exact(a, b):
    return lax.dot_general(
        a, b, (((1,), (0,)), ((), ())), precision=lax.Precision.HIGHEST, preferred_element_type=f32
    )


def silu(v):
    return v * jax.nn.sigmoid(v)


def shifted_down(x, s):
    if s == 0:
        return x
    row = lax.broadcasted_iota(jnp.int32, x.shape, 0)
    return jnp.where(row >= s, pltpu.roll(x, s, 0), 0.0)


def shifted_up(x, s):
    if s == 0:
        return x
    n = x.shape[0]
    row = lax.broadcasted_iota(jnp.int32, x.shape, 0)
    return jnp.where(row < n - s, pltpu.roll(x, n - s, 0), 0.0)


def conv_forward(mixed, weight):
    out = weight[KCONV - 1 : KCONV, :] * mixed
    for s in range(1, KCONV):
        out = out + weight[KCONV - 1 - s : KCONV - s, :] * shifted_down(mixed, s)
    return out


def conv_backward(d_conv, mixed, weight):
    d_mixed = weight[KCONV - 1 : KCONV, :] * d_conv
    rows = [None] * KCONV
    rows[KCONV - 1] = jnp.sum(d_conv * mixed, axis=0, keepdims=True)
    for s in range(1, KCONV):
        up = shifted_up(d_conv, s)
        d_mixed = d_mixed + weight[KCONV - 1 - s : KCONV - s, :] * up
        rows[KCONV - 1 - s] = jnp.sum(up * mixed, axis=0, keepdims=True)
    return d_mixed, jnp.concatenate(rows, axis=0)


def block_masks(n):
    i = lax.broadcasted_iota(jnp.int32, (n, n), 0)
    j = lax.broadcasted_iota(jnp.int32, (n, n), 1)
    x = i ^ j
    same = x < BLOCK
    return x, i > j, jnp.logical_and(same, i >= j), jnp.logical_and(same, i > j), same


def decay_parts(dec, alog_row, bias_row):
    pre = dec + bias_row
    softplus = jnp.maximum(pre, 0.0) + jnp.log1p(jnp.exp(-jnp.abs(pre)))
    log_decay = -jnp.exp(alog_row) * softplus
    n = dec.shape[0]
    i = lax.broadcasted_iota(jnp.int32, (n, n), 0)
    j = lax.broadcasted_iota(jnp.int32, (n, n), 1)
    same = (i ^ j) < BLOCK
    lower = jnp.where(jnp.logical_and(same, i >= j), 1.0, 0.0)
    whole = jnp.where(same, 1.0, 0.0)
    running = mm_exact(lower, log_decay)
    total = mm_exact(whole, log_decay)
    return pre, log_decay, running, total


def lane_of(x, h):
    lane = lax.broadcasted_iota(jnp.int32, x.shape, 1)
    return jnp.sum(jnp.where(lane == h, x, 0.0), axis=1, keepdims=True)


def row_of(x, h):
    row = lax.broadcasted_iota(jnp.int32, x.shape, 0)
    return jnp.sum(jnp.where(row == h, x, 0.0), axis=0, keepdims=True)


def unit_rows(a, scale):
    r = lax.rsqrt(jnp.sum(a * a, axis=1, keepdims=True) + eps_unit)
    return a * r * scale, r


def inverse_blocks(lowers, x, below):
    eye = jnp.where(x == 0, 1.0, 0.0)
    inv = [eye - jnp.where(x == 1, low, 0.0) for low in lowers]
    level = 1
    while (2 << level) <= BLOCK:
        pick = lax.shift_right_logical(x, level) == 1
        half = [mm(jnp.where(pick, low, 0.0), t) for low, t in zip(lowers, inv)]
        inv = [t - mm(t, u) for t, u in zip(inv, half)]
        level += 1
    return inv


def forward_kernel(
    hl,
    pair,
    q_ref,
    k_ref,
    v_ref,
    g_ref,
    dec_ref,
    cq_ref,
    ck_ref,
    cv_ref,
    head_ref,
    gain_ref,
    gated_ref,
    o_ref,
    u_ref,
    w_ref,
    inv_ref,
    s_ref,
):
    p = pl.program_id(0)
    n = TOK_DEV
    blocks = n // BLOCK
    x, below, on_below, strict, same = block_masks(n)
    dec = dec_ref[...]
    pre, log_decay, running, total = decay_parts(dec, head_ref[0:1, :], head_ref[1:2, :])
    running_t = running.T
    heads = range(pair)
    q = silu(conv_forward(q_ref[...], cq_ref[...]))
    k = silu(conv_forward(k_ref[...], ck_ref[...]))
    v = silu(conv_forward(v_ref[...], cv_ref[...])).astype(bf16)
    qn, kn, vn, beta, b, tot, fade, low, score = [], [], [], [], [], [], [], [], []
    for i in heads:
        h = p * pair + i
        qn.append(unit_rows(q[:, i * DK : (i + 1) * DK], DK**-0.5)[0].astype(bf16))
        kn.append(unit_rows(k[:, i * DK : (i + 1) * DK], 1.0)[0].astype(bf16))
        vn.append(v[:, i * DV : (i + 1) * DV])
        beta.append(jax.nn.sigmoid(lane_of(dec, hl + h)))
        b.append(lane_of(running, h))
        tot.append(lane_of(total, h))
        d = jnp.where(on_below, jnp.exp(jnp.where(on_below, b[i] - row_of(running_t, h), 0.0)), 0.0)
        both = mm_nt(jnp.concatenate([kn[i], qn[i]], axis=0), kn[i])
        low.append(jnp.where(strict, beta[i] * d * both[:n], 0.0))
        score.append((both[n:] * d).astype(bf16))
    inv = inverse_blocks(low, x, below)
    e = [jnp.exp(b[i]) for i in heads]
    fin = [jnp.exp(tot[i] - b[i]) for i in heads]
    grow = [jnp.exp(tot[i]) for i in heads]
    inv = [t.astype(bf16) for t in inv]
    right = [
        jnp.concatenate(
            [beta[i] * vn[i].astype(f32), (beta[i] * e[i]) * kn[i].astype(f32)], axis=1
        ).astype(bf16)
        for i in heads
    ]
    uw = [mm(inv[i], right[i]) for i in heads]
    w = [uw[i][:, DV:].astype(bf16) for i in heads]
    state = [jnp.zeros((DK, DV), f32) for i in heads]
    u_parts = [[] for i in heads]
    o_parts = [[] for i in heads]
    for c in range(blocks):
        lo, hi = c * BLOCK, (c + 1) * BLOCK
        for i in heads:
            sb = state[i].astype(bf16)
            s_ref[0, i, c * DK : (c + 1) * DK, :] = sb
            got = mm(jnp.concatenate([w[i][lo:hi], qn[i][lo:hi]], axis=0), sb)
            u = uw[i][lo:hi, :DV] - got[:BLOCK]
            u_parts[i].append(u)
            o_parts[i].append(e[i][lo:hi] * got[BLOCK:])
            if c < blocks - 1:
                state[i] = grow[i][lo : lo + 1] * state[i] + mm_tn(
                    kn[i][lo:hi], fin[i][lo:hi] * u
                )
    gain = gain_ref[0:1, :]
    for i in heads:
        u = jnp.concatenate(u_parts[i], axis=0).astype(bf16)
        out = jnp.concatenate(o_parts[i], axis=0) + mm(score[i], u)
        cols = slice(i * DV, (i + 1) * DV)
        o_ref[:, cols] = out
        u_ref[:, cols] = u
        w_ref[:, i * DK : (i + 1) * DK] = w[i]
        inv_ref[0, i] = inv[i]
        r = lax.rsqrt(jnp.mean(out * out, axis=1, keepdims=True) + eps_norm)
        gated_ref[:, cols] = (out * r * gain * silu(g_ref[:, cols])).astype(bf16)


def mixer_forward(proj, conv, head_rows, gain_row, hl):
    tokens = proj.shape[0]
    slots = tokens // TOK_DEV
    pair = 2 if hl % 2 == 0 else 1
    groups = hl // pair
    qk = pair * DK
    vv = pair * DV
    spec = pl.BlockSpec
    n = TOK_DEV

    def body(*refs):
        forward_kernel(hl, pair, *refs)

    return pl.pallas_call(
        body,
        grid=(groups, slots),
        in_specs=[
            spec((n, qk), lambda p, s: (s, p)),
            spec((n, qk), lambda p, s: (s, groups + p)),
            spec((n, vv), lambda p, s: (s, groups + p)),
            spec((n, vv), lambda p, s: (s, 2 * groups + p)),
            spec((n, 128), lambda p, s: (s, hl * 6)),
            spec((8, qk), lambda p, s: (0, p)),
            spec((8, qk), lambda p, s: (0, groups + p)),
            spec((8, vv), lambda p, s: (0, groups + p)),
            spec((8, 128), lambda p, s: (0, 0)),
            spec((8, DV), lambda p, s: (0, 0)),
        ],
        out_specs=[
            spec((n, vv), lambda p, s: (s, p)),
            spec((n, vv), lambda p, s: (s, p)),
            spec((n, vv), lambda p, s: (s, p)),
            spec((n, qk), lambda p, s: (s, p)),
            spec((1, pair, n, n), lambda p, s: (s, p, 0, 0)),
            spec((1, pair, n // BLOCK * DK, DV), lambda p, s: (s, p, 0, 0)),
        ],
        out_shape=[
            jax.ShapeDtypeStruct((tokens, hl * DV), bf16),
            jax.ShapeDtypeStruct((tokens, hl * DV), f32),
            jax.ShapeDtypeStruct((tokens, hl * DV), bf16),
            jax.ShapeDtypeStruct((tokens, hl * DK), bf16),
            jax.ShapeDtypeStruct((slots, hl, n, n), bf16),
            jax.ShapeDtypeStruct((slots, hl, n // BLOCK * DK, DV), bf16),
        ],
        compiler_params=pltpu.CompilerParams(vmem_limit_bytes=56 * 1024 * 1024),
        cost_estimate=pl.CostEstimate(
            flops=slots * hl * 600_000_000,
            bytes_accessed=slots * hl * 2_500_000,
            transcendentals=slots * hl * 500_000,
        ),
        name="mixer_forward",
    )(proj, proj, proj, proj, proj, conv, conv, conv, head_rows, gain_row)


def backward_kernel(
    hl,
    pair,
    q_ref,
    k_ref,
    v_ref,
    g_ref,
    dec_ref,
    cq_ref,
    ck_ref,
    cv_ref,
    head_ref,
    gain_ref,
    o_ref,
    u_ref,
    w_ref,
    inv_ref,
    s_ref,
    dy_ref,
    dq_out,
    dk_out,
    dv_out,
    dg_out,
    ddec_out,
    gq_out,
    gk_out,
    gv_out,
    small_out,
):
    p = pl.program_id(0)
    slot = pl.program_id(1)
    n = TOK_DEV
    blocks = n // BLOCK
    x, below, on_below, strict, same = block_masks(n)
    dec = dec_ref[...]
    alog_row = head_ref[0:1, :]
    pre, log_decay, running, total = decay_parts(dec, alog_row, head_ref[1:2, :])
    running_t = running.T
    heads = range(pair)
    qc = conv_forward(q_ref[...], cq_ref[...])
    kc = conv_forward(k_ref[...], ck_ref[...])
    vc = conv_forward(v_ref[...], cv_ref[...])
    q_sig = jax.nn.sigmoid(qc)
    k_sig = jax.nn.sigmoid(kc)
    v_sig = jax.nn.sigmoid(vc)
    q = qc * q_sig
    k = kc * k_sig
    v = (vc * v_sig).astype(bf16)
    gain = gain_ref[0:1, :]
    qn, kn, vn, qr, kr, beta, b, tot, d, sim, low, score = ([] for _ in range(12))
    d_out, u = [], []
    gain_rows = jnp.zeros((1, DV), f32)
    for i in heads:
        h = p * pair + i
        cols = slice(i * DV, (i + 1) * DV)
        kcols = slice(i * DK, (i + 1) * DK)
        rows_q, r_q = unit_rows(q[:, kcols], DK**-0.5)
        rows_k, r_k = unit_rows(k[:, kcols], 1.0)
        qr.append((rows_q, r_q))
        kr.append((rows_k, r_k))
        qn.append(rows_q.astype(bf16))
        kn.append(rows_k.astype(bf16))
        vn.append(v[:, cols])
        beta.append(jax.nn.sigmoid(lane_of(dec, hl + h)))
        b.append(lane_of(running, h))
        tot.append(lane_of(total, h))
        d.append(
            jnp.where(on_below, jnp.exp(jnp.where(on_below, b[i] - row_of(running_t, h), 0.0)), 0.0)
        )
        both = mm_nt(jnp.concatenate([kn[i], qn[i]], axis=0), kn[i])
        sim.append(jnp.where(strict, d[i] * both[:n], 0.0))
        score.append(both[n:] * d[i])
        out = o_ref[:, cols]
        gate = g_ref[:, cols]
        dy = dy_ref[:, cols].astype(f32)
        r = lax.rsqrt(jnp.mean(out * out, axis=1, keepdims=True) + eps_norm)
        normed = out * r
        g_sig = jax.nn.sigmoid(gate)
        act = gate * g_sig
        d_act = dy * normed * gain
        dg_out[:, cols] = (d_act * (g_sig * (1.0 + gate * (1.0 - g_sig)))).astype(bf16)
        gain_rows = gain_rows + jnp.sum(dy * normed * act, axis=0, keepdims=True)
        d_normed = dy * gain * act
        d_out.append(r * (d_normed - normed * jnp.mean(d_normed * normed, axis=1, keepdims=True)))
        u.append(u_ref[:, cols])
    e = [jnp.exp(b[i]) for i in heads]
    fin = [jnp.exp(tot[i] - b[i]) for i in heads]
    grow = [jnp.exp(tot[i]) for i in heads]
    d_out16 = [d_out[i].astype(bf16) for i in heads]
    score16 = [score[i].astype(bf16) for i in heads]
    d_u0 = [mm_tn(score16[i], d_out16[i]) for i in heads]
    d_state = [jnp.zeros((DK, DV), f32) for i in heads]
    d_u = [[None] * blocks for i in heads]
    dq_s = [[None] * blocks for i in heads]
    dk_s = [[None] * blocks for i in heads]
    fin_col = [[None] * blocks for i in heads]
    grow_col = [[None] * blocks for i in heads]
    e_out = [(e[i] * d_out[i]).astype(bf16) for i in heads]
    for c in reversed(range(blocks)):
        lo, hi = c * BLOCK, (c + 1) * BLOCK
        for i in heads:
            ds16 = d_state[i].astype(bf16)
            s16 = s_ref[0, i, c * DK : (c + 1) * DK, :]
            u_c = u[i][lo:hi].astype(f32)
            if c == blocks - 1:
                d_u[i][c] = d_u0[i][lo:hi]
                fin_col[i][c] = jnp.zeros((BLOCK, 1), f32)
                grow_col[i][c] = jnp.zeros((1, 1), f32)
                dk_s[i][c] = jnp.zeros((BLOCK, DK), f32)
            else:
                k_ds = mm(kn[i][lo:hi], ds16)
                add = fin[i][lo:hi] * k_ds
                d_u[i][c] = d_u0[i][lo:hi] + add
                fin_col[i][c] = jnp.sum(add * u_c, axis=1, keepdims=True)
                grow_col[i][c] = grow[i][lo : lo + 1] * jnp.sum(
                    jnp.sum(d_state[i] * s16.astype(f32), axis=1, keepdims=True),
                    axis=0,
                    keepdims=True,
                )
                dk_s[i][c] = mm_nt(fin[i][lo:hi] * u_c, ds16)
            if c > 0:
                step = mm_tn(
                    jnp.concatenate([qn[i][lo:hi], w_ref[lo:hi, i * DK : (i + 1) * DK]], axis=0),
                    jnp.concatenate([e_out[i][lo:hi], (-d_u[i][c]).astype(bf16)], axis=0),
                )
                d_state[i] = grow[i][lo : lo + 1] * d_state[i] + step
    lane = lax.broadcasted_iota(jnp.int32, (n, 128), 1)
    d_dec = jnp.zeros((n, 128), f32)
    d_log = jnp.zeros((n, 128), f32)
    dq_all, dk_all, dv_all = [], [], []
    ones = jnp.ones((n, 128), bf16)
    upper_i = lax.broadcasted_iota(jnp.int32, (n, n), 0)
    upper_j = lax.broadcasted_iota(jnp.int32, (n, n), 1)
    upper = jnp.where(jnp.logical_and((upper_i ^ upper_j) < BLOCK, upper_i <= upper_j), 1.0, 0.0)
    for i in heads:
        h = p * pair + i
        du = jnp.concatenate(d_u[i], axis=0)
        d_right = mm_tn(inv_ref[0, i], du)
        dr16 = d_right.astype(bf16)
        outer = mm_nt(jnp.concatenate([d_out16[i], dr16], axis=0), u[i])
        d_score = jnp.where(on_below, outer[:n], 0.0)
        d_low = jnp.where(strict, -outer[n:], 0.0)
        z16 = (-(beta[i] * e[i]) * d_right).astype(bf16)
        recalled = []
        for c in range(blocks):
            lo, hi = c * BLOCK, (c + 1) * BLOCK
            s16 = s_ref[0, i, c * DK : (c + 1) * DK, :]
            if c == 0:
                dq_s[i][c] = jnp.zeros((BLOCK, DK), f32)
                recalled.append(jnp.zeros((BLOCK, 2 * DV), f32))
                continue
            back = mm_nt(jnp.concatenate([e_out[i][lo:hi], z16[lo:hi]], axis=0), s16)
            dq_s[i][c] = back[:BLOCK]
            dk_s[i][c] = dk_s[i][c] + back[BLOCK:]
            got = mm(jnp.concatenate([kn[i][lo:hi], qn[i][lo:hi]], axis=0), s16)
            recalled.append(jnp.concatenate([got[:BLOCK], got[BLOCK:]], axis=1))
        recalled = jnp.concatenate(recalled, axis=0)
        k_s = recalled[:, :DV]
        q_s = recalled[:, DV:]
        d_a = (d_score * d[i]).astype(bf16)
        d_g = d_low * beta[i] * d[i]
        d_g16 = (d_g + d_g.T).astype(bf16)
        dq = jnp.concatenate(dq_s[i], axis=0) + mm(d_a, kn[i])
        dk = jnp.concatenate(dk_s[i], axis=0) + mm_tn(d_a, qn[i]) + mm(d_g16, kn[i])
        dv = beta[i] * d_right
        row_sum = jnp.sum(d_low * sim[i], axis=1, keepdims=True)
        keep = vn[i].astype(f32) - e[i] * k_s
        d_beta = row_sum + jnp.sum(d_right * keep, axis=1, keepdims=True)
        moved = (d_score * score[i] + d_low * beta[i] * sim[i]).astype(bf16)
        d_b = mm(moved, ones) - mm_tn(moved, ones)
        d_b_col = e[i] * jnp.sum(
            d_out[i] * q_s - (beta[i] * d_right) * k_s, axis=1, keepdims=True
        )
        fin_all = jnp.concatenate(fin_col[i], axis=0)
        d_b = jnp.where(lane == h, d_b + (d_b_col - fin_all), 0.0)
        tail = jnp.concatenate(
            [
                jnp.broadcast_to(
                    grow_col[i][c] + jnp.sum(fin_col[i][c], axis=0, keepdims=True), (BLOCK, 1)
                )
                for c in range(blocks)
            ],
            axis=0,
        )
        d_log = d_log + mm_exact(upper, d_b) + jnp.where(lane == h, tail, 0.0)
        d_dec = d_dec + jnp.where(lane == hl + h, d_beta * beta[i] * (1.0 - beta[i]), 0.0)
        rows_q, r_q = qr[i]
        rows_k, r_k = kr[i]
        unit = rows_q * DK**0.5
        dq = (DK**-0.5) * r_q * (dq - unit * jnp.sum(dq * unit, axis=1, keepdims=True))
        dk = r_k * (dk - rows_k * jnp.sum(dk * rows_k, axis=1, keepdims=True))
        dq_all.append(dq)
        dk_all.append(dk)
        dv_all.append(dv)

    def through_conv(d_active, conv, sig, mixed, weight, out, grad):
        d_conv = d_active * (sig * (1.0 + conv * (1.0 - sig)))
        d_mixed, d_weight = conv_backward(d_conv, mixed, weight)
        out[...] = d_mixed.astype(bf16)

        @pl.when(slot == 0)
        def _():
            grad[...] = jnp.zeros_like(grad)

        grad[0:KCONV, :] += d_weight

    through_conv(
        jnp.concatenate(dq_all, axis=1), qc, q_sig, q_ref[...], cq_ref[...], dq_out, gq_out
    )
    through_conv(
        jnp.concatenate(dk_all, axis=1), kc, k_sig, k_ref[...], ck_ref[...], dk_out, gk_out
    )
    through_conv(
        jnp.concatenate(dv_all, axis=1), vc, v_sig, v_ref[...], cv_ref[...], dv_out, gv_out
    )
    mine = jnp.logical_and(lane >= p * pair, lane < (p + 1) * pair)
    d_pre = jnp.where(mine, -jnp.exp(alog_row) * jax.nn.sigmoid(pre) * d_log, 0.0)
    ddec_out[...] = d_dec + d_pre

    @pl.when(slot == 0)
    def _():
        small_out[...] = jnp.zeros_like(small_out)

    small_out[0:1, :] += gain_rows
    small_out[1:2, 0:128] += jnp.sum(jnp.where(mine, d_log * log_decay, 0.0), axis=0, keepdims=True)
    small_out[2:3, 0:128] += jnp.sum(d_pre, axis=0, keepdims=True)


def mixer_backward(proj, conv, head_rows, gain_row, saved, d_gated, hl):
    out, u, w, inv, states = saved
    tokens = proj.shape[0]
    slots = tokens // TOK_DEV
    pair = 2 if hl % 2 == 0 else 1
    groups = hl // pair
    qk = pair * DK
    vv = pair * DV
    spec = pl.BlockSpec
    n = TOK_DEV

    def body(*refs):
        backward_kernel(hl, pair, *refs)

    return pl.pallas_call(
        body,
        grid=(groups, slots),
        in_specs=[
            spec((n, qk), lambda p, s: (s, p)),
            spec((n, qk), lambda p, s: (s, groups + p)),
            spec((n, vv), lambda p, s: (s, groups + p)),
            spec((n, vv), lambda p, s: (s, 2 * groups + p)),
            spec((n, 128), lambda p, s: (s, hl * 6)),
            spec((8, qk), lambda p, s: (0, p)),
            spec((8, qk), lambda p, s: (0, groups + p)),
            spec((8, vv), lambda p, s: (0, groups + p)),
            spec((8, 128), lambda p, s: (0, 0)),
            spec((8, DV), lambda p, s: (0, 0)),
            spec((n, vv), lambda p, s: (s, p)),
            spec((n, vv), lambda p, s: (s, p)),
            spec((n, qk), lambda p, s: (s, p)),
            spec((1, pair, n, n), lambda p, s: (s, p, 0, 0)),
            spec((1, pair, n // BLOCK * DK, DV), lambda p, s: (s, p, 0, 0)),
            spec((n, vv), lambda p, s: (s, p)),
        ],
        out_specs=[
            spec((n, qk), lambda p, s: (s, p)),
            spec((n, qk), lambda p, s: (s, p)),
            spec((n, vv), lambda p, s: (s, p)),
            spec((n, vv), lambda p, s: (s, p)),
            spec((n, 128), lambda p, s: (p * slots + s, 0)),
            spec((8, qk), lambda p, s: (0, p)),
            spec((8, qk), lambda p, s: (0, p)),
            spec((8, vv), lambda p, s: (0, p)),
            spec((8, DV), lambda p, s: (p, 0)),
        ],
        out_shape=[
            jax.ShapeDtypeStruct((tokens, hl * DK), bf16),
            jax.ShapeDtypeStruct((tokens, hl * DK), bf16),
            jax.ShapeDtypeStruct((tokens, hl * DV), bf16),
            jax.ShapeDtypeStruct((tokens, hl * DV), bf16),
            jax.ShapeDtypeStruct((groups * tokens, 128), f32),
            jax.ShapeDtypeStruct((8, hl * DK), f32),
            jax.ShapeDtypeStruct((8, hl * DK), f32),
            jax.ShapeDtypeStruct((8, hl * DV), f32),
            jax.ShapeDtypeStruct((8 * groups, DV), f32),
        ],
        compiler_params=pltpu.CompilerParams(vmem_limit_bytes=56 * 1024 * 1024),
        cost_estimate=pl.CostEstimate(
            flops=slots * hl * 1_000_000_000,
            bytes_accessed=slots * hl * 3_500_000,
            transcendentals=slots * hl * 700_000,
        ),
        name="mixer_backward",
    )(proj, proj, proj, proj, proj, conv, conv, conv, head_rows, gain_row, out, u, w, inv, states, d_gated)


def relative(nf, j):
    return [(i, i ^ (2 * j)) for i in range(nf)]


def swap_core(a, nf):
    return lax.ppermute(a, "fsdp", [(i, i ^ 1) for i in range(nf)])


def to_chip(a, nf, j):
    return lax.ppermute(a, "fsdp", relative(nf, j))


def gather_rows(a, nf):
    chips = nf // 2
    if chips != 4:
        return jnp.concatenate([a] + [to_chip(a, nf, j) for j in range(1, chips)], axis=0)
    half = a.shape[0] // 2
    one = to_chip(a, nf, 1)
    two = to_chip(a, nf, 2)
    three = [to_chip(one[:half], nf, 2), to_chip(two[half:], nf, 1)]
    return jnp.concatenate([a, one, two] + three, axis=0)


def scatter_rows(a, nf):
    chips = nf // 2
    n = a.shape[0] // chips
    parts = [a[j * n : (j + 1) * n] for j in range(chips)]
    if chips != 4:
        total = parts[0].astype(f32)
        for j in range(1, chips):
            total = total + to_chip(parts[j], nf, j).astype(f32)
        return total
    half = n // 2
    low = to_chip(parts[3][:half], nf, 2)
    high = to_chip(parts[3][half:], nf, 1)
    one_high = to_chip(parts[1][half:], nf, 1)
    two_low = to_chip(parts[2][:half], nf, 2)
    one_low = to_chip((parts[1][:half].astype(f32) + low.astype(f32)).astype(bf16), nf, 1)
    two_high = to_chip((parts[2][half:].astype(f32) + high.astype(f32)).astype(bf16), nf, 2)
    own = parts[0].astype(f32)
    return jnp.concatenate(
        [
            own[:half] + one_low.astype(f32) + two_low.astype(f32),
            own[half:] + one_high.astype(f32) + two_high.astype(f32),
        ],
        axis=0,
    )


def sum_over_rep(a, nz):
    if nz != 4:
        return lax.psum(a, "rep")
    z = lax.axis_index("rep")
    first = lax.ppermute(a, "rep", [(0, 1), (3, 2)])
    pair = (a.astype(f32) + first.astype(f32)).astype(bf16)
    other = lax.ppermute(pair, "rep", [(1, 2), (2, 1)])
    total = (pair.astype(f32) + other.astype(f32)).astype(bf16)
    last = lax.ppermute(total, "rep", [(1, 0), (2, 3)])
    return jnp.where(jnp.logical_or(z == 1, z == 2), total, last)


def rms_rows(rows, gain):
    r = lax.rsqrt(jnp.mean(rows * rows, axis=1, keepdims=True) + eps_norm)
    return rows * r * gain, r


def rms_back(rows, r, gain, d_out):
    unit = rows * r
    d_unit = d_out * gain
    d_rows = r * (d_unit - unit * jnp.mean(d_unit * unit, axis=1, keepdims=True))
    return d_rows, jnp.sum(d_out * unit, axis=0)


def chip_ranges(chip, chips, widths):
    spans = []
    start = 0
    for width in widths:
        part = width // chips
        spans.append((start + chip * part, part))
        start += width
    return spans


def take_columns(w, spans):
    rows = w.shape[0]
    return jnp.concatenate(
        [lax.dynamic_slice(w, (0, start), (rows, width)) for start, width in spans], axis=1
    )


def redistribute(w, nf, widths):
    chips = nf // 2
    me = lax.axis_index("fsdp")
    chip, core = me // 2, me % 2
    rows = w.shape[0]
    width = sum(widths) // chips
    out = jnp.zeros((nf * rows, width), w.dtype)
    for j in range(chips):
        part = take_columns(w, chip_ranges(chip ^ j, chips, widths))
        if j:
            part = to_chip(part, nf, j)
        other = swap_core(part, nf)
        base = 2 * (chip ^ j) * rows
        out = lax.dynamic_update_slice(out, part, (base + core * rows, 0))
        out = lax.dynamic_update_slice(out, other, (base + (1 - core) * rows, 0))
    return out


def both_cores(w, nf):
    core = lax.axis_index("fsdp") % 2
    rows = w.shape[0]
    out = jnp.zeros((2 * rows, w.shape[1]), w.dtype)
    out = lax.dynamic_update_slice(out, w, (core * rows, 0))
    return lax.dynamic_update_slice(out, swap_core(w, nf), ((1 - core) * rows, 0))


def sum_cores(a, nf):
    core = lax.axis_index("fsdp") % 2
    rows = a.shape[0] // 2
    mine = lax.dynamic_slice(a, (core * rows, 0), (rows, a.shape[1]))
    theirs = lax.dynamic_slice(a, ((1 - core) * rows, 0), (rows, a.shape[1]))
    return (mine.astype(f32) + swap_core(theirs, nf).astype(f32)).astype(bf16)


def column_gradient(left, right, nf, nz, widths):
    chips = nf // 2
    chip = lax.axis_index("fsdp") // 2
    rows = left.shape[1] // chips
    out = jnp.zeros((rows // 2, sum(widths)), f32)
    for j in reversed(range(chips)):
        part = lax.dynamic_slice(left, (0, (chip ^ j) * rows), (left.shape[0], rows))
        term = sum_cores(mm_tn(part, right).astype(bf16), nf)
        if j:
            term = to_chip(term, nf, j)
        term = sum_over_rep(term, nz).astype(f32)
        at = 0
        for start, width in chip_ranges(chip ^ j, chips, widths):
            out = lax.dynamic_update_slice(out, term[:, at : at + width], (0, start))
            at += width
    return out


def as_rows(a):
    flat = a.reshape(-1)
    return jnp.pad(flat, (0, -flat.shape[0] % 128)).reshape(-1, 128)


def local(
    tokens,
    cotangent,
    lengths,
    slot_owner,
    gain_in,
    w_proj,
    w_decay,
    conv_weight,
    a_log,
    dt_bias,
    o_gain,
    w_out,
    gain_mid,
    w_gate_up,
    w_down,
    *,
    nf,
    nz,
):
    chips = nf // 2
    hl = H // chips
    me = lax.axis_index("fsdp")
    rep = lax.axis_index("rep")
    chip = me // 2
    d_model = tokens.shape[1]
    shard = gain_in.shape[0]
    conv_shard = conv_weight.shape[1]
    channels = conv_shard * nf
    hv = w_out.shape[0] * nf
    hk = (channels - hv) // 2
    ff = w_down.shape[0] * nf
    proj_widths = (hk, hk, hv, hv)
    up_widths = (ff, ff)

    device = rep * nf + (me ^ (2 * jnp.arange(chips, dtype=jnp.int32)))
    held = jnp.sum(
        jnp.where(slot_owner[None, :] == device[:, None], lengths[None, :], 0), axis=1
    )
    live_all = (jnp.arange(TOK_DEV, dtype=jnp.int32)[None, :] < held[:, None]).astype(f32)
    live_own = live_all[0][:, None]
    live_all = live_all.reshape(chips * TOK_DEV, 1)

    pieces = [conv_weight, w_decay.T, gain_in, gain_mid, o_gain, a_log, dt_bias]
    rows = [as_rows(p) for p in pieces]
    counts = [r.shape[0] for r in rows]
    packed = jnp.concatenate(rows, axis=0)
    packed = jnp.pad(packed, ((0, -packed.shape[0] % 16), (0, 0)))
    small = lax.all_gather(packed, "fsdp", axis=0).astype(f32)
    split = []
    at = 0
    for p, count in zip(pieces, counts):
        split.append(
            small[:, at : at + count].reshape(nf, count * 128)[:, : p.size].reshape((nf,) + p.shape)
        )
        at += count
    conv_full = split[0].transpose(1, 0, 2).reshape(KCONV, channels)
    decay_full = split[1].transpose(1, 0, 2).reshape(2 * H, d_model).T
    gain_in_full, gain_mid_full, ogain_full, alog_full, bias_full = (
        s.reshape(-1) for s in split[2:]
    )
    conv_chip = take_columns(conv_full, chip_ranges(chip, chips, proj_widths[:3]))
    conv_chip = jnp.pad(conv_chip, ((0, 8 - KCONV), (0, 0)))
    decay_chip = take_columns(decay_full, chip_ranges(chip, chips, (H, H)))
    decay_chip = jnp.pad(decay_chip, ((0, 0), (0, 128 - 2 * hl))).astype(bf16)
    head_rows = jnp.stack([alog_full, bias_full])
    head_rows = lax.dynamic_slice(head_rows, (0, chip * hl), (2, hl))
    head_rows = jnp.pad(head_rows, ((0, 6), (0, 128 - hl)))
    gain_row = jnp.pad(ogain_full[None, :], ((0, 7), (0, 0)))

    rows_in = gather_rows(tokens, nf).astype(f32)
    normed_in = rms_rows(rows_in, gain_in_full)[0].astype(bf16)
    proj_chip = redistribute(w_proj, nf, proj_widths)
    weight_in = jnp.concatenate([proj_chip, decay_chip], axis=1)
    projected = mm(normed_in, weight_in)
    gated, *saved = mixer_forward(projected, conv_chip, head_rows, gain_row, hl)
    out_chip = both_cores(w_out, nf)
    branch = scatter_rows(mm(gated, out_chip).astype(bf16), nf)

    tokens32 = tokens.astype(f32)
    middle = tokens32 + live_own * branch
    normed_own, r_mid = rms_rows(middle, gain_mid_full)
    normed_mid = gather_rows(normed_own.astype(bf16), nf)
    up_chip = redistribute(w_gate_up, nf, up_widths)
    down_chip = both_cores(w_down, nf)
    seeded = cotangent.astype(f32) * live_own
    d_ffn = gather_rows(seeded.astype(bf16), nf)
    d_hidden = mm_nt(d_ffn, down_chip)
    gate_up = mm(normed_mid, up_chip)
    wide = ff // chips
    gate, up = gate_up[:, :wide], gate_up[:, wide:]
    sig = jax.nn.sigmoid(gate)
    act = gate * sig
    hidden = (act * up).astype(bf16)
    d_gate_up = jnp.concatenate(
        [d_hidden * up * (sig * (1.0 + gate * (1.0 - sig))), d_hidden * act], axis=1
    ).astype(bf16)
    ffn_branch = scatter_rows(mm(hidden, down_chip).astype(bf16), nf)
    output = (middle + live_own * ffn_branch).astype(bf16)

    d_normed_mid = scatter_rows(mm_nt(d_gate_up, up_chip).astype(bf16), nf)
    grad_down = sum_over_rep(sum_cores(mm_tn(hidden, d_ffn).astype(bf16), nf), nz).astype(f32)
    grad_up = column_gradient(normed_mid, d_gate_up, nf, nz, up_widths)
    d_mid, g_gain_mid = rms_back(middle, r_mid, gain_mid_full, d_normed_mid)
    d_middle = seeded + d_mid
    d_branch = gather_rows((live_own * d_middle).astype(bf16), nf)

    d_gated = mm_nt(d_branch, out_chip)
    grad_out = sum_over_rep(sum_cores(mm_tn(gated, d_branch).astype(bf16), nf), nz).astype(f32)
    dq, dk, dv, dg, d_dec, gq, gk, gv, g_small = mixer_backward(
        projected, conv_chip, head_rows, gain_row, saved, d_gated, hl
    )
    groups = g_small.shape[0] // 8
    d_dec = jnp.sum(d_dec.reshape(groups, -1, 128), axis=0).astype(bf16)
    d_proj = jnp.concatenate([dq, dk, dv, dg], axis=1)
    d_normed_in = scatter_rows(
        mm_nt(jnp.concatenate([d_proj, d_dec], axis=1), weight_in).astype(bf16), nf
    )
    grad_proj = column_gradient(normed_in, d_proj, nf, nz, proj_widths)
    g_decay = mm_tn(normed_in, d_dec)[:, : 2 * hl]
    r_in = lax.rsqrt(jnp.mean(tokens32 * tokens32, axis=1, keepdims=True) + eps_norm)
    d_rows, g_gain_in = rms_back(tokens32, r_in, gain_in_full, d_normed_in)
    grad_tokens = d_middle + d_rows

    def spread(values, widths):
        out = jnp.zeros((values.shape[0], sum(widths)), f32)
        at = 0
        for start, width in chip_ranges(chip, chips, widths):
            out = lax.dynamic_update_slice(out, values[:, at : at + width], (0, start))
            at += width
        return out

    g_small = jnp.sum(g_small.reshape(groups, 8, DV), axis=0)
    g_conv = spread(jnp.concatenate([gq, gk, gv], axis=1)[:KCONV], proj_widths[:3])
    g_decay = spread(g_decay, (H, H)).T
    g_alog = spread(g_small[1:2, :hl], (H,))
    g_bias = spread(g_small[2:3, :hl], (H,))
    parts = [
        g_conv.reshape(KCONV, nf, conv_shard).transpose(1, 0, 2),
        g_decay.reshape(2 * H, nf, shard).transpose(1, 0, 2),
        g_gain_in.reshape(nf, shard),
        g_gain_mid.reshape(nf, shard),
        g_small[0].reshape(nf, -1),
        g_alog.reshape(nf, -1),
        g_bias.reshape(nf, -1),
    ]
    flat = []
    for part in parts:
        part = part.reshape(nf, -1)
        flat.append(jnp.pad(part, ((0, 0), (0, -part.shape[1] % 128))))
    flat = jnp.concatenate(flat, axis=1)
    count = flat.shape[1]
    summed = lax.psum_scatter(
        flat.reshape(nf * count // 128, 128), "fsdp", scatter_dimension=0, tiled=True
    )
    summed = lax.psum(summed, "rep").reshape(-1)
    grads = []
    at = 0
    for p in pieces:
        grads.append(summed[at : at + p.size].reshape(p.shape))
        at += p.size + (-p.size % 128)
    s_conv, s_decay, s_gain_in, s_gain_mid, s_ogain, s_alog, s_bias = grads
    return (
        output,
        grad_tokens,
        s_gain_in,
        grad_proj,
        s_decay.T,
        s_conv,
        s_alog,
        s_bias,
        s_ogain,
        grad_out,
        s_gain_mid,
        grad_up,
        grad_down,
    )


def solution(mesh):
    rows = P(("rep", "fsdp"), None)
    one = P("fsdp")
    two = P("fsdp", None)
    columns = P(None, "fsdp")
    in_specs = (rows, rows, P(), P(), one, two, two, columns, one, one, one, two, one, two, two)
    out_specs = (rows, rows, one, two, two, columns, one, one, one, two, one, two, two)
    body = partial(local, nf=mesh.shape["fsdp"], nz=mesh.shape["rep"])
    return jax.shard_map(body, mesh=mesh, in_specs=in_specs, out_specs=out_specs, check_vma=False)
```

time: 2580 us -> 1570 us (0.61)
  other arithmetic: 820 us -> 102 us
  matrix products: 472 us -> 178 us
  waiting for transfers between devices: 1040 us -> 814 us
  starting transfers between devices: 0.62 us -> 177 us
  Pallas kernels: 0 us -> 88.2 us
    ppermute x0 -> x102, waiting for transfers between devices: none -> 814 us  [the longest x52 293 us: to_chip(): return lax.ppermute(a, 'fsdp', relative(nf, j))]
    another operation x59 -> x1, other arithmetic: 668 us -> 0.01 us  [local(): head_rows = jnp.stack([alog_full, bias_full])]
    psum x1 -> x0, waiting for transfers between devices: 551 us -> none  [local(): lax.psum(grad_proj, 'rep').astype(jnp.float32)]
    unnamed x14 -> x1, waiting for transfers between devices: 285 us -> 0.01 us
    dot_general x91 -> x19, matrix products: 437 us -> 178 us  [the longest x11 65.4 us: mm_tn(): lax.dot_general(a.astype(bf16), b.astype(bf16), (((0,), (0,)), ((), ())),...]
    all_gather x4 -> x0, waiting for transfers between devices: 179 us -> none  [the longest x1 179 us: local(): lax.all_gather(w_proj, 'fsdp', axis=0, tiled=True)]
    ppermute x0 -> x102, starting transfers between devices: none -> 176 us  [the longest x10 94 us: sum_over_rep(): first = lax.ppermute(a, 'rep', [(0, 1), (3, 2)])]
    pallas_call x0 -> x2, Pallas kernels: none -> 88.2 us  [the longest x1 49.3 us: mixer_backward(): pl.pallas_call(body, grid=(groups, slots), in_specs=[spec((n, qk), lambda...]
  transfers between devices with their start and end apart: 11 -> 103, of which waited for: 4 -> 41; matrix products, arithmetic and copies ran while one was open for 51% -> 22% of each run, Pallas kernels for 0% -> 6%
where the time goes in v1:
time: 1570 us
  waiting for transfers between devices  814 us (52%)
  matrix products  178 us (11%)
  starting transfers between devices  177 us (11%)
  local copies, waits for them, and re-layouts  133 us (8%)
  other arithmetic  102 us (6%)
  Pallas kernels  88.2 us (6%)
  blocking collectives  71.9 us (5%)
    ppermute x52, waiting for transfers between devices, to_chip(): return lax.ppermute(a, 'fsdp', relative(nf, j))  293 us
    ppermute x10, waiting for transfers between devices, sum_over_rep(): last = lax.ppermute(total, 'rep', [(1, 0), (2, 3)])  267 us
    ppermute x10, waiting for transfers between devices, sum_over_rep(): first = lax.ppermute(a, 'rep', [(0, 1), (3, 2)])  254 us
    ppermute x10, starting transfers between devices, sum_over_rep(): first = lax.ppermute(a, 'rep', [(0, 1), (3, 2)])  94 us
    dot_general x11, matrix products, mm_tn(): lax.dot_general(a.astype(bf16), b.astype(bf16), (((0,), (0,)), ((), ())),...  65.4 us
    dot_general x4, matrix products, mm_nt(): lax.dot_general(a.astype(bf16), b.astype(bf16), (((1,), (1,)), ((), ())),...  58.5 us
    dot_general x4, matrix products, mm(): lax.dot_general(a.astype(bf16), b.astype(bf16), (((1,), (0,)), ((), ())),...  54.5 us
    ppermute x52, starting transfers between devices, to_chip(): return lax.ppermute(a, 'fsdp', relative(nf, j))  53.8 us
  transfers between devices with their start and end apart: 103, of which 41 were waited for; matrix products, arithmetic and copies ran while one was open for 22% of the time, Pallas kernels for 6%

profile of v1, /device:TPU:0, one launch (start us, length us, event | category | flops | bytes accessed | tf_op | source)
XLA Modules:
  0.0 1568.6 jit_solution(14858044113856117214)
XLA Ops:
  13.7 5.2 broadcast_in_dim.50
  21.9 33.6 %all-gather = bf16[896,128]{1,0:T(8,128)(2,1)S(1)} all-gather(bf16[112,128]{1,0:T(8,128)(2,1)S(1)} %pad.46), channel_id=2, replica_groups=mesh['rep'=4,'fsdp'=8] {'fsdp'}, dimensions={0}, use_global_device_ids=true | all-gather | bytes 258048 | tf_op jit(solution)/shard_map/all_gather | solution.py:763
  80.2 6.4 broadcast_in_dim.48
  117.4 14.3 collective-permute-done.23
  136.4 6.4 collective-permute-done.3
  146.0 41.2 %collective-permute-done.39 = bf16[128,2048]{1,0:T(8,128)(2,1)S(1)} collective-permute-done((bf16[128,2048]{1,0:T(8,128)(2,1)S(1)}, bf16[128,2048]{1,0:T(8,128)(2,1)S(1)}, u32[]{:S(2)}, u32[]{:S(2)}) %collective-permute-start.39) | collective-permute-done | bytes 524320 | tf_op jit(solution)/shard_map/ppermute | solution.py:577
  195.7 28.4 %collective-permute-done.9 = bf16[256,3072]{1,0:T(8,128)(2,1)S(1)} collective-permute-done((bf16[256,3072]{1,0:T(8,128)(2,1)S(1)}, bf16[256,3072]{1,0:T(8,128)(2,1)S(1)}, u32[]{:S(2)}, u32[]{:S(2)}) %collective-permute-start.9) | collective-permute-done | bytes 1572896 | tf_op jit(solution)/shard_map/ppermute | solution.py:577
  225.7 29.2 %collective-permute-done.25 = bf16[256,2816]{1,0:T(8,128)(2,1)} collective-permute-done((bf16[256,2816]{1,0:T(8,128)(2,1)}, bf16[256,2816]{1,0:T(8,128)(2,1)}, u32[]{:S(2)}, u32[]{:S(2)}) %collective-permute-start.25) | collective-permute-done | bytes 1441824 | tf_op jit(solution)/shard_map/ppermute | solution.py:577
  262.7 21.8 %fusion.9.refs_0_.refs_1_.refs_2_.refs_3_.refs_4_ = f32[1024,3200]{1,0:T(8,128)} fusion(bf16[1024,2048]{1,0:T(8,128)(2,1)S(1)} %fusion.5, bf16[2048,8]{1,0:T(8,128)(2,1)S(1)} %copy-done.51, bf16[2048,3072]{1,0:T(8,128)(2,1)} %constant_dynamic-update-slice_fusion.50), kind=kOutput, calls=%fused_computation.19 | convolution fusion | flops 13461094400 | bytes 29917184 | tf_op jit(solution)/shard_map/dot_general | solution.py:23
  284.5 38.9 %mixer_forward.1 = (bf16[1024,1024]{1,0:T(8,128)(2,1)}, f32[1024,1024]{1,0:T(8,128)}, bf16[1024,1024]{1,0:T(8,128)(2,1)}, bf16[1024,512]{1,0:T(8,128)(2,1)}, bf1...) custom-call(f32[1024,3200]{1,0:T(8,128)} %fusion.9.refs_0_.refs_1_.refs_2_.refs_3_.refs_4_, ...), custom_call_target="tpu_custom_call" | custom-call | flops 9600000000 | bytes 40000000 | tf_op jit(solution)/shard_map/mixer_forward/pallas_call | solution.py:232
  323.4 6.5 convolution_convert_fusion.12
  337.9 7.1 collective-permute-done.12
  348.2 8.0 collective-permute-done.14
  359.8 9.5 collective-permute-done.13
  380.3 14.0 collective-permute-done.18
  397.3 8.5 collective-permute-done.20
  408.8 17.5 %fusion.69 = f32[1024,2816]{1,0:T(8,128)} fusion(bf16[1024,2048]{1,0:T(8,128)(2,1)S(1)} %constant_dynamic-update-slice_fusion.5, bf16[2048,2816]{1,0:T(8,128)(2,1)} %constant_dynamic-update-slice_fusion.40), kind=kOutput, calls=%fused_computation.314 | convolution fusion | flops 11811160064 | bytes 27262976 | tf_op jit(solution)/shard_map/dot_general | solution.py:23
  426.3 16.6 %multiply_convert_fusion.1 = (bf16[1024,1408]{1,0:T(8,128)(2,1)}, bf16[1024,1408]{1,0:T(8,128)(2,1)}, bf16[1024,1408]{1,0:T(8,128)(2,1)S(1)}) fusion(f32[1024,2816]{1,0:T(8,128)} %fusion.69, bf16[1024,2048]{1,0:T(8,128)(2,1)} %constant_dynamic-update-slice_fusion.10, bf16[1408,2048]{1,0:T(8,128)(2,1)} %constant_dynamic-update-slice_fusion.38), kind=kOutput, calls=%fused_computation.14 | convolution fusion | flops 5927206912 | bytes 30146560 | tf_op jit(solution)/shard_map/dot_general | solution.py:29
  442.8 16.9 %convolution_convert_fusion.9 = bf16[1024,2048]{1,0:T(8,128)(2,1)S(1)} fusion(bf16[2048,2816]{1,0:T(8,128)(2,1)} %constant_dynamic-update-slice_fusion.40, bf16[1024,1408]{1,0:T(8,128)(2,1)} %get-tuple-element.57, bf16[1024,1408]{1,0:T(8,128)(2,1)} %get-tuple-element.56), kind=kOutput, calls=%fused_computation.32 | convolution fusion | flops 11824791552 | bytes 21495808 | tf_op jit(solution)/shard_map/dot_general | solution.py:29
  461.1 8.7 convolution_convert_fusion.10
  471.2 8.5 convolution_convert_fusion
  485.3 6.2 convolution_convert_fusion.4
  491.6 7.2 convolution_convert_fusion.3
  502.1 6.2 convolution_convert_fusion.2
  508.3 7.4 convolution_convert_fusion.1
  523.2 10.0 collective-permute-done.34
  535.6 8.8 collective-permute-done.41
  546.9 8.6 collective-permute-done.33
  555.5 5.6 collective-permute-done.31
  578.8 15.1 collective-permute-done.46
  593.8 4.6 collective-permute-start.95
  601.9 26.4 %collective-permute-done.47 = bf16[256,2048]{1,0:T(8,128)(2,1)S(1)} collective-permute-done((bf16[256,2048]{1,0:T(8,128)(2,1)S(1)}, bf16[256,2048]{1,0:T(8,128)(2,1)S(1)}, u32[]{:S(2)}, u32[]{:S(2)}) %collective-permute-start.47) | collective-permute-done | bytes 1048608 | tf_op jit(solution)/shard_map/ppermute | solution.py:577
  629.9 8.3 collective-permute-done.48
  639.7 6.4 fusion.70.refs_15_
  646.0 49.3 %mixer_backward.1 = (bf16[1024,512]{1,0:T(8,128)(2,1)}, bf16[1024,512]{1,0:T(8,128)(2,1)}, bf16[1024,1024]{1,0:T(8,128)(2,1)}, bf16[1024,1024]{1,0:T(8,128)(2,1)...) custom-call(f32[1024,3200]{1,0:T(8,128)} %fusion.9.refs_0_.refs_1_.r, ...), custom_call_target="tpu_custom_call" | custom-call | flops 16000000000 | bytes 56000000 | tf_op jit(solution)/shard_map/mixer_backward/pallas_call | solution.py:515
  703.5 5.0 convolution_convert_fusion.8
  708.5 5.0 convolution_convert_fusion.7
  713.5 5.4 convolution_convert_fusion.6
  718.9 5.1 convolution_convert_fusion.5
  724.0 6.3 convolution_convert_fusion.11
  734.0 18.7 %fusion.11 = bf16[1024,2048]{1,0:T(8,128)(2,1)S(1)} fusion(bf16[1024,3200]{1,0:T(8,128)(2,1)} %convert_dynamic-update-slice_fusion, bf16[2048,8]{1,0:T(8,128)(2,1)S(1)} %copy-done.52, bf16[2048,3072]{1,0:T(8,128)(2,1)} %constant_dynamic-update-slice_fusion.50), kind=kOutput, calls=%fused_computation.31 | convolution fusion | flops 13463191552 | bytes 23363584 | tf_op jit(solution)/shard_map/dot_general | solution.py:29
  778.5 6.5 collective-permute-done.54
  789.0 4.6 add_convert_fusion.2
  796.2 7.4 collective-permute-done.51
  810.5 18.2 %fusion = f32[112,128]{1,0:T(8,128)S(1)} fusion(f32[824,128]{1,0:T(8,128)} %reshape.180), kind=kCustom, calls=%all-reduce-scatter | all-reduce-scatter fusion | flops 114689 | bytes 479744
  834.4 20.1 %psum.7 = f32[103,128]{1,0:T(8,128)S(1)} all-reduce(f32[103,128]{1,0:T(8,128)S(1)} %constant_dynamic-slice_fusion.38), channel_id=1, replica_groups=mesh['rep'=4,'fsdp'=8] {'rep'}, use_global_device_ids=true, to_apply=%region_11.12 | all-reduce | flops 13184 | bytes 105472 | tf_op jit(solution)/shard_map/psum | solution.py:870
  875.4 19.2 %collective-permute-done.90 = bf16[256,2816]{1,0:T(8,128)(2,1)S(1)} collective-permute-done((bf16[256,2816]{1,0:T(8,128)(2,1)S(1)}, bf16[256,2816]{1,0:T(8,128)(2,1)S(1)}, u32[]{:S(2)}, u32[]{:S(2)}) %collective-permute-start.90) | collective-permute-done | bytes 1441824 | tf_op jit(solution)/shard_map/ppermute | solution.py:577
  905.6 24.8 %collective-permute-done.86 = bf16[256,2816]{1,0:T(8,128)(2,1)S(1)} collective-permute-done((bf16[256,2816]{1,0:T(8,128)(2,1)}, bf16[256,2816]{1,0:T(8,128)(2,1)S(1)}, u32[]{:S(2)}, u32[]{:S(2)}) %collective-permute-start.86) | collective-permute-done | bytes 1441824 | tf_op jit(solution)/shard_map/ppermute | solution.py:621
  932.7 90.0 %collective-permute-done.91 = bf16[256,2816]{1,0:T(8,128)(2,1)S(1)} collective-permute-done((bf16[256,2816]{1,0:T(8,128)(2,1)S(1)}, bf16[256,2816]{1,0:T(8,128)(2,1)S(1)}, u32[]{:S(2)}, u32[]{:S(2)}) %collective-permute-start.91) | collective-permute-done | bytes 1441824 | tf_op jit(solution)/shard_map/ppermute | solution.py:621
  1022.7 4.5 collective-permute-start.72
  1030.7 30.0 %collective-permute-done.72 = bf16[256,3072]{1,0:T(8,128)(2,1)S(1)} collective-permute-done((bf16[256,3072]{1,0:T(8,128)(2,1)S(1)}, bf16[256,3072]{1,0:T(8,128)(2,1)S(1)}, u32[]{:S(2)}, u32[]{:S(2)}) %collective-permute-start.72) | collective-permute-done | bytes 1572896 | tf_op jit(solution)/shard_map/ppermute | solution.py:621
  1064.9 65.6 %collective-permute-start.76 = (bf16[512,2048]{1,0:T(8,128)(2,1)S(1)}, bf16[512,2048]{1,0:T(8,128)(2,1)S(1)}, u32[]{:S(2)}, u32[]{:S(2)}) collective-permute-start(bf16[512,2048]{1,0:T(8,128)(2,1)S(1)} %add_convert_fusion.5), channel_id=1, source_target_pairs={{0,8},{24,16},{1,9},{25,17},{2,10},{26,18},{3,11},{27,19},{4,12},{... | collective-permute-start | bytes 6291464 | tf_op jit(solution)/shard_map/ppermute | solution.py:621
  1133.9 39.6 %collective-permute-done.76 = bf16[512,2048]{1,0:T(8,128)(2,1)S(1)} collective-permute-done((bf16[512,2048]{1,0:T(8,128)(2,1)S(1)}, bf16[512,2048]{1,0:T(8,128)(2,1)S(1)}, u32[]{:S(2)}, u32[]{:S(2)}) %collective-permute-start.76) | collective-permute-done | bytes 2097184 | tf_op jit(solution)/shard_map/ppermute | solution.py:621
  1179.3 27.1 %collective-permute-done.88 = bf16[256,2816]{1,0:T(8,128)(2,1)} collective-permute-done((bf16[256,2816]{1,0:T(8,128)(2,1)S(1)}, bf16[256,2816]{1,0:T(8,128)(2,1)}, u32[]{:S(2)}, u32[]{:S(2)}) %collective-permute-start.88) | collective-permute-done | bytes 1441824 | tf_op jit(solution)/shard_map/ppermute | solution.py:625
  1210.6 4.6 collective-permute-start.58
  1216.6 21.5 %collective-permute-done.93 = bf16[256,2816]{1,0:T(8,128)(2,1)S(1)} collective-permute-done((bf16[256,2816]{1,0:T(8,128)(2,1)S(1)}, bf16[256,2816]{1,0:T(8,128)(2,1)S(1)}, u32[]{:S(2)}, u32[]{:S(2)}) %collective-permute-start.93) | collective-permute-done | bytes 1441824 | tf_op jit(solution)/shard_map/ppermute | solution.py:625
  1240.6 9.3 collective-permute-done.58
  1251.3 32.4 %collective-permute-done.63 = bf16[256,3072]{1,0:T(8,128)(2,1)S(1)} collective-permute-done((bf16[256,3072]{1,0:T(8,128)(2,1)}, bf16[256,3072]{1,0:T(8,128)(2,1)S(1)}, u32[]{:S(2)}, u32[]{:S(2)}) %collective-permute-start.63) | collective-permute-done | bytes 1572896 | tf_op jit(solution)/shard_map/ppermute | solution.py:621
  1287.6 24.8 %collective-permute-done.68 = bf16[256,3072]{1,0:T(8,128)(2,1)S(1)} collective-permute-done((bf16[256,3072]{1,0:T(8,128)(2,1)}, bf16[256,3072]{1,0:T(8,128)(2,1)S(1)}, u32[]{:S(2)}, u32[]{:S(2)}) %collective-permute-start.68) | collective-permute-done | bytes 1572896 | tf_op jit(solution)/shard_map/ppermute | solution.py:621
  1336.7 19.1 %collective-permute-done.74 = bf16[256,3072]{1,0:T(8,128)(2,1)} collective-permute-done((bf16[256,3072]{1,0:T(8,128)(2,1)S(1)}, bf16[256,3072]{1,0:T(8,128)(2,1)}, u32[]{:S(2)}, u32[]{:S(2)}) %collective-permute-start.74) | collective-permute-done | bytes 1572896 | tf_op jit(solution)/shard_map/ppermute | solution.py:625
  1358.7 98.2 %collective-permute-done.60 = bf16[256,3072]{1,0:T(8,128)(2,1)S(1)} collective-permute-done((bf16[256,3072]{1,0:T(8,128)(2,1)S(1)}, bf16[256,3072]{1,0:T(8,128)(2,1)S(1)}, u32[]{:S(2)}, u32[]{:S(2)}) %collective-permute-start.60) | collective-permute-done | bytes 1572896 | tf_op jit(solution)/shard_map/ppermute | solution.py:625
  1458.9 31.8 %collective-permute-done.65 = bf16[256,3072]{1,0:T(8,128)(2,1)} collective-permute-done((bf16[256,3072]{1,0:T(8,128)(2,1)S(1)}, bf16[256,3072]{1,0:T(8,128)(2,1)}, u32[]{:S(2)}, u32[]{:S(2)}) %collective-permute-start.65) | collective-permute-done | bytes 1572896 | tf_op jit(solution)/shard_map/ppermute | solution.py:625
  1492.5 31.8 %collective-permute-done.70 = bf16[256,3072]{1,0:T(8,128)(2,1)S(1)} collective-permute-done((bf16[256,3072]{1,0:T(8,128)(2,1)S(1)}, bf16[256,3072]{1,0:T(8,128)(2,1)S(1)}, u32[]{:S(2)}, u32[]{:S(2)}) %collective-permute-start.70) | collective-permute-done | bytes 1572896 | tf_op jit(solution)/shard_map/ppermute | solution.py:625
  1525.3 37.8 %collective-permute-done.78 = bf16[512,2048]{1,0:T(8,128)(2,1)S(1)} collective-permute-done((bf16[512,2048]{1,0:T(8,128)(2,1)S(1)}, bf16[512,2048]{1,0:T(8,128)(2,1)S(1)}, u32[]{:S(2)}, u32[]{:S(2)}) %collective-permute-start.78) | collective-permute-done | bytes 2097184 | tf_op jit(solution)/shard_map/ppermute | solution.py:625
  (568 shorter events, 333.5 us)
Async XLA Ops:
  0.6 96.3 %collective-permute-start = (bf16[256,2048]{1,0:T(8,128)(2,1)}, bf16[256,2048]{1,0:T(8,128)(2,1)}, u32[]{:S(2)}, u32[]{:S(2)}) collective-permute-start(bf16[256,2048]{1,0:T(8,128)(2,1)} %param.15), channel_id=1, source_target_pairs={{0,2},{1,3},{2,0},{3,1},{4,6},{5,7},{6,4},{7,5},{8,10},{9,11},{10,... | collective-permute-start | bytes 3145736 | tf_op jit(solution)/shard_map/ppermute | solution.py:577
  3.6 97.6 %collective-permute-start.1 = (bf16[256,2048]{1,0:T(8,128)(2,1)}, bf16[256,2048]{1,0:T(8,128)(2,1)}, u32[]{:S(2)}, u32[]{:S(2)}) collective-permute-start(bf16[256,2048]{1,0:T(8,128)(2,1)} %param.15), channel_id=1, source_target_pairs={{0,4},{1,5},{2,6},{3,7},{4,0},{5,1},{6,2},{7,3},{8,12},{9,13},{10,... | collective-permute-start | bytes 3145736 | tf_op jit(solution)/shard_map/ppermute | solution.py:577
  8.9 93.7 %collective-permute-start.36 = (bf16[256,2048]{1,0:T(8,128)(2,1)}, bf16[256,2048]{1,0:T(8,128)(2,1)}, u32[]{:S(2)}, u32[]{:S(2)}) collective-permute-start(bf16[256,2048]{1,0:T(8,128)(2,1)} %get-tuple-element.51), channel_id=1, source_target_pairs={{0,2},{1,3},{2,0},{3,1},{4,6},{5,7},{6,4},{7,5},{8,10},{9,11},{10,... | collective-permute-start | bytes 3145736 | tf_op jit(solution)/shard_map/ppermute | solution.py:577
  9.4 94.7 %collective-permute-start.37 = (bf16[256,2048]{1,0:T(8,128)(2,1)}, bf16[256,2048]{1,0:T(8,128)(2,1)}, u32[]{:S(2)}, u32[]{:S(2)}) collective-permute-start(bf16[256,2048]{1,0:T(8,128)(2,1)} %get-tuple-element.51), channel_id=1, source_target_pairs={{0,4},{1,5},{2,6},{3,7},{4,0},{5,1},{6,2},{7,3},{8,12},{9,13},{10,... | collective-permute-start | bytes 3145736 | tf_op jit(solution)/shard_map/ppermute | solution.py:577
  20.7 93.5 %collective-permute-start.22 = (bf16[256,2816]{1,0:T(8,128)(2,1)}, bf16[256,2816]{1,0:T(8,128)(2,1)}, u32[]{:S(2)}, u32[]{:S(2)}) collective-permute-start(bf16[256,2816]{1,0:T(8,128)(2,1)} %get-tuple-element.122), channel_id=1, source_target_pairs={{0,1},{1,0},{2,3},{3,2},{4,5},{5,4},{6,7},{7,6},{8,9},{9,8},{10,11... | collective-permute-start | bytes 4325384 | tf_op jit(solution)/shard_map/ppermute | solution.py:573
  96.9 34.7 %collective-permute-start.23 = (bf16[256,2816]{1,0:T(8,128)(2,1)}, bf16[256,2816]{1,0:T(8,128)(2,1)}, u32[]{:S(2)}, u32[]{:S(2)}) collective-permute-start(bf16[256,2816]{1,0:T(8,128)(2,1)} %pad_maximum_fusion.8), channel_id=1, source_target_pairs={{0,2},{1,3},{2,0},{3,1},{4,6},{5,7},{6,4},{7,5},{8,10},{9,11},{10,... | collective-permute-start | bytes 4325384 | tf_op jit(solution)/shard_map/ppermute | solution.py:577
  101.3 92.3 %collective-permute-start.11 = (bf16[512,2048]{1,0:T(8,128)(2,1)S(1)}, bf16[512,2048]{1,0:T(8,128)(2,1)S(1)}, u32[]{:S(2)}, u32[]{:S(2)}) collective-permute-start(bf16[512,2048]{1,0:T(8,128)(2,1)S(1)} %copy-done.37), channel_id=1, source_target_pairs={{0,1},{1,0},{2,3},{3,2},{4,5},{5,4},{6,7},{7,6},{8,9},{9,8},{10,11... | collective-permute-start | bytes 6291464 | tf_op jit(solution)/shard_map/ppermute | solution.py:573
  102.5 87.2 %collective-permute-start.4 = (bf16[256,3072]{1,0:T(8,128)(2,1)}, bf16[256,3072]{1,0:T(8,128)(2,1)S(1)}, u32[]{:S(2)}, u32[]{:S(2)}) collective-permute-start(bf16[256,3072]{1,0:T(8,128)(2,1)} %get-tuple-element.120), channel_id=1, source_target_pairs={{0,1},{1,0},{2,3},{3,2},{4,5},{5,4},{6,7},{7,6},{8,9},{9,8},{10,11... | collective-permute-start | bytes 4718600 | tf_op jit(solution)/shard_map/ppermute | solution.py:573
  134.8 56.1 %collective-permute-start.5 = (bf16[256,3072]{1,0:T(8,128)(2,1)S(1)}, bf16[256,3072]{1,0:T(8,128)(2,1)S(1)}, u32[]{:S(2)}, u32[]{:S(2)}) collective-permute-start(bf16[256,3072]{1,0:T(8,128)(2,1)S(1)} %copy-done.41), channel_id=1, source_target_pairs={{0,2},{1,3},{2,0},{3,1},{4,6},{5,7},{6,4},{7,5},{8,10},{9,11},{10,... | collective-permute-start | bytes 4718600 | tf_op jit(solution)/shard_map/ppermute | solution.py:577
  142.8 48.6 %collective-permute-start.7 = (bf16[256,3072]{1,0:T(8,128)(2,1)S(1)}, bf16[256,3072]{1,0:T(8,128)(2,1)S(1)}, u32[]{:S(2)}, u32[]{:S(2)}) collective-permute-start(bf16[256,3072]{1,0:T(8,128)(2,1)S(1)} %copy-done.40), channel_id=1, source_target_pairs={{0,4},{1,5},{2,6},{3,7},{4,0},{5,1},{6,2},{7,3},{8,12},{9,13},{10,... | collective-permute-start | bytes 4718600 | tf_op jit(solution)/shard_map/ppermute | solution.py:577
  144.5 42.7 %collective-permute-start.39 = (bf16[128,2048]{1,0:T(8,128)(2,1)S(1)}, bf16[128,2048]{1,0:T(8,128)(2,1)S(1)}, u32[]{:S(2)}, u32[]{:S(2)}) collective-permute-start(bf16[128,2048]{1,0:T(8,128)(2,1)S(1)} %slice.474), channel_id=1, source_target_pairs={{0,2},{1,3},{2,0},{3,1},{4,6},{5,7},{6,4},{7,5},{8,10},{9,11},{10,... | collective-permute-start | bytes 1572872 | tf_op jit(solution)/shard_map/ppermute | solution.py:577
  187.2 36.9 %collective-permute-start.9 = (bf16[256,3072]{1,0:T(8,128)(2,1)S(1)}, bf16[256,3072]{1,0:T(8,128)(2,1)S(1)}, u32[]{:S(2)}, u32[]{:S(2)}) collective-permute-start(bf16[256,3072]{1,0:T(8,128)(2,1)S(1)} %copy-done.39), channel_id=1, source_target_pairs={{0,6},{1,7},{2,4},{3,5},{4,2},{5,3},{6,0},{7,1},{8,14},{9,15},{10,... | collective-permute-start | bytes 4718600 | tf_op jit(solution)/shard_map/ppermute | solution.py:577
  189.7 34.3 %collective-permute-start.24 = (bf16[256,2816]{1,0:T(8,128)(2,1)}, bf16[256,2816]{1,0:T(8,128)(2,1)S(1)}, u32[]{:S(2)}, u32[]{:S(2)}) collective-permute-start(bf16[256,2816]{1,0:T(8,128)(2,1)} %collective-permute-done.23), channel_id=1, source_target_pairs={{0,1},{1,0},{2,3},{3,2},{4,5},{5,4},{6,7},{7,6},{8,9},{9,8},{10,11... | collective-permute-start | bytes 4325384 | tf_op jit(solution)/shard_map/ppermute | solution.py:573
  190.9 64.0 %collective-permute-start.25 = (bf16[256,2816]{1,0:T(8,128)(2,1)}, bf16[256,2816]{1,0:T(8,128)(2,1)}, u32[]{:S(2)}, u32[]{:S(2)}) collective-permute-start(bf16[256,2816]{1,0:T(8,128)(2,1)} %pad_maximum_fusion.9), channel_id=1, source_target_pairs={{0,4},{1,5},{2,6},{3,7},{4,0},{5,1},{6,2},{7,3},{8,12},{9,13},{10,... | collective-permute-start | bytes 4325384 | tf_op jit(solution)/shard_map/ppermute | solution.py:577
  191.4 65.1 %collective-permute-start.6 = (bf16[256,3072]{1,0:T(8,128)(2,1)S(1)}, bf16[256,3072]{1,0:T(8,128)(2,1)S(1)}, u32[]{:S(2)}, u32[]{:S(2)}) collective-permute-start(bf16[256,3072]{1,0:T(8,128)(2,1)S(1)} %collective-permute-done.5), channel_id=1, source_target_pairs={{0,1},{1,0},{2,3},{3,2},{4,5},{5,4},{6,7},{7,6},{8,9},{9,8},{10,11... | collective-permute-start | bytes 4718600 | tf_op jit(solution)/shard_map/ppermute | solution.py:573
  193.6 65.3 %collective-permute-start.8 = (bf16[256,3072]{1,0:T(8,128)(2,1)S(1)}, bf16[256,3072]{1,0:T(8,128)(2,1)S(1)}, u32[]{:S(2)}, u32[]{:S(2)}) collective-permute-start(bf16[256,3072]{1,0:T(8,128)(2,1)S(1)} %collective-permute-done.7), channel_id=1, source_target_pairs={{0,1},{1,0},{2,3},{3,2},{4,5},{5,4},{6,7},{7,6},{8,9},{9,8},{10,11... | collective-permute-start | bytes 4718600 | tf_op jit(solution)/shard_map/ppermute | solution.py:573
  224.0 148.8 %collective-permute-start.29 = (bf16[704,2048]{1,0:T(8,128)(2,1)}, bf16[704,2048]{1,0:T(8,128)(2,1)}, u32[]{:S(2)}, u32[]{:S(2)}) collective-permute-start(bf16[704,2048]{1,0:T(8,128)(2,1)} %param.29), channel_id=1, source_target_pairs={{0,1},{1,0},{2,3},{3,2},{4,5},{5,4},{6,7},{7,6},{8,9},{9,8},{10,11... | collective-permute-start | bytes 8650760 | tf_op jit(solution)/shard_map/ppermute | solution.py:573
  224.0 37.4 %collective-permute-start.10 = (bf16[256,3072]{1,0:T(8,128)(2,1)S(1)}, bf16[256,3072]{1,0:T(8,128)(2,1)S(1)}, u32[]{:S(2)}, u32[]{:S(2)}) collective-permute-start(bf16[256,3072]{1,0:T(8,128)(2,1)S(1)} %collective-permute-done.9), channel_id=1, source_target_pairs={{0,1},{1,0},{2,3},{3,2},{4,5},{5,4},{6,7},{7,6},{8,9},{9,8},{10,11... | collective-permute-start | bytes 4718600 | tf_op jit(solution)/shard_map/ppermute | solution.py:573
  254.9 92.5 %collective-permute-start.27 = (bf16[256,2816]{1,0:T(8,128)(2,1)S(1)}, bf16[256,2816]{1,0:T(8,128)(2,1)}, u32[]{:S(2)}, u32[]{:S(2)}) collective-permute-start(bf16[256,2816]{1,0:T(8,128)(2,1)S(1)} %copy-done.45), channel_id=1, source_target_pairs={{0,6},{1,7},{2,4},{3,5},{4,2},{5,3},{6,0},{7,1},{8,14},{9,15},{10,... | collective-permute-start | bytes 4325384 | tf_op jit(solution)/shard_map/ppermute | solution.py:577
  256.4 78.3 %collective-permute-start.26 = (bf16[256,2816]{1,0:T(8,128)(2,1)}, bf16[256,2816]{1,0:T(8,128)(2,1)}, u32[]{:S(2)}, u32[]{:S(2)}) collective-permute-start(bf16[256,2816]{1,0:T(8,128)(2,1)} %collective-permute-done.25), channel_id=1, source_target_pairs={{0,1},{1,0},{2,3},{3,2},{4,5},{5,4},{6,7},{7,6},{8,9},{9,8},{10,11... | collective-permute-start | bytes 4325384 | tf_op jit(solution)/shard_map/ppermute | solution.py:573
  479.7 54.4 %collective-permute-start.42 = (bf16[128,2048]{1,0:T(8,128)(2,1)S(1)}, bf16[128,2048]{1,0:T(8,128)(2,1)S(1)}, u32[]{:S(2)}, u32[]{:S(2)}) collective-permute-start(bf16[128,2048]{1,0:T(8,128)(2,1)S(1)} %get-tuple-element.94), channel_id=1, source_target_pairs={{0,4},{1,5},{2,6},{3,7},{4,0},{5,1},{6,2},{7,3},{8,12},{9,13},{10,... | collective-permute-start | bytes 1572872 | tf_op jit(solution)/shard_map/ppermute | solution.py:577
  481.3 37.0 %collective-permute-start.40 = (bf16[128,2048]{1,0:T(8,128)(2,1)}, bf16[128,2048]{1,0:T(8,128)(2,1)S(1)}, u32[]{:S(2)}, u32[]{:S(2)}) collective-permute-start(bf16[128,2048]{1,0:T(8,128)(2,1)} %get-tuple-element.91), channel_id=1, source_target_pairs={{0,4},{1,5},{2,6},{3,7},{4,0},{5,1},{6,2},{7,3},{8,12},{9,13},{10,... | collective-permute-start | bytes 1572872 | tf_op jit(solution)/shard_map/ppermute | solution.py:577
  481.8 37.0 %collective-permute-start.44 = (bf16[128,2048]{1,0:T(8,128)(2,1)}, bf16[128,2048]{1,0:T(8,128)(2,1)S(1)}, u32[]{:S(2)}, u32[]{:S(2)}) collective-permute-start(bf16[128,2048]{1,0:T(8,128)(2,1)} %get-tuple-element.92), channel_id=1, source_target_pairs={{0,2},{1,3},{2,0},{3,1},{4,6},{5,7},{6,4},{7,5},{8,10},{9,11},{10,... | collective-permute-start | bytes 1572872 | tf_op jit(solution)/shard_map/ppermute | solution.py:577
  483.3 52.4 %collective-permute-start.43 = (bf16[128,2048]{1,0:T(8,128)(2,1)S(1)}, bf16[128,2048]{1,0:T(8,128)(2,1)S(1)}, u32[]{:S(2)}, u32[]{:S(2)}) collective-permute-start(bf16[128,2048]{1,0:T(8,128)(2,1)S(1)} %get-tuple-element.93), channel_id=1, source_target_pairs={{0,2},{1,3},{2,0},{3,1},{4,6},{5,7},{6,4},{7,5},{8,10},{9,11},{10,... | collective-permute-start | bytes 1572872 | tf_op jit(solution)/shard_map/ppermute | solution.py:577
  483.8 37.0 %collective-permute-start.30 = (bf16[128,2048]{1,0:T(8,128)(2,1)}, bf16[128,2048]{1,0:T(8,128)(2,1)S(1)}, u32[]{:S(2)}, u32[]{:S(2)}) collective-permute-start(bf16[128,2048]{1,0:T(8,128)(2,1)} %get-tuple-element.97), channel_id=1, source_target_pairs={{0,4},{1,5},{2,6},{3,7},{4,0},{5,1},{6,2},{7,3},{8,12},{9,13},{10,... | collective-permute-start | bytes 1572872 | tf_op jit(solution)/shard_map/ppermute | solution.py:577
  555.5 43.0 %collective-permute-start.89 = (bf16[256,2816]{1,0:T(8,128)(2,1)}, bf16[256,2816]{1,0:T(8,128)(2,1)}, u32[]{:S(2)}, u32[]{:S(2)}) collective-permute-start(bf16[256,2816]{1,0:T(8,128)(2,1)} %constant_dynamic-slice_fusion.2), channel_id=1, source_target_pairs={{0,1},{1,0},{2,3},{3,2},{4,5},{5,4},{6,7},{7,6},{8,9},{9,8},{10,11... | collective-permute-start | bytes 4325384 | tf_op jit(solution)/shard_map/ppermute | solution.py:573
  561.1 227.3 %collective-permute-start.98 = (bf16[704,2048]{1,0:T(8,128)(2,1)}, bf16[704,2048]{1,0:T(8,128)(2,1)}, u32[]{:S(2)}, u32[]{:S(2)}) collective-permute-start(bf16[704,2048]{1,0:T(8,128)(2,1)} %constant_dynamic-slice_fusion), channel_id=1, source_target_pairs={{0,1},{1,0},{2,3},{3,2},{4,5},{5,4},{6,7},{7,6},{8,9},{9,8},{10,11... | collective-permute-start | bytes 8650760 | tf_op jit(solution)/shard_map/ppermute | solution.py:573
  571.3 57.0 %collective-permute-start.47 = (bf16[256,2048]{1,0:T(8,128)(2,1)S(1)}, bf16[256,2048]{1,0:T(8,128)(2,1)S(1)}, u32[]{:S(2)}, u32[]{:S(2)}) collective-permute-start(bf16[256,2048]{1,0:T(8,128)(2,1)S(1)} %get-tuple-element.48), channel_id=1, source_target_pairs={{0,4},{1,5},{2,6},{3,7},{4,0},{5,1},{6,2},{7,3},{8,12},{9,13},{10,... | collective-permute-start | bytes 3145736 | tf_op jit(solution)/shard_map/ppermute | solution.py:577
  575.7 289.8 %collective-permute-start.80 = (bf16[256,2816]{1,0:T(8,128)(2,1)}, bf16[256,2816]{1,0:T(8,128)(2,1)}, u32[]{:S(2)}, u32[]{:S(2)}) collective-permute-start(bf16[256,2816]{1,0:T(8,128)(2,1)} %add_convert_fusion.29), channel_id=1, source_target_pairs={{0,6},{1,7},{2,4},{3,5},{4,2},{5,3},{6,0},{7,1},{8,14},{9,15},{10,... | collective-permute-start | bytes 4325384 | tf_op jit(solution)/shard_map/ppermute | solution.py:577
  593.8 175.4 %collective-permute-start.95 = (bf16[256,2816]{1,0:T(8,128)(2,1)S(1)}, bf16[256,2816]{1,0:T(8,128)(2,1)}, u32[]{:S(2)}, u32[]{:S(2)}) collective-permute-start(bf16[256,2816]{1,0:T(8,128)(2,1)S(1)} %add_convert_fusion.20), channel_id=1, source_target_pairs={{0,8},{24,16},{1,9},{25,17},{2,10},{26,18},{3,11},{27,19},{4,12},{... | collective-permute-start | bytes 4325384 | tf_op jit(solution)/shard_map/ppermute | solution.py:621
  598.5 39.7 %collective-permute-start.48 = (bf16[128,2048]{1,0:T(8,128)(2,1)S(1)}, bf16[128,2048]{1,0:T(8,128)(2,1)S(1)}, u32[]{:S(2)}, u32[]{:S(2)}) collective-permute-start(bf16[128,2048]{1,0:T(8,128)(2,1)S(1)} %slice.484), channel_id=1, source_target_pairs={{0,4},{1,5},{2,6},{3,7},{4,0},{5,1},{6,2},{7,3},{8,12},{9,13},{10,... | collective-permute-start | bytes 1572872 | tf_op jit(solution)/shard_map/ppermute | solution.py:577
  754.2 39.4 %collective-permute-start.52 = (bf16[128,2048]{1,0:T(8,128)(2,1)}, bf16[128,2048]{1,0:T(8,128)(2,1)}, u32[]{:S(2)}, u32[]{:S(2)}) collective-permute-start(bf16[128,2048]{1,0:T(8,128)(2,1)} %get-tuple-element.88), channel_id=1, source_target_pairs={{0,4},{1,5},{2,6},{3,7},{4,0},{5,1},{6,2},{7,3},{8,12},{9,13},{10,... | collective-permute-start | bytes 1572872 | tf_op jit(solution)/shard_map/ppermute | solution.py:577
  793.6 75.8 %collective-permute-start.85 = (bf16[256,2816]{1,0:T(8,128)(2,1)}, bf16[256,2816]{1,0:T(8,128)(2,1)}, u32[]{:S(2)}, u32[]{:S(2)}) collective-permute-start(bf16[256,2816]{1,0:T(8,128)(2,1)} %add_convert_fusion.26), channel_id=1, source_target_pairs={{0,4},{1,5},{2,6},{3,7},{4,0},{5,1},{6,2},{7,3},{8,12},{9,13},{10,... | collective-permute-start | bytes 4325384 | tf_op jit(solution)/shard_map/ppermute | solution.py:577
  796.1 61.1 %collective-permute-start.56 = (bf16[256,3072]{1,0:T(8,128)(2,1)}, bf16[256,3072]{1,0:T(8,128)(2,1)}, u32[]{:S(2)}, u32[]{:S(2)}) collective-permute-start(bf16[256,3072]{1,0:T(8,128)(2,1)} %constant_dynamic-slice_fusion.9), channel_id=1, source_target_pairs={{0,1},{1,0},{2,3},{3,2},{4,5},{5,4},{6,7},{7,6},{8,9},{9,8},{10,11... | collective-permute-start | bytes 4718600 | tf_op jit(solution)/shard_map/ppermute | solution.py:573
  803.5 56.4 %collective-permute-start.61 = (bf16[256,3072]{1,0:T(8,128)(2,1)}, bf16[256,3072]{1,0:T(8,128)(2,1)}, u32[]{:S(2)}, u32[]{:S(2)}) collective-permute-start(bf16[256,3072]{1,0:T(8,128)(2,1)} %constant_dynamic-slice_fusion.8), channel_id=1, source_target_pairs={{0,1},{1,0},{2,3},{3,2},{4,5},{5,4},{6,7},{7,6},{8,9},{9,8},{10,11... | collective-permute-start | bytes 4718600 | tf_op jit(solution)/shard_map/ppermute | solution.py:573
  860.0 34.6 %collective-permute-start.90 = (bf16[256,2816]{1,0:T(8,128)(2,1)S(1)}, bf16[256,2816]{1,0:T(8,128)(2,1)S(1)}, u32[]{:S(2)}, u32[]{:S(2)}) collective-permute-start(bf16[256,2816]{1,0:T(8,128)(2,1)S(1)} %copy-done.46), channel_id=1, source_target_pairs={{0,2},{1,3},{2,0},{3,1},{4,6},{5,7},{6,4},{7,5},{8,10},{9,11},{10,... | collective-permute-start | bytes 4325384 | tf_op jit(solution)/shard_map/ppermute | solution.py:577
  865.5 163.5 %collective-permute-start.75 = (bf16[512,2048]{1,0:T(8,128)(2,1)S(1)}, bf16[512,2048]{1,0:T(8,128)(2,1)S(1)}, u32[]{:S(2)}, u32[]{:S(2)}) collective-permute-start(bf16[512,2048]{1,0:T(8,128)(2,1)S(1)} %copy-done.38), channel_id=1, source_target_pairs={{0,1},{1,0},{2,3},{3,2},{4,5},{5,4},{6,7},{7,6},{8,9},{9,8},{10,11... | collective-permute-start | bytes 6291464 | tf_op jit(solution)/shard_map/ppermute | solution.py:573
  865.8 33.7 %collective-permute-start.81 = (bf16[256,2816]{1,0:T(8,128)(2,1)}, bf16[256,2816]{1,0:T(8,128)(2,1)S(1)}, u32[]{:S(2)}, u32[]{:S(2)}) collective-permute-start(bf16[256,2816]{1,0:T(8,128)(2,1)} %collective-permute-done.80), channel_id=1, source_target_pairs={{0,8},{24,16},{1,9},{25,17},{2,10},{26,18},{3,11},{27,19},{4,12},{... | collective-permute-start | bytes 4325384 | tf_op jit(solution)/shard_map/ppermute | solution.py:621
  869.5 158.1 %collective-permute-start.96 = (bf16[256,2816]{1,0:T(8,128)(2,1)S(1)}, bf16[256,2816]{1,0:T(8,128)(2,1)S(1)}, u32[]{:S(2)}, u32[]{:S(2)}) collective-permute-start(bf16[256,2816]{1,0:T(8,128)(2,1)S(1)} %copy-done.10), channel_id=1, source_target_pairs={{8,16},{16,8},{9,17},{17,9},{10,18},{18,10},{11,19},{19,11},{12,20... | collective-permute-start | bytes 4325384 | tf_op jit(solution)/shard_map/ppermute | solution.py:623
  870.4 60.0 %collective-permute-start.86 = (bf16[256,2816]{1,0:T(8,128)(2,1)}, bf16[256,2816]{1,0:T(8,128)(2,1)S(1)}, u32[]{:S(2)}, u32[]{:S(2)}) collective-permute-start(bf16[256,2816]{1,0:T(8,128)(2,1)} %collective-permute-done.85), channel_id=1, source_target_pairs={{0,8},{24,16},{1,9},{25,17},{2,10},{26,18},{3,11},{27,19},{4,12},{... | collective-permute-start | bytes 4325384 | tf_op jit(solution)/shard_map/ppermute | solution.py:621
  894.6 236.3 %collective-permute-start.99 = (bf16[704,2048]{1,0:T(8,128)(2,1)S(1)}, bf16[704,2048]{1,0:T(8,128)(2,1)S(1)}, u32[]{:S(2)}, u32[]{:S(2)}) collective-permute-start(bf16[704,2048]{1,0:T(8,128)(2,1)S(1)} %copy-done.7), channel_id=1, source_target_pairs={{0,8},{24,16},{1,9},{25,17},{2,10},{26,18},{3,11},{27,19},{4,12},{... | collective-permute-start | bytes 8650760 | tf_op jit(solution)/shard_map/ppermute | solution.py:621
  899.5 123.2 %collective-permute-start.91 = (bf16[256,2816]{1,0:T(8,128)(2,1)S(1)}, bf16[256,2816]{1,0:T(8,128)(2,1)S(1)}, u32[]{:S(2)}, u32[]{:S(2)}) collective-permute-start(bf16[256,2816]{1,0:T(8,128)(2,1)S(1)} %collective-permute-done.90), channel_id=1, source_target_pairs={{0,8},{24,16},{1,9},{25,17},{2,10},{26,18},{3,11},{27,19},{4,12},{... | collective-permute-start | bytes 4325384 | tf_op jit(solution)/shard_map/ppermute | solution.py:621
  930.4 279.3 %collective-permute-start.57 = (bf16[256,3072]{1,0:T(8,128)(2,1)S(1)}, bf16[256,3072]{1,0:T(8,128)(2,1)S(1)}, u32[]{:S(2)}, u32[]{:S(2)}) collective-permute-start(bf16[256,3072]{1,0:T(8,128)(2,1)S(1)} %add_convert_fusion.17), channel_id=1, source_target_pairs={{0,6},{1,7},{2,4},{3,5},{4,2},{5,3},{6,0},{7,1},{8,14},{9,15},{10,... | collective-permute-start | bytes 4718600 | tf_op jit(solution)/shard_map/ppermute | solution.py:577
  1022.7 38.0 %collective-permute-start.72 = (bf16[256,3072]{1,0:T(8,128)(2,1)S(1)}, bf16[256,3072]{1,0:T(8,128)(2,1)S(1)}, u32[]{:S(2)}, u32[]{:S(2)}) collective-permute-start(bf16[256,3072]{1,0:T(8,128)(2,1)S(1)} %add_convert_fusion.8), channel_id=1, source_target_pairs={{0,8},{24,16},{1,9},{25,17},{2,10},{26,18},{3,11},{27,19},{4,12},{... | collective-permute-start | bytes 4718600 | tf_op jit(solution)/shard_map/ppermute | solution.py:621
  1027.6 34.4 %collective-permute-start.82 = (bf16[256,2816]{1,0:T(8,128)(2,1)S(1)}, bf16[256,2816]{1,0:T(8,128)(2,1)S(1)}, u32[]{:S(2)}, u32[]{:S(2)}) collective-permute-start(bf16[256,2816]{1,0:T(8,128)(2,1)S(1)} %add_convert_fusion.28), channel_id=1, source_target_pairs={{8,16},{16,8},{9,17},{17,9},{10,18},{18,10},{11,19},{19,11},{12,20... | collective-permute-start | bytes 4325384 | tf_op jit(solution)/shard_map/ppermute | solution.py:623
  1029.0 181.6 %collective-permute-start.62 = (bf16[256,3072]{1,0:T(8,128)(2,1)}, bf16[256,3072]{1,0:T(8,128)(2,1)}, u32[]{:S(2)}, u32[]{:S(2)}) collective-permute-start(bf16[256,3072]{1,0:T(8,128)(2,1)} %add_convert_fusion.14), channel_id=1, source_target_pairs={{0,4},{1,5},{2,6},{3,7},{4,0},{5,1},{6,2},{7,3},{8,12},{9,13},{10,... | collective-permute-start | bytes 4718600 | tf_op jit(solution)/shard_map/ppermute | solution.py:577
  1063.2 70.4 %collective-permute-start.97 = (bf16[256,2816]{1,0:T(8,128)(2,1)S(1)}, bf16[256,2816]{1,0:T(8,128)(2,1)S(1)}, u32[]{:S(2)}, u32[]{:S(2)}) collective-permute-start(bf16[256,2816]{1,0:T(8,128)(2,1)S(1)} %add_convert_fusion.18), channel_id=1, source_target_pairs={{8,0},{16,24},{9,1},{17,25},{10,2},{18,26},{11,3},{19,27},{12,4},{... | collective-permute-start | bytes 4325384 | tf_op jit(solution)/shard_map/ppermute | solution.py:625
  1064.9 108.6 %collective-permute-start.76 = (bf16[512,2048]{1,0:T(8,128)(2,1)S(1)}, bf16[512,2048]{1,0:T(8,128)(2,1)S(1)}, u32[]{:S(2)}, u32[]{:S(2)}) collective-permute-start(bf16[512,2048]{1,0:T(8,128)(2,1)S(1)} %add_convert_fusion.5), channel_id=1, source_target_pairs={{0,8},{24,16},{1,9},{25,17},{2,10},{26,18},{3,11},{27,19},{4,12},{... | collective-permute-start | bytes 6291464 | tf_op jit(solution)/shard_map/ppermute | solution.py:621
  1130.9 44.8 %collective-permute-start.83 = (bf16[256,2816]{1,0:T(8,128)(2,1)S(1)}, bf16[256,2816]{1,0:T(8,128)(2,1)S(1)}, u32[]{:S(2)}, u32[]{:S(2)}) collective-permute-start(bf16[256,2816]{1,0:T(8,128)(2,1)S(1)} %add_convert_fusion.27), channel_id=1, source_target_pairs={{8,0},{16,24},{9,1},{17,25},{10,2},{18,26},{11,3},{19,27},{12,4},{... | collective-permute-start | bytes 4325384 | tf_op jit(solution)/shard_map/ppermute | solution.py:625
  1133.6 81.5 %collective-permute-start.67 = (bf16[256,3072]{1,0:T(8,128)(2,1)S(1)}, bf16[256,3072]{1,0:T(8,128)(2,1)}, u32[]{:S(2)}, u32[]{:S(2)}) collective-permute-start(bf16[256,3072]{1,0:T(8,128)(2,1)S(1)} %add_convert_fusion.11), channel_id=1, source_target_pairs={{0,2},{1,3},{2,0},{3,1},{4,6},{5,7},{6,4},{7,5},{8,10},{9,11},{10,... | collective-permute-start | bytes 4718600 | tf_op jit(solution)/shard_map/ppermute | solution.py:577
  1173.5 32.8 %collective-permute-start.88 = (bf16[256,2816]{1,0:T(8,128)(2,1)S(1)}, bf16[256,2816]{1,0:T(8,128)(2,1)}, u32[]{:S(2)}, u32[]{:S(2)}) collective-permute-start(bf16[256,2816]{1,0:T(8,128)(2,1)S(1)} %add_convert_fusion.24), channel_id=1, source_target_pairs={{8,0},{16,24},{9,1},{17,25},{10,2},{18,26},{11,3},{19,27},{12,4},{... | collective-permute-start | bytes 4325384 | tf_op jit(solution)/shard_map/ppermute | solution.py:625
  1175.7 139.7 %collective-permute-start.73 = (bf16[256,3072]{1,0:T(8,128)(2,1)S(1)}, bf16[256,3072]{1,0:T(8,128)(2,1)}, u32[]{:S(2)}, u32[]{:S(2)}) collective-permute-start(bf16[256,3072]{1,0:T(8,128)(2,1)S(1)} %add_convert_fusion.7), channel_id=1, source_target_pairs={{8,16},{16,8},{9,17},{17,9},{10,18},{18,10},{11,19},{19,11},{12,20... | collective-permute-start | bytes 4718600 | tf_op jit(solution)/shard_map/ppermute | solution.py:623
  1209.7 109.6 %collective-permute-start.100 = (bf16[704,2048]{1,0:T(8,128)(2,1)S(1)}, bf16[704,2048]{1,0:T(8,128)(2,1)S(1)}, u32[]{:S(2)}, u32[]{:S(2)}) collective-permute-start(bf16[704,2048]{1,0:T(8,128)(2,1)S(1)} %add_convert_fusion.1), channel_id=1, source_target_pairs={{8,16},{16,8},{9,17},{17,9},{10,18},{18,10},{11,19},{19,11},{12,20... | collective-permute-start | bytes 8650760 | tf_op jit(solution)/shard_map/ppermute | solution.py:623
  1210.6 39.3 %collective-permute-start.58 = (bf16[256,3072]{1,0:T(8,128)(2,1)S(1)}, bf16[256,3072]{1,0:T(8,128)(2,1)S(1)}, u32[]{:S(2)}, u32[]{:S(2)}) collective-permute-start(bf16[256,3072]{1,0:T(8,128)(2,1)S(1)} %collective-permute-done.57), channel_id=1, source_target_pairs={{0,8},{24,16},{1,9},{25,17},{2,10},{26,18},{3,11},{27,19},{4,12},{... | collective-permute-start | bytes 4718600 | tf_op jit(solution)/shard_map/ppermute | solution.py:621
  1215.2 68.5 %collective-permute-start.63 = (bf16[256,3072]{1,0:T(8,128)(2,1)}, bf16[256,3072]{1,0:T(8,128)(2,1)S(1)}, u32[]{:S(2)}, u32[]{:S(2)}) collective-permute-start(bf16[256,3072]{1,0:T(8,128)(2,1)} %collective-permute-done.62), channel_id=1, source_target_pairs={{0,8},{24,16},{1,9},{25,17},{2,10},{26,18},{3,11},{27,19},{4,12},{... | collective-permute-start | bytes 4718600 | tf_op jit(solution)/shard_map/ppermute | solution.py:621
  1238.1 74.3 %collective-permute-start.68 = (bf16[256,3072]{1,0:T(8,128)(2,1)}, bf16[256,3072]{1,0:T(8,128)(2,1)S(1)}, u32[]{:S(2)}, u32[]{:S(2)}) collective-permute-start(bf16[256,3072]{1,0:T(8,128)(2,1)} %collective-permute-done.67), channel_id=1, source_target_pairs={{0,8},{24,16},{1,9},{25,17},{2,10},{26,18},{3,11},{27,19},{4,12},{... | collective-permute-start | bytes 4718600 | tf_op jit(solution)/shard_map/ppermute | solution.py:621
  1249.9 84.6 %collective-permute-start.77 = (bf16[512,2048]{1,0:T(8,128)(2,1)S(1)}, bf16[512,2048]{1,0:T(8,128)(2,1)S(1)}, u32[]{:S(2)}, u32[]{:S(2)}) collective-permute-start(bf16[512,2048]{1,0:T(8,128)(2,1)S(1)} %add_convert_fusion.4), channel_id=1, source_target_pairs={{8,16},{16,8},{9,17},{17,9},{10,18},{18,10},{11,19},{19,11},{12,20... | collective-permute-start | bytes 6291464 | tf_op jit(solution)/shard_map/ppermute | solution.py:623
  1283.7 39.8 %collective-permute-start.59 = (bf16[256,3072]{1,0:T(8,128)(2,1)S(1)}, bf16[256,3072]{1,0:T(8,128)(2,1)}, u32[]{:S(2)}, u32[]{:S(2)}) collective-permute-start(bf16[256,3072]{1,0:T(8,128)(2,1)S(1)} %add_convert_fusion.16), channel_id=1, source_target_pairs={{8,16},{16,8},{9,17},{17,9},{10,18},{18,10},{11,19},{19,11},{12,20... | collective-permute-start | bytes 4718600 | tf_op jit(solution)/shard_map/ppermute | solution.py:623
  1319.3 36.4 %collective-permute-start.74 = (bf16[256,3072]{1,0:T(8,128)(2,1)S(1)}, bf16[256,3072]{1,0:T(8,128)(2,1)}, u32[]{:S(2)}, u32[]{:S(2)}) collective-permute-start(bf16[256,3072]{1,0:T(8,128)(2,1)S(1)} %add_convert_fusion.6), channel_id=1, source_target_pairs={{8,0},{16,24},{9,1},{17,25},{10,2},{18,26},{11,3},{19,27},{12,4},{... | collective-permute-start | bytes 4718600 | tf_op jit(solution)/shard_map/ppermute | solution.py:625
  1323.5 241.9 %collective-permute-start.101 = (bf16[704,2048]{1,0:T(8,128)(2,1)}, bf16[704,2048]{1,0:T(8,128)(2,1)S(1)}, u32[]{:S(2)}, u32[]{:S(2)}) collective-permute-start(bf16[704,2048]{1,0:T(8,128)(2,1)} %add_convert_fusion), channel_id=1, source_target_pairs={{8,0},{16,24},{9,1},{17,25},{10,2},{18,26},{11,3},{19,27},{12,4},{... | collective-permute-start | bytes 8650760 | tf_op jit(solution)/shard_map/ppermute | solution.py:625
  1327.9 128.9 %collective-permute-start.60 = (bf16[256,3072]{1,0:T(8,128)(2,1)S(1)}, bf16[256,3072]{1,0:T(8,128)(2,1)S(1)}, u32[]{:S(2)}, u32[]{:S(2)}) collective-permute-start(bf16[256,3072]{1,0:T(8,128)(2,1)S(1)} %add_convert_fusion.15), channel_id=1, source_target_pairs={{8,0},{16,24},{9,1},{17,25},{10,2},{18,26},{11,3},{19,27},{12,4},{... | collective-permute-start | bytes 4718600 | tf_op jit(solution)/shard_map/ppermute | solution.py:625
  1331.2 159.4 %collective-permute-start.65 = (bf16[256,3072]{1,0:T(8,128)(2,1)S(1)}, bf16[256,3072]{1,0:T(8,128)(2,1)}, u32[]{:S(2)}, u32[]{:S(2)}) collective-permute-start(bf16[256,3072]{1,0:T(8,128)(2,1)S(1)} %add_convert_fusion.12), channel_id=1, source_target_pairs={{8,0},{16,24},{9,1},{17,25},{10,2},{18,26},{11,3},{19,27},{12,4},{... | collective-permute-start | bytes 4718600 | tf_op jit(solution)/shard_map/ppermute | solution.py:625
  1334.5 189.7 %collective-permute-start.70 = (bf16[256,3072]{1,0:T(8,128)(2,1)S(1)}, bf16[256,3072]{1,0:T(8,128)(2,1)S(1)}, u32[]{:S(2)}, u32[]{:S(2)}) collective-permute-start(bf16[256,3072]{1,0:T(8,128)(2,1)S(1)} %add_convert_fusion.9), channel_id=1, source_target_pairs={{8,0},{16,24},{9,1},{17,25},{10,2},{18,26},{11,3},{19,27},{12,4},{... | collective-permute-start | bytes 4718600 | tf_op jit(solution)/shard_map/ppermute | solution.py:625
  1355.7 207.3 %collective-permute-start.78 = (bf16[512,2048]{1,0:T(8,128)(2,1)S(1)}, bf16[512,2048]{1,0:T(8,128)(2,1)S(1)}, u32[]{:S(2)}, u32[]{:S(2)}) collective-permute-start(bf16[512,2048]{1,0:T(8,128)(2,1)S(1)} %add_convert_fusion.3), channel_id=1, source_target_pairs={{8,0},{16,24},{9,1},{17,25},{10,2},{18,26},{11,3},{19,27},{12,4},{... | collective-permute-start | bytes 6291464 | tf_op jit(solution)/shard_map/ppermute | solution.py:625
  (117 other events, 1824.8 us)

commit v2 on v1

v2 whole, which is shorter than its diff:
```python
from functools import partial

import jax
import jax.numpy as jnp
from jax import lax
from jax.experimental import pallas as pl
from jax.experimental.pallas import tpu as pltpu
from jax.sharding import PartitionSpec as P

H = 16
DK = 128
DV = 256
KCONV = 4
BLOCK = 64
TOK_DEV = 256
eps_norm = 1e-05
eps_unit = 1e-06
bf16 = jnp.bfloat16
f32 = jnp.float32


def mm(a, b):
    return lax.dot_general(
        a.astype(bf16), b.astype(bf16), (((1,), (0,)), ((), ())), preferred_element_type=f32
    )


def mm_nt(a, b):
    return lax.dot_general(
        a.astype(bf16), b.astype(bf16), (((1,), (1,)), ((), ())), preferred_element_type=f32
    )


def mm_tn(a, b):
    return lax.dot_general(
        a.astype(bf16), b.astype(bf16), (((0,), (0,)), ((), ())), preferred_element_type=f32
    )


def mm_exact(a, b):
    return lax.dot_general(
        a, b, (((1,), (0,)), ((), ())), precision=lax.Precision.HIGHEST, preferred_element_type=f32
    )


def silu(v):
    return v * jax.nn.sigmoid(v)


def shifted_down(x, s):
    if s == 0:
        return x
    row = lax.broadcasted_iota(jnp.int32, x.shape, 0)
    return jnp.where(row >= s, pltpu.roll(x, s, 0), 0.0)


def shifted_up(x, s):
    if s == 0:
        return x
    n = x.shape[0]
    row = lax.broadcasted_iota(jnp.int32, x.shape, 0)
    return jnp.where(row < n - s, pltpu.roll(x, n - s, 0), 0.0)


def conv_forward(mixed, weight):
    out = weight[KCONV - 1 : KCONV, :] * mixed
    for s in range(1, KCONV):
        out = out + weight[KCONV - 1 - s : KCONV - s, :] * shifted_down(mixed, s)
    return out


def conv_backward(d_conv, mixed, weight):
    d_mixed = weight[KCONV - 1 : KCONV, :] * d_conv
    rows = [None] * KCONV
    rows[KCONV - 1] = jnp.sum(d_conv * mixed, axis=0, keepdims=True)
    for s in range(1, KCONV):
        up = shifted_up(d_conv, s)
        d_mixed = d_mixed + weight[KCONV - 1 - s : KCONV - s, :] * up
        rows[KCONV - 1 - s] = jnp.sum(up * mixed, axis=0, keepdims=True)
    return d_mixed, jnp.concatenate(rows, axis=0)


def block_masks(n):
    i = lax.broadcasted_iota(jnp.int32, (n, n), 0)
    j = lax.broadcasted_iota(jnp.int32, (n, n), 1)
    x = i ^ j
    same = x < BLOCK
    return x, i > j, jnp.logical_and(same, i >= j), jnp.logical_and(same, i > j), same


def decay_parts(dec, alog_row, bias_row):
    pre = dec + bias_row
    softplus = jnp.maximum(pre, 0.0) + jnp.log1p(jnp.exp(-jnp.abs(pre)))
    log_decay = -jnp.exp(alog_row) * softplus
    n = dec.shape[0]
    i = lax.broadcasted_iota(jnp.int32, (n, n), 0)
    j = lax.broadcasted_iota(jnp.int32, (n, n), 1)
    same = (i ^ j) < BLOCK
    lower = jnp.where(jnp.logical_and(same, i >= j), 1.0, 0.0)
    whole = jnp.where(same, 1.0, 0.0)
    running = mm_exact(lower, log_decay)
    total = mm_exact(whole, log_decay)
    return pre, log_decay, running, total


def lane_of(x, h):
    lane = lax.broadcasted_iota(jnp.int32, x.shape, 1)
    return jnp.sum(jnp.where(lane == h, x, 0.0), axis=1, keepdims=True)


def row_of(x, h):
    row = lax.broadcasted_iota(jnp.int32, x.shape, 0)
    return jnp.sum(jnp.where(row == h, x, 0.0), axis=0, keepdims=True)


def unit_rows(a, scale):
    r = lax.rsqrt(jnp.sum(a * a, axis=1, keepdims=True) + eps_unit)
    return a * r * scale, r


def inverse_blocks(lowers, x, below):
    eye = jnp.where(x == 0, 1.0, 0.0)
    inv = [eye - jnp.where(x == 1, low, 0.0) for low in lowers]
    level = 1
    while (2 << level) <= BLOCK:
        pick = lax.shift_right_logical(x, level) == 1
        half = [mm(jnp.where(pick, low, 0.0), t) for low, t in zip(lowers, inv)]
        inv = [t - mm(t, u) for t, u in zip(inv, half)]
        level += 1
    return inv


def forward_kernel(
    hl,
    pair,
    p,
    ids_ref,
    x_ref,
    dec_ref,
    conv_ref,
    head_ref,
    gain_ref,
    gated_ref,
    o_ref,
    u_ref,
    w_ref,
    inv_ref,
    s_ref,
):
    n = TOK_DEV
    qk, vv = pair * DK, pair * DV
    blocks = n // BLOCK
    x, below, on_below, strict, same = block_masks(n)
    dec = dec_ref[...]
    pre, log_decay, running, total = decay_parts(dec, head_ref[0:1, :], head_ref[1:2, :])
    running_t = running.T
    heads = range(pair)
    q = silu(conv_forward(x_ref[:, :qk], conv_ref[:, :qk]))
    k = silu(conv_forward(x_ref[:, qk : 2 * qk], conv_ref[:, qk : 2 * qk]))
    v = silu(conv_forward(x_ref[:, 2 * qk : 2 * qk + vv], conv_ref[:, 2 * qk :])).astype(bf16)
    qn, kn, vn, beta, b, tot, fade, low, score = [], [], [], [], [], [], [], [], []
    for i in heads:
        h = ids_ref[0] * hl + p * pair + i
        qn.append(unit_rows(q[:, i * DK : (i + 1) * DK], DK**-0.5)[0].astype(bf16))
        kn.append(unit_rows(k[:, i * DK : (i + 1) * DK], 1.0)[0].astype(bf16))
        vn.append(v[:, i * DV : (i + 1) * DV])
        beta.append(jax.nn.sigmoid(lane_of(dec, H + h)))
        b.append(lane_of(running, h))
        tot.append(lane_of(total, h))
        d = jnp.where(on_below, jnp.exp(jnp.where(on_below, b[i] - row_of(running_t, h), 0.0)), 0.0)
        both = mm_nt(jnp.concatenate([kn[i], qn[i]], axis=0), kn[i])
        low.append(jnp.where(strict, beta[i] * d * both[:n], 0.0))
        score.append((both[n:] * d).astype(bf16))
    inv = inverse_blocks(low, x, below)
    e = [jnp.exp(b[i]) for i in heads]
    fin = [jnp.exp(tot[i] - b[i]) for i in heads]
    grow = [jnp.exp(tot[i]) for i in heads]
    inv = [t.astype(bf16) for t in inv]
    right = [
        jnp.concatenate(
            [beta[i] * vn[i].astype(f32), (beta[i] * e[i]) * kn[i].astype(f32)], axis=1
        ).astype(bf16)
        for i in heads
    ]
    uw = [mm(inv[i], right[i]) for i in heads]
    w = [uw[i][:, DV:].astype(bf16) for i in heads]
    state = [jnp.zeros((DK, DV), f32) for i in heads]
    u_parts = [[] for i in heads]
    o_parts = [[] for i in heads]
    for c in range(blocks):
        lo, hi = c * BLOCK, (c + 1) * BLOCK
        for i in heads:
            sb = state[i].astype(bf16)
            s_ref[0, i, c * DK : (c + 1) * DK, :] = sb
            got = mm(jnp.concatenate([w[i][lo:hi], qn[i][lo:hi]], axis=0), sb)
            u = uw[i][lo:hi, :DV] - got[:BLOCK]
            u_parts[i].append(u)
            o_parts[i].append(e[i][lo:hi] * got[BLOCK:])
            if c < blocks - 1:
                state[i] = grow[i][lo : lo + 1] * state[i] + mm_tn(
                    kn[i][lo:hi], fin[i][lo:hi] * u
                )
    gain = gain_ref[0:1, :]
    for i in heads:
        u = jnp.concatenate(u_parts[i], axis=0).astype(bf16)
        out = jnp.concatenate(o_parts[i], axis=0) + mm(score[i], u)
        cols = slice(i * DV, (i + 1) * DV)
        o_ref[:, cols] = out
        u_ref[:, cols] = u
        w_ref[:, i * DK : (i + 1) * DK] = w[i]
        inv_ref[0, i] = inv[i]
        r = lax.rsqrt(jnp.mean(out * out, axis=1, keepdims=True) + eps_norm)
        gated_ref[:, cols] = (out * r * gain * silu(x_ref[:, 2 * qk + vv + i * DV : 2 * qk + vv + (i + 1) * DV])).astype(bf16)


def mixer_forward(ids, proj, dec, conv, head_rows, gain_row, hl, pair, p):
    tokens = proj.shape[0]
    slots = tokens // TOK_DEV
    qk = pair * DK
    vv = pair * DV
    spec = pl.BlockSpec
    n = TOK_DEV

    def body(*refs):
        forward_kernel(hl, pair, p, *refs)

    return pl.pallas_call(
        body,
        grid=(slots,),
        in_specs=[
            pl.BlockSpec(memory_space=pltpu.SMEM),
            spec((n, 2 * qk + 2 * vv), lambda s: (s, 0)),
            spec((n, 128), lambda s: (s, dec.shape[1] // 128 - 1)),
            spec((8, 2 * qk + vv), lambda s: (0, 0)),
            spec((8, 128), lambda s: (0, 0)),
            spec((8, DV), lambda s: (0, 0)),
        ],
        out_specs=[
            spec((n, vv), lambda s: (s, 0)),
            spec((n, vv), lambda s: (s, 0)),
            spec((n, vv), lambda s: (s, 0)),
            spec((n, qk), lambda s: (s, 0)),
            spec((1, pair, n, n), lambda s: (s, 0, 0, 0)),
            spec((1, pair, n // BLOCK * DK, DV), lambda s: (s, 0, 0, 0)),
        ],
        out_shape=[
            jax.ShapeDtypeStruct((tokens, vv), bf16),
            jax.ShapeDtypeStruct((tokens, vv), f32),
            jax.ShapeDtypeStruct((tokens, vv), bf16),
            jax.ShapeDtypeStruct((tokens, qk), bf16),
            jax.ShapeDtypeStruct((slots, pair, n, n), bf16),
            jax.ShapeDtypeStruct((slots, pair, n // BLOCK * DK, DV), bf16),
        ],
        compiler_params=pltpu.CompilerParams(vmem_limit_bytes=56 * 1024 * 1024),
        cost_estimate=pl.CostEstimate(flops=1, bytes_accessed=1, transcendentals=0),
        name="mixer_forward",
    )(ids, proj, dec, conv, head_rows, gain_row)


def backward_kernel(
    hl,
    pair,
    p,
    ids_ref,
    x_ref,
    dec_ref,
    conv_ref,
    head_ref,
    gain_ref,
    o_ref,
    u_ref,
    w_ref,
    inv_ref,
    s_ref,
    dy_ref,
    dx_out,
    ddec_out,
    conv_out,
    small_out,
):
    slot = pl.program_id(0)
    n = TOK_DEV
    qk, vv = pair * DK, pair * DV
    q_at = slice(0, qk)
    k_at = slice(qk, 2 * qk)
    v_at = slice(2 * qk, 2 * qk + vv)
    blocks = n // BLOCK
    x, below, on_below, strict, same = block_masks(n)
    dec = dec_ref[...]
    alog_row = head_ref[0:1, :]
    pre, log_decay, running, total = decay_parts(dec, alog_row, head_ref[1:2, :])
    running_t = running.T
    heads = range(pair)
    qc = conv_forward(x_ref[:, q_at], conv_ref[:, q_at])
    kc = conv_forward(x_ref[:, k_at], conv_ref[:, k_at])
    vc = conv_forward(x_ref[:, v_at], conv_ref[:, v_at])
    q_sig = jax.nn.sigmoid(qc)
    k_sig = jax.nn.sigmoid(kc)
    v_sig = jax.nn.sigmoid(vc)
    q = qc * q_sig
    k = kc * k_sig
    v = (vc * v_sig).astype(bf16)
    gain = gain_ref[0:1, :]
    qn, kn, vn, qr, kr, beta, b, tot, d, sim, low, score = ([] for _ in range(12))
    d_out, u = [], []
    gain_rows = jnp.zeros((1, DV), f32)
    for i in heads:
        h = ids_ref[0] * hl + p * pair + i
        cols = slice(i * DV, (i + 1) * DV)
        kcols = slice(i * DK, (i + 1) * DK)
        rows_q, r_q = unit_rows(q[:, kcols], DK**-0.5)
        rows_k, r_k = unit_rows(k[:, kcols], 1.0)
        qr.append((rows_q, r_q))
        kr.append((rows_k, r_k))
        qn.append(rows_q.astype(bf16))
        kn.append(rows_k.astype(bf16))
        vn.append(v[:, cols])
        beta.append(jax.nn.sigmoid(lane_of(dec, H + h)))
        b.append(lane_of(running, h))
        tot.append(lane_of(total, h))
        d.append(
            jnp.where(on_below, jnp.exp(jnp.where(on_below, b[i] - row_of(running_t, h), 0.0)), 0.0)
        )
        both = mm_nt(jnp.concatenate([kn[i], qn[i]], axis=0), kn[i])
        sim.append(jnp.where(strict, d[i] * both[:n], 0.0))
        score.append(both[n:] * d[i])
        out = o_ref[:, cols]
        g_at = slice(2 * qk + vv + i * DV, 2 * qk + vv + (i + 1) * DV)
        gate = x_ref[:, g_at]
        dy = dy_ref[:, cols].astype(f32)
        r = lax.rsqrt(jnp.mean(out * out, axis=1, keepdims=True) + eps_norm)
        normed = out * r
        g_sig = jax.nn.sigmoid(gate)
        act = gate * g_sig
        d_act = dy * normed * gain
        dx_out[:, g_at] = (d_act * (g_sig * (1.0 + gate * (1.0 - g_sig)))).astype(bf16)
        gain_rows = gain_rows + jnp.sum(dy * normed * act, axis=0, keepdims=True)
        d_normed = dy * gain * act
        d_out.append(r * (d_normed - normed * jnp.mean(d_normed * normed, axis=1, keepdims=True)))
        u.append(u_ref[:, cols])
    e = [jnp.exp(b[i]) for i in heads]
    fin = [jnp.exp(tot[i] - b[i]) for i in heads]
    grow = [jnp.exp(tot[i]) for i in heads]
    d_out16 = [d_out[i].astype(bf16) for i in heads]
    score16 = [score[i].astype(bf16) for i in heads]
    d_u0 = [mm_tn(score16[i], d_out16[i]) for i in heads]
    d_state = [jnp.zeros((DK, DV), f32) for i in heads]
    d_u = [[None] * blocks for i in heads]
    dq_s = [[None] * blocks for i in heads]
    dk_s = [[None] * blocks for i in heads]
    fin_col = [[None] * blocks for i in heads]
    grow_col = [[None] * blocks for i in heads]
    e_out = [(e[i] * d_out[i]).astype(bf16) for i in heads]
    for c in reversed(range(blocks)):
        lo, hi = c * BLOCK, (c + 1) * BLOCK
        for i in heads:
            ds16 = d_state[i].astype(bf16)
            s16 = s_ref[0, i, c * DK : (c + 1) * DK, :]
            u_c = u[i][lo:hi].astype(f32)
            if c == blocks - 1:
                d_u[i][c] = d_u0[i][lo:hi]
                fin_col[i][c] = jnp.zeros((BLOCK, 1), f32)
                grow_col[i][c] = jnp.zeros((1, 1), f32)
                dk_s[i][c] = jnp.zeros((BLOCK, DK), f32)
            else:
                k_ds = mm(kn[i][lo:hi], ds16)
                add = fin[i][lo:hi] * k_ds
                d_u[i][c] = d_u0[i][lo:hi] + add
                fin_col[i][c] = jnp.sum(add * u_c, axis=1, keepdims=True)
                grow_col[i][c] = grow[i][lo : lo + 1] * jnp.sum(
                    jnp.sum(d_state[i] * s16.astype(f32), axis=1, keepdims=True),
                    axis=0,
                    keepdims=True,
                )
                dk_s[i][c] = mm_nt(fin[i][lo:hi] * u_c, ds16)
            if c > 0:
                step = mm_tn(
                    jnp.concatenate([qn[i][lo:hi], w_ref[lo:hi, i * DK : (i + 1) * DK]], axis=0),
                    jnp.concatenate([e_out[i][lo:hi], (-d_u[i][c]).astype(bf16)], axis=0),
                )
                d_state[i] = grow[i][lo : lo + 1] * d_state[i] + step
    lane = lax.broadcasted_iota(jnp.int32, (n, 128), 1)
    d_dec = jnp.zeros((n, 128), f32)
    d_log = jnp.zeros((n, 128), f32)
    dq_all, dk_all, dv_all = [], [], []
    ones = jnp.ones((n, 128), bf16)
    upper_i = lax.broadcasted_iota(jnp.int32, (n, n), 0)
    upper_j = lax.broadcasted_iota(jnp.int32, (n, n), 1)
    upper = jnp.where(jnp.logical_and((upper_i ^ upper_j) < BLOCK, upper_i <= upper_j), 1.0, 0.0)
    for i in heads:
        h = ids_ref[0] * hl + p * pair + i
        du = jnp.concatenate(d_u[i], axis=0)
        d_right = mm_tn(inv_ref[0, i], du)
        dr16 = d_right.astype(bf16)
        outer = mm_nt(jnp.concatenate([d_out16[i], dr16], axis=0), u[i])
        d_score = jnp.where(on_below, outer[:n], 0.0)
        d_low = jnp.where(strict, -outer[n:], 0.0)
        z16 = (-(beta[i] * e[i]) * d_right).astype(bf16)
        recalled = []
        for c in range(blocks):
            lo, hi = c * BLOCK, (c + 1) * BLOCK
            s16 = s_ref[0, i, c * DK : (c + 1) * DK, :]
            if c == 0:
                dq_s[i][c] = jnp.zeros((BLOCK, DK), f32)
                recalled.append(jnp.zeros((BLOCK, 2 * DV), f32))
                continue
            back = mm_nt(jnp.concatenate([e_out[i][lo:hi], z16[lo:hi]], axis=0), s16)
            dq_s[i][c] = back[:BLOCK]
            dk_s[i][c] = dk_s[i][c] + back[BLOCK:]
            got = mm(jnp.concatenate([kn[i][lo:hi], qn[i][lo:hi]], axis=0), s16)
            recalled.append(jnp.concatenate([got[:BLOCK], got[BLOCK:]], axis=1))
        recalled = jnp.concatenate(recalled, axis=0)
        k_s = recalled[:, :DV]
        q_s = recalled[:, DV:]
        d_a = (d_score * d[i]).astype(bf16)
        d_g = d_low * beta[i] * d[i]
        d_g16 = (d_g + d_g.T).astype(bf16)
        dq = jnp.concatenate(dq_s[i], axis=0) + mm(d_a, kn[i])
        dk = jnp.concatenate(dk_s[i], axis=0) + mm_tn(d_a, qn[i]) + mm(d_g16, kn[i])
        dv = beta[i] * d_right
        row_sum = jnp.sum(d_low * sim[i], axis=1, keepdims=True)
        keep = vn[i].astype(f32) - e[i] * k_s
        d_beta = row_sum + jnp.sum(d_right * keep, axis=1, keepdims=True)
        moved = (d_score * score[i] + d_low * beta[i] * sim[i]).astype(bf16)
        d_b = mm(moved, ones) - mm_tn(moved, ones)
        d_b_col = e[i] * jnp.sum(
            d_out[i] * q_s - (beta[i] * d_right) * k_s, axis=1, keepdims=True
        )
        fin_all = jnp.concatenate(fin_col[i], axis=0)
        d_b = jnp.where(lane == h, d_b + (d_b_col - fin_all), 0.0)
        tail = jnp.concatenate(
            [
                jnp.broadcast_to(
                    grow_col[i][c] + jnp.sum(fin_col[i][c], axis=0, keepdims=True), (BLOCK, 1)
                )
                for c in range(blocks)
            ],
            axis=0,
        )
        d_log = d_log + mm_exact(upper, d_b) + jnp.where(lane == h, tail, 0.0)
        d_dec = d_dec + jnp.where(lane == H + h, d_beta * beta[i] * (1.0 - beta[i]), 0.0)
        rows_q, r_q = qr[i]
        rows_k, r_k = kr[i]
        unit = rows_q * DK**0.5
        dq = (DK**-0.5) * r_q * (dq - unit * jnp.sum(dq * unit, axis=1, keepdims=True))
        dk = r_k * (dk - rows_k * jnp.sum(dk * rows_k, axis=1, keepdims=True))
        dq_all.append(dq)
        dk_all.append(dk)
        dv_all.append(dv)

    @pl.when(slot == 0)
    def _():
        conv_out[...] = jnp.zeros_like(conv_out)
        small_out[...] = jnp.zeros_like(small_out)

    def through_conv(d_active, conv, sig, at):
        d_conv = d_active * (sig * (1.0 + conv * (1.0 - sig)))
        d_mixed, d_weight = conv_backward(d_conv, x_ref[:, at], conv_ref[:, at])
        dx_out[:, at] = d_mixed.astype(bf16)
        conv_out[0:KCONV, at] += d_weight

    through_conv(jnp.concatenate(dq_all, axis=1), qc, q_sig, q_at)
    through_conv(jnp.concatenate(dk_all, axis=1), kc, k_sig, k_at)
    through_conv(jnp.concatenate(dv_all, axis=1), vc, v_sig, v_at)
    first = ids_ref[0] * hl + p * pair
    mine = jnp.logical_and(lane >= first, lane < first + pair)
    d_pre = jnp.where(mine, -jnp.exp(alog_row) * jax.nn.sigmoid(pre) * d_log, 0.0)
    ddec_out[...] = d_dec + d_pre

    small_out[0:1, :] += gain_rows
    small_out[1:2, 0:128] += jnp.sum(jnp.where(mine, d_log * log_decay, 0.0), axis=0, keepdims=True)
    small_out[2:3, 0:128] += jnp.sum(d_pre, axis=0, keepdims=True)


def mixer_backward(ids, proj, dec, conv, head_rows, gain_row, saved, d_gated, hl, pair, p):
    out, u, w, inv, states = saved
    tokens = proj.shape[0]
    slots = tokens // TOK_DEV
    qk = pair * DK
    vv = pair * DV
    spec = pl.BlockSpec
    n = TOK_DEV

    def body(*refs):
        backward_kernel(hl, pair, p, *refs)

    return pl.pallas_call(
        body,
        grid=(slots,),
        in_specs=[
            pl.BlockSpec(memory_space=pltpu.SMEM),
            spec((n, 2 * qk + 2 * vv), lambda s: (s, 0)),
            spec((n, 128), lambda s: (s, dec.shape[1] // 128 - 1)),
            spec((8, 2 * qk + vv), lambda s: (0, 0)),
            spec((8, 128), lambda s: (0, 0)),
            spec((8, DV), lambda s: (0, 0)),
            spec((n, vv), lambda s: (s, 0)),
            spec((n, vv), lambda s: (s, 0)),
            spec((n, qk), lambda s: (s, 0)),
            spec((1, pair, n, n), lambda s: (s, 0, 0, 0)),
            spec((1, pair, n // BLOCK * DK, DV), lambda s: (s, 0, 0, 0)),
            spec((n, vv), lambda s: (s, 0)),
        ],
        out_specs=[
            spec((n, 2 * qk + 2 * vv), lambda s: (s, 0)),
            spec((n, 128), lambda s: (s, 0)),
            spec((8, 2 * qk + vv), lambda s: (0, 0)),
            spec((8, DV), lambda s: (0, 0)),
        ],
        out_shape=[
            jax.ShapeDtypeStruct((tokens, 2 * qk + 2 * vv), bf16),
            jax.ShapeDtypeStruct((tokens, 128), f32),
            jax.ShapeDtypeStruct((8, 2 * qk + vv), f32),
            jax.ShapeDtypeStruct((8, DV), f32),
        ],
        compiler_params=pltpu.CompilerParams(vmem_limit_bytes=56 * 1024 * 1024),
        cost_estimate=pl.CostEstimate(flops=1, bytes_accessed=1, transcendentals=0),
        name="mixer_backward",
    )(ids, proj, dec, conv, head_rows, gain_row, out, u, w, inv, states, d_gated)


VMEM_LIMIT = 58 * 1024 * 1024
ANY = pl.BlockSpec(memory_space=pl.ANY)
SMEM = pl.BlockSpec(memory_space=pltpu.SMEM)


def params(**more):
    return pltpu.CompilerParams(vmem_limit_bytes=VMEM_LIMIT, **more)


def cost(flops, moved):
    return pl.CostEstimate(flops=1, bytes_accessed=1, transcendentals=0)


def pack_columns(w, extra, table, rows, plane, ids):
    chips = len(table)
    width = sum(size for _, size in table[0])
    more = 0 if extra is None else extra.shape[1]

    def body(ids_ref, w_ref, *refs):
        out = refs[-1]
        for c in range(chips):
            at = 0
            for start, size in table[c]:
                out[c, :, at : at + size] = w_ref[:, start : start + size]
                at += size
            if more:
                out[c, :, at : at + more] = refs[0][...]

    def block(i, ids_ref):
        return (ids_ref[2] if plane else 0, 0)

    def whole(i, ids_ref):
        return (0, 0)

    return pl.pallas_call(
        body,
        grid_spec=pltpu.PrefetchScalarGridSpec(
            num_scalar_prefetch=1,
            grid=(1,),
            in_specs=[pl.BlockSpec((rows, w.shape[1]), block)]
            + ([pl.BlockSpec((rows, more), whole)] if more else []),
            out_specs=pl.BlockSpec((chips, rows, width + more), lambda i, ids_ref: (0, 0, 0)),
        ),
        out_shape=jax.ShapeDtypeStruct((chips, rows, width + more), bf16),
        compiler_params=params(),
        cost_estimate=cost(0, 2 * rows * w.shape[1] + 2 * chips * rows * (width + more)),
        name="pack_columns",
    )(ids, w, *([extra] if more else []))


def pack_relative(w, extra, table, plane, ids):
    rows = w.shape[0] // 4 if plane else w.shape[0]
    chips = len(table)
    more = 0 if extra is None else extra.shape[1]
    width = sum(size for _, size in table[0]) + more

    def body(ids_ref, w_ref, *refs):
        outs = refs[-chips:]
        for j in range(chips):
            c = jnp.bitwise_xor(ids_ref[0], j)
            at = 0
            for r, (start, size) in enumerate(table[0]):
                step = table[1][r][0] - start
                lane = pl.multiple_of(start + c * step, 128)
                outs[j][:, at : at + size] = w_ref[:, pl.ds(lane, size)]
                at += size
            if more:
                outs[j][:, at : at + more] = refs[0][...]

    def block(i, ids_ref):
        return (ids_ref[2] if plane else 0, 0)

    def whole(i, ids_ref):
        return (0, 0)

    return pl.pallas_call(
        body,
        grid_spec=pltpu.PrefetchScalarGridSpec(
            num_scalar_prefetch=1,
            grid=(1,),
            in_specs=[pl.BlockSpec((rows, w.shape[1]), block)]
            + ([pl.BlockSpec((rows, more), block)] if more else []),
            out_specs=[pl.BlockSpec((rows, width), whole)] * chips,
        ),
        out_shape=[jax.ShapeDtypeStruct((rows, width), bf16)] * chips,
        compiler_params=params(),
        cost_estimate=cost(0, 4 * rows * w.shape[1]),
        name="pack_relative",
    )(ids, w, *([extra] if more else []))


def join_cores(mine, theirs, ids):
    rows, n = mine.shape
    tile = 512

    def body(ids_ref, mine_ref, theirs_ref, o_ref):
        core = ids_ref[1]
        o_ref[pl.ds(pl.multiple_of(core * rows, 16), rows), :] = mine_ref[...]
        o_ref[pl.ds(pl.multiple_of((1 - core) * rows, 16), rows), :] = theirs_ref[...]

    return pl.pallas_call(
        body,
        grid=(n // tile,),
        in_specs=[SMEM] + [pl.BlockSpec((rows, tile), lambda i: (0, i))] * 2,
        out_specs=pl.BlockSpec((2 * rows, tile), lambda i: (0, i)),
        out_shape=jax.ShapeDtypeStruct((2 * rows, n), bf16),
        compiler_params=params(),
        cost_estimate=cost(0, 8 * rows * n),
        name="join_cores",
    )(ids, mine, theirs)


def norm_rows(parts, gain):
    d = parts[0].shape[1]
    total = sum(p.shape[0] for p in parts)

    def body(gain_ref, *refs):
        out = refs[-1]
        at = 0
        for ref in refs[:-1]:
            for m in range(0, ref.shape[0], 128):
                rows = ref[m : m + 128, :].astype(f32)
                r = lax.rsqrt(jnp.mean(rows * rows, axis=1, keepdims=True) + eps_norm)
                out[at : at + 128, :] = (rows * r * gain_ref[0:1, :]).astype(bf16)
                at += 128

    return pl.pallas_call(
        body,
        out_shape=jax.ShapeDtypeStruct((total, d), bf16),
        compiler_params=params(),
        cost_estimate=cost(8 * total * d, 4 * total * d),
        name="norm_rows",
    )(gain, *parts)


def small_layout(shapes):
    lanes = []
    at = 0
    for size in shapes:
        lanes.append(at)
        at += size + (-size % 128)
    return lanes, at


def pack_small(conv, vectors, nf):
    lanes, used = small_layout([v.shape[1] for v in vectors])
    channels = conv.shape[1]

    def body(conv_ref, *refs):
        out = refs[-1]
        out[...] = jnp.zeros_like(out)
        for d in range(nf):
            out[d, 0:KCONV, :] = conv_ref[...].astype(f32)
            for ref, lane in zip(refs[:-1], lanes):
                out[d, KCONV : KCONV + 1, lane : lane + ref.shape[1]] = ref[...].astype(f32)

    out = pl.pallas_call(
        body,
        out_shape=jax.ShapeDtypeStruct((nf, 8, channels), f32),
        compiler_params=params(),
        cost_estimate=cost(0, 0),
        name="pack_small",
    )(conv, *vectors)
    return out.astype(bf16)


def small_ranges(chip, hk, qk, vv, groups, p, conv_shard):
    at = chip * groups + p
    found = []
    for start, size in ((at * qk, qk), (hk + at * qk, qk), (2 * hk + at * vv, vv)):
        lane = pl.multiple_of(lax.rem(start, conv_shard), 128)
        found.append((lax.div(start, conv_shard), lane, size))
    return found


def unpack_small(gathered, sizes, ids, hk, qk, vv, groups):
    nf, _, conv_shard = gathered.shape
    lanes, _ = small_layout(sizes)
    d = nf * sizes[0]

    def body(ids_ref, g_ref, gains_ref, heads_ref, ogain_ref, *convs):
        gains_ref[...] = jnp.zeros_like(gains_ref)
        heads_ref[...] = jnp.zeros_like(heads_ref)
        ogain_ref[...] = jnp.zeros_like(ogain_ref)
        for n, out, row in (
            (0, gains_ref, 0),
            (1, gains_ref, 1),
            (2, ogain_ref, 0),
            (3, heads_ref, 0),
            (4, heads_ref, 1),
        ):
            size = sizes[n]
            for i in range(nf):
                out[row : row + 1, i * size : (i + 1) * size] = g_ref[
                    i, KCONV : KCONV + 1, lanes[n] : lanes[n] + size
                ]
        for p, out in enumerate(convs):
            at = 0
            for dev, lane, size in small_ranges(ids_ref[0], hk, qk, vv, groups, p, conv_shard):
                out[:, at : at + size] = g_ref[dev, :, pl.ds(lane, size)]
                at += size

    return pl.pallas_call(
        body,
        in_specs=[SMEM, pl.BlockSpec(memory_space=pltpu.VMEM)],
        out_shape=[
            jax.ShapeDtypeStruct((8, d), f32),
            jax.ShapeDtypeStruct((8, 128), f32),
            jax.ShapeDtypeStruct((8, nf * sizes[2]), f32),
        ]
        + [jax.ShapeDtypeStruct((8, 2 * qk + vv), f32)] * groups,
        compiler_params=params(),
        name="unpack_small",
    )(ids, gathered.astype(f32))


def pack_small_grads(g_conv, g_heads, gain_in, gain_mid, sizes, ids, nf, conv_shard, hk, qk, vv):
    lanes, _ = small_layout(sizes)
    groups = len(g_conv)

    def body(ids_ref, gin_ref, gmid_ref, *refs):
        out = refs[-1]
        out[...] = jnp.zeros_like(out)
        heads = refs[groups][...]
        for ref in refs[groups + 1 : -1]:
            heads = heads + ref[...]
        for n, row in (
            (0, gin_ref[0:1, :]),
            (1, gmid_ref[0:1, :]),
            (2, heads[0:1, :]),
            (3, heads[1:2, :]),
            (4, heads[2:3, :]),
        ):
            size = sizes[n]
            for i in range(nf):
                out[i, KCONV : KCONV + 1, lanes[n] : lanes[n] + size] = row[
                    :, i * size : (i + 1) * size
                ]
        for p in range(groups):
            at = 0
            for dev, lane, size in small_ranges(ids_ref[0], hk, qk, vv, groups, p, conv_shard):
                out[dev, 0:KCONV, pl.ds(lane, size)] = refs[p][0:KCONV, at : at + size]
                at += size

    vmem = pl.BlockSpec(memory_space=pltpu.VMEM)
    return pl.pallas_call(
        body,
        in_specs=[SMEM] + [vmem] * (2 + 2 * groups),
        out_shape=jax.ShapeDtypeStruct((nf, 8, conv_shard), f32),
        compiler_params=params(),
        name="pack_small_grads",
    )(ids, gain_in, gain_mid, *g_conv, *g_heads)


def place_blocks(whole, pair_values, ids, c, shape):
    t, last = pair_values
    rows, n = t.shape
    old = [] if whole is None else [whole]

    def body(ids_ref, t_ref, last_ref, *refs):
        middle = jnp.logical_or(ids_ref[2] == 1, ids_ref[2] == 2)
        refs[-1][0] = jnp.where(middle, t_ref[...], last_ref[...])

    half = n // 2
    return pl.pallas_call(
        body,
        grid=(2,),
        in_specs=[SMEM]
        + [pl.BlockSpec((rows, half), lambda i: (0, i))] * 2
        + [ANY] * len(old),
        out_specs=pl.BlockSpec((1, rows, half), lambda i: (c, 0, i)),
        out_shape=jax.ShapeDtypeStruct(shape, bf16),
        input_output_aliases={3: 0} if old else {},
        compiler_params=params(),
        cost_estimate=cost(0, 6 * rows * n),
        name="place_blocks",
    )(ids, t, last, *old)


def finish_projection(whole, pair_values, ids, chunk, p, groups, shape, widths):
    t, last = pair_values
    rows = shape[0]
    unit = 256
    starts = []
    for c in chunk:
        base = 0
        for width in widths:
            size = width // (4 * groups)
            starts.append([base + (c * groups + p) * size + s for s in range(0, size, unit)])
            base += width
    starts = sum(starts, [])
    each = len(starts) // len(chunk)
    old = [] if whole is None else [whole]

    def body(ids_ref, t_ref, last_ref, *refs):
        middle = jnp.logical_or(ids_ref[2] == 1, ids_ref[2] == 2)
        refs[-1][...] = jnp.where(middle, t_ref[...], last_ref[...]).astype(f32)

    def column(i):
        at = starts[-1] // unit
        for n in reversed(range(len(starts) - 1)):
            at = jnp.where(i == n, starts[n] // unit, at)
        return (0, at)

    return pl.pallas_call(
        body,
        grid=(len(starts),),
        in_specs=[SMEM]
        + [pl.BlockSpec((rows, unit), lambda i: (lax.div(i, each), lax.rem(i, each)))] * 2
        + [ANY] * len(old),
        out_specs=pl.BlockSpec((rows, unit), column),
        out_shape=jax.ShapeDtypeStruct(shape, f32),
        input_output_aliases={3: 0} if old else {},
        compiler_params=params(),
        cost_estimate=cost(0, 8 * rows * unit * len(starts)),
        name="finish_projection",
    )(ids, t, last, *old)


def finish_feed_forward(blocks):
    chips, rows, n = blocks.shape
    wide = n // 2

    def body(x_ref, o_ref):
        which = pl.program_id(1)
        for s in range(2):

            @pl.when(which == s)
            def _():
                for at in range(0, wide, 128):
                    start = 2 * at + 128 * s
                    o_ref[:, at : at + 128] = x_ref[0, :, start : start + 128].astype(f32)

    return pl.pallas_call(
        body,
        grid=(chips, 2),
        in_specs=[pl.BlockSpec((1, rows, n), lambda c, s: (c, 0, 0))],
        out_specs=pl.BlockSpec((rows, wide), lambda c, s: (0, s * chips + c)),
        out_shape=jax.ShapeDtypeStruct((rows, chips * n), f32),
        compiler_params=params(),
        cost_estimate=cost(0, 6 * chips * rows * n),
        name="finish_feed_forward",
    )(blocks)


def fill_rows(w_ref, own_ref, other_ref, core, chip=0):
    planes, chips, rows, _ = own_ref.shape
    for z in range(planes):
        for j in range(chips):
            c = jnp.bitwise_xor(chip, j)
            for ref, k in ((own_ref, core), (other_ref, 1 - core)):
                at = pl.multiple_of((2 * c + k) * planes * rows + z * rows, rows)
                w_ref[pl.ds(at, rows), :] = ref[z, j]


def project_planes(x, own, other, ids):
    tokens, k = x.shape
    planes, chips, rows, n = own.shape
    tile = 256

    def body(ids_ref, x_ref, own_ref, other_ref, o_ref, w_ref):
        fill_rows(w_ref, own_ref, other_ref, ids_ref[1], ids_ref[0])
        o_ref[...] = jnp.dot(x_ref[...], w_ref[...], preferred_element_type=f32)

    return pl.pallas_call(
        body,
        grid=(pl.cdiv(n, tile),),
        in_specs=[SMEM, pl.BlockSpec((tokens, k), lambda i: (0, 0))]
        + [pl.BlockSpec((planes, chips, rows, tile), lambda i: (0, 0, 0, i))] * 2,
        out_specs=pl.BlockSpec((tokens, tile), lambda i: (0, i)),
        out_shape=jax.ShapeDtypeStruct((tokens, n), f32),
        scratch_shapes=[pltpu.VMEM((k, tile), bf16)],
        compiler_params=params(),
        cost_estimate=cost(2 * tokens * k * n, 2 * tokens * k + 2 * k * n + 4 * tokens * n),
        name="project",
    )(ids, x, own, other)


def project(x, own, other, ids):
    tokens, k = x.shape
    rows, n = own[0].shape
    chips = len(own)
    tile = 256

    def body(ids_ref, x_ref, *refs):
        o_ref, w_ref = refs[2 * chips :]
        for j in range(chips):
            c = jnp.bitwise_xor(ids_ref[0], j)
            for ref, core in ((refs[j], ids_ref[1]), (refs[chips + j], 1 - ids_ref[1])):
                at = pl.multiple_of((2 * c + core) * rows, rows)
                w_ref[pl.ds(at, rows), :] = ref[...]
        o_ref[...] = jnp.dot(x_ref[...], w_ref[...], preferred_element_type=f32)

    return pl.pallas_call(
        body,
        grid=(pl.cdiv(n, tile),),
        in_specs=[SMEM, pl.BlockSpec((tokens, k), lambda i: (0, 0))]
        + [pl.BlockSpec((rows, tile), lambda i: (0, i))] * (2 * chips),
        out_specs=pl.BlockSpec((tokens, tile), lambda i: (0, i)),
        out_shape=jax.ShapeDtypeStruct((tokens, n), f32),
        scratch_shapes=[pltpu.VMEM((k, tile), bf16)],
        compiler_params=params(),
        cost_estimate=cost(2 * tokens * k * n, 2 * tokens * k + 2 * k * n + 4 * tokens * n),
        name="project",
    )(ids, x, *own, *other)


def feed_forward(x, own, other, down, d_ffn, ids):
    tokens, k = x.shape
    planes, chips, rows, n = own.shape
    wide = n // 2
    tile = 512

    def body(ids_ref, x_ref, own_ref, other_ref, down_ref, d_ref, h_ref, g_ref, w_ref):
        fill_rows(w_ref, own_ref, other_ref, ids_ref[1])
        for m in range(0, tokens, 256):
            rows_at = slice(m, m + 256)
            both = jnp.dot(x_ref[rows_at, :], w_ref[...], preferred_element_type=f32)
            d_hidden = mm_nt(d_ref[rows_at, :], down_ref[...])
            for s in range(tile // 256):
                gate = both[:, 256 * s : 256 * s + 128]
                up = both[:, 256 * s + 128 : 256 * s + 256]
                dh = d_hidden[:, 128 * s : 128 * s + 128]
                sig = jax.nn.sigmoid(gate)
                act = gate * sig
                h_ref[rows_at, 128 * s : 128 * s + 128] = (act * up).astype(bf16)
                g_ref[rows_at, 256 * s : 256 * s + 128] = (
                    dh * up * (sig * (1.0 + gate * (1.0 - sig)))
                ).astype(bf16)
                g_ref[rows_at, 256 * s + 128 : 256 * s + 256] = (dh * act).astype(bf16)

    return pl.pallas_call(
        body,
        grid=(pl.cdiv(n, tile),),
        in_specs=[
            SMEM,
            pl.BlockSpec((tokens, k), lambda i: (0, 0)),
            pl.BlockSpec((planes, chips, rows, tile), lambda i: (0, 0, 0, i)),
            pl.BlockSpec((planes, chips, rows, tile), lambda i: (0, 0, 0, i)),
            pl.BlockSpec((tile // 2, k), lambda i: (i, 0)),
            pl.BlockSpec((tokens, k), lambda i: (0, 0)),
        ],
        out_specs=[
            pl.BlockSpec((tokens, tile // 2), lambda i: (0, i)),
            pl.BlockSpec((tokens, tile), lambda i: (0, i)),
        ],
        out_shape=[
            jax.ShapeDtypeStruct((tokens, wide), bf16),
            jax.ShapeDtypeStruct((tokens, n), bf16),
        ],
        scratch_shapes=[pltpu.VMEM((k, tile), bf16)],
        compiler_params=params(),
        cost_estimate=cost(3 * tokens * k * n, 4 * tokens * k + 3 * k * n + 3 * tokens * n),
        name="feed_forward",
    )(ids, x, own, other, down, d_ffn)


def halves_of(i, tiles):
    half = tiles // 2
    return jnp.minimum(i, half - 1), jnp.maximum(i - half, 0)


def scatter_outputs(tokens, n, tile, refs=None):
    size = tokens // 2
    tiles = n // tile
    first = pl.BlockSpec((size, tile), lambda i, *ids: (0, halves_of(i, tiles)[0]))
    second = pl.BlockSpec((size, tile), lambda i, *ids: (0, halves_of(i, tiles)[1]))
    return [first, first, second, second], [jax.ShapeDtypeStruct((size, n // 2), bf16)] * 4


def write_scattered(outs, total_ref, tiles):
    size = total_ref.shape[0] // 4
    i = pl.program_id(0)

    for half, rows in ((0, ((1, 3), (0, 2))), (1, ((2, 3), (0, 1)))):

        @pl.when((i < tiles // 2) if half == 0 else (i >= tiles // 2))
        def _():
            for out, chips in zip(outs[2 * half : 2 * half + 2], rows):
                for n, m in enumerate(chips):
                    out[n * size : (n + 1) * size, :] = total_ref[m * size : (m + 1) * size, :]


def times_rows(lefts, mine, theirs, ids):
    tokens = lefts[0].shape[0]
    half, n = mine.shape
    tile = 256
    specs, shapes = scatter_outputs(tokens, n, tile)

    def body(ids_ref, *refs):
        left_refs = refs[: len(lefts)]
        mine_ref, theirs_ref = refs[len(lefts) : len(lefts) + 2]
        outs = refs[len(lefts) + 2 : -2]
        right_ref, total_ref = refs[-2:]
        core = ids_ref[1]
        right_ref[pl.ds(pl.multiple_of(core * half, 16), half), :] = mine_ref[...]
        right_ref[pl.ds(pl.multiple_of((1 - core) * half, 16), half), :] = theirs_ref[...]
        total = None
        at = 0
        for ref in left_refs:
            width = ref.shape[1]
            term = jnp.dot(ref[...], right_ref[at : at + width, :], preferred_element_type=f32)
            total = term if total is None else total + term
            at += width
        total_ref[...] = total.astype(bf16)
        write_scattered(outs, total_ref, n // tile)

    return pl.pallas_call(
        body,
        grid=(n // tile,),
        in_specs=[SMEM]
        + [pl.BlockSpec(a.shape, lambda i: (0, 0)) for a in lefts]
        + [pl.BlockSpec((half, tile), lambda i: (0, i))] * 2,
        out_specs=specs,
        out_shape=shapes,
        scratch_shapes=[pltpu.VMEM((2 * half, tile), bf16), pltpu.VMEM((tokens, tile), bf16)],
        compiler_params=params(),
        cost_estimate=cost(4 * tokens * half * n, 2 * (tokens * half + half * n + tokens * n)),
        name="times_rows",
    )(ids, *lefts, mine, theirs)


def times_transposed(pairs, ids, relative):
    tokens = pairs[0][0].shape[0]
    planes, chips, rows, _ = pairs[0][1].shape
    rows *= planes
    total_n = sum(left.shape[1] for left, own, other in pairs)
    k = 2 * chips * rows
    specs_out, shapes = scatter_outputs(tokens, k, rows)

    def body(ids_ref, *refs):
        count = len(pairs)
        outs = refs[3 * count : 3 * count + 4]
        piece_refs = refs[3 * count + 4 : -1]
        total_ref = refs[-1]
        mine = pl.program_id(0) % 2 == ids_ref[1]

        def choose(which):
            for n in range(count):
                piece = refs[3 * n + which][:, 0]
                piece_refs[n][...] = piece.reshape(rows, piece.shape[2])

        @pl.when(mine)
        def _():
            choose(1)

        @pl.when(jnp.logical_not(mine))
        def _():
            choose(2)

        total = None
        for n in range(count):
            term = mm_nt(refs[3 * n][...], piece_refs[n][...])
            total = term if total is None else total + term
        total_ref[...] = total.astype(bf16)
        write_scattered(outs, total_ref, 2 * chips)

    def piece_at(i, ids_ref):
        c = lax.div(i, 2)
        if relative:
            c = jnp.bitwise_xor(c, ids_ref[0])
        return (0, c, 0, 0)

    specs = []
    args = []
    for left, own, other in pairs:
        specs.append(pl.BlockSpec(left.shape, lambda i, ids_ref: (0, 0)))
        block = (own.shape[0], 1) + own.shape[2:]
        specs += [pl.BlockSpec(block, piece_at)] * 2
        args += [left, own, other]
    return pl.pallas_call(
        body,
        grid_spec=pltpu.PrefetchScalarGridSpec(
            num_scalar_prefetch=1,
            grid=(2 * chips,),
            in_specs=specs,
            out_specs=specs_out,
            scratch_shapes=[pltpu.VMEM((rows, own.shape[3]), bf16) for _, own, _ in pairs]
            + [pltpu.VMEM((tokens, rows), bf16)],
        ),
        out_shape=shapes,
        compiler_params=params(),
        cost_estimate=cost(
            2 * tokens * k * total_n, 2 * (tokens * k + k * total_n + tokens * total_n)
        ),
        name="times_transposed",
    )(ids, *args)


def column_terms(lefts, rights, ids):
    tokens, k = lefts[0].shape
    n = rights[0].shape[1]
    chips = 4
    rows = k // (2 * chips)

    def body(ids_ref, a_ref, b_ref, ra_ref, rb_ref, o_ref):
        total = mm_tn(a_ref[...], ra_ref[...]) + mm_tn(b_ref[...], rb_ref[...])
        o_ref[0] = total.astype(bf16)

    def column(i, ids_ref):
        return (0, 2 * i + ids_ref[1])

    def whole(i, ids_ref):
        return (0, 0)

    return pl.pallas_call(
        body,
        grid_spec=pltpu.PrefetchScalarGridSpec(
            num_scalar_prefetch=1,
            grid=(chips,),
            in_specs=[pl.BlockSpec((tokens, rows), column)] * 2
            + [pl.BlockSpec((tokens, n), whole)] * 2,
            out_specs=pl.BlockSpec((1, rows, n), lambda i, ids_ref: (i, 0, 0)),
        ),
        out_shape=jax.ShapeDtypeStruct((chips, rows, n), bf16),
        compiler_params=params(),
        cost_estimate=cost(2 * tokens * k * n, 4 * (tokens * k + tokens * n + k * n)),
        name="column_terms",
    )(ids, *lefts, *rights)


def row_terms(lefts, right, ids):
    tokens, n = right.shape
    k = sum(a.shape[1] for a in lefts)
    tile = 512
    half = k // 2

    def body(ids_ref, *refs):
        left_refs = refs[: len(lefts)]
        right_ref, mine_ref, theirs_ref, acc = refs[len(lefts) :]
        core = ids_ref[1]
        at = 0
        for ref in left_refs:
            width = ref.shape[1]
            acc[at : at + width, :] = mm_tn(ref[...], right_ref[...])
            at += width
        mine_ref[...] = acc[pl.ds(pl.multiple_of(core * half, 16), half), :].astype(bf16)
        theirs_ref[...] = acc[pl.ds(pl.multiple_of((1 - core) * half, 16), half), :].astype(bf16)

    out = pl.BlockSpec((half, tile), lambda i: (0, i))
    return pl.pallas_call(
        body,
        grid=(n // tile,),
        in_specs=[SMEM]
        + [pl.BlockSpec(a.shape, lambda i: (0, 0)) for a in lefts]
        + [pl.BlockSpec((tokens, tile), lambda i: (0, i))],
        out_specs=[out, out],
        out_shape=[jax.ShapeDtypeStruct((half, n), bf16)] * 2,
        scratch_shapes=[pltpu.VMEM((k, tile), f32)],
        compiler_params=params(),
        cost_estimate=cost(2 * tokens * k * n, 2 * (tokens * k + tokens * n + k * n)),
        name="row_terms",
    )(ids, *lefts, right)


def after(values, *earlier):
    if not earlier:
        return values
    return lax.optimization_barrier((values, earlier))[0]


def to_chip(a, nf, j):
    return lax.ppermute(a, "fsdp", [(i, i ^ (2 * j)) for i in range(nf)])


def swap_core(a, nf):
    return lax.ppermute(a, "fsdp", [(i, i ^ 1) for i in range(nf)])


RIGHT = [(0, 1), (1, 2), (2, 3)]
LEFT = [(1, 0), (2, 1), (3, 2)]
INWARD = [(0, 1), (3, 2)]
MIDDLE = [(1, 2), (2, 1)]
OUTWARD = [(1, 0), (2, 3)]
SWAP = [(0, 1), (1, 0), (2, 3), (3, 2)]


def along(a, pairs):
    return lax.ppermute(a, "rep", pairs)


def add16(a, b):
    return (a.astype(f32) + b.astype(f32)).astype(bf16)


def gather_small(a, nf):
    me = lax.axis_index("fsdp")
    out = a[None]
    bit = 1
    while bit < nf:
        other = lax.ppermute(out, "fsdp", [(i, i ^ bit) for i in range(nf)])
        upper = (me & bit) != 0
        out = jnp.concatenate(
            [jnp.where(upper, other, out), jnp.where(upper, out, other)], axis=0
        )
        bit *= 2
    return out


def sum_small(a, nf):
    me = lax.axis_index("fsdp")
    bit = nf // 2
    while bit:
        half = a.shape[0] // 2
        upper = (me & bit) != 0
        keep = jnp.where(upper, a[half:], a[:half])
        send = jnp.where(upper, a[:half], a[half:])
        a = keep + lax.ppermute(send, "fsdp", [(i, i ^ bit) for i in range(nf)])
        bit //= 2
    return a[0]


class Line:
    def __init__(self, nz):
        self.nz = nz
        self.tokens = ()
        self.first = None
        self.second = None
        z = lax.axis_index("rep")
        self.middle = jnp.logical_or(z == 1, z == 2)

    def step(self, new, *earlier):
        if self.nz != 4:
            return new and (new[0], (lax.psum(new[1], "rep"),) * 2)
        chunk = None if new is None else new[1]
        first = None if self.first is None else self.first[1:]
        second = None if self.second is None else self.second[1:]
        chunk, first, second, _, _ = lax.optimization_barrier(
            (chunk, first, second, self.tokens, earlier)
        )
        outward = None if second is None else second[0] + second[1]
        across = None if first is None else first[0] + first[1]
        finished = next_first = next_second = None
        tokens = []
        if chunk is not None and outward is not None and outward.shape != chunk.shape:
            got = along(chunk, INWARD)
            last = along(outward, OUTWARD)
            tokens += [got, last]
            finished = (self.second[0], (outward, last))
            next_first = (new[0], chunk, got)
        elif chunk is not None or outward is not None:
            send = chunk if outward is None else outward
            if chunk is not None and outward is not None:
                send = jnp.where(self.middle, outward, chunk)
            got = along(send, SWAP)
            tokens.append(got)
            if outward is not None:
                finished = (self.second[0], (send, got))
            if chunk is not None:
                next_first = (new[0], chunk, got)
        if across is not None:
            met = along(across, MIDDLE)
            tokens.append(met)
            next_second = (self.first[0], across, met)
        self.first, self.second, self.tokens = next_first, next_second, tuple(tokens)
        return finished


def gather_first(a, nf, *earlier):
    chips = nf // 2
    a = after(a, *earlier)
    if chips != 4:
        return [a] + [to_chip(a, nf, j) for j in range(1, chips)]
    return [a, to_chip(a, nf, 1), to_chip(a, nf, 2)]


def gather_second(parts, nf, *earlier):
    if nf != 8:
        return jnp.concatenate(parts, axis=0)
    a, one, two = parts
    half = a.shape[0] // 2
    low, high = after((one[:half], two[half:]), *earlier)
    return jnp.concatenate([a, one, two, to_chip(low, nf, 2), to_chip(high, nf, 1)], axis=0)


def scatter_first(a, nf, *earlier):
    chips = nf // 2
    n = a.shape[0] // chips
    parts = [a[j * n : (j + 1) * n] for j in range(chips)]
    if chips != 4:
        return [parts[0]] + [to_chip(parts[j], nf, j) for j in range(1, chips)]
    half = n // 2
    low, high, one, two = after(
        (parts[3][:half], parts[3][half:], parts[1][half:], parts[2][:half]), *earlier
    )
    low = to_chip(low, nf, 2)
    high = to_chip(high, nf, 1)
    one = to_chip(one, nf, 1)
    two = to_chip(two, nf, 2)
    return [
        parts[0],
        one,
        two,
        add16(parts[1][:half], low),
        add16(parts[2][half:], high),
    ]


def scatter_second(parts, nf, *earlier):
    if nf != 8:
        total = parts[0].astype(f32)
        for part in parts[1:]:
            total = total + part.astype(f32)
        return total
    own, one, two, one_low, two_high = parts
    one_low, two_high = after((one_low, two_high), *earlier)
    one_low = to_chip(one_low, nf, 1)
    two_high = to_chip(two_high, nf, 2)
    own = own.astype(f32)
    half = own.shape[0] // 2
    return jnp.concatenate(
        [
            own[:half] + one_low.astype(f32) + two.astype(f32),
            own[half:] + one.astype(f32) + two_high.astype(f32),
        ],
        axis=0,
    )


def rms_back(rows, r, gain, d_out):
    unit = rows * r
    d_unit = d_out * gain
    d_rows = r * (d_unit - unit * jnp.mean(d_unit * unit, axis=1, keepdims=True))
    return d_rows, jnp.sum(d_out * unit, axis=0)


def scale_of(rows):
    return lax.rsqrt(jnp.mean(rows * rows, axis=1, keepdims=True) + eps_norm)


def exchange(a, nf):
    groups = [[2 * c + k for c in range(nf // 2)] for k in range(2)]
    return lax.all_to_all(a, "fsdp", 0, 0, axis_index_groups=groups, tiled=True)


def column_blocks(w, widths, chips, groups, p):
    rows = w.shape[0]
    start = 0
    parts = []
    for width in widths:
        part = w[:, start : start + width].reshape(rows, chips, groups, width // (chips * groups))
        parts.append(part[:, :, p].transpose(1, 0, 2))
        start += width
    return jnp.concatenate(parts, axis=2)


def from_column_blocks(blocks, widths):
    chips, rows, _ = blocks.shape
    parts = []
    at = 0
    for width in widths:
        part = blocks[:, :, at : at + width // chips]
        parts.append(part.transpose(1, 0, 2).reshape(rows, width))
        at += width // chips
    return parts


def both_core_rows(own, nf):
    core = lax.axis_index("fsdp") % 2
    other = swap_core(own, nf)
    first = core == 0
    chips, rows, width = own.shape
    both = jnp.stack([jnp.where(first, own, other), jnp.where(first, other, own)], axis=1)
    return both.reshape(chips * 2 * rows, width)


def core_half(x, chips, which):
    tokens, width = x.shape
    x = x.reshape(tokens, chips, 2, width // (2 * chips))
    x = lax.dynamic_index_in_dim(x, which, 2, keepdims=False)
    return x.reshape(tokens, width // 2)


def column_gradient(left, right, nf, *earlier):
    core = lax.axis_index("fsdp") % 2
    chips = nf // 2
    theirs = mm_tn(core_half(left, chips, 1 - core), right).astype(bf16)
    got = swap_core(theirs, nf)
    mine = mm_tn(core_half(left, chips, core), right) + got.astype(f32)
    return mine.astype(bf16).reshape(chips, -1, right.shape[1])


def both_cores(w, nf, *earlier):
    core = lax.axis_index("fsdp") % 2
    other = swap_core(after(w, *earlier), nf)
    first = core == 0
    return jnp.concatenate([jnp.where(first, w, other), jnp.where(first, other, w)], axis=0)


def halves(a):
    core = lax.axis_index("fsdp") % 2
    rows = a.shape[0] // 2
    mine = lax.dynamic_slice(a, (core * rows, 0), (rows, a.shape[1]))
    theirs = lax.dynamic_slice(a, ((1 - core) * rows, 0), (rows, a.shape[1]))
    return mine, theirs


def sum_cores(a, nf):
    mine, theirs = halves(a)
    return add16(mine, swap_core(theirs, nf))


def as_rows(a):
    flat = a.reshape(-1)
    return jnp.pad(flat, (0, -flat.shape[0] % 128)).reshape(-1, 128)


def gather_pieces(parts, nf, *earlier):
    a, one, two = parts
    half = a.shape[0] // 2
    low, high = after((one[:half], two[half:]), *earlier)
    return [a, one, two, to_chip(low, nf, 2), to_chip(high, nf, 1)]


def scatter_start(parts, nf, *earlier):
    over_x, over_y = after((parts[0], parts[2]), *earlier)
    return [parts[1], to_chip(over_x, nf, 1), parts[3], to_chip(over_y, nf, 2)]


def scatter_middle(parts, nf, *earlier):
    stay_x, got_x, stay_y, got_y = after(parts, *earlier)
    size = stay_x.shape[0] // 2
    over_y = to_chip(stay_x[size:] + got_x[size:], nf, 2)
    over_x = to_chip(stay_y[size:] + got_y[size:], nf, 1)
    return [stay_x[:size], got_x[:size], over_y, stay_y[:size], got_y[:size], over_x]


def scatter_end(parts):
    parts = [p.astype(f32) for p in parts]
    return jnp.concatenate([sum(parts[:3]), sum(parts[3:])], axis=1)


def local_fast(
    tokens,
    cotangent,
    lengths,
    slot_owner,
    gain_in,
    w_proj,
    w_decay,
    conv_weight,
    a_log,
    dt_bias,
    o_gain,
    w_out,
    gain_mid,
    w_gate_up,
    w_down,
    *,
    nf,
    nz,
):
    chips = nf // 2
    hl = H // chips
    pair = 2
    groups = hl // pair
    me = lax.axis_index("fsdp")
    rep = lax.axis_index("rep")
    ids = jnp.stack([me // 2, me % 2, rep, me]).astype(jnp.int32)
    shard = gain_in.shape[0]
    conv_shard = conv_weight.shape[1]
    hv = w_out.shape[0] * nf
    hk = (conv_shard * nf - hv) // 2
    ff = w_down.shape[0] * nf
    wide = ff // chips
    qk, vv = pair * DK, pair * DV
    span = 2 * qk + 2 * vv
    proj_widths = (hk, hk, hv, hv)

    def proj_table(p):
        table = []
        for c in range(chips):
            at = c * groups + p
            table.append(
                [
                    (at * qk, qk),
                    (hk + at * qk, qk),
                    (2 * hk + at * vv, vv),
                    (2 * hk + hv + at * vv, vv),
                ]
            )
        return table

    up_table = [
        [(s * ff + c * wide + at, 128) for at in range(0, wide, 128) for s in range(2)]
        for c in range(chips)
    ]
    plane = shard // nz

    vectors = [v.reshape(1, -1) for v in (gain_in, gain_mid, o_gain, a_log, dt_bias)]
    sizes = [v.shape[1] for v in vectors]
    small = lax.all_to_all(pack_small(conv_weight, vectors, nf), "fsdp", 0, 0, tiled=True)
    decay_pad = jnp.pad(w_decay, ((0, 0), (0, 128 - 2 * H)))
    plane_rows = pack_relative(w_proj, decay_pad, proj_table(0), True, ids)
    packed = pack_relative(w_proj, None, proj_table(1), False, ids)

    def spread(own, *earlier):
        sends = after(own[1:], *earlier)
        return [own[0]] + [to_chip(a, nf, j + 1) for j, a in enumerate(sends)]

    def swap_all(own, *earlier):
        return [swap_core(a, nf) for a in after(own, *earlier)]

    out_other = swap_core(w_out, nf)
    down_other = swap_core(w_down, nf)
    first = jnp.stack(after(spread(plane_rows), packed))
    tok = gather_first(tokens, nf, small, first)
    first = lax.all_gather(first, "rep", axis=0)
    gains, head_rows, gain_row, *conv_pair = unpack_small(small, sizes, ids, hk, qk, vv, groups)
    tok = gather_pieces(tok, nf, gains, out_other, down_other)
    own = spread(packed, tok)

    held = jnp.sum(jnp.where(slot_owner == rep * nf + me, lengths, 0))
    live_own = (jnp.arange(TOK_DEV, dtype=jnp.int32) < held).astype(f32)[:, None]
    tokens32 = tokens.astype(f32)
    seeded = cotangent.astype(f32) * live_own
    d_ffn_own = seeded.astype(bf16)
    up_plane = pack_columns(after(w_gate_up, packed), None, up_table, plane, True, ids)

    normed_in = norm_rows(after(tok, up_plane, d_ffn_own), gains)
    first_other = swap_core(after(first, tok), nf)
    projected = [project_planes(normed_in, first, first_other, ids)]
    up_plane = exchange(after(up_plane, own, projected[0]), nf)
    ffn_parts = gather_first(d_ffn_own, nf, own, projected[0])

    def forward(p, *before):
        return mixer_forward(
            ids, after(projected[p], *before), projected[0], conv_pair[p], head_rows, gain_row,
            hl, pair, p,
        )

    gated0, *saved0 = forward(0, own)
    other = swap_all(own, projected[0])
    up_own = lax.all_gather(after(up_plane, gated0), "rep", axis=0)
    projected.append(project(after(normed_in, gated0), own, other, ids))
    ffn_parts = gather_pieces(ffn_parts, nf, projected[1])
    gated1, *saved1 = forward(1, ffn_parts[:3])
    gated = [gated0, gated1]
    saved = [saved0, saved1]
    branch_parts = scatter_start(
        times_rows(after(gated, ffn_parts), w_out, out_other, ids), nf
    )
    d_ffn = jnp.concatenate(after(ffn_parts, branch_parts[0]), axis=0)
    pieces_in = [
        (first, first_other),
        (jnp.stack(after(own, branch_parts[0]))[None], jnp.stack(after(other, branch_parts[0]))[None]),
    ]
    down_chip = join_cores(w_down, after(down_other, branch_parts[0]), ids)
    out_chip = join_cores(w_out, after(out_other, branch_parts[0]), ids)
    branch_parts = scatter_middle(branch_parts, nf, d_ffn, pieces_in[1], down_chip)
    branch = scatter_end(branch_parts)
    up_own = after(up_own, branch_parts)
    up_other = swap_core(up_own, nf)
    in_other = swap_core(after(normed_in, up_other), nf)

    middle = tokens32 + live_own * branch
    r_mid = scale_of(middle)
    normed_own = (middle * r_mid * gains[1]).astype(bf16)
    normed_mid = gather_first(normed_own, nf)
    normed_mid = jnp.concatenate(gather_pieces(normed_mid, nf), axis=0)
    hidden, d_gate_up = feed_forward(normed_mid, up_own, up_other, down_chip, d_ffn, ids)

    line = Line(nz)
    done = {}

    def step(new, *earlier):
        got = line.step(new, *earlier)
        if got is not None:
            done[got[0]] = got[1]

    d_up_other = swap_core(d_gate_up, nf)
    mid_other = swap_core(normed_mid, nf)
    mine, theirs = row_terms([hidden], after(d_ffn, mid_other), ids)
    theirs = swap_core(theirs, nf)
    half = mine.shape[0] // 2
    down0 = mine[:half] + theirs[:half]
    down1 = mine[half:] + theirs[half:]
    step(("down0", down0), down1)
    z = line.tokens
    partial_mid = times_transposed(
        [(after(d_gate_up, down0, down1, d_up_other), up_own, up_other)], ids, False
    )
    mid_parts = scatter_start(partial_mid, nf)
    partial_ffn = times_rows(after([hidden], partial_mid, z), w_down, down_other, ids)
    step(("down1", down1), partial_mid)
    mid_first = mid_parts
    mid_parts = scatter_middle(mid_parts, nf, partial_ffn)
    grad_up = column_terms(
        [normed_mid, mid_other],
        [after(d_gate_up, partial_ffn, mid_first[1], mid_first[3]), d_up_other],
        ids,
    )
    z = line.tokens
    step(("up0", grad_up[0]))
    d_normed_mid = scatter_end(after(mid_parts, grad_up, z))
    z = line.tokens
    d_mid, g_gain_mid = rms_back(middle, r_mid, gains[1], d_normed_mid)
    d_middle = seeded + d_mid
    d_branch_own = (live_own * d_middle).astype(bf16)
    branch_parts = gather_first(d_branch_own, nf)
    ffn_first = scatter_start(partial_ffn, nf, mid_parts, grad_up)
    d_branch = gather_pieces(branch_parts, nf, z, ffn_first)
    step(("up1", grad_up[1]))
    z = line.tokens
    ffn_sends = scatter_middle(ffn_first, nf, d_branch)
    d_branch = jnp.concatenate(d_branch, axis=0)
    d_gated = [mm_nt(d_branch, out_chip[p * vv : (p + 1) * vv]) for p in range(groups)]

    def backward(p, *before):
        return mixer_backward(
            ids, projected[p], projected[0], conv_pair[p], head_rows, gain_row, saved[p],
            after(d_gated[p], *before), hl, pair, p,
        )

    step(("up2", grad_up[2]))
    d_x1, d_dec, g_conv1, g_heads1 = backward(1, d_gated, z, ffn_sends)
    z = line.tokens
    d_x1_other = swap_core(after(d_x1, line.tokens), nf)
    step(("up3", grad_up[3]), d_x1)
    mine, theirs = row_terms(gated, after(d_branch, d_x1, z), ids)
    half = mine.shape[0] // 2
    theirs = [swap_core(theirs[:half], nf), swap_core(theirs[half:], nf)]
    cols1 = column_terms([normed_in, in_other], [after(d_x1, mine), d_x1_other], ids)
    z = line.tokens
    grad_out = [after(mine, cols1)[:half] + theirs[0], mine[half:] + theirs[1]]
    cols1_all = exchange(after(cols1, z), nf)
    step(("out0", grad_out[0]), cols1)
    d_x0, dec, g_conv0, g_heads0 = backward(0, cols1, z, grad_out)
    z = line.tokens
    d_x0 = jnp.concatenate([after(d_x0, z, cols1_all), (d_dec + dec).astype(bf16)], axis=1)
    d_x0_other = swap_core(d_x0, nf)
    step(("out1", grad_out[1]), d_x0)
    z = line.tokens
    cols0 = column_terms([normed_in, in_other], [d_x0, d_x0_other], ids)
    queue = [(1, (0, 1)), (1, (2, 3))] + [(0, (c,)) for c in range(chips)]
    grad_cols = [exchange(after(cols0, z), nf), cols1_all]

    def chunk_of(key):
        p, chunk = key
        block = grad_cols[p][chunk[0] : chunk[-1] + 1]
        return (key, block.reshape(len(chunk) * shard, block.shape[2]))

    grad_proj = None

    def place(grad_proj, key, *before):
        return finish_projection(
            grad_proj, after(done[key], *before), ids, key[1], key[0], groups, w_proj.shape,
            proj_widths,
        )

    right = [d_x0, d_x1]
    step(chunk_of(queue[0]), cols0)
    partial_in = times_transposed(
        [(after(right[p], cols0, z),) + pieces_in[p] for p in range(groups)], ids, True
    )
    in_first = scatter_start(partial_in, nf)
    g_conv = [g_conv0, g_conv1]
    g_heads = [g_heads0, g_heads1]
    z = line.tokens
    step(chunk_of(queue[1]), partial_in, grad_cols[0])
    grad_up = None
    for j in range(chips):
        grad_up = place_blocks(
            grad_up, after(done["up%d" % j], z), ids, j, (chips, shard, 2 * wide)
        )
    in_sends = scatter_middle(in_first, nf, grad_up)
    output = (middle + live_own * scatter_end(after(ffn_sends, z))).astype(bf16)
    z = line.tokens
    step(chunk_of(queue[2]))
    d_normed_in = scatter_end(after(in_sends, z))
    d_rows, g_gain_in = rms_back(tokens32, scale_of(tokens32), gains[0], d_normed_in)
    grad_tokens = d_middle + d_rows
    blocks = pack_small_grads(
        g_conv,
        g_heads,
        g_gain_in.reshape(1, -1),
        g_gain_mid.reshape(1, -1),
        sizes,
        ids,
        nf,
        conv_shard,
        hk,
        qk,
        vv,
    )
    small_sum = sum_small(blocks, nf)
    grad_up_all = exchange(after(grad_up, small_sum), nf)
    z = line.tokens
    step(chunk_of(queue[3]), grad_tokens)
    grad_proj = place(grad_proj, queue[0], z)
    z = line.tokens
    step(chunk_of(queue[4]), grad_proj)
    grad_proj = place(grad_proj, queue[1], z)
    z = line.tokens
    key, chunk = chunk_of(queue[5])
    small_sum = jnp.pad(
        small_sum.astype(bf16), ((0, 16 - small_sum.shape[0]), (0, chunk.shape[1] - small_sum.shape[1]))
    )
    step((key, jnp.concatenate([chunk, small_sum], axis=0)), grad_proj)
    grad_proj = place(grad_proj, queue[2], z)
    z = line.tokens
    step(None, grad_proj)
    grad_proj = place(grad_proj, queue[3], z)
    z = line.tokens
    step(None, grad_proj)
    grad_up = finish_feed_forward(after(grad_up_all, z))
    for key in queue[4:]:
        grad_proj = place(grad_proj, key)
    summed = [v[shard : shard + 8] for v in done[queue[5]]]
    middle_two = jnp.logical_or(rep == 1, rep == 2)

    def pick(name):
        return jnp.where(middle_two, *done[name])

    summed = jnp.where(middle_two, *summed).astype(f32)
    lanes, _ = small_layout(sizes)
    s_gain_in, s_gain_mid, s_ogain, s_alog, s_bias = (
        summed[KCONV, lane : lane + size] for lane, size in zip(lanes, sizes)
    )
    grad_decay = sum(
        jnp.where(middle_two, *(v[:shard, span : span + 2 * H] for v in done[(0, (c,))])).astype(f32)
        for c in range(chips)
    )
    grad_down = jnp.concatenate([pick("down0"), pick("down1")], axis=0).astype(f32)
    grad_out = jnp.concatenate([pick("out0"), pick("out1")], axis=0).astype(f32)
    return (
        output,
        grad_tokens,
        s_gain_in,
        grad_proj,
        grad_decay,
        summed[:KCONV, :conv_shard],
        s_alog,
        s_bias,
        s_ogain,
        grad_out,
        s_gain_mid,
        grad_up,
        grad_down,
    )


def local_general(
    tokens,
    cotangent,
    lengths,
    slot_owner,
    gain_in,
    w_proj,
    w_decay,
    conv_weight,
    a_log,
    dt_bias,
    o_gain,
    w_out,
    gain_mid,
    w_gate_up,
    w_down,
    *,
    nf,
    nz,
):
    chips = nf // 2
    hl = H // chips
    pair = 2 if hl % 2 == 0 else 1
    groups = hl // pair
    me = lax.axis_index("fsdp")
    rep = lax.axis_index("rep")
    chip, core = me // 2, me % 2
    ids = jnp.stack([chip, core, rep, rep]).astype(jnp.int32)
    d_model = tokens.shape[1]
    shard = gain_in.shape[0]
    conv_shard = conv_weight.shape[1]
    channels = conv_shard * nf
    hv = w_out.shape[0] * nf
    hk = (channels - hv) // 2
    ff = w_down.shape[0] * nf
    wide = ff // chips
    qk, vv = pair * DK, pair * DV
    span = 2 * qk + 2 * vv
    proj_widths = (hk, hk, hv, hv)
    up_widths = (ff, ff)

    def proj_blocks(w, dec, p):
        blocks = column_blocks(w, proj_widths, chips, groups, p)
        if p:
            return blocks
        extra = jnp.pad(dec, ((0, 0), (0, 128 - 2 * H)))
        extra = jnp.broadcast_to(extra, (chips,) + extra.shape)
        return jnp.concatenate([blocks, extra], axis=2)

    def plane_rows(w):
        rows = w.shape[0] // nz
        return lax.dynamic_slice(w, (rep * rows, 0), (rows, w.shape[1]))

    def over_planes(blocks):
        got = lax.all_gather(blocks, "rep", axis=0)
        return got.transpose(1, 0, 2, 3).reshape(chips, -1, blocks.shape[2])

    pieces = [conv_weight, gain_in, gain_mid, o_gain, a_log, dt_bias]
    rows = [as_rows(p) for p in pieces]
    counts = [r.shape[0] for r in rows]
    packed = jnp.concatenate(rows, axis=0)
    packed = jnp.pad(packed, ((0, -packed.shape[0] % 16), (0, 0)))

    plane_proj = plane_rows(w_proj)
    rest = [exchange(proj_blocks(plane_proj, None, p), nf) for p in range(1, groups)]
    first = exchange(proj_blocks(w_proj, w_decay, 0), nf)
    tok = gather_first(tokens, nf)
    small = gather_small(packed, nf)
    tokens_all = gather_second(tok, nf)
    rest = [over_planes(r) for r in rest]
    up_plane = exchange(
        after(column_blocks(plane_rows(w_gate_up), up_widths, chips, 1, 0), first), nf
    )
    up_own = over_planes(after(up_plane, *rest))

    device = rep * nf + me
    held = jnp.sum(jnp.where(slot_owner == device, lengths, 0))
    live_own = (jnp.arange(TOK_DEV, dtype=jnp.int32) < held).astype(f32)[:, None]

    small = small.astype(f32)
    split = []
    at = 0
    for p, count in zip(pieces, counts):
        split.append(
            small[:, at : at + count].reshape(nf, count * 128)[:, : p.size].reshape((nf,) + p.shape)
        )
        at += count
    conv_full = split[0].transpose(1, 0, 2).reshape(KCONV, channels)
    gain_in_full, gain_mid_full, ogain_full, alog_full, bias_full = (
        s.reshape(-1) for s in split[1:]
    )
    conv_pair = []
    for p in range(groups):
        blocks = column_blocks(conv_full, proj_widths[:3], chips, groups, p)
        mine = lax.dynamic_index_in_dim(blocks, chip, 0, keepdims=False)
        conv_pair.append(jnp.pad(mine, ((0, 8 - KCONV), (0, 0))))
    head_rows = jnp.stack([alog_full, bias_full])
    head_rows = jnp.pad(head_rows, ((0, 6), (0, 128 - H)))
    gain_row = jnp.pad(ogain_full[None, :], ((0, 7), (0, 0)))

    rows_in = tokens_all.astype(f32)
    normed_in = (rows_in * scale_of(rows_in) * gain_in_full).astype(bf16)
    seeded = cotangent.astype(f32) * live_own
    weight_in = [both_core_rows(first, nf)]
    out_chip = both_cores(w_out, nf, weight_in[0])
    down_chip = both_cores(w_down, nf, weight_in[0])
    weight_in += [both_core_rows(r, nf) for r in rest]
    ffn_parts = gather_first(seeded.astype(bf16), nf, up_plane)
    d_ffn = gather_second(ffn_parts, nf)
    projected = []
    gated = []
    saved = []
    for p in range(groups):
        projected.append(mm(normed_in, weight_in[p]))
        got = mixer_forward(
            ids, projected[p], projected[0], conv_pair[p], head_rows, gain_row, hl, pair, p
        )
        gated.append(got[0])
        saved.append(got[1:])
    gated = jnp.concatenate(gated, axis=1)
    branch_parts = scatter_first(mm(gated, out_chip).astype(bf16), nf, d_ffn)
    d_hidden = mm_nt(after(d_ffn, gated), down_chip)
    up_chip = both_core_rows(after(up_own, gated), nf)
    branch = scatter_second(branch_parts, nf)

    tokens32 = tokens.astype(f32)
    middle = tokens32 + live_own * branch
    r_mid = scale_of(middle)
    normed_own = (middle * r_mid * gain_mid_full).astype(bf16)
    normed_mid = gather_second(gather_first(normed_own, nf), nf)
    gate_up = mm(normed_mid, up_chip)
    gate, up = gate_up[:, :wide], gate_up[:, wide:]
    sig = jax.nn.sigmoid(gate)
    act = gate * sig
    hidden = (act * up).astype(bf16)
    d_gate_up = jnp.concatenate(
        [d_hidden * up * (sig * (1.0 + gate * (1.0 - sig))), d_hidden * act], axis=1
    ).astype(bf16)

    line = Line(nz)
    done = {}

    def step(new, *earlier):
        for item in new or [None]:
            got = line.step(item, *earlier)
            if got is not None:
                done[got[0]] = got[1][0]

    grad_down = sum_cores(mm_tn(hidden, d_ffn).astype(bf16), nf)
    down_parts = jnp.split(grad_down, 2, axis=0)
    step([("down0", down_parts[0])])
    partial_mid = mm_nt(after(d_gate_up, down_parts[0]), up_chip).astype(bf16)
    mid_parts = scatter_first(partial_mid, nf)
    grad_up = column_gradient(normed_mid, after(d_gate_up, partial_mid), nf)
    step([("down1", down_parts[1])], grad_up)
    d_normed_mid = scatter_second(mid_parts, nf)
    d_mid, g_gain_mid = rms_back(middle, r_mid, gain_mid_full, d_normed_mid)
    d_middle = seeded + d_mid
    d_branch_own = (live_own * d_middle).astype(bf16)
    branch_parts = gather_first(d_branch_own, nf)
    partial_ffn = mm(after(hidden, d_branch_own), down_chip).astype(bf16)
    step([("up0", grad_up[0])], partial_ffn)
    d_branch = gather_second(branch_parts, nf)
    step([("up1", grad_up[1])], d_branch)
    d_gated = [mm_nt(d_branch, out_chip[p * vv : (p + 1) * vv]) for p in range(groups)]
    grad_out = sum_cores(mm_tn(gated, d_branch).astype(bf16), nf)
    d_x = [None] * groups
    d_dec = None
    g_conv = [None] * groups
    g_heads = None
    ups = [("up%d" % j, grad_up[j]) for j in range(2, chips)]
    for n, p in enumerate(reversed(range(groups))):
        d_x[p], dec, g_conv[p], heads = mixer_backward(
            ids, projected[p], projected[0], conv_pair[p], head_rows, gain_row, saved[p],
            d_gated[p], hl, pair, p,
        )
        d_dec = dec if d_dec is None else d_dec + dec
        g_heads = heads if g_heads is None else g_heads + heads
        step(ups[n : n + 1] if n + 1 < groups else ups[n:], d_x[p])
        if p:
            d_gated[p - 1] = after(d_gated[p - 1], d_x[p])
    d_dec = d_dec.astype(bf16)
    right = [jnp.concatenate([d_x[0], d_dec], axis=1)] + d_x[1:]
    grad_cols = [None] * groups
    for p in reversed(range(groups)):
        grad_cols[p] = exchange(column_gradient(normed_in, right[p], nf), nf)
    ffn_parts = scatter_first(partial_ffn, nf, grad_cols[0])
    step([("out", grad_out)], right[0])
    partial_in = mm_nt(right[0], weight_in[0])
    for p in range(1, groups):
        partial_in = partial_in + mm_nt(right[p], weight_in[p])
    partial_in = partial_in.astype(bf16)
    queue = []
    for p in reversed(range(groups)):
        size = 1 if p == 0 else 2
        for c in range(0, chips, size):
            queue.append(((p, c), grad_cols[p][c : c + size]))
    for n, item in enumerate(queue):
        if n == 1:
            ffn_branch = scatter_second(ffn_parts, nf, line.tokens)
            output = (middle + live_own * ffn_branch).astype(bf16)
            in_parts = scatter_first(partial_in, nf, ffn_branch)
        if n == 2:
            d_normed_in = scatter_second(in_parts, nf, line.tokens)
            d_rows, g_gain_in = rms_back(tokens32, scale_of(tokens32), gain_in_full, d_normed_in)
            grad_tokens = d_middle + d_rows
            ups = jnp.stack([done["up%d" % j] for j in range(chips)])
            grad_up = exchange(after(ups, d_normed_in), nf)
        step([item])

    g_conv = [g[:KCONV] for g in g_conv]
    blocks = jnp.concatenate(
        [g[:, a:b] for a, b in ((0, qk), (qk, 2 * qk), (2 * qk, 2 * qk + vv)) for g in g_conv],
        axis=1,
    )
    conv_grad = jnp.zeros((KCONV, chips, channels // chips), f32)
    conv_grad = lax.dynamic_update_slice(conv_grad, blocks[:, None], (0, chip, 0))
    conv_grad = jnp.concatenate(from_column_blocks(conv_grad.transpose(1, 0, 2), proj_widths[:3]), axis=1)
    heads_grad = g_heads[1:3, :H]
    parts = [
        conv_grad.reshape(KCONV, nf, conv_shard).transpose(1, 0, 2),
        g_gain_in.reshape(nf, shard),
        g_gain_mid.reshape(nf, shard),
        g_heads[0].reshape(nf, -1),
        heads_grad[0].reshape(nf, -1),
        heads_grad[1].reshape(nf, -1),
    ]
    flat = []
    for part in parts:
        part = part.reshape(nf, -1)
        flat.append(jnp.pad(part, ((0, 0), (0, -part.shape[1] % 128))))
    flat = jnp.concatenate(flat, axis=1)
    summed = lax.psum(sum_small(flat.reshape(nf, -1, 128), nf), "rep").reshape(-1)
    grads = []
    at = 0
    for p in pieces:
        grads.append(summed[at : at + p.size].reshape(p.shape))
        at += p.size + (-p.size % 128)
    s_conv, s_gain_in, s_gain_mid, s_ogain, s_alog, s_bias = grads

    step([])
    step([])
    grad_up = jnp.concatenate(from_column_blocks(grad_up, up_widths), axis=1).astype(f32)
    wholes = []
    for p in range(groups):
        size = 1 if p == 0 else 2
        wholes.append(jnp.concatenate([done[(p, c)] for c in range(0, chips, size)], axis=0))
    parts = []
    at = 0
    for width in (qk, qk, vv, vv):
        part = jnp.stack([w[:, :, at : at + width] for w in wholes], axis=1)
        parts.append(part.transpose(2, 0, 1, 3).reshape(shard, -1))
        at += width
    grad_proj = jnp.concatenate(parts, axis=1).astype(f32)
    grad_decay = jnp.sum(wholes[0][:, :, span : span + 2 * H].astype(f32), axis=0)
    grad_down = jnp.concatenate([done["down0"], done["down1"]], axis=0).astype(f32)
    grad_out = done["out"].astype(f32)
    return (
        output,
        grad_tokens,
        s_gain_in,
        grad_proj,
        grad_decay,
        s_conv,
        s_alog,
        s_bias,
        s_ogain,
        grad_out,
        s_gain_mid,
        grad_up,
        grad_down,
    )


def solution(mesh):
    rows = P(("rep", "fsdp"), None)
    one = P("fsdp")
    two = P("fsdp", None)
    columns = P(None, "fsdp")
    in_specs = (rows, rows, P(), P(), one, two, two, columns, one, one, one, two, one, two, two)
    out_specs = (rows, rows, one, two, two, columns, one, one, one, two, one, two, two)
    nf, nz = mesh.shape["fsdp"], mesh.shape["rep"]
    body = partial(local_fast if (nf, nz) == (8, 4) else local_general, nf=nf, nz=nz)
    return jax.shard_map(body, mesh=mesh, in_specs=in_specs, out_specs=out_specs, check_vma=False)
```

time: 1570 us -> 1020 us (0.65)
  waiting for transfers between devices: 814 us -> 267 us
  Pallas kernels: 88.2 us -> 368 us
  matrix products: 178 us -> 7.45 us
  local copies, waits for them, and re-layouts: 133 us -> 46.5 us
  blocking collectives: 71.9 us -> 8.12 us
  other arithmetic: 102 us -> 125 us
    ppermute x82 -> x80, waiting for transfers between devices: 814 us -> 237 us  [the longest x38 114 us: to_chip(): return lax.ppermute(a, 'fsdp', [(i, i ^ 2 * j) for i in range(nf)])]
    pallas_call x2 -> x36, Pallas kernels: 88.2 us -> 368 us  [the longest x2 52 us: mixer_backward(): pl.pallas_call(body, grid=(slots,), in_specs=[pl.BlockSpec(memory_space=p...]
    dot_general x15 -> x0, matrix products: 120 us -> none  [the longest x11 65.4 us: mm_tn(): lax.dot_general(a.astype(bf16), b.astype(bf16), (((0,), (0,)), ((), ())),...]
    add x6 -> x48, other arithmetic: 6.34 us -> 83.2 us  [the longest x14 30.1 us: step(): across = None if first is None else first[0] + first[1]]
    convert_element_type x49 -> x9, other arithmetic: 68.7 us -> 13.1 us  [the longest x1 3.31 us: local_fast(): jnp.concatenate([pick('down0'), pick('down1')], axis=0).astype(f32)]
    dot_general x4 -> x2, matrix products: 58.5 us -> 7.45 us  [mm_nt(): lax.dot_general(a.astype(bf16), b.astype(bf16), (((1,), (1,)), ((), ())),...]
    dynamic_update_slice x50 -> x0, local copies, waits for them, and re-layouts: 35.8 us -> none  [the longest x8 12.6 us: redistribute(): out = lax.dynamic_update_slice(out, other, (base + (1 - core) * rows, 0))]
    all_gather x1 -> x0, blocking collectives: 33.6 us -> none  [local(): small = lax.all_gather(packed, 'fsdp', axis=0).astype(f32)]
  transfers between devices with their start and end apart: 103 -> 102, of which waited for: 41 -> 40; matrix products, arithmetic and copies ran while one was open for 22% -> 16% of each run, Pallas kernels for 6% -> 36%
where the time goes in v2:
time: 1020 us; the launch traced here: 1000 us
  Pallas kernels  368 us (36%)
  waiting for transfers between devices  267 us (26%)
  starting transfers between devices  167 us (16%)
  other arithmetic  125 us (12%)
  local copies, waits for them, and re-layouts  46.5 us (5%)
  between operations  15.9 us (2%)
    ppermute x38, waiting for transfers between devices, to_chip(): return lax.ppermute(a, 'fsdp', [(i, i ^ 2 * j) for i in range(nf)])  114 us
    ppermute x39, waiting for transfers between devices, along(): return lax.ppermute(a, 'rep', pairs)  114 us
    ppermute x39, starting transfers between devices, along(): return lax.ppermute(a, 'rep', pairs)  101 us
    pallas_call x2, Pallas kernels, mixer_backward(): pl.pallas_call(body, grid=(slots,), in_specs=[pl.BlockSpec(memory_space=p...  52 us
    pallas_call x3, Pallas kernels, column_terms(): pl.pallas_call(body, grid_spec=pltpu.PrefetchScalarGridSpec(num_scalar_pr...  44.8 us
    pallas_call x2, Pallas kernels, times_transposed(): pl.pallas_call(body, grid_spec=pltpu.PrefetchScalarGridSpec(num_scalar_pr...  43.6 us
    ppermute x38, starting transfers between devices, to_chip(): return lax.ppermute(a, 'fsdp', [(i, i ^ 2 * j) for i in range(nf)])  43.4 us
    pallas_call x2, Pallas kernels, mixer_forward(): pl.pallas_call(body, grid=(slots,), in_specs=[pl.BlockSpec(memory_space=p...  40.7 us
  transfers between devices with their start and end apart: 102, of which 40 were waited for; matrix products, arithmetic and copies ran while one was open for 16% of the time, Pallas kernels for 36%

profile of v2, /device:TPU:0, one launch (start us, length us, event | category | flops | bytes accessed | tf_op | source)
XLA Modules:
  0.0 1005.0 jit_solution(1957255730135778663)
XLA Ops:
  16.9 5.6 pack_relative.3
  22.5 4.3 collective-permute-done.1
  32.0 8.1 all_to_all.25
  43.7 21.2 %collective-permute-done.3.refs_1_ = bf16[256,2048]{1,0:T(8,128)(2,1)S(1)} collective-permute-done((bf16[256,2048]{1,0:T(8,128)(2,1)S(1)}, bf16[256,2048]{1,0:T(8,128)(2,1)S(1)}, u32[]{:S(2)}, u32[]{:S(2)}) %collective-permute-start.3) | collective-permute-done | bytes 1048608 | tf_op jit(solution)/shard_map/ppermute | solution.py:1184
  68.2 11.4 %collective-permute-done.7.refs_3_ = bf16[128,2048]{1,0:T(8,128)(2,1)} collective-permute-done((bf16[128,2048]{1,0:T(8,128)(2,1)S(1)}, bf16[128,2048]{1,0:T(8,128)(2,1)}, u32[]{:S(2)}, u32[]{:S(2)}) %collective-permute-start.7) | collective-permute-done | bytes 524320 | tf_op jit(solution)/shard_map/ppermute | solution.py:1184
  79.9 16.3 %all-gather.5.cloned.1.call-done = bf16[16,64,1664]{2,1,0:T(8,128)(2,1)} async-done(((bf16[4,64,1664]{2,1,0:T(8,128)(2,1)}), bf16[16,64,1664]{2,1,0:T(8,128)(2,1)}) %all-gather.5.cloned.1.call-update) | async-done | bytes 3407888 | tf_op jit(solution)/shard_map/all_gather | solution.py:1529
  106.8 5.8 norm_rows.1.x_ref.a_ref
  114.3 13.3 %project.2.refs_1_.refs_2_ = f32[1024,1664]{1,0:T(8,128)} custom-call(s32[4]{0:T(128)} %pad_add_fusion.ids_ref.refs_0_, bf16[1024,2048]{1,0:T(8,128)(2,1)} %norm_rows.1.x_ref.a_ref, bf16[4,4,64,1664]{3,2,1,0:T(8,128)(2,1)} %bitcast.63, bf16[4,4,64,1664]{3,2,1,0:T(8,128)(2,1)} %copy-done.7), custom_call_target="tpu_custom_call" | custom-call | flops 1 | bytes 1 | tf_op jit(solution)/shard_map/project/pallas_call | solution.py:886
  127.6 6.9 collective-permute-done.11.refs_2_
  138.3 20.4 %mixer_forward.2 = (bf16[1024,512]{1,0:T(8,128)(2,1)}, f32[1024,512]{1,0:T(8,128)}, bf16[1024,512]{1,0:T(8,128)(2,1)}, bf16[1024,256]{1,0:T(8,128)(2,1)}, bf16[4...) custom-call(s32[4]{0:T(128)} %pad_add_fusion.ids_ref.refs_0_, f32[1024,1664]{1,0:T(8,128)} %project.2.refs_1_.refs_2_, ...), custom_call_target="tpu_custom_call" | custom-call | flops 1 | bytes 1 | tf_op jit(solution)/shard_map/mixer_forward/pallas_call | solution.py:227
  169.0 12.8 %project.3.refs_1_ = f32[1024,1536]{1,0:T(8,128)} custom-call(s32[4]{0:T(128)} %pad_add_fusion.ids_ref.refs_0_, bf16[1024,2048]{1,0:T(8,128)(2,1)} %norm_rows.1.x_ref.a_ref, bf16[256,1536]{1,0:T(8,128)(2,1)} %get-tuple-element.310.refs_0_, bf16[256,1536]{1,0:T(8,128)(2,1)} %collective-permute-done.10.refs_1_, ...), custom_call_target="tpu_custom_call" | custom-call | flops 1 | bytes 1 | tf_op jit(solution)/shard_map/project/pallas_call | solution.py:915
  190.4 20.3 %mixer_forward.3 = (bf16[1024,512]{1,0:T(8,128)(2,1)}, f32[1024,512]{1,0:T(8,128)}, bf16[1024,512]{1,0:T(8,128)(2,1)}, bf16[1024,256]{1,0:T(8,128)(2,1)}, bf16[4...) custom-call(s32[4]{0:T(128)} %pad_add_fusion.ids_ref.refs_0_, f32[1024,1536]{1,0:T(8,128)} %project.3.refs_1_, ...), custom_call_target="tpu_custom_call" | custom-call | flops 1 | bytes 1 | tf_op jit(solution)/shard_map/mixer_forward/pallas_call | solution.py:227
  210.8 10.8 %times_rows.2 = (bf16[512,1024]{1,0:T(8,128)(2,1)}, bf16[512,1024]{1,0:T(8,128)(2,1)}, bf16[512,1024]{1,0:T(8,128)(2,1)}, bf16[512,1024]{1,0:T(8,128)(2,1)}) custom-call(s32[4]{0:T(128)} %pad_add_fusion.ids_ref.refs_0_, bf16[1024,512]{1,0:T(8,128)(2,1)} %get-tuple-element.299.refs_0_, bf16[1024,512]{1,0:T(8,128)(2,1)} %get-tuple-element.300.refs_1_, ...), custom_call_target="tpu_custom_call" | custom-call | flops 1 | bytes 1 | tf_op jit(solution)/shard_map/times_rows/pallas_call | solution.py:1029
  225.3 5.7 join_cores.2.down_ref
  232.1 6.4 maximum_bitcast_fusion
  238.5 7.7 collective-permute-done.21
  251.8 7.8 collective-permute-done.24
  273.7 22.5 %collective-permute-done.25 = bf16[256,2048]{1,0:T(8,128)(2,1)S(1)} collective-permute-done((bf16[256,2048]{1,0:T(8,128)(2,1)S(1)}, bf16[256,2048]{1,0:T(8,128)(2,1)S(1)}, u32[]{:S(2)}, u32[]{:S(2)}) %collective-permute-start.25) | collective-permute-done | bytes 1048608 | tf_op jit(solution)/shard_map/ppermute | solution.py:1184
  301.6 8.1 collective-permute-done.27
  311.9 28.1 %feed_forward.1 = (bf16[1024,1408]{1,0:T(8,128)(2,1)}, bf16[1024,2816]{1,0:T(8,128)(2,1)}) custom-call(s32[4]{0:T(128)} %pad_add_fusion.ids_ref.refs_0_, bf16[1024,2048]{1,0:T(8,128)(2,1)} %constant_dynamic-update-slice_fusion.5.x_ref.a_ref, bf16[4,4,64,2816]{3,2,1,0:T(8,128)(2,1)} %bitcast.60, ...), custom_call_target="tpu_custom_call" | custom-call | flops 1 | bytes 1 | tf_op jit(solution)/shard_map/feed_forward/pallas_call | solution.py:953
  340.4 10.7 %row_terms.2 = (bf16[704,2048]{1,0:T(8,128)(2,1)}, bf16[704,2048]{1,0:T(8,128)(2,1)}) custom-call(s32[4]{0:T(128)} %pad_add_fusion.ids_ref.refs_0_, bf16[1024,1408]{1,0:T(8,128)(2,1)} %get-tuple-element.337.refs_0_, bf16[1024,2048]{1,0:T(8,128)(2,1)} %copy-done.4), custom_call_target="tpu_custom_call" | custom-call | flops 1 | bytes 1 | tf_op jit(solution)/shard_map/row_terms/pallas_call | solution.py:1162
  351.1 5.5 collective-permute-done.31
  359.9 20.4 %times_transposed.2 = (bf16[512,1024]{1,0:T(8,128)(2,1)}, bf16[512,1024]{1,0:T(8,128)(2,1)}, bf16[512,1024]{1,0:T(8,128)(2,1)}, bf16[512,1024]{1,0:T(8,128)(2,1)}) custom-call(s32[4]{0:T(128)} %pad_add_fusion.ids_ref.refs_0_, bf16[1024,2816]{1,0:T(8,128)(2,1)} %get-tuple-element.346.refs_0_.ra_ref, bf16[4,4,64,2816]{3,2,1,0:T(8,128)(2,1)} %bitcast.61, ...), custom_call_target="tpu_custom_call" | custom-call | flops 1 | bytes 1 | tf_op jit(solution)/shard_map/times_transposed/pallas_call | solution.py:1092
  382.8 10.8 %collective-permute-done.33 = bf16[352,2048]{1,0:T(8,128)(2,1)} collective-permute-done((bf16[352,2048]{1,0:T(8,128)(2,1)S(1)}, bf16[352,2048]{1,0:T(8,128)(2,1)}, u32[]{:S(2)}, u32[]{:S(2)}) %collective-permute-start.33) | collective-permute-done | bytes 1441824 | tf_op jit(solution)/shard_map/ppermute | solution.py:1200
  398.1 12.9 %times_rows.3 = (bf16[512,1024]{1,0:T(8,128)(2,1)}, bf16[512,1024]{1,0:T(8,128)(2,1)}, bf16[512,1024]{1,0:T(8,128)(2,1)}, bf16[512,1024]{1,0:T(8,128)(2,1)}) custom-call(s32[4]{0:T(128)} %pad_add_fusion.ids_ref.refs_0_, bf16[1024,1408]{1,0:T(8,128)(2,1)} %get-tuple-element.337.refs_0_, bf16[704,2048]{1,0:T(8,128)(2,1)} %refs_1_.1, ...), custom_call_target="tpu_custom_call" | custom-call | flops 1 | bytes 1 | tf_op jit(solution)/shard_map/times_rows/pallas_call | solution.py:1029
  418.4 19.2 %column_terms.3 = bf16[4,256,2816]{2,1,0:T(8,128)(2,1)} custom-call(s32[4]{0:T(128)} %pad_add_fusion.ids_ref.refs_0_, bf16[1024,2048]{1,0:T(8,128)(2,1)} %constant_dynamic-update-slice_fusion.5.x_ref.a_ref, bf16[1024,2048]{1,0:T(8,128)(2,1)} %collective-permute-done.30.b_ref, bf16[1024,2816]{1,0:T(8,128)(2,1)} %get-tuple-element.346.refs_0_.ra_ref, ...), custom_call_target="tpu_custom_call" | custom-call | flops 1 | bytes 1 | tf_op jit(solution)/shard_map/column_terms/pallas_call | solution.py:1127
  437.6 4.8 slice_bitcast_fusion
  460.9 14.9 %collective-permute-done.44 = bf16[256,2816]{1,0:T(8,128)(2,1)S(1)} collective-permute-done((bf16[256,2816]{1,0:T(8,128)(2,1)S(1)}, bf16[256,2816]{1,0:T(8,128)(2,1)S(1)}, u32[]{:S(2)}, u32[]{:S(2)}) %collective-permute-start.44) | collective-permute-done | bytes 1441824 | tf_op jit(solution)/shard_map/ppermute | solution.py:1200
  476.4 5.6 collective-permute-done.45
  483.1 8.3 collective-permute-start.52
  499.2 5.9 collective-permute-done.38
  507.9 4.8 join_cores.3
  531.1 4.3 collective-permute-start.55
  549.2 26.0 %mixer_backward.2 = (bf16[1024,1536]{1,0:T(8,128)(2,1)}, f32[1024,128]{1,0:T(8,128)}, f32[8,1024]{1,0:T(8,128)}, f32[8,256]{1,0:T(8,128)}) custom-call(s32[4]{0:T(128)} %pad_add_fusion.ids_ref.refs_0_, f32[1024,1536]{1,0:T(8,128)} %project.3.refs_1_, f32[1024,1664]{1,0:T(8,128)} %project.2.refs_1_.refs_2_, f32[8,1024]{1,0:T(8,128)} %get-tuple-element.295.refs_3_, ...), custom_call_target="tpu_custom_call" | custom-call | flops 1 | bytes 1 | tf_op jit(solution)/shard_map/mixer_backward/pallas_call | solution.py:487
  584.7 8.6 row_terms.3
  596.6 12.1 %column_terms.4 = bf16[4,256,1536]{2,1,0:T(8,128)(2,1)} custom-call(s32[4]{0:T(128)} %pad_add_fusion.ids_ref.refs_0_, bf16[1024,2048]{1,0:T(8,128)(2,1)} %norm_rows.1.x_ref.a_ref, bf16[1024,2048]{1,0:T(8,128)(2,1)} %collective-permute-done.51.b_ref, bf16[1024,1536]{1,0:T(8,128)(2,1)} %get-tuple-element.432.ra_ref.refs_3_, ...), custom_call_target="tpu_custom_call" | custom-call | flops 1 | bytes 1 | tf_op jit(solution)/shard_map/column_terms/pallas_call | solution.py:1127
  608.7 4.2 collective-permute-done.58.last_ref
  612.9 4.7 all-to-all-start.2
  627.1 11.6 %collective-permute-start.62 = (bf16[256,2048]{1,0:T(8,128)(2,1)S(1)}, bf16[256,2048]{1,0:T(8,128)(2,1)}, u32[]{:S(2)}, u32[]{:S(2)}) collective-permute-start(bf16[256,2048]{1,0:T(8,128)(2,1)S(1)} %slice_add_fusion.2), channel_id=1, source_target_pairs={{0,8},{24,16},{1,9},{25,17},{2,10},{26,18},{3,11},{27,19},{4,12},{... | collective-permute-start | bytes 3145736 | tf_op jit(solution)/shard_map/ppermute | solution.py:1200
  639.8 26.0 %mixer_backward.3 = (bf16[1024,1536]{1,0:T(8,128)(2,1)}, f32[1024,128]{1,0:T(8,128)}, f32[8,1024]{1,0:T(8,128)}, f32[8,256]{1,0:T(8,128)}) custom-call(s32[4]{0:T(128)} %pad_add_fusion.ids_ref.refs_0_, f32[1024,1664]{1,0:T(8,128)} %project.2.refs_1_.refs_2_, f32[1024,1664]{1,0:T(8,128)} %project.2.refs_1_.refs_2_, f32[8,1024]{1,0:T(8,128)} %get-tuple-element.284.refs_3_, ...), custom_call_target="tpu_custom_call" | custom-call | flops 1 | bytes 1 | tf_op jit(solution)/shard_map/mixer_backward/pallas_call | solution.py:487
  673.5 6.7 collective-permute-start.65
  683.8 13.4 %column_terms.5 = bf16[4,256,1664]{2,1,0:T(8,128)(2,1)} custom-call(s32[4]{0:T(128)} %pad_add_fusion.ids_ref.refs_0_, bf16[1024,2048]{1,0:T(8,128)(2,1)} %norm_rows.1.x_ref.a_ref, bf16[1024,2048]{1,0:T(8,128)(2,1)} %collective-permute-done.51.b_ref, bf16[1024,1664]{1,0:T(8,128)(2,1)} %copy-done.3, bf16[1024,1664]{1,0:T(8,128)(2,1)} %collective-permute-done.68.rb_ref), custom_call_target="tpu_custom_call" | custom-call | flops 1 | bytes 1 | tf_op jit(solution)/shard_map/column_terms/pallas_call | solution.py:1127
  697.3 4.4 collective-permute-done.65
  701.7 6.2 collective-permute-done.67.last_ref
  707.9 4.7 all-to-all-start.3
  724.9 23.3 %times_transposed.3 = (bf16[512,1024]{1,0:T(8,128)(2,1)}, bf16[512,1024]{1,0:T(8,128)(2,1)}, bf16[512,1024]{1,0:T(8,128)(2,1)}, bf16[512,1024]{1,0:T(8,128)(2,1)}) custom-call(s32[4]{0:T(128)} %pad_add_fusion.ids_ref.refs_0_, bf16[1024,1664]{1,0:T(8,128)(2,1)} %copy-done.3, bf16[4,4,64,1664]{3,2,1,0:T(8,128)(2,1)} %bitcast.64, ...), custom_call_target="tpu_custom_call" | custom-call | flops 1 | bytes 1 | tf_op jit(solution)/shard_map/times_transposed/pallas_call | solution.py:1092
  752.7 8.9 collective-permute-start.76
  786.8 5.9 collective-permute-done.74
  794.4 8.7 collective-permute-done.77
  820.2 28.7 %collective-permute-done.84.last_ref = bf16[512,1536]{1,0:T(8,128)(2,1)} collective-permute-done((bf16[512,1536]{1,0:T(8,128)(2,1)}, bf16[512,1536]{1,0:T(8,128)(2,1)}, u32[]{:S(2)}, u32[]{:S(2)}) %collective-permute-start.84) | collective-permute-done | bytes 1572896 | tf_op jit(solution)/shard_map/ppermute | solution.py:1200
  853.2 4.4 collective-permute-done.79
  858.6 6.6 collective-permute-start.85
  875.0 5.3 all-to-all-start.4
  880.3 8.2 finish_projection.6.refs_0_
  894.0 8.2 finish_projection.7.refs_0_
  902.2 9.1 collective-permute-done.88.last_ref
  911.3 8.1 collective-permute-start.90
  928.7 4.7 finish_projection.8.refs_0_
  933.4 10.7 %collective-permute-done.92.last_ref = bf16[256,1664]{1,0:T(8,128)(2,1)S(1)} collective-permute-done((bf16[256,1664]{1,0:T(8,128)(2,1)S(1)}, bf16[256,1664]{1,0:T(8,128)(2,1)S(1)}, u32[]{:S(2)}, u32[]{:S(2)}) %collective-permute-start.92) | collective-permute-done | bytes 852000 | tf_op jit(solution)/shard_map/ppermute | solution.py:1200
  952.6 4.7 finish_projection.9.refs_0_
  957.4 10.4 %collective-permute-done.94.last_ref = bf16[256,1664]{1,0:T(8,128)(2,1)} collective-permute-done((bf16[256,1664]{1,0:T(8,128)(2,1)S(1)}, bf16[256,1664]{1,0:T(8,128)(2,1)}, u32[]{:S(2)}, u32[]{:S(2)}) %collective-permute-start.94) | collective-permute-done | bytes 852000 | tf_op jit(solution)/shard_map/ppermute | solution.py:1200
  974.0 10.6 %finish_feed_forward.1 = f32[256,11264]{1,0:T(8,128)} custom-call(bf16[4,256,2816]{2,1,0:T(8,128)(2,1)} %all-to-all-done.4.x_ref), custom_call_target="tpu_custom_call" | custom-call | flops 1 | bytes 1 | tf_op jit(solution)/shard_map/finish_feed_forward/pallas_call | solution.py:855
  984.6 4.7 finish_projection.10.refs_0_
  993.3 4.7 finish_projection.11
  (487 shorter events, 313.2 us)
Async XLA Ops:
  7.2 89.0 %all-gather.5.cloned.1.call-start = ((), (), s32[]{:S(2)}) async-start(), calls=%async_computation.5 | async-start | bytes 4259840 | tf_op jit(solution)/shard_map/all_gather | solution.py:1529
  27.9 38.9 %collective-permute-start.6 = (bf16[704,2048]{1,0:T(8,128)(2,1)}, bf16[704,2048]{1,0:T(8,128)(2,1)}, u32[]{:S(2)}, u32[]{:S(2)}) collective-permute-start(bf16[704,2048]{1,0:T(8,128)(2,1)} %refs_1_.1), channel_id=1, source_target_pairs={{0,1},{1,0},{2,3},{3,2},{4,5},{5,4},{6,7},{7,6},{8,9},{9,8},{10,11... | collective-permute-start | bytes 8650760 | tf_op jit(solution)/shard_map/ppermute | solution.py:1188
  28.0 38.9 %collective-permute-start.5 = (bf16[512,2048]{1,0:T(8,128)(2,1)}, bf16[512,2048]{1,0:T(8,128)(2,1)}, u32[]{:S(2)}, u32[]{:S(2)}) collective-permute-start(bf16[512,2048]{1,0:T(8,128)(2,1)} %mine_ref.3), channel_id=1, source_target_pairs={{0,1},{1,0},{2,3},{3,2},{4,5},{5,4},{6,7},{7,6},{8,9},{9,8},{10,11... | collective-permute-start | bytes 6291464 | tf_op jit(solution)/shard_map/ppermute | solution.py:1188
  40.2 24.7 %collective-permute-start.3 = (bf16[256,2048]{1,0:T(8,128)(2,1)S(1)}, bf16[256,2048]{1,0:T(8,128)(2,1)S(1)}, u32[]{:S(2)}, u32[]{:S(2)}) collective-permute-start(bf16[256,2048]{1,0:T(8,128)(2,1)S(1)} %copy-done.5), channel_id=1, source_target_pairs={{0,2},{1,3},{2,0},{3,1},{4,6},{5,7},{6,4},{7,5},{8,10},{9,11},{10,... | collective-permute-start | bytes 3145736 | tf_op jit(solution)/shard_map/ppermute | solution.py:1184
  40.7 24.5 %collective-permute-start.4 = (bf16[256,2048]{1,0:T(8,128)(2,1)S(1)}, bf16[256,2048]{1,0:T(8,128)(2,1)S(1)}, u32[]{:S(2)}, u32[]{:S(2)}) collective-permute-start(bf16[256,2048]{1,0:T(8,128)(2,1)S(1)} %copy-done.5), channel_id=1, source_target_pairs={{0,4},{1,5},{2,6},{3,7},{4,0},{5,1},{6,2},{7,3},{8,12},{9,13},{10,... | collective-permute-start | bytes 3145736 | tf_op jit(solution)/shard_map/ppermute | solution.py:1184
  96.2 31.4 %collective-permute-start.10 = (bf16[256,1536]{1,0:T(8,128)(2,1)}, bf16[256,1536]{1,0:T(8,128)(2,1)}, u32[]{:S(2)}, u32[]{:S(2)}) collective-permute-start(bf16[256,1536]{1,0:T(8,128)(2,1)} %get-tuple-element.280), channel_id=1, source_target_pairs={{0,2},{1,3},{2,0},{3,1},{4,6},{5,7},{6,4},{7,5},{8,10},{9,11},{10,... | collective-permute-start | bytes 2359304 | tf_op jit(solution)/shard_map/ppermute | solution.py:1184
  97.7 36.8 %collective-permute-start.11 = (bf16[256,1536]{1,0:T(8,128)(2,1)}, bf16[256,1536]{1,0:T(8,128)(2,1)}, u32[]{:S(2)}, u32[]{:S(2)}) collective-permute-start(bf16[256,1536]{1,0:T(8,128)(2,1)} %get-tuple-element.281), channel_id=1, source_target_pairs={{0,4},{1,5},{2,6},{3,7},{4,0},{5,1},{6,2},{7,3},{8,12},{9,13},{10,... | collective-permute-start | bytes 2359304 | tf_op jit(solution)/shard_map/ppermute | solution.py:1184
  99.1 35.4 %collective-permute-start.12 = (bf16[256,1536]{1,0:T(8,128)(2,1)}, bf16[256,1536]{1,0:T(8,128)(2,1)}, u32[]{:S(2)}, u32[]{:S(2)}) collective-permute-start(bf16[256,1536]{1,0:T(8,128)(2,1)} %get-tuple-element.282), channel_id=1, source_target_pairs={{0,6},{1,7},{2,4},{3,5},{4,2},{5,3},{6,0},{7,1},{8,14},{9,15},{10,... | collective-permute-start | bytes 2359304 | tf_op jit(solution)/shard_map/ppermute | solution.py:1184
  134.5 24.2 %all-to-all-start.1 = ((bf16[4,64,2816]{2,1,0:T(8,128)(2,1)}), bf16[4,64,2816]{2,1,0:T(8,128)(2,1)S(1)}, u32[]{:S(2)}, u32[]{:S(2)}) async-start(bf16[4,64,2816]{2,1,0:T(8,128)(2,1)} %pack_columns.1), calls=%async_computation.1 | async-start | bytes 2883584 | tf_op jit(solution)/shard_map/all_to_all | solution.py:1354
  138.1 127.7 %all-gather.7.cloned.1.call-start = ((), (), s32[]{:S(2)}) async-start(), calls=%async_computation.6 | async-start | bytes 7208960 | tf_op jit(solution)/shard_map/all_gather | solution.py:1555
  159.9 25.8 %collective-permute-start.17 = (bf16[256,2048]{1,0:T(8,128)(2,1)S(1)}, bf16[256,2048]{1,0:T(8,128)(2,1)S(1)}, u32[]{:S(2)}, u32[]{:S(2)}) collective-permute-start(bf16[256,2048]{1,0:T(8,128)(2,1)S(1)} %copy-done.32), channel_id=1, source_target_pairs={{0,2},{1,3},{2,0},{3,1},{4,6},{5,7},{6,4},{7,5},{8,10},{9,11},{10,... | collective-permute-start | bytes 3145736 | tf_op jit(solution)/shard_map/ppermute | solution.py:1184
  161.9 25.3 %collective-permute-start.18 = (bf16[256,2048]{1,0:T(8,128)(2,1)S(1)}, bf16[256,2048]{1,0:T(8,128)(2,1)}, u32[]{:S(2)}, u32[]{:S(2)}) collective-permute-start(bf16[256,2048]{1,0:T(8,128)(2,1)S(1)} %copy-done.32), channel_id=1, source_target_pairs={{0,4},{1,5},{2,6},{3,7},{4,0},{5,1},{6,2},{7,3},{8,12},{9,13},{10,... | collective-permute-start | bytes 3145736 | tf_op jit(solution)/shard_map/ppermute | solution.py:1184
  188.3 22.4 %collective-permute-start.19 = (bf16[128,2048]{1,0:T(8,128)(2,1)S(1)}, bf16[128,2048]{1,0:T(8,128)(2,1)S(1)}, u32[]{:S(2)}, u32[]{:S(2)}) collective-permute-start(bf16[128,2048]{1,0:T(8,128)(2,1)S(1)} %slice.345), channel_id=1, source_target_pairs={{0,4},{1,5},{2,6},{3,7},{4,0},{5,1},{6,2},{7,3},{8,12},{9,13},{10,... | collective-permute-start | bytes 1572872 | tf_op jit(solution)/shard_map/ppermute | solution.py:1184
  221.6 24.7 %collective-permute-start.21 = (bf16[512,1024]{1,0:T(8,128)(2,1)}, bf16[512,1024]{1,0:T(8,128)(2,1)}, u32[]{:S(2)}, u32[]{:S(2)}) collective-permute-start(bf16[512,1024]{1,0:T(8,128)(2,1)} %get-tuple-element.302), channel_id=1, source_target_pairs={{0,2},{1,3},{2,0},{3,1},{4,6},{5,7},{6,4},{7,5},{8,10},{9,11},{10,... | collective-permute-start | bytes 3145736 | tf_op jit(solution)/shard_map/ppermute | solution.py:1184
  223.1 23.9 %collective-permute-start.22 = (bf16[512,1024]{1,0:T(8,128)(2,1)}, bf16[512,1024]{1,0:T(8,128)(2,1)}, u32[]{:S(2)}, u32[]{:S(2)}) collective-permute-start(bf16[512,1024]{1,0:T(8,128)(2,1)} %get-tuple-element.304), channel_id=1, source_target_pairs={{0,4},{1,5},{2,6},{3,7},{4,0},{5,1},{6,2},{7,3},{8,12},{9,13},{10,... | collective-permute-start | bytes 3145736 | tf_op jit(solution)/shard_map/ppermute | solution.py:1184
  265.8 46.1 %collective-permute-start.29 = (bf16[4,4,64,2816]{3,2,1,0:T(8,128)(2,1)}, bf16[4,4,64,2816]{3,2,1,0:T(8,128)(2,1)}, u32[]{:S(2)}, u32[]{:S(2)}) collective-permute-start(bf16[4,4,64,2816]{3,2,1,0:T(8,128)(2,1)} %bitcast.59), channel_id=1, source_target_pairs={{0,1},{1,0},{2,3},{3,2},{4,5},{5,4},{6,7},{7,6},{8,9},{9,8},{10,11... | collective-permute-start | bytes 17301512 | tf_op jit(solution)/shard_map/ppermute | solution.py:1188
  270.8 25.4 %collective-permute-start.25 = (bf16[256,2048]{1,0:T(8,128)(2,1)S(1)}, bf16[256,2048]{1,0:T(8,128)(2,1)S(1)}, u32[]{:S(2)}, u32[]{:S(2)}) collective-permute-start(bf16[256,2048]{1,0:T(8,128)(2,1)S(1)} %get-tuple-element.535), channel_id=1, source_target_pairs={{0,2},{1,3},{2,0},{3,1},{4,6},{5,7},{6,4},{7,5},{8,10},{9,11},{10,... | collective-permute-start | bytes 3145736 | tf_op jit(solution)/shard_map/ppermute | solution.py:1184
  272.3 25.5 %collective-permute-start.26 = (bf16[256,2048]{1,0:T(8,128)(2,1)S(1)}, bf16[256,2048]{1,0:T(8,128)(2,1)S(1)}, u32[]{:S(2)}, u32[]{:S(2)}) collective-permute-start(bf16[256,2048]{1,0:T(8,128)(2,1)S(1)} %get-tuple-element.535), channel_id=1, source_target_pairs={{0,4},{1,5},{2,6},{3,7},{4,0},{5,1},{6,2},{7,3},{8,12},{9,13},{10,... | collective-permute-start | bytes 3145736 | tf_op jit(solution)/shard_map/ppermute | solution.py:1184
  311.9 28.6 %collective-permute-start.30 = (bf16[1024,2048]{1,0:T(8,128)(2,1)}, bf16[1024,2048]{1,0:T(8,128)(2,1)}, u32[]{:S(2)}, u32[]{:S(2)}) collective-permute-start(bf16[1024,2048]{1,0:T(8,128)(2,1)} %constant_dynamic-update-slice_fusion.5.x_ref.a_ref), channel_id=1, source_target_pairs={{0,1},{1,0},{2,3},{3,2},{4,5},{5,4},{6,7},{7,6},{8,9},{9,8},{10,11... | collective-permute-start | bytes 12582920 | tf_op jit(solution)/shard_map/ppermute | solution.py:1188
  359.9 33.7 %collective-permute-start.33 = (bf16[352,2048]{1,0:T(8,128)(2,1)S(1)}, bf16[352,2048]{1,0:T(8,128)(2,1)}, u32[]{:S(2)}, u32[]{:S(2)}) collective-permute-start(bf16[352,2048]{1,0:T(8,128)(2,1)S(1)} %get-tuple-element.350), channel_id=1, source_target_pairs={{0,8},{8,0},{16,24},{24,16},{1,9},{9,1},{17,25},{25,17},{2,10},{10... | collective-permute-start | bytes 4325384 | tf_op jit(solution)/shard_map/ppermute | solution.py:1200
  380.2 30.7 %collective-permute-start.34 = (bf16[512,1024]{1,0:T(8,128)(2,1)}, bf16[512,1024]{1,0:T(8,128)(2,1)}, u32[]{:S(2)}, u32[]{:S(2)}) collective-permute-start(bf16[512,1024]{1,0:T(8,128)(2,1)} %get-tuple-element.332), channel_id=1, source_target_pairs={{0,2},{1,3},{2,0},{3,1},{4,6},{5,7},{6,4},{7,5},{8,10},{9,11},{10,... | collective-permute-start | bytes 3145736 | tf_op jit(solution)/shard_map/ppermute | solution.py:1184
  381.8 29.2 %collective-permute-start.35 = (bf16[512,1024]{1,0:T(8,128)(2,1)}, bf16[512,1024]{1,0:T(8,128)(2,1)}, u32[]{:S(2)}, u32[]{:S(2)}) collective-permute-start(bf16[512,1024]{1,0:T(8,128)(2,1)} %get-tuple-element.334), channel_id=1, source_target_pairs={{0,4},{1,5},{2,6},{3,7},{4,0},{5,1},{6,2},{7,3},{8,12},{9,13},{10,... | collective-permute-start | bytes 3145736 | tf_op jit(solution)/shard_map/ppermute | solution.py:1184
  393.6 48.9 %collective-permute-start.40 = (bf16[352,2048]{1,0:T(8,128)(2,1)}, bf16[352,2048]{1,0:T(8,128)(2,1)}, u32[]{:S(2)}, u32[]{:S(2)}) collective-permute-start(bf16[352,2048]{1,0:T(8,128)(2,1)} %get-tuple-element.361), channel_id=1, source_target_pairs={{0,8},{8,0},{16,24},{24,16},{1,9},{9,1},{17,25},{25,17},{2,10},{10... | collective-permute-start | bytes 4325384 | tf_op jit(solution)/shard_map/ppermute | solution.py:1200
  396.3 46.2 %collective-permute-start.41 = (bf16[352,2048]{1,0:T(8,128)(2,1)S(1)}, bf16[352,2048]{1,0:T(8,128)(2,1)}, u32[]{:S(2)}, u32[]{:S(2)}) collective-permute-start(bf16[352,2048]{1,0:T(8,128)(2,1)S(1)} %add.243), channel_id=1, source_target_pairs={{8,16},{16,8},{9,17},{17,9},{10,18},{18,10},{11,19},{19,11},{12,20... | collective-permute-start | bytes 4325384 | tf_op jit(solution)/shard_map/ppermute | solution.py:1200
  413.6 39.3 %collective-permute-start.36 = (bf16[256,1024]{1,0:T(8,128)(2,1)}, bf16[256,1024]{1,0:T(8,128)(2,1)}, u32[]{:S(2)}, u32[]{:S(2)}) collective-permute-start(bf16[256,1024]{1,0:T(8,128)(2,1)} %get-tuple-element.568), channel_id=1, source_target_pairs={{0,4},{1,5},{2,6},{3,7},{4,0},{5,1},{6,2},{7,3},{8,12},{9,13},{10,... | collective-permute-start | bytes 1572872 | tf_op jit(solution)/shard_map/ppermute | solution.py:1184
  417.0 36.0 %collective-permute-start.37 = (bf16[256,1024]{1,0:T(8,128)(2,1)}, bf16[256,1024]{1,0:T(8,128)(2,1)}, u32[]{:S(2)}, u32[]{:S(2)}) collective-permute-start(bf16[256,1024]{1,0:T(8,128)(2,1)} %get-tuple-element.565), channel_id=1, source_target_pairs={{0,2},{1,3},{2,0},{3,1},{4,6},{5,7},{6,4},{7,5},{8,10},{9,11},{10,... | collective-permute-start | bytes 1572872 | tf_op jit(solution)/shard_map/ppermute | solution.py:1184
  442.5 33.3 %collective-permute-start.44 = (bf16[256,2816]{1,0:T(8,128)(2,1)S(1)}, bf16[256,2816]{1,0:T(8,128)(2,1)S(1)}, u32[]{:S(2)}, u32[]{:S(2)}) collective-permute-start(bf16[256,2816]{1,0:T(8,128)(2,1)S(1)} %get-tuple-element.379), channel_id=1, source_target_pairs={{0,8},{24,16},{1,9},{25,17},{2,10},{26,18},{3,11},{27,19},{4,12},{... | collective-permute-start | bytes 4325384 | tf_op jit(solution)/shard_map/ppermute | solution.py:1200
  448.3 33.7 %collective-permute-start.45 = (bf16[352,2048]{1,0:T(8,128)(2,1)S(1)}, bf16[352,2048]{1,0:T(8,128)(2,1)S(1)}, u32[]{:S(2)}, u32[]{:S(2)}) collective-permute-start(bf16[352,2048]{1,0:T(8,128)(2,1)S(1)} %add.249), channel_id=1, source_target_pairs={{8,0},{16,24},{9,1},{17,25},{10,2},{18,26},{11,3},{19,27},{12,4},{... | collective-permute-start | bytes 4325384 | tf_op jit(solution)/shard_map/ppermute | solution.py:1200
  452.1 31.0 %collective-permute-start.46 = (bf16[352,2048]{1,0:T(8,128)(2,1)S(1)}, bf16[352,2048]{1,0:T(8,128)(2,1)S(1)}, u32[]{:S(2)}, u32[]{:S(2)}) collective-permute-start(bf16[352,2048]{1,0:T(8,128)(2,1)S(1)} %add.250), channel_id=1, source_target_pairs={{8,16},{16,8},{9,17},{17,9},{10,18},{18,10},{11,19},{19,11},{12,20... | collective-permute-start | bytes 4325384 | tf_op jit(solution)/shard_map/ppermute | solution.py:1200
  459.3 35.2 %collective-permute-start.42 = (bf16[256,2048]{1,0:T(8,128)(2,1)S(1)}, bf16[256,2048]{1,0:T(8,128)(2,1)S(1)}, u32[]{:S(2)}, u32[]{:S(2)}) collective-permute-start(bf16[256,2048]{1,0:T(8,128)(2,1)S(1)} %get-tuple-element.532), channel_id=1, source_target_pairs={{0,2},{1,3},{2,0},{3,1},{4,6},{5,7},{6,4},{7,5},{8,10},{9,11},{10,... | collective-permute-start | bytes 3145736 | tf_op jit(solution)/shard_map/ppermute | solution.py:1184
  459.9 35.9 %collective-permute-start.43 = (bf16[256,2048]{1,0:T(8,128)(2,1)S(1)}, bf16[256,2048]{1,0:T(8,128)(2,1)S(1)}, u32[]{:S(2)}, u32[]{:S(2)}) collective-permute-start(bf16[256,2048]{1,0:T(8,128)(2,1)S(1)} %get-tuple-element.532), channel_id=1, source_target_pairs={{0,4},{1,5},{2,6},{3,7},{4,0},{5,1},{6,2},{7,3},{8,12},{9,13},{10,... | collective-permute-start | bytes 3145736 | tf_op jit(solution)/shard_map/ppermute | solution.py:1184
  475.8 29.3 %collective-permute-start.38 = (bf16[512,1024]{1,0:T(8,128)(2,1)S(1)}, bf16[512,1024]{1,0:T(8,128)(2,1)}, u32[]{:S(2)}, u32[]{:S(2)}) collective-permute-start(bf16[512,1024]{1,0:T(8,128)(2,1)S(1)} %copy-done.91), channel_id=1, source_target_pairs={{0,2},{1,3},{2,0},{3,1},{4,6},{5,7},{6,4},{7,5},{8,10},{9,11},{10,... | collective-permute-start | bytes 3145736 | tf_op jit(solution)/shard_map/ppermute | solution.py:1184
  482.0 23.4 %collective-permute-start.39 = (bf16[512,1024]{1,0:T(8,128)(2,1)S(1)}, bf16[512,1024]{1,0:T(8,128)(2,1)}, u32[]{:S(2)}, u32[]{:S(2)}) collective-permute-start(bf16[512,1024]{1,0:T(8,128)(2,1)S(1)} %copy-done.90), channel_id=1, source_target_pairs={{0,4},{1,5},{2,6},{3,7},{4,0},{5,1},{6,2},{7,3},{8,12},{9,13},{10,... | collective-permute-start | bytes 3145736 | tf_op jit(solution)/shard_map/ppermute | solution.py:1184
  483.1 42.9 %collective-permute-start.52 = (bf16[256,2816]{1,0:T(8,128)(2,1)}, bf16[256,2816]{1,0:T(8,128)(2,1)}, u32[]{:S(2)}, u32[]{:S(2)}) collective-permute-start(bf16[256,2816]{1,0:T(8,128)(2,1)} %get-tuple-element.386), channel_id=1, source_target_pairs={{0,8},{24,16},{1,9},{25,17},{2,10},{26,18},{3,11},{27,19},{4,12},{... | collective-permute-start | bytes 4325384 | tf_op jit(solution)/shard_map/ppermute | solution.py:1200
  494.4 33.3 %collective-permute-start.53 = (bf16[352,2048]{1,0:T(8,128)(2,1)}, bf16[352,2048]{1,0:T(8,128)(2,1)}, u32[]{:S(2)}, u32[]{:S(2)}) collective-permute-start(bf16[352,2048]{1,0:T(8,128)(2,1)} %add.253), channel_id=1, source_target_pairs={{8,0},{16,24},{9,1},{17,25},{10,2},{18,26},{11,3},{19,27},{12,4},{... | collective-permute-start | bytes 4325384 | tf_op jit(solution)/shard_map/ppermute | solution.py:1200
  495.7 32.0 %collective-permute-start.54 = (bf16[256,2816]{1,0:T(8,128)(2,1)}, bf16[256,2816]{1,0:T(8,128)(2,1)}, u32[]{:S(2)}, u32[]{:S(2)}) collective-permute-start(bf16[256,2816]{1,0:T(8,128)(2,1)} %add.254), channel_id=1, source_target_pairs={{8,16},{16,8},{9,17},{17,9},{10,18},{18,10},{11,19},{19,11},{12,20... | collective-permute-start | bytes 4325384 | tf_op jit(solution)/shard_map/ppermute | solution.py:1200
  517.4 79.2 %collective-permute-start.51 = (bf16[1024,2048]{1,0:T(8,128)(2,1)S(1)}, bf16[1024,2048]{1,0:T(8,128)(2,1)}, u32[]{:S(2)}, u32[]{:S(2)}) collective-permute-start(bf16[1024,2048]{1,0:T(8,128)(2,1)S(1)} %copy-done), channel_id=1, source_target_pairs={{0,1},{1,0},{2,3},{3,2},{4,5},{5,4},{6,7},{7,6},{8,9},{9,8},{10,11... | collective-permute-start | bytes 12582920 | tf_op jit(solution)/shard_map/ppermute | solution.py:1188
  520.7 27.5 %collective-permute-start.49 = (bf16[256,1024]{1,0:T(8,128)(2,1)S(1)}, bf16[256,1024]{1,0:T(8,128)(2,1)S(1)}, u32[]{:S(2)}, u32[]{:S(2)}) collective-permute-start(bf16[256,1024]{1,0:T(8,128)(2,1)S(1)} %get-tuple-element.562), channel_id=1, source_target_pairs={{0,4},{1,5},{2,6},{3,7},{4,0},{5,1},{6,2},{7,3},{8,12},{9,13},{10,... | collective-permute-start | bytes 1572872 | tf_op jit(solution)/shard_map/ppermute | solution.py:1184
  526.0 22.2 %collective-permute-start.50 = (bf16[256,1024]{1,0:T(8,128)(2,1)S(1)}, bf16[256,1024]{1,0:T(8,128)(2,1)S(1)}, u32[]{:S(2)}, u32[]{:S(2)}) collective-permute-start(bf16[256,1024]{1,0:T(8,128)(2,1)S(1)} %get-tuple-element.559), channel_id=1, source_target_pairs={{0,2},{1,3},{2,0},{3,1},{4,6},{5,7},{6,4},{7,5},{8,10},{9,11},{10,... | collective-permute-start | bytes 1572872 | tf_op jit(solution)/shard_map/ppermute | solution.py:1184
  531.1 44.2 %collective-permute-start.55 = (bf16[256,2816]{1,0:T(8,128)(2,1)}, bf16[256,2816]{1,0:T(8,128)(2,1)}, u32[]{:S(2)}, u32[]{:S(2)}) collective-permute-start(bf16[256,2816]{1,0:T(8,128)(2,1)} %add_select_fusion.1.t_ref), channel_id=1, source_target_pairs={{0,8},{8,0},{16,24},{24,16},{1,9},{9,1},{17,25},{25,17},{2,10},{10... | collective-permute-start | bytes 4325384 | tf_op jit(solution)/shard_map/ppermute | solution.py:1200
  538.7 36.6 %collective-permute-start.56 = (bf16[256,2816]{1,0:T(8,128)(2,1)}, bf16[256,2816]{1,0:T(8,128)(2,1)}, u32[]{:S(2)}, u32[]{:S(2)}) collective-permute-start(bf16[256,2816]{1,0:T(8,128)(2,1)} %add.256), channel_id=1, source_target_pairs={{8,16},{16,8},{9,17},{17,9},{10,18},{18,10},{11,19},{19,11},{12,20... | collective-permute-start | bytes 4325384 | tf_op jit(solution)/shard_map/ppermute | solution.py:1200
  578.7 34.3 %collective-permute-start.58 = (bf16[256,2816]{1,0:T(8,128)(2,1)}, bf16[256,2816]{1,0:T(8,128)(2,1)}, u32[]{:S(2)}, u32[]{:S(2)}) collective-permute-start(bf16[256,2816]{1,0:T(8,128)(2,1)} %add_select_fusion.t_ref), channel_id=1, source_target_pairs={{0,8},{8,0},{16,24},{24,16},{1,9},{9,1},{17,25},{25,17},{2,10},{10... | collective-permute-start | bytes 4325384 | tf_op jit(solution)/shard_map/ppermute | solution.py:1200
  582.7 30.2 %collective-permute-start.59 = (bf16[256,2816]{1,0:T(8,128)(2,1)}, bf16[256,2816]{1,0:T(8,128)(2,1)}, u32[]{:S(2)}, u32[]{:S(2)}) collective-permute-start(bf16[256,2816]{1,0:T(8,128)(2,1)} %add.258), channel_id=1, source_target_pairs={{8,16},{16,8},{9,17},{17,9},{10,18},{18,10},{11,19},{19,11},{12,20... | collective-permute-start | bytes 4325384 | tf_op jit(solution)/shard_map/ppermute | solution.py:1200
  612.9 54.0 %all-to-all-start.2 = ((bf16[4,256,1536]{2,1,0:T(8,128)(2,1)}), bf16[4,256,1536]{2,1,0:T(8,128)(2,1)}, u32[]{:S(2)}, u32[]{:S(2)}) async-start(bf16[4,256,1536]{2,1,0:T(8,128)(2,1)} %column_terms.4), calls=%async_computation.2 | async-start | bytes 6291456 | tf_op jit(solution)/shard_map/all_to_all | solution.py:1354
  621.8 45.2 %collective-permute-start.63 = (bf16[256,2816]{1,0:T(8,128)(2,1)S(1)}, bf16[256,2816]{1,0:T(8,128)(2,1)}, u32[]{:S(2)}, u32[]{:S(2)}) collective-permute-start(bf16[256,2816]{1,0:T(8,128)(2,1)S(1)} %add.261), channel_id=1, source_target_pairs={{8,16},{16,8},{9,17},{17,9},{10,18},{18,10},{11,19},{19,11},{12,20... | collective-permute-start | bytes 4325384 | tf_op jit(solution)/shard_map/ppermute | solution.py:1200
  625.8 41.1 %collective-permute-start.64 = (bf16[256,2816]{1,0:T(8,128)(2,1)S(1)}, bf16[256,2816]{1,0:T(8,128)(2,1)}, u32[]{:S(2)}, u32[]{:S(2)}) collective-permute-start(bf16[256,2816]{1,0:T(8,128)(2,1)S(1)} %add.262.t_ref), channel_id=1, source_target_pairs={{8,0},{16,24},{9,1},{17,25},{10,2},{18,26},{11,3},{19,27},{12,4},{... | collective-permute-start | bytes 4325384 | tf_op jit(solution)/shard_map/ppermute | solution.py:1200
  627.1 39.8 %collective-permute-start.62 = (bf16[256,2048]{1,0:T(8,128)(2,1)S(1)}, bf16[256,2048]{1,0:T(8,128)(2,1)}, u32[]{:S(2)}, u32[]{:S(2)}) collective-permute-start(bf16[256,2048]{1,0:T(8,128)(2,1)S(1)} %slice_add_fusion.2), channel_id=1, source_target_pairs={{0,8},{24,16},{1,9},{25,17},{2,10},{26,18},{3,11},{27,19},{4,12},{... | collective-permute-start | bytes 3145736 | tf_op jit(solution)/shard_map/ppermute | solution.py:1200
  672.2 35.7 %collective-permute-start.67 = (bf16[256,2816]{1,0:T(8,128)(2,1)S(1)}, bf16[256,2816]{1,0:T(8,128)(2,1)}, u32[]{:S(2)}, u32[]{:S(2)}) collective-permute-start(bf16[256,2816]{1,0:T(8,128)(2,1)S(1)} %add.265.t_ref), channel_id=1, source_target_pairs={{8,0},{16,24},{9,1},{17,25},{10,2},{18,26},{11,3},{19,27},{12,4},{... | collective-permute-start | bytes 4325384 | tf_op jit(solution)/shard_map/ppermute | solution.py:1200
  673.5 28.2 %collective-permute-start.65 = (bf16[256,2048]{1,0:T(8,128)(2,1)S(1)}, bf16[256,2048]{1,0:T(8,128)(2,1)}, u32[]{:S(2)}, u32[]{:S(2)}) collective-permute-start(bf16[256,2048]{1,0:T(8,128)(2,1)S(1)} %copy-done.24), channel_id=1, source_target_pairs={{0,8},{24,16},{1,9},{25,17},{2,10},{26,18},{3,11},{27,19},{4,12},{... | collective-permute-start | bytes 3145736 | tf_op jit(solution)/shard_map/ppermute | solution.py:1200
  707.9 44.8 %all-to-all-start.3 = ((bf16[4,256,1664]{2,1,0:T(8,128)(2,1)}), bf16[4,256,1664]{2,1,0:T(8,128)(2,1)}, u32[]{:S(2)}, u32[]{:S(2)}) async-start(bf16[4,256,1664]{2,1,0:T(8,128)(2,1)} %column_terms.5), calls=%async_computation.3 | async-start | bytes 6815744 | tf_op jit(solution)/shard_map/all_to_all | solution.py:1354
  715.8 36.9 %collective-permute-start.69 = (bf16[512,1536]{1,0:T(8,128)(2,1)S(1)}, bf16[512,1536]{1,0:T(8,128)(2,1)}, u32[]{:S(2)}, u32[]{:S(2)}) collective-permute-start(bf16[512,1536]{1,0:T(8,128)(2,1)S(1)} %bitcast.67), channel_id=1, source_target_pairs={{0,8},{24,16},{1,9},{25,17},{2,10},{26,18},{3,11},{27,19},{4,12},{... | collective-permute-start | bytes 4718600 | tf_op jit(solution)/shard_map/ppermute | solution.py:1200
  721.2 30.4 %collective-permute-start.70 = (bf16[256,2048]{1,0:T(8,128)(2,1)}, bf16[256,2048]{1,0:T(8,128)(2,1)}, u32[]{:S(2)}, u32[]{:S(2)}) collective-permute-start(bf16[256,2048]{1,0:T(8,128)(2,1)} %add.266), channel_id=1, source_target_pairs={{8,0},{16,24},{9,1},{17,25},{10,2},{18,26},{11,3},{19,27},{12,4},{... | collective-permute-start | bytes 3145736 | tf_op jit(solution)/shard_map/ppermute | solution.py:1200
  724.1 27.5 %collective-permute-start.71 = (bf16[256,2048]{1,0:T(8,128)(2,1)S(1)}, bf16[256,2048]{1,0:T(8,128)(2,1)S(1)}, u32[]{:S(2)}, u32[]{:S(2)}) collective-permute-start(bf16[256,2048]{1,0:T(8,128)(2,1)S(1)} %add.267), channel_id=1, source_target_pairs={{8,16},{16,8},{9,17},{17,9},{10,18},{18,10},{11,19},{19,11},{12,20... | collective-permute-start | bytes 3145736 | tf_op jit(solution)/shard_map/ppermute | solution.py:1200
  748.1 29.6 %collective-permute-start.72 = (bf16[512,1024]{1,0:T(8,128)(2,1)}, bf16[512,1024]{1,0:T(8,128)(2,1)}, u32[]{:S(2)}, u32[]{:S(2)}) collective-permute-start(bf16[512,1024]{1,0:T(8,128)(2,1)} %get-tuple-element.434), channel_id=1, source_target_pairs={{0,2},{1,3},{2,0},{3,1},{4,6},{5,7},{6,4},{7,5},{8,10},{9,11},{10,... | collective-permute-start | bytes 3145736 | tf_op jit(solution)/shard_map/ppermute | solution.py:1184
  750.1 27.6 %collective-permute-start.73 = (bf16[512,1024]{1,0:T(8,128)(2,1)}, bf16[512,1024]{1,0:T(8,128)(2,1)}, u32[]{:S(2)}, u32[]{:S(2)}) collective-permute-start(bf16[512,1024]{1,0:T(8,128)(2,1)} %get-tuple-element.436), channel_id=1, source_target_pairs={{0,4},{1,5},{2,6},{3,7},{4,0},{5,1},{6,2},{7,3},{8,12},{9,13},{10,... | collective-permute-start | bytes 3145736 | tf_op jit(solution)/shard_map/ppermute | solution.py:1184
  752.7 50.4 %collective-permute-start.76 = (bf16[512,1536]{1,0:T(8,128)(2,1)}, bf16[512,1536]{1,0:T(8,128)(2,1)}, u32[]{:S(2)}, u32[]{:S(2)}) collective-permute-start(bf16[512,1536]{1,0:T(8,128)(2,1)} %bitcast.65), channel_id=1, source_target_pairs={{0,8},{24,16},{1,9},{25,17},{2,10},{26,18},{3,11},{27,19},{4,12},{... | collective-permute-start | bytes 4718600 | tf_op jit(solution)/shard_map/ppermute | solution.py:1200
  765.0 38.1 %collective-permute-start.78 = (bf16[512,1536]{1,0:T(8,128)(2,1)}, bf16[512,1536]{1,0:T(8,128)(2,1)}, u32[]{:S(2)}, u32[]{:S(2)}) collective-permute-start(bf16[512,1536]{1,0:T(8,128)(2,1)} %add.277), channel_id=1, source_target_pairs={{8,16},{16,8},{9,17},{17,9},{10,18},{18,10},{11,19},{19,11},{12,20... | collective-permute-start | bytes 4718600 | tf_op jit(solution)/shard_map/ppermute | solution.py:1200
  778.2 24.8 %collective-permute-start.77 = (bf16[256,2048]{1,0:T(8,128)(2,1)S(1)}, bf16[256,2048]{1,0:T(8,128)(2,1)S(1)}, u32[]{:S(2)}, u32[]{:S(2)}) collective-permute-start(bf16[256,2048]{1,0:T(8,128)(2,1)S(1)} %add.276), channel_id=1, source_target_pairs={{8,0},{16,24},{9,1},{17,25},{10,2},{18,26},{11,3},{19,27},{12,4},{... | collective-permute-start | bytes 3145736 | tf_op jit(solution)/shard_map/ppermute | solution.py:1200
  813.7 35.2 %collective-permute-start.84 = (bf16[512,1536]{1,0:T(8,128)(2,1)}, bf16[512,1536]{1,0:T(8,128)(2,1)}, u32[]{:S(2)}, u32[]{:S(2)}) collective-permute-start(bf16[512,1536]{1,0:T(8,128)(2,1)} %add.287.t_ref), channel_id=1, source_target_pairs={{8,0},{16,24},{9,1},{17,25},{10,2},{18,26},{11,3},{19,27},{12,4},{... | collective-permute-start | bytes 4718600 | tf_op jit(solution)/shard_map/ppermute | solution.py:1200
  851.3 37.2 %collective-permute-start.87 = (bf16[512,1536]{1,0:T(8,128)(2,1)S(1)}, bf16[512,1536]{1,0:T(8,128)(2,1)}, u32[]{:S(2)}, u32[]{:S(2)}) collective-permute-start(bf16[512,1536]{1,0:T(8,128)(2,1)S(1)} %add.289.t_ref), channel_id=1, source_target_pairs={{8,0},{16,24},{9,1},{17,25},{10,2},{18,26},{11,3},{19,27},{12,4},{... | collective-permute-start | bytes 4718600 | tf_op jit(solution)/shard_map/ppermute | solution.py:1200
  858.6 29.8 %collective-permute-start.85 = (bf16[256,1664]{1,0:T(8,128)(2,1)S(1)}, bf16[256,1664]{1,0:T(8,128)(2,1)}, u32[]{:S(2)}, u32[]{:S(2)}) collective-permute-start(bf16[256,1664]{1,0:T(8,128)(2,1)S(1)} %copy-done.39), channel_id=1, source_target_pairs={{0,8},{24,16},{1,9},{25,17},{2,10},{26,18},{3,11},{27,19},{4,12},{... | collective-permute-start | bytes 2555912 | tf_op jit(solution)/shard_map/ppermute | solution.py:1200
  875.0 99.0 %all-to-all-start.4 = ((bf16[4,256,2816]{2,1,0:T(8,128)(2,1)}), bf16[4,256,2816]{2,1,0:T(8,128)(2,1)}, u32[]{:S(2)}, u32[]{:S(2)}) async-start(bf16[4,256,2816]{2,1,0:T(8,128)(2,1)} %place_blocks.7), calls=%async_computation.4 | async-start | bytes 11534336 | tf_op jit(solution)/shard_map/all_to_all | solution.py:1354
  911.3 32.8 %collective-permute-start.90 = (bf16[272,1664]{1,0:T(8,128)(2,1)S(1)}, bf16[272,1664]{1,0:T(8,128)(2,1)}, u32[]{:S(2)}, u32[]{:S(2)}) collective-permute-start(bf16[272,1664]{1,0:T(8,128)(2,1)S(1)} %fusion.17), channel_id=1, source_target_pairs={{0,8},{24,16},{1,9},{25,17},{2,10},{26,18},{3,11},{27,19},{4,12},{... | collective-permute-start | bytes 2715656 | tf_op jit(solution)/shard_map/ppermute | solution.py:1200
  945.8 21.9 %collective-permute-start.93 = (bf16[272,1664]{1,0:T(8,128)(2,1)S(1)}, bf16[272,1664]{1,0:T(8,128)(2,1)}, u32[]{:S(2)}, u32[]{:S(2)}) collective-permute-start(bf16[272,1664]{1,0:T(8,128)(2,1)S(1)} %add.294), channel_id=1, source_target_pairs={{8,16},{16,8},{9,17},{17,9},{10,18},{18,10},{11,19},{19,11},{12,20... | collective-permute-start | bytes 2715656 | tf_op jit(solution)/shard_map/ppermute | solution.py:1200
  (132 other events, 1769.7 us)
Sparse Core Ops, SparseCore 0:
  28.0 68.1 all-gather.4
  159.9 105.7 all-gather.6

commit v3 on v2

--- a/solution.py
+++ b/solution.py
@@ -273,11 +273,10 @@
     inv_ref,
     s_ref,
     dy_ref,
-    dx_out,
-    ddec_out,
-    conv_out,
-    small_out,
+    *refs,
 ):
+    more_ref = refs[0] if len(refs) == 5 else None
+    dx_out, ddec_out, conv_out, small_out = refs[-4:]
     slot = pl.program_id(0)
     n = TOK_DEV
     qk, vv = pair * DK, pair * DV
@@ -466,13 +465,15 @@
     mine = jnp.logical_and(lane >= first, lane < first + pair)
     d_pre = jnp.where(mine, -jnp.exp(alog_row) * jax.nn.sigmoid(pre) * d_log, 0.0)
     ddec_out[...] = d_dec + d_pre
+    if more_ref is not None:
+        dx_out[:, 2 * qk + 2 * vv :] = (more_ref[...] + (d_dec + d_pre)).astype(bf16)
 
     small_out[0:1, :] += gain_rows
     small_out[1:2, 0:128] += jnp.sum(jnp.where(mine, d_log * log_decay, 0.0), axis=0, keepdims=True)
     small_out[2:3, 0:128] += jnp.sum(d_pre, axis=0, keepdims=True)
 
 
-def mixer_backward(ids, proj, dec, conv, head_rows, gain_row, saved, d_gated, hl, pair, p):
+def mixer_backward(ids, proj, dec, conv, head_rows, gain_row, saved, d_gated, hl, pair, p, more=None):
     out, u, w, inv, states = saved
     tokens = proj.shape[0]
     slots = tokens // TOK_DEV
@@ -480,6 +481,7 @@
     vv = pair * DV
     spec = pl.BlockSpec
     n = TOK_DEV
+    width = 2 * qk + 2 * vv + (128 if more is not None else 0)
 
     def body(*refs):
         backward_kernel(hl, pair, p, *refs)
@@ -500,15 +502,16 @@
             spec((1, pair, n, n), lambda s: (s, 0, 0, 0)),
             spec((1, pair, n // BLOCK * DK, DV), lambda s: (s, 0, 0, 0)),
             spec((n, vv), lambda s: (s, 0)),
-        ],
+        ]
+        + ([spec((n, 128), lambda s: (s, 0))] if more is not None else []),
         out_specs=[
-            spec((n, 2 * qk + 2 * vv), lambda s: (s, 0)),
+            spec((n, width), lambda s: (s, 0)),
             spec((n, 128), lambda s: (s, 0)),
             spec((8, 2 * qk + vv), lambda s: (0, 0)),
             spec((8, DV), lambda s: (0, 0)),
         ],
         out_shape=[
-            jax.ShapeDtypeStruct((tokens, 2 * qk + 2 * vv), bf16),
+            jax.ShapeDtypeStruct((tokens, width), bf16),
             jax.ShapeDtypeStruct((tokens, 128), f32),
             jax.ShapeDtypeStruct((8, 2 * qk + vv), f32),
             jax.ShapeDtypeStruct((8, DV), f32),
@@ -516,7 +519,7 @@
         compiler_params=pltpu.CompilerParams(vmem_limit_bytes=56 * 1024 * 1024),
         cost_estimate=pl.CostEstimate(flops=1, bytes_accessed=1, transcendentals=0),
         name="mixer_backward",
-    )(ids, proj, dec, conv, head_rows, gain_row, out, u, w, inv, states, d_gated)
+    )(ids, proj, dec, conv, head_rows, gain_row, out, u, w, inv, states, d_gated, *([more] if more is not None else []))
 
 
 VMEM_LIMIT = 58 * 1024 * 1024
@@ -608,6 +611,148 @@
         cost_estimate=cost(0, 4 * rows * w.shape[1]),
         name="pack_relative",
     )(ids, w, *([extra] if more else []))
+
+
+def scatter_add(stay_x, got_x, stay_y, got_y):
+    rows, n = stay_x.shape
+    block = pl.BlockSpec((rows // 2, n), lambda i: (1, 0))
+    out = pl.BlockSpec((rows // 2, n), lambda i: (0, 0))
+
+    def body(a_ref, b_ref, c_ref, d_ref, x_ref, y_ref):
+        x_ref[...] = a_ref[...] + b_ref[...]
+        y_ref[...] = c_ref[...] + d_ref[...]
+
+    return pl.pallas_call(
+        body,
+        grid=(1,),
+        in_specs=[block] * 4,
+        out_specs=[out] * 2,
+        out_shape=[jax.ShapeDtypeStruct((rows // 2, n), bf16)] * 2,
+        compiler_params=params(),
+        cost_estimate=cost(0, 0),
+        name="scatter_add",
+    )(stay_x, got_x, stay_y, got_y)
+
+
+def parts_specs(parts):
+    rows = parts[2].shape[0]
+    return [pl.BlockSpec((rows, p.shape[1]), lambda i: (0, 0)) for p in parts]
+
+
+def sum_parts(refs):
+    halves = []
+    for h in range(2):
+        a, b, c = refs[3 * h : 3 * h + 3]
+        halves.append(a[...].astype(f32) + b[...].astype(f32) + c[...].astype(f32))
+    return jnp.concatenate(halves, axis=1)
+
+
+def live_rows(ids_ref, rows):
+    return lax.broadcasted_iota(jnp.int32, (rows, 1), 0) < ids_ref[3]
+
+
+def middle_rows(parts, tokens, gains, ids):
+    rows, d = tokens.shape
+
+    def body(ids_ref, t_ref, g_ref, *refs):
+        mid_ref, out_ref = refs[-2:]
+        branch = jnp.where(live_rows(ids_ref, rows), sum_parts(refs[:6]), 0.0)
+        mid = t_ref[...].astype(f32) + branch
+        mid_ref[...] = mid
+        r = lax.rsqrt(jnp.mean(mid * mid, axis=1, keepdims=True) + eps_norm)
+        out_ref[...] = (mid * r * g_ref[1:2, :]).astype(bf16)
+
+    whole = pl.BlockSpec((rows, d), lambda i: (0, 0))
+    return pl.pallas_call(
+        body,
+        grid=(1,),
+        in_specs=[SMEM, whole, pl.BlockSpec((8, d), lambda i: (0, 0))] + parts_specs(parts),
+        out_specs=[whole, whole],
+        out_shape=[jax.ShapeDtypeStruct((rows, d), f32), jax.ShapeDtypeStruct((rows, d), bf16)],
+        compiler_params=params(),
+        cost_estimate=cost(0, 0),
+        name="middle_rows",
+    )(ids, tokens, gains, *parts)
+
+
+def rms_parts(unit, r, gain, d_out):
+    d_unit = d_out * gain
+    d_rows = r * (d_unit - unit * jnp.mean(d_unit * unit, axis=1, keepdims=True))
+    return d_rows, jnp.sum(d_out * unit, axis=0, keepdims=True)
+
+
+def middle_back(parts, middle, cotangent, gains, ids):
+    rows, d = middle.shape
+
+    def body(ids_ref, m_ref, c_ref, g_ref, *refs):
+        d_ref, b_ref, s_ref = refs[-3:]
+        mid = m_ref[...]
+        r = lax.rsqrt(jnp.mean(mid * mid, axis=1, keepdims=True) + eps_norm)
+        d_rows, s_ref[...] = rms_parts(mid * r, r, g_ref[1:2, :], sum_parts(refs[:6]))
+        live = live_rows(ids_ref, rows)
+        total = jnp.where(live, c_ref[...].astype(f32), 0.0) + d_rows
+        d_ref[...] = total
+        b_ref[...] = jnp.where(live, total, 0.0).astype(bf16)
+
+    whole = pl.BlockSpec((rows, d), lambda i: (0, 0))
+    return pl.pallas_call(
+        body,
+        grid=(1,),
+        in_specs=[SMEM, whole, whole, pl.BlockSpec((8, d), lambda i: (0, 0))]
+        + parts_specs(parts),
+        out_specs=[whole, whole, pl.BlockSpec((1, d), lambda i: (0, 0))],
+        out_shape=[
+            jax.ShapeDtypeStruct((rows, d), f32),
+            jax.ShapeDtypeStruct((rows, d), bf16),
+            jax.ShapeDtypeStruct((1, d), f32),
+        ],
+        compiler_params=params(),
+        cost_estimate=cost(0, 0),
+        name="middle_back",
+    )(ids, middle, cotangent, gains, *parts)
+
+
+def tokens_back(parts, tokens, d_middle, gains):
+    rows, d = tokens.shape
+
+    def body(t_ref, m_ref, g_ref, *refs):
+        d_ref, s_ref = refs[-2:]
+        x = t_ref[...].astype(f32)
+        r = lax.rsqrt(jnp.mean(x * x, axis=1, keepdims=True) + eps_norm)
+        d_rows, s_ref[...] = rms_parts(x * r, r, g_ref[0:1, :], sum_parts(refs[:6]))
+        d_ref[...] = m_ref[...] + d_rows
+
+    whole = pl.BlockSpec((rows, d), lambda i: (0, 0))
+    return pl.pallas_call(
+        body,
+        grid=(1,),
+        in_specs=[whole, whole, pl.BlockSpec((8, d), lambda i: (0, 0))] + parts_specs(parts),
+        out_specs=[whole, pl.BlockSpec((1, d), lambda i: (0, 0))],
+        out_shape=[jax.ShapeDtypeStruct((rows, d), f32), jax.ShapeDtypeStruct((1, d), f32)],
+        compiler_params=params(),
+        cost_estimate=cost(0, 0),
+        name="tokens_back",
+    )(tokens, d_middle, gains, *parts)
+
+
+def stack_blocks(parts):
+    rows, n = parts[0].shape
+    tile = n // 2
+
+    def body(*refs):
+        for j in range(len(parts)):
+            refs[-1][0, j] = refs[j][...]
+
+    return pl.pallas_call(
+        body,
+        grid=(2,),
+        in_specs=[pl.BlockSpec((rows, tile), lambda i: (0, i))] * len(parts),
+        out_specs=pl.BlockSpec((1, len(parts), rows, tile), lambda i: (0, 0, 0, i)),
+        out_shape=jax.ShapeDtypeStruct((1, len(parts), rows, n), bf16),
+        compiler_params=params(),
+        cost_estimate=cost(0, 0),
+        name="stack_blocks",
+    )(*parts)
 
 
 def join_cores(mine, theirs, ids):
@@ -773,23 +918,60 @@
     )(ids, gain_in, gain_mid, *g_conv, *g_heads)
 
 
+def line_values(ids, chunk, got, pair, met, new):
+    rows, n = chunk.shape if chunk is not None else (new if new is not None else pair).shape
+    steps = 2
+    args = [a for a in (chunk, got, pair, met, new) if a is not None]
+    count = (pair is not None or new is not None) + (chunk is not None)
+
+    def body(ids_ref, *refs):
+        refs = list(refs)
+        outs = refs[len(args) :]
+        if chunk is not None:
+            outs[-1][...] = refs.pop(0)[...] + refs.pop(0)[...]
+        if pair is not None:
+            total = refs.pop(0)[...] + refs.pop(0)[...]
+            if new is not None:
+                middle = jnp.logical_or(ids_ref[2] == 1, ids_ref[2] == 2)
+                total = jnp.where(middle, total, refs.pop(0)[...])
+            outs[0][...] = total
+
+    block = pl.BlockSpec((rows // steps, n), lambda i: (i, 0))
+    return list(pl.pallas_call(
+        body,
+        grid=(steps,),
+        in_specs=[SMEM] + [block] * len(args),
+        out_specs=[block] * count,
+        out_shape=[jax.ShapeDtypeStruct((rows, n), bf16)] * count,
+        compiler_params=params(),
+        cost_estimate=cost(0, 0),
+        name="line_values",
+    )(ids, *args))
+
+
 def place_blocks(whole, pair_values, ids, c, shape):
     t, last = pair_values
-    rows, n = t.shape
+    rows, n = shape[1:]
     old = [] if whole is None else [whole]
+    tiles = n // 128
 
     def body(ids_ref, t_ref, last_ref, *refs):
+        out = refs[-1]
         middle = jnp.logical_or(ids_ref[2] == 1, ids_ref[2] == 2)
-        refs[-1][0] = jnp.where(middle, t_ref[...], last_ref[...])
-
-    half = n // 2
+        for k in range(tiles):
+            band = slice(16 * k, 16 * k + 16)
+            value = jnp.where(middle, t_ref[band, :], last_ref[band, :])
+            for s in range(rows // 16):
+                out[0, 16 * s : 16 * s + 16, 128 * k : 128 * k + 128] = value[
+                    :, 128 * s : 128 * s + 128
+                ]
+
+    vmem = pl.BlockSpec(t.shape, lambda i: (0, 0))
     return pl.pallas_call(
         body,
-        grid=(2,),
-        in_specs=[SMEM]
-        + [pl.BlockSpec((rows, half), lambda i: (0, i))] * 2
-        + [ANY] * len(old),
-        out_specs=pl.BlockSpec((1, rows, half), lambda i: (c, 0, i)),
+        grid=(1,),
+        in_specs=[SMEM, vmem, vmem] + [ANY] * len(old),
+        out_specs=pl.BlockSpec((1, rows, n), lambda i: (c, 0, 0)),
         out_shape=jax.ShapeDtypeStruct(shape, bf16),
         input_output_aliases={3: 0} if old else {},
         compiler_params=params(),
@@ -798,44 +980,40 @@
     )(ids, t, last, *old)
 
 
-def finish_projection(whole, pair_values, ids, chunk, p, groups, shape, widths):
+def finish_projection(whole, pair_values, ids, bands, shape):
     t, last = pair_values
     rows = shape[0]
-    unit = 256
-    starts = []
-    for c in chunk:
-        base = 0
-        for width in widths:
-            size = width // (4 * groups)
-            starts.append([base + (c * groups + p) * size + s for s in range(0, size, unit)])
-            base += width
-    starts = sum(starts, [])
-    each = len(starts) // len(chunk)
     old = [] if whole is None else [whole]
-
-    def body(ids_ref, t_ref, last_ref, *refs):
+    table = jnp.array([b for b, _ in bands] + [c // 2 for _, c in bands], jnp.int32)
+    count = len(bands)
+
+    def body(table_ref, ids_ref, t_ref, last_ref, *refs):
         middle = jnp.logical_or(ids_ref[2] == 1, ids_ref[2] == 2)
-        refs[-1][...] = jnp.where(middle, t_ref[...], last_ref[...]).astype(f32)
-
-    def column(i):
-        at = starts[-1] // unit
-        for n in reversed(range(len(starts) - 1)):
-            at = jnp.where(i == n, starts[n] // unit, at)
-        return (0, at)
+        at = pl.multiple_of(16 * table_ref[pl.program_id(0)], 16)
+        value = jnp.where(middle, t_ref[pl.ds(at, 32), :], last_ref[pl.ds(at, 32), :])
+        for k in range(2):
+            for s in range(rows // 16):
+                refs[-1][16 * s : 16 * s + 16, 128 * k : 128 * k + 128] = value[
+                    16 * k : 16 * k + 16, 128 * s : 128 * s + 128
+                ].astype(f32)
+
+    def whole_chunk(i, table_ref):
+        return (0, 0)
 
     return pl.pallas_call(
         body,
-        grid=(len(starts),),
-        in_specs=[SMEM]
-        + [pl.BlockSpec((rows, unit), lambda i: (lax.div(i, each), lax.rem(i, each)))] * 2
-        + [ANY] * len(old),
-        out_specs=pl.BlockSpec((rows, unit), column),
+        grid_spec=pltpu.PrefetchScalarGridSpec(
+            num_scalar_prefetch=1,
+            grid=(count,),
+            in_specs=[SMEM] + [pl.BlockSpec(t.shape, whole_chunk)] * 2 + [ANY] * len(old),
+            out_specs=pl.BlockSpec((rows, 256), lambda i, table_ref: (0, table_ref[count + i])),
+        ),
         out_shape=jax.ShapeDtypeStruct(shape, f32),
-        input_output_aliases={3: 0} if old else {},
+        input_output_aliases={4: 0} if old else {},
         compiler_params=params(),
-        cost_estimate=cost(0, 8 * rows * unit * len(starts)),
+        cost_estimate=cost(0, 8 * rows * 256 * count),
         name="finish_projection",
-    )(ids, t, last, *old)
+    )(table, ids, t, last, *old)
 
 
 def finish_feed_forward(blocks):
@@ -1108,15 +1286,37 @@
     )(ids, *args)
 
 
-def column_terms(lefts, rights, ids):
+STREAM = 2048
+
+
+def pack_bands(value, out, rows, tiles):
+    for t in range(tiles):
+        for s in range(rows // 16):
+            out[16 * t : 16 * t + 16, 128 * s : 128 * s + 128] = value[
+                16 * s : 16 * s + 16, 128 * t : 128 * t + 128
+            ]
+
+
+def column_terms(lefts, rights, ids, split):
     tokens, k = lefts[0].shape
     n = rights[0].shape[1]
     chips = 4
     rows = k // (2 * chips)
-
-    def body(ids_ref, a_ref, b_ref, ra_ref, rb_ref, o_ref):
+    tiles = n // 128
+
+    def body(ids_ref, a_ref, b_ref, ra_ref, rb_ref, *refs):
+        total_ref = refs[-1]
         total = mm_tn(a_ref[...], ra_ref[...]) + mm_tn(b_ref[...], rb_ref[...])
-        o_ref[0] = total.astype(bf16)
+        if not split:
+            total_ref[...] = total.astype(bf16)
+            pack_bands(total_ref, refs[0].at[0], rows, tiles)
+            return
+        total_ref[...] = total.astype(bf16)
+        for c in range(chips):
+
+            @pl.when(pl.program_id(0) == c)
+            def _():
+                pack_bands(total_ref, refs[c], rows, tiles)
 
     def column(i, ids_ref):
         return (0, 2 * i + ids_ref[1])
@@ -1124,6 +1324,12 @@
     def whole(i, ids_ref):
         return (0, 0)
 
+    if split:
+        out_specs = [pl.BlockSpec((16 * tiles, STREAM), whole)] * chips
+        out_shape = [jax.ShapeDtypeStruct((16 * tiles, STREAM), bf16)] * chips
+    else:
+        out_specs = pl.BlockSpec((1, 16 * tiles, STREAM), lambda i, ids_ref: (i, 0, 0))
+        out_shape = jax.ShapeDtypeStruct((chips, 16 * tiles, STREAM), bf16)
     return pl.pallas_call(
         body,
         grid_spec=pltpu.PrefetchScalarGridSpec(
@@ -1131,16 +1337,17 @@
             grid=(chips,),
             in_specs=[pl.BlockSpec((tokens, rows), column)] * 2
             + [pl.BlockSpec((tokens, n), whole)] * 2,
-            out_specs=pl.BlockSpec((1, rows, n), lambda i, ids_ref: (i, 0, 0)),
+            out_specs=out_specs,
+            scratch_shapes=[pltpu.VMEM((rows, n), bf16)],
         ),
-        out_shape=jax.ShapeDtypeStruct((chips, rows, n), bf16),
+        out_shape=out_shape,
         compiler_params=params(),
         cost_estimate=cost(2 * tokens * k * n, 4 * (tokens * k + tokens * n + k * n)),
         name="column_terms",
     )(ids, *lefts, *rights)
 
 
-def row_terms(lefts, right, ids):
+def row_terms(lefts, right, ids, in_order=False):
     tokens, n = right.shape
     k = sum(a.shape[1] for a in lefts)
     tile = 512
@@ -1153,7 +1360,17 @@
         at = 0
         for ref in left_refs:
             width = ref.shape[1]
-            acc[at : at + width, :] = mm_tn(ref[...], right_ref[...])
+            if not in_order:
+                acc[at : at + width, :] = mm_tn(ref[...], right_ref[...])
+            else:
+                total = None
+                size = tokens // 4
+                for m in range(4):
+                    chip = jnp.bitwise_xor(ids_ref[0], m)
+                    rows = right_ref[pl.ds(pl.multiple_of(chip * size, size), size), :]
+                    term = mm_tn(ref[m * size : (m + 1) * size, :], rows)
+                    total = term if total is None else total + term
+                acc[at : at + width, :] = total
             at += width
         mine_ref[...] = acc[pl.ds(pl.multiple_of(core * half, 16), half), :].astype(bf16)
         theirs_ref[...] = acc[pl.ds(pl.multiple_of((1 - core) * half, 16), half), :].astype(bf16)
@@ -1226,54 +1443,59 @@
         upper = (me & bit) != 0
         keep = jnp.where(upper, a[half:], a[:half])
         send = jnp.where(upper, a[:half], a[half:])
-        a = keep + lax.ppermute(send, "fsdp", [(i, i ^ bit) for i in range(nf)])
+        got = lax.ppermute(send, "fsdp", [(i, i ^ bit) for i in range(nf)])
+        a = keep + got
         bit //= 2
-    return a[0]
+    return a[0], got
+
+
+def sum_line(a):
+    z = lax.axis_index("rep")
+    a = a + along(a, INWARD)
+    a = a + along(a, MIDDLE)
+    return jnp.where(jnp.logical_or(z == 1, z == 2), a, along(a, OUTWARD))
 
 
 class Line:
-    def __init__(self, nz):
+    def __init__(self, nz, ids):
         self.nz = nz
+        self.ids = ids
         self.tokens = ()
         self.first = None
         self.second = None
-        z = lax.axis_index("rep")
-        self.middle = jnp.logical_or(z == 1, z == 2)
 
     def step(self, new, *earlier):
         if self.nz != 4:
             return new and (new[0], (lax.psum(new[1], "rep"),) * 2)
         chunk = None if new is None else new[1]
-        first = None if self.first is None else self.first[1:]
-        second = None if self.second is None else self.second[1:]
+        first = (None, None) if self.first is None else self.first[1:]
+        second = (None, None) if self.second is None else self.second[1:]
         chunk, first, second, _, _ = lax.optimization_barrier(
             (chunk, first, second, self.tokens, earlier)
         )
-        outward = None if second is None else second[0] + second[1]
-        across = None if first is None else first[0] + first[1]
         finished = next_first = next_second = None
         tokens = []
-        if chunk is not None and outward is not None and outward.shape != chunk.shape:
-            got = along(chunk, INWARD)
-            last = along(outward, OUTWARD)
-            tokens += [got, last]
-            finished = (self.second[0], (outward, last))
-            next_first = (new[0], chunk, got)
-        elif chunk is not None or outward is not None:
-            send = chunk if outward is None else outward
-            if chunk is not None and outward is not None:
-                send = jnp.where(self.middle, outward, chunk)
-            got = along(send, SWAP)
+        values = []
+        if self.first is not None or self.second is not None:
+            if chunk is not None and self.second is None:
+                values = [chunk] + line_values(self.ids, *first, None, None, None)
+            else:
+                values = line_values(self.ids, *first, *second, chunk)
+        elif chunk is not None:
+            values = [chunk]
+        if chunk is not None or self.second is not None:
+            got = along(values[0], OUTWARD if chunk is None else SWAP)
             tokens.append(got)
-            if outward is not None:
-                finished = (self.second[0], (send, got))
+            if self.second is not None:
+                finished = (self.second[0], (values[0], got))
             if chunk is not None:
                 next_first = (new[0], chunk, got)
-        if across is not None:
-            met = along(across, MIDDLE)
+        if self.first is not None:
+            met = along(values[-1], MIDDLE)
             tokens.append(met)
-            next_second = (self.first[0], across, met)
+            next_second = (self.first[0], values[-1], met)
         self.first, self.second, self.tokens = next_first, next_second, tuple(tokens)
+        self.sent = tuple(values)
         return finished
 
 
@@ -1440,14 +1662,13 @@
 
 def scatter_middle(parts, nf, *earlier):
     stay_x, got_x, stay_y, got_y = after(parts, *earlier)
-    size = stay_x.shape[0] // 2
-    over_y = to_chip(stay_x[size:] + got_x[size:], nf, 2)
-    over_x = to_chip(stay_y[size:] + got_y[size:], nf, 1)
-    return [stay_x[:size], got_x[:size], over_y, stay_y[:size], got_y[:size], over_x]
+    over_y, over_x = scatter_add(stay_x, got_x, stay_y, got_y)
+    return [stay_x, got_x, to_chip(over_y, nf, 2), stay_y, got_y, to_chip(over_x, nf, 1)]
 
 
 def scatter_end(parts):
-    parts = [p.astype(f32) for p in parts]
+    size = parts[2].shape[0]
+    parts = [p[:size].astype(f32) for p in parts]
     return jnp.concatenate([sum(parts[:3]), sum(parts[3:])], axis=1)
 
 
@@ -1477,7 +1698,8 @@
     groups = hl // pair
     me = lax.axis_index("fsdp")
     rep = lax.axis_index("rep")
-    ids = jnp.stack([me // 2, me % 2, rep, me]).astype(jnp.int32)
+    held = jnp.sum(jnp.where(slot_owner == rep * nf + me, lengths, 0))
+    ids = jnp.stack([me // 2, me % 2, rep, held]).astype(jnp.int32)
     shard = gain_in.shape[0]
     conv_shard = conv_weight.shape[1]
     hv = w_out.shape[0] * nf
@@ -1524,25 +1746,29 @@
 
     out_other = swap_core(w_out, nf)
     down_other = swap_core(w_down, nf)
-    first = jnp.stack(after(spread(plane_rows), packed))
-    tok = gather_first(tokens, nf, small, first)
+    first_rows = spread(plane_rows)
+    first = jnp.stack(after(first_rows, packed))
+    tok = gather_first(tokens, nf, small, first_rows, out_other, down_other)
+    sends = after(packed[1:], first_rows, out_other, down_other)
+    own = [packed[0], to_chip(sends[0], nf, 1), to_chip(sends[1], nf, 2)]
     first = lax.all_gather(first, "rep", axis=0)
     gains, head_rows, gain_row, *conv_pair = unpack_small(small, sizes, ids, hk, qk, vv, groups)
-    tok = gather_pieces(tok, nf, gains, out_other, down_other)
-    own = spread(packed, tok)
-
-    held = jnp.sum(jnp.where(slot_owner == rep * nf + me, lengths, 0))
+    tok = gather_pieces(tok, nf, gains)
+    own.append(to_chip(after(sends[2], tok[3:]), nf, 3))
+    up_plane = pack_columns(after(w_gate_up, packed), None, up_table, plane, True, ids)
+    up_plane = exchange(after(up_plane, tok[3:]), nf)
+
     live_own = (jnp.arange(TOK_DEV, dtype=jnp.int32) < held).astype(f32)[:, None]
-    tokens32 = tokens.astype(f32)
     seeded = cotangent.astype(f32) * live_own
     d_ffn_own = seeded.astype(bf16)
-    up_plane = pack_columns(after(w_gate_up, packed), None, up_table, plane, True, ids)
-
-    normed_in = norm_rows(after(tok, up_plane, d_ffn_own), gains)
-    first_other = swap_core(after(first, tok), nf)
+
+    normed_in = norm_rows(after(tok, d_ffn_own), gains)
+    first_other = swap_core(after(first, tok, own[1], own[2]), nf)
     projected = [project_planes(normed_in, first, first_other, ids)]
-    up_plane = exchange(after(up_plane, own, projected[0]), nf)
-    ffn_parts = gather_first(d_ffn_own, nf, own, projected[0])
+    own = stack_blocks(after(own, projected[0]))
+    other = swap_core(own, nf)
+    ffn_parts = gather_first(d_ffn_own, nf, own)
+    up_own = lax.all_gather(after(up_plane, own), "rep", axis=0)
 
     def forward(p, *before):
         return mixer_forward(
@@ -1551,37 +1777,29 @@
         )
 
     gated0, *saved0 = forward(0, own)
-    other = swap_all(own, projected[0])
-    up_own = lax.all_gather(after(up_plane, gated0), "rep", axis=0)
-    projected.append(project(after(normed_in, gated0), own, other, ids))
-    ffn_parts = gather_pieces(ffn_parts, nf, projected[1])
-    gated1, *saved1 = forward(1, ffn_parts[:3])
+    projected.append(project_planes(after(normed_in, gated0, ffn_parts), own, other, ids))
+    ffn_parts = gather_pieces(ffn_parts, nf, gated0)
+    gated1, *saved1 = forward(1)
     gated = [gated0, gated1]
     saved = [saved0, saved1]
     branch_parts = scatter_start(
         times_rows(after(gated, ffn_parts), w_out, out_other, ids), nf
     )
     d_ffn = jnp.concatenate(after(ffn_parts, branch_parts[0]), axis=0)
-    pieces_in = [
-        (first, first_other),
-        (jnp.stack(after(own, branch_parts[0]))[None], jnp.stack(after(other, branch_parts[0]))[None]),
-    ]
+    pieces_in = [(first, first_other), (own, other)]
     down_chip = join_cores(w_down, after(down_other, branch_parts[0]), ids)
     out_chip = join_cores(w_out, after(out_other, branch_parts[0]), ids)
-    branch_parts = scatter_middle(branch_parts, nf, d_ffn, pieces_in[1], down_chip)
-    branch = scatter_end(branch_parts)
+    branch_parts = scatter_middle(branch_parts, nf, d_ffn, down_chip, out_chip)
     up_own = after(up_own, branch_parts)
     up_other = swap_core(up_own, nf)
     in_other = swap_core(after(normed_in, up_other), nf)
 
-    middle = tokens32 + live_own * branch
-    r_mid = scale_of(middle)
-    normed_own = (middle * r_mid * gains[1]).astype(bf16)
+    middle, normed_own = middle_rows(branch_parts, tokens, gains, ids)
     normed_mid = gather_first(normed_own, nf)
     normed_mid = jnp.concatenate(gather_pieces(normed_mid, nf), axis=0)
     hidden, d_gate_up = feed_forward(normed_mid, up_own, up_other, down_chip, d_ffn, ids)
 
-    line = Line(nz)
+    line = Line(nz, ids)
     done = {}
 
     def step(new, *earlier):
@@ -1602,100 +1820,90 @@
         [(after(d_gate_up, down0, down1, d_up_other), up_own, up_other)], ids, False
     )
     mid_parts = scatter_start(partial_mid, nf)
-    partial_ffn = times_rows(after([hidden], partial_mid, z), w_down, down_other, ids)
-    step(("down1", down1), partial_mid)
+    partial_ffn = times_rows(after([hidden], partial_mid), w_down, down_other, ids)
+    step(("down1", down1), partial_ffn, mid_parts[1], mid_parts[3])
     mid_first = mid_parts
-    mid_parts = scatter_middle(mid_parts, nf, partial_ffn)
     grad_up = column_terms(
         [normed_mid, mid_other],
-        [after(d_gate_up, partial_ffn, mid_first[1], mid_first[3]), d_up_other],
+        [after(d_gate_up, line.sent, mid_first[1], mid_first[3]), d_up_other],
         ids,
+        True,
+    )
+    mid_parts = scatter_middle(mid_parts, nf)
+    z = line.tokens
+    step(("up0", grad_up[0]))
+    d_middle, d_branch_own, g_gain_mid = middle_back(
+        after(mid_parts, line.sent), middle, cotangent, gains, ids
     )
     z = line.tokens
-    step(("up0", grad_up[0]))
-    d_normed_mid = scatter_end(after(mid_parts, grad_up, z))
-    z = line.tokens
-    d_mid, g_gain_mid = rms_back(middle, r_mid, gains[1], d_normed_mid)
-    d_middle = seeded + d_mid
-    d_branch_own = (live_own * d_middle).astype(bf16)
     branch_parts = gather_first(d_branch_own, nf)
-    ffn_first = scatter_start(partial_ffn, nf, mid_parts, grad_up)
-    d_branch = gather_pieces(branch_parts, nf, z, ffn_first)
+    d_branch = gather_pieces(branch_parts, nf, z)
     step(("up1", grad_up[1]))
     z = line.tokens
-    ffn_sends = scatter_middle(ffn_first, nf, d_branch)
     d_branch = jnp.concatenate(d_branch, axis=0)
     d_gated = [mm_nt(d_branch, out_chip[p * vv : (p + 1) * vv]) for p in range(groups)]
 
-    def backward(p, *before):
+    def backward(p, *before, more=None):
         return mixer_backward(
             ids, projected[p], projected[0], conv_pair[p], head_rows, gain_row, saved[p],
-            after(d_gated[p], *before), hl, pair, p,
+            after(d_gated[p], *before), hl, pair, p, more,
         )
 
-    step(("up2", grad_up[2]))
-    d_x1, d_dec, g_conv1, g_heads1 = backward(1, d_gated, z, ffn_sends)
-    z = line.tokens
-    d_x1_other = swap_core(after(d_x1, line.tokens), nf)
-    step(("up3", grad_up[3]), d_x1)
-    mine, theirs = row_terms(gated, after(d_branch, d_x1, z), ids)
+    mine, theirs = row_terms(gated, after(d_branch, d_gated), ids)
     half = mine.shape[0] // 2
     theirs = [swap_core(theirs[:half], nf), swap_core(theirs[half:], nf)]
-    cols1 = column_terms([normed_in, in_other], [after(d_x1, mine), d_x1_other], ids)
+    step(("up2", grad_up[2]), mine)
+    ffn_first = scatter_start(partial_ffn, nf, line.sent)
+    d_x1, d_dec, g_conv1, g_heads1 = backward(1, line.sent)
+    d_x1_other = swap_core(after(d_x1, line.tokens, ffn_first, theirs), nf)
+    grad_out = mine + jnp.concatenate(theirs, axis=0)
+    step(("up3", grad_up[3]), d_x1)
+    ffn_sends = scatter_middle(ffn_first, nf, line.sent)
+    cols1 = column_terms([normed_in, in_other], [after(d_x1, line.sent, ffn_sends[2], ffn_sends[5]), d_x1_other], ids, False)
+    cols1_all = exchange(cols1, nf)
+    size = down0.shape[0]
+    rest = grad_out.shape[0] - size
+    step(("out0", grad_out[:size]), cols1)
+    d_x0, dec, g_conv0, g_heads0 = backward(0, line.sent, more=d_dec)
     z = line.tokens
-    grad_out = [after(mine, cols1)[:half] + theirs[0], mine[half:] + theirs[1]]
-    cols1_all = exchange(after(cols1, z), nf)
-    step(("out0", grad_out[0]), cols1)
-    d_x0, dec, g_conv0, g_heads0 = backward(0, cols1, z, grad_out)
+    d_x0_other = swap_core(after(d_x0, z, cols1_all), nf)
+    bands1 = cols1_all.reshape(-1, STREAM)
+    at1 = size - rest
+    step(("mix0", jnp.concatenate([grad_out[size:], bands1[:at1]], axis=0)), d_x0)
+    cols0 = column_terms([normed_in, in_other], [after(d_x0, line.sent), d_x0_other], ids, False)
     z = line.tokens
-    d_x0 = jnp.concatenate([after(d_x0, z, cols1_all), (d_dec + dec).astype(bf16)], axis=1)
-    d_x0_other = swap_core(d_x0, nf)
-    step(("out1", grad_out[1]), d_x0)
-    z = line.tokens
-    cols0 = column_terms([normed_in, in_other], [d_x0, d_x0_other], ids)
-    queue = [(1, (0, 1)), (1, (2, 3))] + [(0, (c,)) for c in range(chips)]
-    grad_cols = [exchange(after(cols0, z), nf), cols1_all]
-
-    def chunk_of(key):
-        p, chunk = key
-        block = grad_cols[p][chunk[0] : chunk[-1] + 1]
-        return (key, block.reshape(len(chunk) * shard, block.shape[2]))
-
-    grad_proj = None
-
-    def place(grad_proj, key, *before):
-        return finish_projection(
-            grad_proj, after(done[key], *before), ids, key[1], key[0], groups, w_proj.shape,
-            proj_widths,
+    step(("p1", bands1[at1 : at1 + size]), cols0)
+    bands0_all = exchange(cols0, nf)
+    bands0 = bands0_all.reshape(-1, STREAM)
+    right = [d_x0, d_x1]
+    partial_in = times_transposed(
+        [(after(right[p], line.sent),) + pieces_in[p] for p in range(groups)], ids, True
+    )
+    at1 += size
+    left = bands1.shape[0] - at1
+    at0 = size - left
+    step(("mix1", jnp.concatenate([bands1[at1:], bands0[:at0]], axis=0)), partial_in)
+    in_first = scatter_start(partial_in, nf, line.sent)
+    grad_up = None
+    for j in range(2):
+        grad_up = place_blocks(
+            grad_up, after(done["up%d" % j], line.sent), ids, j, (chips, shard, 2 * wide)
         )
-
-    right = [d_x0, d_x1]
-    step(chunk_of(queue[0]), cols0)
-    partial_in = times_transposed(
-        [(after(right[p], cols0, z),) + pieces_in[p] for p in range(groups)], ids, True
-    )
-    in_first = scatter_start(partial_in, nf)
-    g_conv = [g_conv0, g_conv1]
-    g_heads = [g_heads0, g_heads1]
-    z = line.tokens
-    step(chunk_of(queue[1]), partial_in, grad_cols[0])
-    grad_up = None
-    for j in range(chips):
+    step(("p0", bands0[at0 : at0 + size]), grad_up)
+    for j in range(2, chips):
         grad_up = place_blocks(
-            grad_up, after(done["up%d" % j], z), ids, j, (chips, shard, 2 * wide)
+            grad_up, after(done["up%d" % j], line.sent), ids, j, (chips, shard, 2 * wide)
         )
     in_sends = scatter_middle(in_first, nf, grad_up)
-    output = (middle + live_own * scatter_end(after(ffn_sends, z))).astype(bf16)
-    z = line.tokens
-    step(chunk_of(queue[2]))
-    d_normed_in = scatter_end(after(in_sends, z))
-    d_rows, g_gain_in = rms_back(tokens32, scale_of(tokens32), gains[0], d_normed_in)
-    grad_tokens = d_middle + d_rows
+    output = (middle + live_own * scatter_end(after(ffn_sends, line.sent))).astype(bf16)
+    grad_up_all = exchange(after(grad_up, in_sends[2], in_sends[5]), nf)
+    step(("p0last", bands0[at0 + size :]))
+    grad_tokens, g_gain_in = tokens_back(after(in_sends, line.sent), tokens, d_middle, gains)
     blocks = pack_small_grads(
-        g_conv,
-        g_heads,
-        g_gain_in.reshape(1, -1),
-        g_gain_mid.reshape(1, -1),
+        [g_conv0, g_conv1],
+        [g_heads0, g_heads1],
+        g_gain_in,
+        g_gain_mid,
         sizes,
         ids,
         nf,
@@ -1704,46 +1912,67 @@
         qk,
         vv,
     )
-    small_sum = sum_small(blocks, nf)
-    grad_up_all = exchange(after(grad_up, small_sum), nf)
-    z = line.tokens
-    step(chunk_of(queue[3]), grad_tokens)
-    grad_proj = place(grad_proj, queue[0], z)
-    z = line.tokens
-    step(chunk_of(queue[4]), grad_proj)
-    grad_proj = place(grad_proj, queue[1], z)
-    z = line.tokens
-    key, chunk = chunk_of(queue[5])
-    small_sum = jnp.pad(
-        small_sum.astype(bf16), ((0, 16 - small_sum.shape[0]), (0, chunk.shape[1] - small_sum.shape[1]))
-    )
-    step((key, jnp.concatenate([chunk, small_sum], axis=0)), grad_proj)
-    grad_proj = place(grad_proj, queue[2], z)
-    z = line.tokens
+    def tile_of(p, c, t):
+        at = c * groups + p
+        q_tiles, v_tiles = qk // 128, vv // 128
+        if t < q_tiles:
+            return at * q_tiles + t
+        if t < 2 * q_tiles:
+            return hk // 128 + at * q_tiles + t - q_tiles
+        if t < 2 * q_tiles + v_tiles:
+            return 2 * hk // 128 + at * v_tiles + t - 2 * q_tiles
+        return (2 * hk + hv) // 128 + at * v_tiles + t - 2 * q_tiles - v_tiles
+
+    each = span // 128
+    bands = [(1, c, t) for c in range(chips) for t in range(each)]
+    bands += [(0, c, t) for c in range(chips) for t in range(each + 1)]
+    slots = [("mix0", n) for n in range(rest // 16, size // 16)]
+    slots += [("p1", n) for n in range(size // 16)]
+    slots += [("mix1", n) for n in range(size // 16)]
+    slots += [("p0", n) for n in range(size // 16)]
+    slots += [("p0last", n) for n in range(size // 16)]
+    where = dict(zip(bands, slots))
+
+    def place(grad_proj, name, *before):
+        pairs = [
+            (where[key][1], tile_of(*key))
+            for key in bands
+            if where[key][0] == name and key[2] < each and key[2] % 2 == 0
+        ]
+        return finish_projection(grad_proj, after(done[name], *before), ids, pairs, w_proj.shape)
+
+    step(None, grad_tokens)
+    grad_proj = place(None, "mix0", line.sent)
+    grad_proj = place(grad_proj, "p1", line.sent)
+    grad_proj = place(grad_proj, "mix1")
+    small_sum = lax.all_to_all(after(blocks, grad_proj, grad_up_all), "fsdp", 0, 0, tiled=True)
     step(None, grad_proj)
-    grad_proj = place(grad_proj, queue[3], z)
-    z = line.tokens
-    step(None, grad_proj)
-    grad_up = finish_feed_forward(after(grad_up_all, z))
-    for key in queue[4:]:
-        grad_proj = place(grad_proj, key)
-    summed = [v[shard : shard + 8] for v in done[queue[5]]]
+    grad_up = finish_feed_forward(after(grad_up_all, line.sent))
+    grad_proj = place(grad_proj, "p0", grad_up)
+    small_sum = lax.all_gather(jnp.sum(after(small_sum, grad_proj), axis=0), "rep", axis=0)
+    small_sum = jnp.sum(small_sum, axis=0)
+    done["p0last"] = after(done["p0last"], grad_proj)
+    grad_proj = place(grad_proj, "p0last")
     middle_two = jnp.logical_or(rep == 1, rep == 2)
 
     def pick(name):
         return jnp.where(middle_two, *done[name])
 
-    summed = jnp.where(middle_two, *summed).astype(f32)
+    tail = pick("p0last")
+    summed = small_sum
     lanes, _ = small_layout(sizes)
     s_gain_in, s_gain_mid, s_ogain, s_alog, s_bias = (
-        summed[KCONV, lane : lane + size] for lane, size in zip(lanes, sizes)
+        summed[KCONV, lane : lane + width] for lane, width in zip(lanes, sizes)
     )
-    grad_decay = sum(
-        jnp.where(middle_two, *(v[:shard, span : span + 2 * H] for v in done[(0, (c,))])).astype(f32)
-        for c in range(chips)
-    )
+    grad_decay = 0.0
+    for c in range(chips):
+        name, n = where[(0, c, each)]
+        band = tail if name == "p0last" else pick(name)
+        band = band[16 * n : 16 * n + 16].astype(f32).reshape(16, shard // 16, 128)
+        grad_decay = grad_decay + band.transpose(1, 0, 2).reshape(shard, 128)
+    grad_decay = grad_decay[:, : 2 * H]
     grad_down = jnp.concatenate([pick("down0"), pick("down1")], axis=0).astype(f32)
-    grad_out = jnp.concatenate([pick("out0"), pick("out1")], axis=0).astype(f32)
+    grad_out = jnp.concatenate([pick("out0"), pick("mix0")[:rest]], axis=0).astype(f32)
     return (
         output,
         grad_tokens,
@@ -1900,7 +2129,7 @@
         [d_hidden * up * (sig * (1.0 + gate * (1.0 - sig))), d_hidden * act], axis=1
     ).astype(bf16)
 
-    line = Line(nz)
+    line = Line(nz, ids)
     done = {}
 
     def step(new, *earlier):
@@ -1993,7 +2222,7 @@
         part = part.reshape(nf, -1)
         flat.append(jnp.pad(part, ((0, 0), (0, -part.shape[1] % 128))))
     flat = jnp.concatenate(flat, axis=1)
-    summed = lax.psum(sum_small(flat.reshape(nf, -1, 128), nf), "rep").reshape(-1)
+    summed = lax.psum(sum_small(flat.reshape(nf, -1, 128), nf)[0], "rep").reshape(-1)
     grads = []
     at = 0
     for p in pieces:

time: 1020 us -> 956 us (0.937)
  other arithmetic: 125 us -> 33.4 us
  Pallas kernels: 368 us -> 453 us
  starting transfers between devices: 167 us -> 120 us
  waiting for transfers between devices: 267 us -> 235 us
  blocking collectives: 8.12 us -> 24.3 us
    add x39 -> x2, other arithmetic: 73.5 us -> 4.02 us  [the longest x1 3.12 us: local_fast(): grad_out = mine + jnp.concatenate(theirs, axis=0)]
    pallas_call x11 -> x30, Pallas kernels: 58.8 us -> 127 us  [the longest x13 53.5 us: line_values(): pl.pallas_call(body, grid=(steps,), in_specs=[SMEM] + [block] * len(args)...]
    ppermute x38, waiting for transfers between devices: 114 us -> 178 us  [to_chip(): return lax.ppermute(a, 'fsdp', [(i, i ^ 2 * j) for i in range(nf)])]
    ppermute x39 -> x26, waiting for transfers between devices: 114 us -> 50.7 us  [along(): return lax.ppermute(a, 'rep', pairs)]
    ppermute x39 -> x26, starting transfers between devices: 101 us -> 54.7 us  [along(): return lax.ppermute(a, 'rep', pairs)]
    all_gather x0 -> x1, blocking collectives: none -> 16.2 us  [local_fast(): lax.all_gather(jnp.sum(after(small_sum, grad_proj), axis=0), 'rep', axis=0)]
    all_gather x1, waiting for transfers between devices: 16.3 us -> 1.16 us  [local_fast(): first = lax.all_gather(first, 'rep', axis=0)]
    unnamed x200 -> x138, local copies, waits for them, and re-layouts: 21.9 us -> 36.8 us
  transfers between devices with their start and end apart: 102 -> 84, of which waited for: 40 -> 34; matrix products, arithmetic and copies ran while one was open for 16% -> 7% of each run, Pallas kernels for 36% -> 46%
where the time goes in v3:
time: 956 us; the launch traced here: 949 us
  Pallas kernels  453 us (47%)
  waiting for transfers between devices  235 us (25%)
  starting transfers between devices  120 us (13%)
  local copies, waits for them, and re-layouts  56.4 us (6%)
  other arithmetic  33.4 us (3%)
  blocking collectives  24.3 us (3%)
  between operations  15.4 us (2%)
  matrix products  10.5 us (1%)
    ppermute x38, waiting for transfers between devices, to_chip(): return lax.ppermute(a, 'fsdp', [(i, i ^ 2 * j) for i in range(nf)])  178 us
    ppermute x26, starting transfers between devices, along(): return lax.ppermute(a, 'rep', pairs)  54.7 us
    pallas_call x13, Pallas kernels, line_values(): pl.pallas_call(body, grid=(steps,), in_specs=[SMEM] + [block] * len(args)...  53.5 us
    pallas_call x2, Pallas kernels, mixer_backward(): pl.pallas_call(body, grid=(slots,), in_specs=[pl.BlockSpec(memory_space=p...  52.4 us
    ppermute x26, waiting for transfers between devices, along(): return lax.ppermute(a, 'rep', pairs)  50.7 us
    pallas_call x3, Pallas kernels, column_terms(): pl.pallas_call(body, grid_spec=pltpu.PrefetchScalarGridSpec(num_scalar_pr...  48.7 us
    pallas_call x2, Pallas kernels, times_transposed(): pl.pallas_call(body, grid_spec=pltpu.PrefetchScalarGridSpec(num_scalar_pr...  43.7 us
    ppermute x38, starting transfers between devices, to_chip(): return lax.ppermute(a, 'fsdp', [(i, i ^ 2 * j) for i in range(nf)])  42.4 us
  transfers between devices with their start and end apart: 84, of which 34 were waited for; matrix products, arithmetic and copies ran while one was open for 7% of the time, Pallas kernels for 46%

profile of v3, /device:TPU:0, one launch (start us, length us, event | category | flops | bytes accessed | tf_op | source)
XLA Modules:
  0.0 948.7 jit_solution(626144597610102911)
XLA Ops:
  18.8 5.8 pack_relative.3
  24.6 4.1 collective-permute-done.1
  34.0 8.1 all_to_all.30
  49.9 19.9 %collective-permute-done.5.refs_1_ = bf16[256,2048]{1,0:T(8,128)(2,1)S(1)} collective-permute-done((bf16[256,2048]{1,0:T(8,128)(2,1)}, bf16[256,2048]{1,0:T(8,128)(2,1)S(1)}, u32[]{:S(2)}, u32[]{:S(2)}) %collective-permute-start.5) | collective-permute-done | bytes 1048608 | tf_op jit(solution)/shard_map/ppermute | solution.py:1401
  73.4 13.3 %collective-permute-done.9.refs_1_ = bf16[256,1536]{1,0:T(8,128)(2,1)} collective-permute-done((bf16[256,1536]{1,0:T(8,128)(2,1)}, bf16[256,1536]{1,0:T(8,128)(2,1)}, u32[]{:S(2)}, u32[]{:S(2)}) %collective-permute-start.9) | collective-permute-done | bytes 786464 | tf_op jit(solution)/shard_map/ppermute | solution.py:1401
  87.3 9.7 %collective-permute-done.7.refs_3_ = bf16[128,2048]{1,0:T(8,128)(2,1)} collective-permute-done((bf16[128,2048]{1,0:T(8,128)(2,1)S(1)}, bf16[128,2048]{1,0:T(8,128)(2,1)}, u32[]{:S(2)}, u32[]{:S(2)}) %collective-permute-start.7) | collective-permute-done | bytes 524320 | tf_op jit(solution)/shard_map/ppermute | solution.py:1401
  101.5 4.3 all-to-all-start.1
  111.8 5.8 norm_rows.1.x_ref.a_ref
  119.4 13.5 %project.2.refs_1_.refs_2_ = f32[1024,1664]{1,0:T(8,128)} custom-call(s32[4]{0:T(128)} %pad_add_fusion.ids_ref.refs_0_, bf16[1024,2048]{1,0:T(8,128)(2,1)} %norm_rows.1.x_ref.a_ref, bf16[4,4,64,1664]{3,2,1,0:T(8,128)(2,1)} %bitcast.42, bf16[4,4,64,1664]{3,2,1,0:T(8,128)(2,1)} %copy-done.3), custom_call_target="tpu_custom_call" | custom-call | flops 1 | bytes 1 | tf_op jit(solution)/shard_map/project/pallas_call | solution.py:1064
  132.9 9.5 collective-permute-done.12.refs_3_
  147.5 20.3 %mixer_forward.2 = (bf16[1024,512]{1,0:T(8,128)(2,1)}, f32[1024,512]{1,0:T(8,128)}, bf16[1024,512]{1,0:T(8,128)(2,1)}, bf16[1024,256]{1,0:T(8,128)(2,1)}, bf16[4...) custom-call(s32[4]{0:T(128)} %pad_add_fusion.ids_ref.refs_0_, f32[1024,1664]{1,0:T(8,128)} %project.2.refs_1_.refs_2_, ...), custom_call_target="tpu_custom_call" | custom-call | flops 1 | bytes 1 | tf_op jit(solution)/shard_map/mixer_forward/pallas_call | solution.py:227
  167.8 4.3 collective-permute-done.13
  176.2 12.2 %project.3.refs_1_ = f32[1024,1536]{1,0:T(8,128)} custom-call(s32[4]{0:T(128)} %pad_add_fusion.ids_ref.refs_0_, bf16[1024,2048]{1,0:T(8,128)(2,1)} %norm_rows.1.x_ref.a_ref, bf16[1,4,256,1536]{3,2,1,0:T(8,128)(2,1)} %stack_blocks.1.own_ref.refs_4_, bf16[1,4,256,1536]{3,2,1,0:T(8,128)(2,1)} %copy-done.6), custom_call_target="tpu_custom_call" | custom-call | flops 1 | bytes 1 | tf_op jit(solution)/shard_map/project/pallas_call | solution.py:1064
  188.4 20.3 %mixer_forward.3 = (bf16[1024,512]{1,0:T(8,128)(2,1)}, f32[1024,512]{1,0:T(8,128)}, bf16[1024,512]{1,0:T(8,128)(2,1)}, bf16[1024,256]{1,0:T(8,128)(2,1)}, bf16[4...) custom-call(s32[4]{0:T(128)} %pad_add_fusion.ids_ref.refs_0_, f32[1024,1536]{1,0:T(8,128)} %project.3.refs_1_, ...), custom_call_target="tpu_custom_call" | custom-call | flops 1 | bytes 1 | tf_op jit(solution)/shard_map/mixer_forward/pallas_call | solution.py:227
  208.7 10.7 %times_rows.2 = (bf16[512,1024]{1,0:T(8,128)(2,1)}, bf16[512,1024]{1,0:T(8,128)(2,1)}, bf16[512,1024]{1,0:T(8,128)(2,1)}, bf16[512,1024]{1,0:T(8,128)(2,1)}) custom-call(s32[4]{0:T(128)} %pad_add_fusion.ids_ref.refs_0_, bf16[1024,512]{1,0:T(8,128)(2,1)} %get-tuple-element.318.refs_0_, bf16[1024,512]{1,0:T(8,128)(2,1)} %get-tuple-element.319.refs_1_, ...), custom_call_target="tpu_custom_call" | custom-call | flops 1 | bytes 1 | tf_op jit(solution)/shard_map/times_rows/pallas_call | solution.py:1207
  222.8 5.6 join_cores.2.down_ref
  228.5 5.0 join_cores.3
  236.1 7.6 collective-permute-done.18.b_ref.refs_1_
  249.6 10.2 %collective-permute-done.20.refs_2_ = bf16[256,1024]{1,0:T(8,128)(2,1)} collective-permute-done((bf16[256,1024]{1,0:T(8,128)(2,1)}, bf16[256,1024]{1,0:T(8,128)(2,1)}, u32[]{:S(2)}, u32[]{:S(2)}) %collective-permute-start.20) | collective-permute-done | bytes 524320 | tf_op jit(solution)/shard_map/ppermute | solution.py:1401
  260.6 4.6 middle_rows.1
  267.6 23.4 %collective-permute-done.22 = bf16[256,2048]{1,0:T(8,128)(2,1)S(1)} collective-permute-done((bf16[256,2048]{1,0:T(8,128)(2,1)}, bf16[256,2048]{1,0:T(8,128)(2,1)S(1)}, u32[]{:S(2)}, u32[]{:S(2)}) %collective-permute-start.22) | collective-permute-done | bytes 1048608 | tf_op jit(solution)/shard_map/ppermute | solution.py:1401
  298.1 6.6 collective-permute-done.24
  311.1 28.1 %feed_forward.1 = (bf16[1024,1408]{1,0:T(8,128)(2,1)}, bf16[1024,2816]{1,0:T(8,128)(2,1)}) custom-call(s32[4]{0:T(128)} %pad_add_fusion.ids_ref.refs_0_, bf16[1024,2048]{1,0:T(8,128)(2,1)} %constant_dynamic-update-slice_fusion.5.x_ref.a_ref, bf16[4,4,64,2816]{3,2,1,0:T(8,128)(2,1)} %bitcast.39, bf16[4,4,64,2816]{3,2,1,0:T(8,128)(2,1)} %copy-done.1, ...), custom_call_target="tpu_custom_call" | custom-call | flops 1 | bytes 1 | tf_op jit(solution)/shard_map/feed_forward/pallas_call | solution.py:1131
  339.7 10.7 %row_terms.2 = (bf16[704,2048]{1,0:T(8,128)(2,1)}, bf16[704,2048]{1,0:T(8,128)(2,1)}) custom-call(s32[4]{0:T(128)} %pad_add_fusion.ids_ref.refs_0_, bf16[1024,1408]{1,0:T(8,128)(2,1)} %get-tuple-element.353.refs_0_, bf16[1024,2048]{1,0:T(8,128)(2,1)} %copy-done.2), custom_call_target="tpu_custom_call" | custom-call | flops 1 | bytes 1 | tf_op jit(solution)/shard_map/row_terms/pallas_call | solution.py:1379
  350.4 5.5 collective-permute-done.28
  358.5 20.4 %times_transposed.2 = (bf16[512,1024]{1,0:T(8,128)(2,1)}, bf16[512,1024]{1,0:T(8,128)(2,1)}, bf16[512,1024]{1,0:T(8,128)(2,1)}, bf16[512,1024]{1,0:T(8,128)(2,1)}) custom-call(s32[4]{0:T(128)} %pad_add_fusion.ids_ref.refs_0_, bf16[1024,2816]{1,0:T(8,128)(2,1)} %get-tuple-element.362.refs_0_.ra_ref, bf16[4,4,64,2816]{3,2,1,0:T(8,128)(2,1)} %bitcast.40, ...), custom_call_target="tpu_custom_call" | custom-call | flops 1 | bytes 1 | tf_op jit(solution)/shard_map/times_transposed/pallas_call | solution.py:1270
  380.9 12.5 %times_rows.3 = (bf16[512,1024]{1,0:T(8,128)(2,1)}, bf16[512,1024]{1,0:T(8,128)(2,1)}, bf16[512,1024]{1,0:T(8,128)(2,1)}, bf16[512,1024]{1,0:T(8,128)(2,1)}) custom-call(s32[4]{0:T(128)} %pad_add_fusion.ids_ref.refs_0_, bf16[1024,1408]{1,0:T(8,128)(2,1)} %get-tuple-element.353.refs_0_, bf16[704,2048]{1,0:T(8,128)(2,1)} %refs_1_.1, ...), custom_call_target="tpu_custom_call" | custom-call | flops 1 | bytes 1 | tf_op jit(solution)/shard_map/times_rows/pallas_call | solution.py:1207
  393.4 10.8 %collective-permute-done.31.b_ref.refs_1_ = bf16[512,1024]{1,0:T(8,128)(2,1)S(1)} collective-permute-done((bf16[512,1024]{1,0:T(8,128)(2,1)}, bf16[512,1024]{1,0:T(8,128)(2,1)S(1)}, u32[]{:S(2)}, u32[]{:S(2)}) %collective-permute-start.31) | collective-permute-done | bytes 1048608 | tf_op jit(solution)/shard_map/ppermute | solution.py:1401
  415.8 22.1 %column_terms.3 = (bf16[352,2048]{1,0:T(8,128)(2,1)}, bf16[352,2048]{1,0:T(8,128)(2,1)}, bf16[352,2048]{1,0:T(8,128)(2,1)}, bf16[352,2048]{1,0:T(8,128)(2,1)}) custom-call(s32[4]{0:T(128)} %pad_add_fusion.ids_ref.refs_0_, bf16[1024,2048]{1,0:T(8,128)(2,1)} %constant_dynamic-update-slice_fusion.5.x_ref.a_ref, ...), custom_call_target="tpu_custom_call" | custom-call | flops 1 | bytes 1 | tf_op jit(solution)/shard_map/column_terms/pallas_call | solution.py:1333
  439.0 4.3 line_values.14
  443.4 5.5 collective-permute-start.35
  450.6 6.3 middle_back.1
  458.5 21.0 %collective-permute-done.41 = bf16[256,2048]{1,0:T(8,128)(2,1)S(1)} collective-permute-done((bf16[256,2048]{1,0:T(8,128)(2,1)}, bf16[256,2048]{1,0:T(8,128)(2,1)S(1)}, u32[]{:S(2)}, u32[]{:S(2)}) %collective-permute-start.41) | collective-permute-done | bytes 1048608 | tf_op jit(solution)/shard_map/ppermute | solution.py:1401
  483.5 4.4 line_values.15
  494.8 6.8 fusion.2.refs_11_
  505.4 8.8 row_terms.3
  520.2 4.5 line_values.16
  531.4 26.0 %mixer_backward.2 = (bf16[1024,1536]{1,0:T(8,128)(2,1)}, f32[1024,128]{1,0:T(8,128)}, f32[8,1024]{1,0:T(8,128)}, f32[8,256]{1,0:T(8,128)}) custom-call(s32[4]{0:T(128)} %pad_add_fusion.ids_ref.refs_0_, f32[1024,1536]{1,0:T(8,128)} %project.3.refs_1_, f32[1024,1664]{1,0:T(8,128)} %project.2.refs_1_.refs_2_, f32[8,1024]{1,0:T(8,128)} %get-tuple-element.314.refs_3_, ...), custom_call_target="tpu_custom_call" | custom-call | flops 1 | bytes 1 | tf_op jit(solution)/shard_map/mixer_backward/pallas_call | solution.py:489
  559.6 4.3 line_values.17
  571.2 9.8 %collective-permute-done.49 = bf16[256,1024]{1,0:T(8,128)(2,1)S(1)} collective-permute-done((bf16[256,1024]{1,0:T(8,128)(2,1)}, bf16[256,1024]{1,0:T(8,128)(2,1)S(1)}, u32[]{:S(2)}, u32[]{:S(2)}) %collective-permute-start.49) | collective-permute-done | bytes 524320 | tf_op jit(solution)/shard_map/ppermute | solution.py:1401
  582.4 12.5 %collective-permute-done.50 = bf16[256,1024]{1,0:T(8,128)(2,1)S(1)} collective-permute-done((bf16[256,1024]{1,0:T(8,128)(2,1)}, bf16[256,1024]{1,0:T(8,128)(2,1)S(1)}, u32[]{:S(2)}, u32[]{:S(2)}) %collective-permute-start.50) | collective-permute-done | bytes 524320 | tf_op jit(solution)/shard_map/ppermute | solution.py:1401
  595.7 12.6 %column_terms.4 = bf16[4,192,2048]{2,1,0:T(8,128)(2,1)} custom-call(s32[4]{0:T(128)} %pad_add_fusion.ids_ref.refs_0_, bf16[1024,2048]{1,0:T(8,128)(2,1)} %norm_rows.1.x_ref.a_ref, bf16[1024,2048]{1,0:T(8,128)(2,1)} %collective-permute-done.51.b_ref, bf16[1024,1536]{1,0:T(8,128)(2,1)} %get-tuple-element.459.ra_ref.refs_3_, ...), custom_call_target="tpu_custom_call" | custom-call | flops 1 | bytes 1 | tf_op jit(solution)/shard_map/column_terms/pallas_call | solution.py:1333
  617.7 4.4 line_values.18
  626.2 26.4 %mixer_backward.3 = (bf16[1024,1664]{1,0:T(8,128)(2,1)}, f32[1024,128]{1,0:T(8,128)}, f32[8,1024]{1,0:T(8,128)}, f32[8,256]{1,0:T(8,128)}) custom-call(s32[4]{0:T(128)} %pad_add_fusion.ids_ref.refs_0_, f32[1024,1664]{1,0:T(8,128)} %project.2.refs_1_.refs_2_, f32[1024,1664]{1,0:T(8,128)} %project.2.refs_1_.refs_2_, f32[8,1024]{1,0:T(8,128)} %get-tuple-element.308.refs_3_, ...), custom_call_target="tpu_custom_call" | custom-call | flops 1 | bytes 1 | tf_op jit(solution)/shard_map/mixer_backward/pallas_call | solution.py:489
  659.3 4.4 line_values.19
  668.1 14.0 %column_terms.5 = bf16[4,208,2048]{2,1,0:T(8,128)(2,1)} custom-call(s32[4]{0:T(128)} %pad_add_fusion.ids_ref.refs_0_, bf16[1024,2048]{1,0:T(8,128)(2,1)} %norm_rows.1.x_ref.a_ref, bf16[1024,2048]{1,0:T(8,128)(2,1)} %collective-permute-done.51.b_ref, bf16[1024,1664]{1,0:T(8,128)(2,1)} %get-tuple-element.458.ra_ref.refs_0_, ...), custom_call_target="tpu_custom_call" | custom-call | flops 1 | bytes 1 | tf_op jit(solution)/shard_map/column_terms/pallas_call | solution.py:1333
  688.6 8.9 collective-permute-done.60.refs_1_.last_ref
  697.5 4.3 line_values.20
  709.5 23.3 %times_transposed.3 = (bf16[512,1024]{1,0:T(8,128)(2,1)}, bf16[512,1024]{1,0:T(8,128)(2,1)}, bf16[512,1024]{1,0:T(8,128)(2,1)}, bf16[512,1024]{1,0:T(8,128)(2,1)}) custom-call(s32[4]{0:T(128)} %pad_add_fusion.ids_ref.refs_0_, bf16[1024,1664]{1,0:T(8,128)(2,1)} %get-tuple-element.458.ra_ref.refs_0_, bf16[4,4,64,1664]{3,2,1,0:T(8,128)(2,1)} %bitcast.43, ...), custom_call_target="tpu_custom_call" | custom-call | flops 1 | bytes 1 | tf_op jit(solution)/shard_map/times_transposed/pallas_call | solution.py:1270
  735.7 4.3 line_values.21
  756.7 16.2 %collective-permute-done.64.refs_1_.last_ref = bf16[352,2048]{1,0:T(8,128)(2,1)S(1)} collective-permute-done((bf16[352,2048]{1,0:T(8,128)(2,1)}, bf16[352,2048]{1,0:T(8,128)(2,1)S(1)}, u32[]{:S(2)}, u32[]{:S(2)}) %collective-permute-start.64) | collective-permute-done | bytes 1441824 | tf_op jit(solution)/shard_map/ppermute | solution.py:1417
  774.1 4.6 line_values.22
  795.0 6.9 collective-permute-done.68.refs_2_
  803.5 5.2 all-to-all-start.4
  811.2 4.5 line_values.23
  824.4 5.9 tokens_back.1
  830.3 15.9 %collective-permute-done.72.refs_1_.last_ref = bf16[352,2048]{1,0:T(8,128)(2,1)S(1)} collective-permute-done((bf16[352,2048]{1,0:T(8,128)(2,1)}, bf16[352,2048]{1,0:T(8,128)(2,1)S(1)}, u32[]{:S(2)}, u32[]{:S(2)}) %collective-permute-start.72) | collective-permute-done | bytes 1441824 | tf_op jit(solution)/shard_map/ppermute | solution.py:1417
  859.9 4.8 finish_projection.5.refs_0_
  864.6 6.9 finish_projection.6.refs_0_
  871.5 6.9 finish_projection.7.refs_0_
  896.7 10.6 %finish_feed_forward.1 = f32[256,11264]{1,0:T(8,128)} custom-call(bf16[4,256,2816]{2,1,0:T(8,128)(2,1)} %all-to-all-done.4.x_ref), custom_call_target="tpu_custom_call" | custom-call | flops 1 | bytes 1 | tf_op jit(solution)/shard_map/finish_feed_forward/pallas_call | solution.py:1033
  907.2 6.4 finish_projection.8.refs_0_
  913.6 16.2 %all-gather.2 = f32[32,1024]{1,0:T(8,128)S(1)} all-gather(f32[8,1024]{1,0:T(8,128)S(1)} %reduce_sum.28), channel_id=4, replica_groups=mesh['rep'=4,'fsdp'=8] {'rep'}, dimensions={0}, use_global_device_ids=true | all-gather | bytes 163840 | tf_op jit(solution)/shard_map/all_gather | solution.py:1952
  933.6 6.3 finish_projection.9
  (355 shorter events, 264.5 us)
Async XLA Ops:
  7.2 91.0 %all-gather.6.cloned.1.call-start = ((), (), s32[]{:S(2)}) async-start(), calls=%async_computation.6 | async-start | bytes 4259840 | tf_op jit(solution)/shard_map/all_gather | solution.py:1754
  43.5 26.3 %collective-permute-start.5 = (bf16[256,2048]{1,0:T(8,128)(2,1)}, bf16[256,2048]{1,0:T(8,128)(2,1)S(1)}, u32[]{:S(2)}, u32[]{:S(2)}) collective-permute-start(bf16[256,2048]{1,0:T(8,128)(2,1)} %t_ref.3), channel_id=1, source_target_pairs={{0,2},{1,3},{2,0},{3,1},{4,6},{5,7},{6,4},{7,5},{8,10},{9,11},{10,... | collective-permute-start | bytes 3145736 | tf_op jit(solution)/shard_map/ppermute | solution.py:1401
  44.0 26.7 %collective-permute-start.6 = (bf16[256,2048]{1,0:T(8,128)(2,1)}, bf16[256,2048]{1,0:T(8,128)(2,1)S(1)}, u32[]{:S(2)}, u32[]{:S(2)}) collective-permute-start(bf16[256,2048]{1,0:T(8,128)(2,1)} %t_ref.3), channel_id=1, source_target_pairs={{0,4},{1,5},{2,6},{3,7},{4,0},{5,1},{6,2},{7,3},{8,12},{9,13},{10,... | collective-permute-start | bytes 3145736 | tf_op jit(solution)/shard_map/ppermute | solution.py:1401
  44.6 42.1 %collective-permute-start.9 = (bf16[256,1536]{1,0:T(8,128)(2,1)}, bf16[256,1536]{1,0:T(8,128)(2,1)}, u32[]{:S(2)}, u32[]{:S(2)}) collective-permute-start(bf16[256,1536]{1,0:T(8,128)(2,1)} %get-tuple-element.298), channel_id=1, source_target_pairs={{0,2},{1,3},{2,0},{3,1},{4,6},{5,7},{6,4},{7,5},{8,10},{9,11},{10,... | collective-permute-start | bytes 2359304 | tf_op jit(solution)/shard_map/ppermute | solution.py:1401
  46.0 41.2 %collective-permute-start.10 = (bf16[256,1536]{1,0:T(8,128)(2,1)}, bf16[256,1536]{1,0:T(8,128)(2,1)}, u32[]{:S(2)}, u32[]{:S(2)}) collective-permute-start(bf16[256,1536]{1,0:T(8,128)(2,1)} %get-tuple-element.299), channel_id=1, source_target_pairs={{0,4},{1,5},{2,6},{3,7},{4,0},{5,1},{6,2},{7,3},{8,12},{9,13},{10,... | collective-permute-start | bytes 2359304 | tf_op jit(solution)/shard_map/ppermute | solution.py:1401
  71.8 25.2 %collective-permute-start.7 = (bf16[128,2048]{1,0:T(8,128)(2,1)S(1)}, bf16[128,2048]{1,0:T(8,128)(2,1)}, u32[]{:S(2)}, u32[]{:S(2)}) collective-permute-start(bf16[128,2048]{1,0:T(8,128)(2,1)S(1)} %slice.164), channel_id=1, source_target_pairs={{0,4},{1,5},{2,6},{3,7},{4,0},{5,1},{6,2},{7,3},{8,12},{9,13},{10,... | collective-permute-start | bytes 1572872 | tf_op jit(solution)/shard_map/ppermute | solution.py:1401
  72.4 24.6 %collective-permute-start.8 = (bf16[128,2048]{1,0:T(8,128)(2,1)S(1)}, bf16[128,2048]{1,0:T(8,128)(2,1)}, u32[]{:S(2)}, u32[]{:S(2)}) collective-permute-start(bf16[128,2048]{1,0:T(8,128)(2,1)S(1)} %slice.165), channel_id=1, source_target_pairs={{0,2},{1,3},{2,0},{3,1},{4,6},{5,7},{6,4},{7,5},{8,10},{9,11},{10,... | collective-permute-start | bytes 1572872 | tf_op jit(solution)/shard_map/ppermute | solution.py:1401
  98.1 19.5 %collective-permute-start.11 = (bf16[4,4,64,1664]{3,2,1,0:T(8,128)(2,1)}, bf16[4,4,64,1664]{3,2,1,0:T(8,128)(2,1)S(1)}, u32[]{:S(2)}, u32[]{:S(2)}) collective-permute-start(bf16[4,4,64,1664]{3,2,1,0:T(8,128)(2,1)} %bitcast.41), channel_id=1, source_target_pairs={{0,1},{1,0},{2,3},{3,2},{4,5},{5,4},{6,7},{7,6},{8,9},{9,8},{10,11... | collective-permute-start | bytes 10223624 | tf_op jit(solution)/shard_map/ppermute | solution.py:1405
  101.5 44.9 %all-to-all-start.1 = ((bf16[4,64,2816]{2,1,0:T(8,128)(2,1)}), bf16[4,64,2816]{2,1,0:T(8,128)(2,1)}, u32[]{:S(2)}, u32[]{:S(2)}) async-start(bf16[4,64,2816]{2,1,0:T(8,128)(2,1)} %pack_columns.1), calls=%async_computation.1 | async-start | bytes 2883584 | tf_op jit(solution)/shard_map/all_to_all | solution.py:1576
  105.8 154.8 %all-gather.8.cloned.1.call-start = ((), (), s32[]{:S(2)}) async-start(), calls=%async_computation.7 | async-start | bytes 7208960 | tf_op jit(solution)/shard_map/all_gather | solution.py:1771
  105.9 36.5 %collective-permute-start.12 = (bf16[256,1536]{1,0:T(8,128)(2,1)}, bf16[256,1536]{1,0:T(8,128)(2,1)S(1)}, u32[]{:S(2)}, u32[]{:S(2)}) collective-permute-start(bf16[256,1536]{1,0:T(8,128)(2,1)} %get-tuple-element.302), channel_id=1, source_target_pairs={{0,6},{1,7},{2,4},{3,5},{4,2},{5,3},{6,0},{7,1},{8,14},{9,15},{10,... | collective-permute-start | bytes 2359304 | tf_op jit(solution)/shard_map/ppermute | solution.py:1401
  146.5 28.1 %collective-permute-start.15 = (bf16[1,4,256,1536]{3,2,1,0:T(8,128)(2,1)}, bf16[1,4,256,1536]{3,2,1,0:T(8,128)(2,1)S(1)}, u32[]{:S(2)}, u32[]{:S(2)}) collective-permute-start(bf16[1,4,256,1536]{3,2,1,0:T(8,128)(2,1)} %stack_blocks.1.own_ref.refs_4_), channel_id=1, source_target_pairs={{0,1},{1,0},{2,3},{3,2},{4,5},{5,4},{6,7},{7,6},{8,9},{9,8},{10,11... | collective-permute-start | bytes 9437192 | tf_op jit(solution)/shard_map/ppermute | solution.py:1405
  146.5 25.6 %collective-permute-start.13 = (bf16[256,2048]{1,0:T(8,128)(2,1)S(1)}, bf16[256,2048]{1,0:T(8,128)(2,1)S(1)}, u32[]{:S(2)}, u32[]{:S(2)}) collective-permute-start(bf16[256,2048]{1,0:T(8,128)(2,1)S(1)} %copy-done.29), channel_id=1, source_target_pairs={{0,2},{1,3},{2,0},{3,1},{4,6},{5,7},{6,4},{7,5},{8,10},{9,11},{10,... | collective-permute-start | bytes 3145736 | tf_op jit(solution)/shard_map/ppermute | solution.py:1401
  147.1 25.2 %collective-permute-start.14 = (bf16[256,2048]{1,0:T(8,128)(2,1)S(1)}, bf16[256,2048]{1,0:T(8,128)(2,1)S(1)}, u32[]{:S(2)}, u32[]{:S(2)}) collective-permute-start(bf16[256,2048]{1,0:T(8,128)(2,1)S(1)} %copy-done.29), channel_id=1, source_target_pairs={{0,4},{1,5},{2,6},{3,7},{4,0},{5,1},{6,2},{7,3},{8,12},{9,13},{10,... | collective-permute-start | bytes 3145736 | tf_op jit(solution)/shard_map/ppermute | solution.py:1401
  172.4 36.3 %collective-permute-start.16 = (bf16[128,2048]{1,0:T(8,128)(2,1)S(1)}, bf16[128,2048]{1,0:T(8,128)(2,1)S(1)}, u32[]{:S(2)}, u32[]{:S(2)}) collective-permute-start(bf16[128,2048]{1,0:T(8,128)(2,1)S(1)} %slice.166), channel_id=1, source_target_pairs={{0,4},{1,5},{2,6},{3,7},{4,0},{5,1},{6,2},{7,3},{8,12},{9,13},{10,... | collective-permute-start | bytes 1572872 | tf_op jit(solution)/shard_map/ppermute | solution.py:1401
  173.2 35.5 %collective-permute-start.17 = (bf16[128,2048]{1,0:T(8,128)(2,1)S(1)}, bf16[128,2048]{1,0:T(8,128)(2,1)S(1)}, u32[]{:S(2)}, u32[]{:S(2)}) collective-permute-start(bf16[128,2048]{1,0:T(8,128)(2,1)S(1)} %slice.167), channel_id=1, source_target_pairs={{0,2},{1,3},{2,0},{3,1},{4,6},{5,7},{6,4},{7,5},{8,10},{9,11},{10,... | collective-permute-start | bytes 1572872 | tf_op jit(solution)/shard_map/ppermute | solution.py:1401
  219.5 24.2 %collective-permute-start.18 = (bf16[512,1024]{1,0:T(8,128)(2,1)}, bf16[512,1024]{1,0:T(8,128)(2,1)S(1)}, u32[]{:S(2)}, u32[]{:S(2)}) collective-permute-start(bf16[512,1024]{1,0:T(8,128)(2,1)} %get-tuple-element.321), channel_id=1, source_target_pairs={{0,2},{1,3},{2,0},{3,1},{4,6},{5,7},{6,4},{7,5},{8,10},{9,11},{10,... | collective-permute-start | bytes 3145736 | tf_op jit(solution)/shard_map/ppermute | solution.py:1401
  220.2 24.6 %collective-permute-start.19 = (bf16[512,1024]{1,0:T(8,128)(2,1)}, bf16[512,1024]{1,0:T(8,128)(2,1)}, u32[]{:S(2)}, u32[]{:S(2)}) collective-permute-start(bf16[512,1024]{1,0:T(8,128)(2,1)} %get-tuple-element.323), channel_id=1, source_target_pairs={{0,4},{1,5},{2,6},{3,7},{4,0},{5,1},{6,2},{7,3},{8,12},{9,13},{10,... | collective-permute-start | bytes 3145736 | tf_op jit(solution)/shard_map/ppermute | solution.py:1401
  260.6 48.0 %collective-permute-start.26 = (bf16[4,4,64,2816]{3,2,1,0:T(8,128)(2,1)}, bf16[4,4,64,2816]{3,2,1,0:T(8,128)(2,1)S(1)}, u32[]{:S(2)}, u32[]{:S(2)}) collective-permute-start(bf16[4,4,64,2816]{3,2,1,0:T(8,128)(2,1)} %bitcast.38), channel_id=1, source_target_pairs={{0,1},{1,0},{2,3},{3,2},{4,5},{5,4},{6,7},{7,6},{8,9},{9,8},{10,11... | collective-permute-start | bytes 17301512 | tf_op jit(solution)/shard_map/ppermute | solution.py:1405
  265.2 25.8 %collective-permute-start.22 = (bf16[256,2048]{1,0:T(8,128)(2,1)}, bf16[256,2048]{1,0:T(8,128)(2,1)S(1)}, u32[]{:S(2)}, u32[]{:S(2)}) collective-permute-start(bf16[256,2048]{1,0:T(8,128)(2,1)} %get-tuple-element.338), channel_id=1, source_target_pairs={{0,2},{1,3},{2,0},{3,1},{4,6},{5,7},{6,4},{7,5},{8,10},{9,11},{10,... | collective-permute-start | bytes 3145736 | tf_op jit(solution)/shard_map/ppermute | solution.py:1401
  266.0 28.3 %collective-permute-start.23 = (bf16[256,2048]{1,0:T(8,128)(2,1)}, bf16[256,2048]{1,0:T(8,128)(2,1)S(1)}, u32[]{:S(2)}, u32[]{:S(2)}) collective-permute-start(bf16[256,2048]{1,0:T(8,128)(2,1)} %get-tuple-element.338), channel_id=1, source_target_pairs={{0,4},{1,5},{2,6},{3,7},{4,0},{5,1},{6,2},{7,3},{8,12},{9,13},{10,... | collective-permute-start | bytes 3145736 | tf_op jit(solution)/shard_map/ppermute | solution.py:1401
  308.6 31.1 %collective-permute-start.27 = (bf16[1024,2048]{1,0:T(8,128)(2,1)}, bf16[1024,2048]{1,0:T(8,128)(2,1)}, u32[]{:S(2)}, u32[]{:S(2)}) collective-permute-start(bf16[1024,2048]{1,0:T(8,128)(2,1)} %constant_dynamic-update-slice_fusion.5.x_ref.a_ref), channel_id=1, source_target_pairs={{0,1},{1,0},{2,3},{3,2},{4,5},{5,4},{6,7},{7,6},{8,9},{9,8},{10,11... | collective-permute-start | bytes 12582920 | tf_op jit(solution)/shard_map/ppermute | solution.py:1405
  358.0 35.3 %collective-permute-start.30 = (bf16[352,2048]{1,0:T(8,128)(2,1)S(1)}, bf16[352,2048]{1,0:T(8,128)(2,1)}, u32[]{:S(2)}, u32[]{:S(2)}) collective-permute-start(bf16[352,2048]{1,0:T(8,128)(2,1)S(1)} %get-tuple-element.360.refs_0_), channel_id=1, source_target_pairs={{0,8},{8,0},{16,24},{24,16},{1,9},{9,1},{17,25},{25,17},{2,10},{10... | collective-permute-start | bytes 4325384 | tf_op jit(solution)/shard_map/ppermute | solution.py:1417
  378.9 25.3 %collective-permute-start.31 = (bf16[512,1024]{1,0:T(8,128)(2,1)}, bf16[512,1024]{1,0:T(8,128)(2,1)S(1)}, u32[]{:S(2)}, u32[]{:S(2)}) collective-permute-start(bf16[512,1024]{1,0:T(8,128)(2,1)} %get-tuple-element.349), channel_id=1, source_target_pairs={{0,2},{1,3},{2,0},{3,1},{4,6},{5,7},{6,4},{7,5},{8,10},{9,11},{10,... | collective-permute-start | bytes 3145736 | tf_op jit(solution)/shard_map/ppermute | solution.py:1401
  380.5 24.9 %collective-permute-start.32 = (bf16[512,1024]{1,0:T(8,128)(2,1)}, bf16[512,1024]{1,0:T(8,128)(2,1)S(1)}, u32[]{:S(2)}, u32[]{:S(2)}) collective-permute-start(bf16[512,1024]{1,0:T(8,128)(2,1)} %get-tuple-element.351), channel_id=1, source_target_pairs={{0,4},{1,5},{2,6},{3,7},{4,0},{5,1},{6,2},{7,3},{8,12},{9,13},{10,... | collective-permute-start | bytes 3145736 | tf_op jit(solution)/shard_map/ppermute | solution.py:1401
  405.4 32.5 %collective-permute-start.33 = (bf16[352,2048]{1,0:T(8,128)(2,1)S(1)}, bf16[352,2048]{1,0:T(8,128)(2,1)S(1)}, u32[]{:S(2)}, u32[]{:S(2)}) collective-permute-start(bf16[352,2048]{1,0:T(8,128)(2,1)S(1)} %get-tuple-element.367.refs_0_), channel_id=1, source_target_pairs={{0,8},{8,0},{16,24},{24,16},{1,9},{9,1},{17,25},{25,17},{2,10},{10... | collective-permute-start | bytes 4325384 | tf_op jit(solution)/shard_map/ppermute | solution.py:1417
  409.7 28.2 %collective-permute-start.34 = (bf16[352,2048]{1,0:T(8,128)(2,1)}, bf16[352,2048]{1,0:T(8,128)(2,1)}, u32[]{:S(2)}, u32[]{:S(2)}) collective-permute-start(bf16[352,2048]{1,0:T(8,128)(2,1)} %line_values.13.refs_2_), channel_id=1, source_target_pairs={{8,16},{16,8},{9,17},{17,9},{10,18},{18,10},{11,19},{19,11},{12,20... | collective-permute-start | bytes 4325384 | tf_op jit(solution)/shard_map/ppermute | solution.py:1417
  414.1 35.5 %collective-permute-start.39 = (bf16[256,1024]{1,0:T(8,128)(2,1)}, bf16[256,1024]{1,0:T(8,128)(2,1)S(1)}, u32[]{:S(2)}, u32[]{:S(2)}) collective-permute-start(bf16[256,1024]{1,0:T(8,128)(2,1)} %get-tuple-element.380), channel_id=1, source_target_pairs={{0,4},{1,5},{2,6},{3,7},{4,0},{5,1},{6,2},{7,3},{8,12},{9,13},{10,... | collective-permute-start | bytes 1572872 | tf_op jit(solution)/shard_map/ppermute | solution.py:1401
  414.5 35.1 %collective-permute-start.40 = (bf16[256,1024]{1,0:T(8,128)(2,1)}, bf16[256,1024]{1,0:T(8,128)(2,1)S(1)}, u32[]{:S(2)}, u32[]{:S(2)}) collective-permute-start(bf16[256,1024]{1,0:T(8,128)(2,1)} %get-tuple-element.381), channel_id=1, source_target_pairs={{0,2},{1,3},{2,0},{3,1},{4,6},{5,7},{6,4},{7,5},{8,10},{9,11},{10,... | collective-permute-start | bytes 1572872 | tf_op jit(solution)/shard_map/ppermute | solution.py:1401
  443.4 37.4 %collective-permute-start.35 = (bf16[352,2048]{1,0:T(8,128)(2,1)}, bf16[352,2048]{1,0:T(8,128)(2,1)S(1)}, u32[]{:S(2)}, u32[]{:S(2)}) collective-permute-start(bf16[352,2048]{1,0:T(8,128)(2,1)} %get-tuple-element.371), channel_id=1, source_target_pairs={{0,8},{8,0},{16,24},{24,16},{1,9},{9,1},{17,25},{25,17},{2,10},{10... | collective-permute-start | bytes 4325384 | tf_op jit(solution)/shard_map/ppermute | solution.py:1417
  448.8 31.9 %collective-permute-start.36 = (bf16[352,2048]{1,0:T(8,128)(2,1)}, bf16[352,2048]{1,0:T(8,128)(2,1)S(1)}, u32[]{:S(2)}, u32[]{:S(2)}) collective-permute-start(bf16[352,2048]{1,0:T(8,128)(2,1)} %get-tuple-element.376.refs_2_), channel_id=1, source_target_pairs={{8,16},{16,8},{9,17},{17,9},{10,18},{18,10},{11,19},{19,11},{12,20... | collective-permute-start | bytes 4325384 | tf_op jit(solution)/shard_map/ppermute | solution.py:1417
  456.9 22.7 %collective-permute-start.41 = (bf16[256,2048]{1,0:T(8,128)(2,1)}, bf16[256,2048]{1,0:T(8,128)(2,1)S(1)}, u32[]{:S(2)}, u32[]{:S(2)}) collective-permute-start(bf16[256,2048]{1,0:T(8,128)(2,1)} %get-tuple-element.388), channel_id=1, source_target_pairs={{0,2},{1,3},{2,0},{3,1},{4,6},{5,7},{6,4},{7,5},{8,10},{9,11},{10,... | collective-permute-start | bytes 3145736 | tf_op jit(solution)/shard_map/ppermute | solution.py:1401
  457.9 22.8 %collective-permute-start.42 = (bf16[256,2048]{1,0:T(8,128)(2,1)}, bf16[256,2048]{1,0:T(8,128)(2,1)S(1)}, u32[]{:S(2)}, u32[]{:S(2)}) collective-permute-start(bf16[256,2048]{1,0:T(8,128)(2,1)} %get-tuple-element.388), channel_id=1, source_target_pairs={{0,4},{1,5},{2,6},{3,7},{4,0},{5,1},{6,2},{7,3},{8,12},{9,13},{10,... | collective-permute-start | bytes 3145736 | tf_op jit(solution)/shard_map/ppermute | solution.py:1401
  487.9 31.1 %collective-permute-start.37 = (bf16[352,2048]{1,0:T(8,128)(2,1)}, bf16[352,2048]{1,0:T(8,128)(2,1)S(1)}, u32[]{:S(2)}, u32[]{:S(2)}) collective-permute-start(bf16[352,2048]{1,0:T(8,128)(2,1)} %get-tuple-element.378), channel_id=1, source_target_pairs={{0,8},{8,0},{16,24},{24,16},{1,9},{9,1},{17,25},{25,17},{2,10},{10... | collective-permute-start | bytes 4325384 | tf_op jit(solution)/shard_map/ppermute | solution.py:1417
  490.8 28.3 %collective-permute-start.38 = (bf16[352,2048]{1,0:T(8,128)(2,1)}, bf16[352,2048]{1,0:T(8,128)(2,1)}, u32[]{:S(2)}, u32[]{:S(2)}) collective-permute-start(bf16[352,2048]{1,0:T(8,128)(2,1)} %get-tuple-element.395.refs_2_), channel_id=1, source_target_pairs={{8,16},{16,8},{9,17},{17,9},{10,18},{18,10},{11,19},{19,11},{12,20... | collective-permute-start | bytes 4325384 | tf_op jit(solution)/shard_map/ppermute | solution.py:1417
  524.6 33.6 %collective-permute-start.47 = (bf16[352,2048]{1,0:T(8,128)(2,1)}, bf16[352,2048]{1,0:T(8,128)(2,1)S(1)}, u32[]{:S(2)}, u32[]{:S(2)}) collective-permute-start(bf16[352,2048]{1,0:T(8,128)(2,1)} %get-tuple-element.473.t_ref), channel_id=1, source_target_pairs={{0,8},{8,0},{16,24},{24,16},{1,9},{9,1},{17,25},{25,17},{2,10},{10... | collective-permute-start | bytes 4325384 | tf_op jit(solution)/shard_map/ppermute | solution.py:1417
  527.3 31.2 %collective-permute-start.48 = (bf16[352,2048]{1,0:T(8,128)(2,1)}, bf16[352,2048]{1,0:T(8,128)(2,1)}, u32[]{:S(2)}, u32[]{:S(2)}) collective-permute-start(bf16[352,2048]{1,0:T(8,128)(2,1)} %get-tuple-element.412.refs_2_), channel_id=1, source_target_pairs={{8,16},{16,8},{9,17},{17,9},{10,18},{18,10},{11,19},{19,11},{12,20... | collective-permute-start | bytes 4325384 | tf_op jit(solution)/shard_map/ppermute | solution.py:1417
  529.0 28.4 %collective-permute-start.45 = (bf16[512,1024]{1,0:T(8,128)(2,1)}, bf16[512,1024]{1,0:T(8,128)(2,1)S(1)}, u32[]{:S(2)}, u32[]{:S(2)}) collective-permute-start(bf16[512,1024]{1,0:T(8,128)(2,1)} %get-tuple-element.400), channel_id=1, source_target_pairs={{0,2},{1,3},{2,0},{3,1},{4,6},{5,7},{6,4},{7,5},{8,10},{9,11},{10,... | collective-permute-start | bytes 3145736 | tf_op jit(solution)/shard_map/ppermute | solution.py:1401
  529.9 27.5 %collective-permute-start.46 = (bf16[512,1024]{1,0:T(8,128)(2,1)}, bf16[512,1024]{1,0:T(8,128)(2,1)S(1)}, u32[]{:S(2)}, u32[]{:S(2)}) collective-permute-start(bf16[512,1024]{1,0:T(8,128)(2,1)} %get-tuple-element.401), channel_id=1, source_target_pairs={{0,4},{1,5},{2,6},{3,7},{4,0},{5,1},{6,2},{7,3},{8,12},{9,13},{10,... | collective-permute-start | bytes 3145736 | tf_op jit(solution)/shard_map/ppermute | solution.py:1401
  531.4 63.4 %collective-permute-start.51 = (bf16[1024,2048]{1,0:T(8,128)(2,1)S(1)}, bf16[1024,2048]{1,0:T(8,128)(2,1)}, u32[]{:S(2)}, u32[]{:S(2)}) collective-permute-start(bf16[1024,2048]{1,0:T(8,128)(2,1)S(1)} %copy-done), channel_id=1, source_target_pairs={{0,1},{1,0},{2,3},{3,2},{4,5},{5,4},{6,7},{7,6},{8,9},{9,8},{10,11... | collective-permute-start | bytes 12582920 | tf_op jit(solution)/shard_map/ppermute | solution.py:1405
  558.8 36.9 %collective-permute-start.56 = (bf16[1024,1536]{1,0:T(8,128)(2,1)}, bf16[1024,1536]{1,0:T(8,128)(2,1)}, u32[]{:S(2)}, u32[]{:S(2)}) collective-permute-start(bf16[1024,1536]{1,0:T(8,128)(2,1)} %get-tuple-element.459.ra_ref.refs_3_), channel_id=1, source_target_pairs={{0,1},{1,0},{2,3},{3,2},{4,5},{5,4},{6,7},{7,6},{8,9},{9,8},{10,11... | collective-permute-start | bytes 9437192 | tf_op jit(solution)/shard_map/ppermute | solution.py:1405
  567.0 50.6 %collective-permute-start.54 = (bf16[352,2048]{1,0:T(8,128)(2,1)}, bf16[352,2048]{1,0:T(8,128)(2,1)}, u32[]{:S(2)}, u32[]{:S(2)}) collective-permute-start(bf16[352,2048]{1,0:T(8,128)(2,1)} %get-tuple-element.471.t_ref), channel_id=1, source_target_pairs={{0,8},{8,0},{16,24},{24,16},{1,9},{9,1},{17,25},{25,17},{2,10},{10... | collective-permute-start | bytes 4325384 | tf_op jit(solution)/shard_map/ppermute | solution.py:1417
  569.5 48.2 %collective-permute-start.55 = (bf16[352,2048]{1,0:T(8,128)(2,1)}, bf16[352,2048]{1,0:T(8,128)(2,1)}, u32[]{:S(2)}, u32[]{:S(2)}) collective-permute-start(bf16[352,2048]{1,0:T(8,128)(2,1)} %get-tuple-element.434.refs_2_), channel_id=1, source_target_pairs={{8,16},{16,8},{9,17},{17,9},{10,18},{18,10},{11,19},{19,11},{12,20... | collective-permute-start | bytes 4325384 | tf_op jit(solution)/shard_map/ppermute | solution.py:1417
  608.2 48.4 %all-to-all-start.2 = ((bf16[4,192,2048]{2,1,0:T(8,128)(2,1)}), bf16[4,192,2048]{2,1,0:T(8,128)(2,1)S(1)}, u32[]{:S(2)}, u32[]{:S(2)}) async-start(bf16[4,192,2048]{2,1,0:T(8,128)(2,1)} %column_terms.4), calls=%async_computation.2 | async-start | bytes 6291456 | tf_op jit(solution)/shard_map/all_to_all | solution.py:1576
  622.1 33.4 %collective-permute-start.57 = (bf16[352,2048]{1,0:T(8,128)(2,1)}, bf16[352,2048]{1,0:T(8,128)(2,1)S(1)}, u32[]{:S(2)}, u32[]{:S(2)}) collective-permute-start(bf16[352,2048]{1,0:T(8,128)(2,1)} %get-tuple-element.493.t_ref), channel_id=1, source_target_pairs={{0,8},{8,0},{16,24},{24,16},{1,9},{9,1},{17,25},{25,17},{2,10},{10... | collective-permute-start | bytes 4325384 | tf_op jit(solution)/shard_map/ppermute | solution.py:1417
  624.5 32.1 %collective-permute-start.58 = (bf16[352,2048]{1,0:T(8,128)(2,1)}, bf16[352,2048]{1,0:T(8,128)(2,1)}, u32[]{:S(2)}, u32[]{:S(2)}) collective-permute-start(bf16[352,2048]{1,0:T(8,128)(2,1)} %get-tuple-element.444.refs_2_), channel_id=1, source_target_pairs={{8,16},{16,8},{9,17},{17,9},{10,18},{18,10},{11,19},{19,11},{12,20... | collective-permute-start | bytes 4325384 | tf_op jit(solution)/shard_map/ppermute | solution.py:1417
  663.7 33.8 %collective-permute-start.60 = (bf16[352,2048]{1,0:T(8,128)(2,1)}, bf16[352,2048]{1,0:T(8,128)(2,1)}, u32[]{:S(2)}, u32[]{:S(2)}) collective-permute-start(bf16[352,2048]{1,0:T(8,128)(2,1)} %get-tuple-element.491.t_ref), channel_id=1, source_target_pairs={{0,8},{8,0},{16,24},{24,16},{1,9},{9,1},{17,25},{25,17},{2,10},{10... | collective-permute-start | bytes 4325384 | tf_op jit(solution)/shard_map/ppermute | solution.py:1417
  666.4 31.2 %collective-permute-start.61 = (bf16[352,2048]{1,0:T(8,128)(2,1)}, bf16[352,2048]{1,0:T(8,128)(2,1)}, u32[]{:S(2)}, u32[]{:S(2)}) collective-permute-start(bf16[352,2048]{1,0:T(8,128)(2,1)} %get-tuple-element.454.refs_2_), channel_id=1, source_target_pairs={{8,16},{16,8},{9,17},{17,9},{10,18},{18,10},{11,19},{19,11},{12,20... | collective-permute-start | bytes 4325384 | tf_op jit(solution)/shard_map/ppermute | solution.py:1417
  682.1 50.7 %all-to-all-start.3 = ((bf16[4,208,2048]{2,1,0:T(8,128)(2,1)}), bf16[4,208,2048]{2,1,0:T(8,128)(2,1)S(1)}, u32[]{:S(2)}, u32[]{:S(2)}) async-start(bf16[4,208,2048]{2,1,0:T(8,128)(2,1)} %column_terms.5), calls=%async_computation.3 | async-start | bytes 6815744 | tf_op jit(solution)/shard_map/all_to_all | solution.py:1576
  701.9 33.9 %collective-permute-start.62 = (bf16[352,2048]{1,0:T(8,128)(2,1)}, bf16[352,2048]{1,0:T(8,128)(2,1)}, u32[]{:S(2)}, u32[]{:S(2)}) collective-permute-start(bf16[352,2048]{1,0:T(8,128)(2,1)} %get-tuple-element.456), channel_id=1, source_target_pairs={{0,8},{8,0},{16,24},{24,16},{1,9},{9,1},{17,25},{25,17},{2,10},{10... | collective-permute-start | bytes 4325384 | tf_op jit(solution)/shard_map/ppermute | solution.py:1417
  705.5 30.2 %collective-permute-start.63 = (bf16[352,2048]{1,0:T(8,128)(2,1)}, bf16[352,2048]{1,0:T(8,128)(2,1)}, u32[]{:S(2)}, u32[]{:S(2)}) collective-permute-start(bf16[352,2048]{1,0:T(8,128)(2,1)} %get-tuple-element.467.refs_2_), channel_id=1, source_target_pairs={{8,16},{16,8},{9,17},{17,9},{10,18},{18,10},{11,19},{19,11},{12,20... | collective-permute-start | bytes 4325384 | tf_op jit(solution)/shard_map/ppermute | solution.py:1417
  740.1 32.9 %collective-permute-start.64 = (bf16[352,2048]{1,0:T(8,128)(2,1)}, bf16[352,2048]{1,0:T(8,128)(2,1)S(1)}, u32[]{:S(2)}, u32[]{:S(2)}) collective-permute-start(bf16[352,2048]{1,0:T(8,128)(2,1)} %get-tuple-element.529.t_ref), channel_id=1, source_target_pairs={{0,8},{8,0},{16,24},{24,16},{1,9},{9,1},{17,25},{25,17},{2,10},{10... | collective-permute-start | bytes 4325384 | tf_op jit(solution)/shard_map/ppermute | solution.py:1417
  743.7 29.2 %collective-permute-start.65 = (bf16[352,2048]{1,0:T(8,128)(2,1)}, bf16[352,2048]{1,0:T(8,128)(2,1)}, u32[]{:S(2)}, u32[]{:S(2)}) collective-permute-start(bf16[352,2048]{1,0:T(8,128)(2,1)} %get-tuple-element.477.refs_2_), channel_id=1, source_target_pairs={{8,16},{16,8},{9,17},{17,9},{10,18},{18,10},{11,19},{19,11},{12,20... | collective-permute-start | bytes 4325384 | tf_op jit(solution)/shard_map/ppermute | solution.py:1417
  745.5 42.8 %collective-permute-start.66 = (bf16[512,1024]{1,0:T(8,128)(2,1)}, bf16[512,1024]{1,0:T(8,128)(2,1)S(1)}, u32[]{:S(2)}, u32[]{:S(2)}) collective-permute-start(bf16[512,1024]{1,0:T(8,128)(2,1)} %get-tuple-element.489), channel_id=1, source_target_pairs={{0,2},{1,3},{2,0},{3,1},{4,6},{5,7},{6,4},{7,5},{8,10},{9,11},{10,... | collective-permute-start | bytes 3145736 | tf_op jit(solution)/shard_map/ppermute | solution.py:1401
  747.2 41.1 %collective-permute-start.67 = (bf16[512,1024]{1,0:T(8,128)(2,1)}, bf16[512,1024]{1,0:T(8,128)(2,1)}, u32[]{:S(2)}, u32[]{:S(2)}) collective-permute-start(bf16[512,1024]{1,0:T(8,128)(2,1)} %get-tuple-element.490), channel_id=1, source_target_pairs={{0,4},{1,5},{2,6},{3,7},{4,0},{5,1},{6,2},{7,3},{8,12},{9,13},{10,... | collective-permute-start | bytes 3145736 | tf_op jit(solution)/shard_map/ppermute | solution.py:1401
  778.7 30.9 %collective-permute-start.70 = (bf16[352,2048]{1,0:T(8,128)(2,1)}, bf16[352,2048]{1,0:T(8,128)(2,1)S(1)}, u32[]{:S(2)}, u32[]{:S(2)}) collective-permute-start(bf16[352,2048]{1,0:T(8,128)(2,1)} %get-tuple-element.527.t_ref), channel_id=1, source_target_pairs={{0,8},{8,0},{16,24},{24,16},{1,9},{9,1},{17,25},{25,17},{2,10},{10... | collective-permute-start | bytes 4325384 | tf_op jit(solution)/shard_map/ppermute | solution.py:1417
  781.3 28.3 %collective-permute-start.71 = (bf16[352,2048]{1,0:T(8,128)(2,1)}, bf16[352,2048]{1,0:T(8,128)(2,1)S(1)}, u32[]{:S(2)}, u32[]{:S(2)}) collective-permute-start(bf16[352,2048]{1,0:T(8,128)(2,1)} %get-tuple-element.503.refs_2_), channel_id=1, source_target_pairs={{8,16},{16,8},{9,17},{17,9},{10,18},{18,10},{11,19},{19,11},{12,20... | collective-permute-start | bytes 4325384 | tf_op jit(solution)/shard_map/ppermute | solution.py:1417
  803.5 87.9 %all-to-all-start.4 = ((bf16[4,256,2816]{2,1,0:T(8,128)(2,1)}), bf16[4,256,2816]{2,1,0:T(8,128)(2,1)}, u32[]{:S(2)}, u32[]{:S(2)}) async-start(bf16[4,256,2816]{2,1,0:T(8,128)(2,1)} %place_blocks.7), calls=%async_computation.4 | async-start | bytes 11534336 | tf_op jit(solution)/shard_map/all_to_all | solution.py:1576
  815.6 30.5 %collective-permute-start.72 = (bf16[352,2048]{1,0:T(8,128)(2,1)}, bf16[352,2048]{1,0:T(8,128)(2,1)S(1)}, u32[]{:S(2)}, u32[]{:S(2)}) collective-permute-start(bf16[352,2048]{1,0:T(8,128)(2,1)} %get-tuple-element.506.t_ref), channel_id=1, source_target_pairs={{0,8},{8,0},{16,24},{24,16},{1,9},{9,1},{17,25},{25,17},{2,10},{10... | collective-permute-start | bytes 4325384 | tf_op jit(solution)/shard_map/ppermute | solution.py:1417
  818.8 27.4 %collective-permute-start.73 = (bf16[352,2048]{1,0:T(8,128)(2,1)}, bf16[352,2048]{1,0:T(8,128)(2,1)}, u32[]{:S(2)}, u32[]{:S(2)}) collective-permute-start(bf16[352,2048]{1,0:T(8,128)(2,1)} %get-tuple-element.523.refs_2_), channel_id=1, source_target_pairs={{8,16},{16,8},{9,17},{17,9},{10,18},{18,10},{11,19},{19,11},{12,20... | collective-permute-start | bytes 4325384 | tf_op jit(solution)/shard_map/ppermute | solution.py:1417
  851.3 30.7 %collective-permute-start.74 = (bf16[352,2048]{1,0:T(8,128)(2,1)}, bf16[352,2048]{1,0:T(8,128)(2,1)S(1)}, u32[]{:S(2)}, u32[]{:S(2)}) collective-permute-start(bf16[352,2048]{1,0:T(8,128)(2,1)} %get-tuple-element.536.t_ref), channel_id=1, source_target_pairs={{8,0},{16,24},{9,1},{17,25},{10,2},{18,26},{11,3},{19,27},{12,4},{... | collective-permute-start | bytes 4325384 | tf_op jit(solution)/shard_map/ppermute | solution.py:1417
  852.7 29.3 %collective-permute-start.75 = (bf16[352,2048]{1,0:T(8,128)(2,1)}, bf16[352,2048]{1,0:T(8,128)(2,1)S(1)}, u32[]{:S(2)}, u32[]{:S(2)}) collective-permute-start(bf16[352,2048]{1,0:T(8,128)(2,1)} %get-tuple-element.533.refs_0_), channel_id=1, source_target_pairs={{8,16},{16,8},{9,17},{17,9},{10,18},{18,10},{11,19},{19,11},{12,20... | collective-permute-start | bytes 4325384 | tf_op jit(solution)/shard_map/ppermute | solution.py:1417
  885.9 46.2 %collective-permute-start.76 = (bf16[352,2048]{1,0:T(8,128)(2,1)}, bf16[352,2048]{1,0:T(8,128)(2,1)}, u32[]{:S(2)}, u32[]{:S(2)}) collective-permute-start(bf16[352,2048]{1,0:T(8,128)(2,1)} %line_values.25.t_ref), channel_id=1, source_target_pairs={{8,0},{16,24},{9,1},{17,25},{10,2},{18,26},{11,3},{19,27},{12,4},{... | collective-permute-start | bytes 4325384 | tf_op jit(solution)/shard_map/ppermute | solution.py:1417
  891.4 22.2 %all-to-all-start.5 = ((f32[8,8,1024]{2,1,0:T(8,128)}), f32[8,8,1024]{2,1,0:T(8,128)S(1)}, u32[]{:S(2)}, u32[]{:S(2)}) async-start(f32[8,8,1024]{2,1,0:T(8,128)} %pack_small_grads.1), calls=%async_computation.5 | async-start | bytes 524288 | tf_op jit(solution)/shard_map/all_to_all | solution.py:1948
  (83 other events, 591.6 us)
Sparse Core Ops, SparseCore 0:
  30.0 68.1 all-gather.5
  146.6 105.0 all-gather.7

commit v4 on v3

--- a/solution.py
+++ b/solution.py
@@ -1499,6 +1499,56 @@
         return finished
 
 
+class Overlapped:
+    def __init__(self, nz, ids):
+        self.nz = nz
+        self.ids = ids
+        self.value = None
+        self.new = None
+        self.total = None
+        self.inward = None
+        self.met = []
+        self.got = self.arriving = ()
+        self.sent = ()
+        self.done = {}
+
+    def prepare(self, new, *earlier):
+        if self.nz != 4:
+            if new:
+                self.done[new[0]] = (lax.psum(new[1], "rep"),) * 2
+            return
+        chunk = new and new[1]
+        pair = (None, None)
+        self.total = None
+        if len(self.met) > 1 or (self.met and new is None):
+            self.total, *pair = self.met.pop(0)
+        chunk, pair, _ = lax.optimization_barrier((chunk, tuple(pair), (self.sent, earlier)))
+        self.new = new and (new[0], chunk)
+        self.value = chunk
+        if self.total is not None:
+            self.value = line_values(self.ids, None, None, *pair, chunk)[0]
+            self.sent = self.value
+
+    def step(self, *earlier):
+        if self.nz != 4:
+            return
+        before = self.inward
+        if self.value is not None:
+            value = after(self.value, self.sent, self.got, earlier)
+            got = along(value, OUTWARD if self.new is None else SWAP)
+            self.got = got
+            if self.total is not None:
+                self.done[self.total] = (value, got)
+        self.inward = self.new and (self.new[0], self.new[1], got)
+        if before is not None:
+            name, *pair = before
+            pair = after(tuple(pair), self.sent, earlier)
+            value = line_values(self.ids, *pair, None, None, None)[0]
+            self.sent = (value,) + tuple(pair[2] for pair in self.met[-1:])
+            self.met.append((name, value, along(value, MIDDLE)))
+            self.arriving = (self.got, self.met[-1][2])
+
+
 def gather_first(a, nf, *earlier):
     chips = nf // 2
     a = after(a, *earlier)
@@ -1756,19 +1806,17 @@
     tok = gather_pieces(tok, nf, gains)
     own.append(to_chip(after(sends[2], tok[3:]), nf, 3))
     up_plane = pack_columns(after(w_gate_up, packed), None, up_table, plane, True, ids)
-    up_plane = exchange(after(up_plane, tok[3:]), nf)
 
     live_own = (jnp.arange(TOK_DEV, dtype=jnp.int32) < held).astype(f32)[:, None]
     seeded = cotangent.astype(f32) * live_own
     d_ffn_own = seeded.astype(bf16)
 
     normed_in = norm_rows(after(tok, d_ffn_own), gains)
-    first_other = swap_core(after(first, tok, own[1], own[2]), nf)
-    projected = [project_planes(normed_in, first, first_other, ids)]
-    own = stack_blocks(after(own, projected[0]))
+    first_other = swap_core(after(first, normed_in, up_plane, own[1], own[2]), nf)
+    up_plane = exchange(after(up_plane, own[3]), nf)
+    own = stack_blocks(own)
     other = swap_core(own, nf)
-    ffn_parts = gather_first(d_ffn_own, nf, own)
-    up_own = lax.all_gather(after(up_plane, own), "rep", axis=0)
+    projected = [project_planes(after(normed_in, own), first, first_other, ids)]
 
     def forward(p, *before):
         return mixer_forward(
@@ -1776,36 +1824,31 @@
             hl, pair, p,
         )
 
-    gated0, *saved0 = forward(0, own)
-    projected.append(project_planes(after(normed_in, gated0, ffn_parts), own, other, ids))
-    ffn_parts = gather_pieces(ffn_parts, nf, gated0)
+    gated0, *saved0 = forward(0, other)
+    up_own = lax.all_gather(after(up_plane, gated0), "rep", axis=0)
+    sends = after(d_ffn_own, gated0, up_plane)
+    ffn_parts = [d_ffn_own] + [to_chip(sends, nf, j) for j in range(1, chips)]
+    projected.append(project_planes(after(normed_in, gated0), own, other, ids))
     gated1, *saved1 = forward(1)
     gated = [gated0, gated1]
     saved = [saved0, saved1]
-    branch_parts = scatter_start(
-        times_rows(after(gated, ffn_parts), w_out, out_other, ids), nf
-    )
+    branch_parts = scatter_start(times_rows(gated, w_out, out_other, ids), nf)
     d_ffn = jnp.concatenate(after(ffn_parts, branch_parts[0]), axis=0)
     pieces_in = [(first, first_other), (own, other)]
     down_chip = join_cores(w_down, after(down_other, branch_parts[0]), ids)
     out_chip = join_cores(w_out, after(out_other, branch_parts[0]), ids)
     branch_parts = scatter_middle(branch_parts, nf, d_ffn, down_chip, out_chip)
-    up_own = after(up_own, branch_parts)
+
+    middle, normed_own = middle_rows(branch_parts, tokens, gains, ids)
+    normed_mid = gather_first(normed_own, nf)
+    up_own = after(up_own, normed_mid)
     up_other = swap_core(up_own, nf)
     in_other = swap_core(after(normed_in, up_other), nf)
-
-    middle, normed_own = middle_rows(branch_parts, tokens, gains, ids)
-    normed_mid = gather_first(normed_own, nf)
     normed_mid = jnp.concatenate(gather_pieces(normed_mid, nf), axis=0)
     hidden, d_gate_up = feed_forward(normed_mid, up_own, up_other, down_chip, d_ffn, ids)
 
-    line = Line(nz, ids)
-    done = {}
-
-    def step(new, *earlier):
-        got = line.step(new, *earlier)
-        if got is not None:
-            done[got[0]] = got[1]
+    line = Overlapped(nz, ids)
+    done = line.done
 
     d_up_other = swap_core(d_gate_up, nf)
     mid_other = swap_core(normed_mid, nf)
@@ -1814,33 +1857,33 @@
     half = mine.shape[0] // 2
     down0 = mine[:half] + theirs[:half]
     down1 = mine[half:] + theirs[half:]
-    step(("down0", down0), down1)
-    z = line.tokens
+    line.prepare(("down0", down0), down1)
+    line.step()
     partial_mid = times_transposed(
         [(after(d_gate_up, down0, down1, d_up_other), up_own, up_other)], ids, False
     )
     mid_parts = scatter_start(partial_mid, nf)
     partial_ffn = times_rows(after([hidden], partial_mid), w_down, down_other, ids)
-    step(("down1", down1), partial_ffn, mid_parts[1], mid_parts[3])
-    mid_first = mid_parts
+    line.prepare(("down1", down1), partial_ffn)
+    line.step()
+    mid_parts = scatter_middle(mid_parts, nf, line.sent)
     grad_up = column_terms(
         [normed_mid, mid_other],
-        [after(d_gate_up, line.sent, mid_first[1], mid_first[3]), d_up_other],
+        [after(d_gate_up, line.sent, mid_parts[0]), d_up_other],
         ids,
         True,
     )
-    mid_parts = scatter_middle(mid_parts, nf)
-    z = line.tokens
-    step(("up0", grad_up[0]))
+    line.prepare(("up0", grad_up[0]))
+    line.step(grad_up[0])
     d_middle, d_branch_own, g_gain_mid = middle_back(
         after(mid_parts, line.sent), middle, cotangent, gains, ids
     )
-    z = line.tokens
     branch_parts = gather_first(d_branch_own, nf)
-    d_branch = gather_pieces(branch_parts, nf, z)
-    step(("up1", grad_up[1]))
-    z = line.tokens
-    d_branch = jnp.concatenate(d_branch, axis=0)
+    d_branch = gather_pieces(branch_parts, nf, line.sent)
+    line.prepare(("up1", grad_up[1]), branch_parts)
+    line.step()
+    line.prepare(("up2", grad_up[2]))
+    d_branch = jnp.concatenate(after(d_branch, line.sent), axis=0)
     d_gated = [mm_nt(d_branch, out_chip[p * vv : (p + 1) * vv]) for p in range(groups)]
 
     def backward(p, *before, more=None):
@@ -1849,55 +1892,59 @@
             after(d_gated[p], *before), hl, pair, p, more,
         )
 
-    mine, theirs = row_terms(gated, after(d_branch, d_gated), ids)
+    d_x1, d_dec, g_conv1, g_heads1 = backward(1, line.sent)
+    arriving = line.arriving
+    line.step(d_x1)
+    line.prepare(("up3", grad_up[3]))
+    d_x1_other = swap_core(after(d_x1, arriving), nf)
+    mine, theirs = row_terms(gated, after(d_branch, line.sent), ids)
     half = mine.shape[0] // 2
     theirs = [swap_core(theirs[:half], nf), swap_core(theirs[half:], nf)]
-    step(("up2", grad_up[2]), mine)
-    ffn_first = scatter_start(partial_ffn, nf, line.sent)
-    d_x1, d_dec, g_conv1, g_heads1 = backward(1, line.sent)
-    d_x1_other = swap_core(after(d_x1, line.tokens, ffn_first, theirs), nf)
-    grad_out = mine + jnp.concatenate(theirs, axis=0)
-    step(("up3", grad_up[3]), d_x1)
-    ffn_sends = scatter_middle(ffn_first, nf, line.sent)
-    cols1 = column_terms([normed_in, in_other], [after(d_x1, line.sent, ffn_sends[2], ffn_sends[5]), d_x1_other], ids, False)
-    cols1_all = exchange(cols1, nf)
+    cols1 = column_terms([normed_in, in_other], [after(d_x1, mine), d_x1_other], ids, False)
+    cols1_all = exchange(after(cols1, line.arriving), nf)
+    grad_out = mine + jnp.concatenate(after(theirs, cols1), axis=0)
+    line.step(cols1)
+    d_x0, dec, g_conv0, g_heads0 = backward(0, line.sent, theirs, more=d_dec)
+    arriving = line.arriving
     size = down0.shape[0]
     rest = grad_out.shape[0] - size
-    step(("out0", grad_out[:size]), cols1)
-    d_x0, dec, g_conv0, g_heads0 = backward(0, line.sent, more=d_dec)
-    z = line.tokens
-    d_x0_other = swap_core(after(d_x0, z, cols1_all), nf)
+    line.prepare(("out0", grad_out[:size]), d_x0)
+    line.step()
+    d_x0_other = swap_core(after(d_x0, arriving, cols1_all), nf)
+    cols0 = column_terms([normed_in, in_other], [after(d_x0, line.sent), d_x0_other], ids, False)
+    bands0_all = exchange(after(cols0, line.arriving), nf)
     bands1 = cols1_all.reshape(-1, STREAM)
     at1 = size - rest
-    step(("mix0", jnp.concatenate([grad_out[size:], bands1[:at1]], axis=0)), d_x0)
-    cols0 = column_terms([normed_in, in_other], [after(d_x0, line.sent), d_x0_other], ids, False)
-    z = line.tokens
-    step(("p1", bands1[at1 : at1 + size]), cols0)
-    bands0_all = exchange(cols0, nf)
-    bands0 = bands0_all.reshape(-1, STREAM)
+    line.prepare(("mix0", jnp.concatenate([grad_out[size:], bands1[:at1]], axis=0)), cols0)
+    line.step()
+    line.prepare(("p1", bands1[at1 : at1 + size]))
     right = [d_x0, d_x1]
     partial_in = times_transposed(
         [(after(right[p], line.sent),) + pieces_in[p] for p in range(groups)], ids, True
     )
+    line.step(partial_in)
+    bands0 = bands0_all.reshape(-1, STREAM)
     at1 += size
     left = bands1.shape[0] - at1
     at0 = size - left
-    step(("mix1", jnp.concatenate([bands1[at1:], bands0[:at0]], axis=0)), partial_in)
     in_first = scatter_start(partial_in, nf, line.sent)
     grad_up = None
-    for j in range(2):
+    for j in range(3):
         grad_up = place_blocks(
             grad_up, after(done["up%d" % j], line.sent), ids, j, (chips, shard, 2 * wide)
         )
-    step(("p0", bands0[at0 : at0 + size]), grad_up)
-    for j in range(2, chips):
-        grad_up = place_blocks(
-            grad_up, after(done["up%d" % j], line.sent), ids, j, (chips, shard, 2 * wide)
-        )
-    in_sends = scatter_middle(in_first, nf, grad_up)
-    output = (middle + live_own * scatter_end(after(ffn_sends, line.sent))).astype(bf16)
-    grad_up_all = exchange(after(grad_up, in_sends[2], in_sends[5]), nf)
-    step(("p0last", bands0[at0 + size :]))
+    line.prepare(("mix1", jnp.concatenate([bands1[at1:], bands0[:at0]], axis=0)), grad_up)
+    line.step()
+    line.prepare(("p0", bands0[at0 : at0 + size]))
+    in_sends = scatter_middle(in_first, nf, line.sent)
+    grad_up = place_blocks(
+        grad_up, after(done["up3"], line.sent, in_sends[0]), ids, 3, (chips, shard, 2 * wide)
+    )
+    arriving = line.arriving
+    line.step(grad_up)
+    line.prepare(("p0last", bands0[at0 + size :]))
+    grad_up_all = exchange(after(grad_up, arriving, in_sends[2], in_sends[5]), nf)
+    ffn_first = scatter_start(partial_ffn, nf, grad_up_all)
     grad_tokens, g_gain_in = tokens_back(after(in_sends, line.sent), tokens, d_middle, gains)
     blocks = pack_small_grads(
         [g_conv0, g_conv1],
@@ -1912,6 +1959,8 @@
         qk,
         vv,
     )
+    line.step(blocks)
+    line.prepare(None)
     def tile_of(p, c, t):
         at = c * groups + p
         q_tiles, v_tiles = qk // 128, vv // 128
@@ -1941,15 +1990,20 @@
         ]
         return finish_projection(grad_proj, after(done[name], *before), ids, pairs, w_proj.shape)
 
-    step(None, grad_tokens)
     grad_proj = place(None, "mix0", line.sent)
+    line.step(grad_proj)
+    line.prepare(None)
+    grad_up = finish_feed_forward(after(grad_up_all, line.sent))
+    ffn_sends = scatter_middle(ffn_first, nf, grad_up)
+    line.step(grad_up)
+    line.prepare(None)
     grad_proj = place(grad_proj, "p1", line.sent)
-    grad_proj = place(grad_proj, "mix1")
-    small_sum = lax.all_to_all(after(blocks, grad_proj, grad_up_all), "fsdp", 0, 0, tiled=True)
-    step(None, grad_proj)
-    grad_up = finish_feed_forward(after(grad_up_all, line.sent))
-    grad_proj = place(grad_proj, "p0", grad_up)
-    small_sum = lax.all_gather(jnp.sum(after(small_sum, grad_proj), axis=0), "rep", axis=0)
+    grad_proj = place(grad_proj, "mix1", line.sent)
+    small_sum = lax.all_to_all(after(blocks, ffn_sends[2], ffn_sends[5]), "fsdp", 0, 0, tiled=True)
+    output = (middle + live_own * scatter_end(after(ffn_sends, grad_proj))).astype(bf16)
+    line.step(grad_proj, output)
+    small_sum = lax.all_gather(jnp.sum(after(small_sum, line.sent), axis=0), "rep", axis=0)
+    grad_proj = place(grad_proj, "p0", line.sent)
     small_sum = jnp.sum(small_sum, axis=0)
     done["p0last"] = after(done["p0last"], grad_proj)
     grad_proj = place(grad_proj, "p0last")

time: 956 us -> 947 us (level)
  waiting for transfers between devices: 235 us -> 202 us
  Pallas kernels: 453 us -> 470 us
    ppermute x38 -> x37, waiting for transfers between devices: 178 us -> 133 us  [to_chip(): return lax.ppermute(a, 'fsdp', [(i, i ^ 2 * j) for i in range(nf)])]
    pallas_call x13 -> x24, Pallas kernels: 53.5 us -> 69.5 us  [line_values(): pl.pallas_call(body, grid=(steps,), in_specs=[SMEM] + [block] * len(args)...]
    ppermute x26 -> x27, waiting for transfers between devices: 50.7 us -> 63.5 us  [along(): return lax.ppermute(a, 'rep', pairs)]
    unnamed x138 -> x127, local copies, waits for them, and re-layouts: 36.8 us -> 31.8 us
    ppermute x38 -> x37, starting transfers between devices: 42.4 us -> 47.3 us  [to_chip(): return lax.ppermute(a, 'fsdp', [(i, i ^ 2 * j) for i in range(nf)])]
    ppermute x26 -> x27, starting transfers between devices: 54.7 us -> 54.2 us  [along(): return lax.ppermute(a, 'rep', pairs)]
  transfers between devices with their start and end apart: 84 -> 84, of which waited for: 34 -> 30; matrix products, arithmetic and copies ran while one was open for 7% -> 8% of each run, Pallas kernels for 46% -> 48%
where the time goes in v4:
time: 947 us; the launch traced here: 939 us
  Pallas kernels  470 us (50%)
  waiting for transfers between devices  202 us (21%)
  starting transfers between devices  124 us (13%)
  local copies, waits for them, and re-layouts  54 us (6%)
  other arithmetic  36.9 us (4%)
  blocking collectives  27 us (3%)
  between operations  15.1 us (2%)
    ppermute x37, waiting for transfers between devices, to_chip(): return lax.ppermute(a, 'fsdp', [(i, i ^ 2 * j) for i in range(nf)])  133 us
    pallas_call x24, Pallas kernels, line_values(): pl.pallas_call(body, grid=(steps,), in_specs=[SMEM] + [block] * len(args)...  69.5 us
    ppermute x27, waiting for transfers between devices, along(): return lax.ppermute(a, 'rep', pairs)  63.5 us
    ppermute x27, starting transfers between devices, along(): return lax.ppermute(a, 'rep', pairs)  54.2 us
    pallas_call x2, Pallas kernels, mixer_backward(): pl.pallas_call(body, grid=(slots,), in_specs=[pl.BlockSpec(memory_space=p...  52.5 us
    pallas_call x3, Pallas kernels, column_terms(): pl.pallas_call(body, grid_spec=pltpu.PrefetchScalarGridSpec(num_scalar_pr...  48.8 us
    ppermute x37, starting transfers between devices, to_chip(): return lax.ppermute(a, 'fsdp', [(i, i ^ 2 * j) for i in range(nf)])  47.3 us
    pallas_call x2, Pallas kernels, times_transposed(): pl.pallas_call(body, grid_spec=pltpu.PrefetchScalarGridSpec(num_scalar_pr...  43.7 us
  transfers between devices with their start and end apart: 84, of which 30 were waited for; matrix products, arithmetic and copies ran while one was open for 8% of the time, Pallas kernels for 48%

profile of v4, /device:TPU:0, one launch (start us, length us, event | category | flops | bytes accessed | tf_op | source)
XLA Modules:
  0.0 938.7 jit_solution(5114803602863977485)
XLA Ops:
  18.9 5.7 pack_relative.3
  24.6 4.2 collective-permute-done.1
  34.1 8.1 all_to_all.30
  45.8 21.4 %collective-permute-done.5.refs_1_ = bf16[256,2048]{1,0:T(8,128)(2,1)S(1)} collective-permute-done((bf16[256,2048]{1,0:T(8,128)(2,1)}, bf16[256,2048]{1,0:T(8,128)(2,1)S(1)}, u32[]{:S(2)}, u32[]{:S(2)}) %collective-permute-start.5) | collective-permute-done | bytes 1048608 | tf_op jit(solution)/shard_map/ppermute | solution.py:1401
  71.7 10.8 %collective-permute-done.7.refs_3_ = bf16[128,2048]{1,0:T(8,128)(2,1)S(1)} collective-permute-done((bf16[128,2048]{1,0:T(8,128)(2,1)S(1)}, bf16[128,2048]{1,0:T(8,128)(2,1)S(1)}, u32[]{:S(2)}, u32[]{:S(2)}) %collective-permute-start.7) | collective-permute-done | bytes 524320 | tf_op jit(solution)/shard_map/ppermute | solution.py:1401
  86.0 3.5 pack_columns.1
  90.9 5.8 norm_rows.1.x_ref.a_ref
  100.9 14.3 %collective-permute-done.11.refs_3_ = bf16[256,1536]{1,0:T(8,128)(2,1)} collective-permute-done((bf16[256,1536]{1,0:T(8,128)(2,1)}, bf16[256,1536]{1,0:T(8,128)(2,1)}, u32[]{:S(2)}, u32[]{:S(2)}) %collective-permute-start.11) | collective-permute-done | bytes 786464 | tf_op jit(solution)/shard_map/ppermute | solution.py:1401
  118.3 4.3 all-to-all-start.1
  124.7 13.3 %project.2.refs_1_.refs_2_ = f32[1024,1664]{1,0:T(8,128)} custom-call(s32[4]{0:T(128)} %pad_add_fusion.ids_ref.refs_0_, bf16[1024,2048]{1,0:T(8,128)(2,1)} %norm_rows.1.x_ref.a_ref, bf16[4,4,64,1664]{3,2,1,0:T(8,128)(2,1)} %bitcast.42, bf16[4,4,64,1664]{3,2,1,0:T(8,128)(2,1)} %copy-done.2), custom_call_target="tpu_custom_call" | custom-call | flops 1 | bytes 1 | tf_op jit(solution)/shard_map/project/pallas_call | solution.py:1064
  138.1 20.4 %mixer_forward.2 = (bf16[1024,512]{1,0:T(8,128)(2,1)}, f32[1024,512]{1,0:T(8,128)}, bf16[1024,512]{1,0:T(8,128)(2,1)}, bf16[1024,256]{1,0:T(8,128)(2,1)}, bf16[4...) custom-call(s32[4]{0:T(128)} %pad_add_fusion.ids_ref.refs_0_, f32[1024,1664]{1,0:T(8,128)} %project.2.refs_1_.refs_2_, ...), custom_call_target="tpu_custom_call" | custom-call | flops 1 | bytes 1 | tf_op jit(solution)/shard_map/mixer_forward/pallas_call | solution.py:227
  162.1 12.4 %project.3.refs_1_ = f32[1024,1536]{1,0:T(8,128)} custom-call(s32[4]{0:T(128)} %pad_add_fusion.ids_ref.refs_0_, bf16[1024,2048]{1,0:T(8,128)(2,1)} %norm_rows.1.x_ref.a_ref, bf16[1,4,256,1536]{3,2,1,0:T(8,128)(2,1)} %stack_blocks.1.own_ref.refs_4_, bf16[1,4,256,1536]{3,2,1,0:T(8,128)(2,1)} %collective-permute-done.13.other_ref.refs_5_), custom_call_target="tpu_custom_call" | custom-call | flops 1 | bytes 1 | tf_op jit(solution)/shard_map/project/pallas_call | solution.py:1064
  174.4 20.3 %mixer_forward.3 = (bf16[1024,512]{1,0:T(8,128)(2,1)}, f32[1024,512]{1,0:T(8,128)}, bf16[1024,512]{1,0:T(8,128)(2,1)}, bf16[1024,256]{1,0:T(8,128)(2,1)}, bf16[4...) custom-call(s32[4]{0:T(128)} %pad_add_fusion.ids_ref.refs_0_, f32[1024,1536]{1,0:T(8,128)} %project.3.refs_1_, ...), custom_call_target="tpu_custom_call" | custom-call | flops 1 | bytes 1 | tf_op jit(solution)/shard_map/mixer_forward/pallas_call | solution.py:227
  194.7 10.6 %times_rows.2 = (bf16[512,1024]{1,0:T(8,128)(2,1)}, bf16[512,1024]{1,0:T(8,128)(2,1)}, bf16[512,1024]{1,0:T(8,128)(2,1)}, bf16[512,1024]{1,0:T(8,128)(2,1)}) custom-call(s32[4]{0:T(128)} %pad_add_fusion.ids_ref.refs_0_, bf16[1024,512]{1,0:T(8,128)(2,1)} %get-tuple-element.308.refs_0_, bf16[1024,512]{1,0:T(8,128)(2,1)} %get-tuple-element.311.refs_1_, ...), custom_call_target="tpu_custom_call" | custom-call | flops 1 | bytes 1 | tf_op jit(solution)/shard_map/times_rows/pallas_call | solution.py:1207
  208.7 5.7 join_cores.2.down_ref
  214.4 5.1 join_cores.3
  225.1 5.2 collective-permute-done.14.b_ref.refs_1_
  237.3 10.2 %collective-permute-done.19.refs_2_ = bf16[256,1024]{1,0:T(8,128)(2,1)S(1)} collective-permute-done((bf16[256,1024]{1,0:T(8,128)(2,1)}, bf16[256,1024]{1,0:T(8,128)(2,1)S(1)}, u32[]{:S(2)}, u32[]{:S(2)}) %collective-permute-start.19) | collective-permute-done | bytes 524320 | tf_op jit(solution)/shard_map/ppermute | solution.py:1401
  249.4 4.6 middle_rows.1
  256.0 20.6 %collective-permute-done.21 = bf16[256,2048]{1,0:T(8,128)(2,1)} collective-permute-done((bf16[256,2048]{1,0:T(8,128)(2,1)}, bf16[256,2048]{1,0:T(8,128)(2,1)}, u32[]{:S(2)}, u32[]{:S(2)}) %collective-permute-start.21) | collective-permute-done | bytes 1048608 | tf_op jit(solution)/shard_map/ppermute | solution.py:1401
  289.0 4.0 collective-permute-done.23
  293.8 3.7 collective-permute-done.24
  300.9 28.0 %feed_forward.1 = (bf16[1024,1408]{1,0:T(8,128)(2,1)}, bf16[1024,2816]{1,0:T(8,128)(2,1)}) custom-call(s32[4]{0:T(128)} %pad_add_fusion.ids_ref.refs_0_, bf16[1024,2048]{1,0:T(8,128)(2,1)} %constant_dynamic-update-slice_fusion.4.x_ref.a_ref, bf16[4,4,64,2816]{3,2,1,0:T(8,128)(2,1)} %bitcast.39, bf16[4,4,64,2816]{3,2,1,0:T(8,128)(2,1)} %copy-done.1, ...), custom_call_target="tpu_custom_call" | custom-call | flops 1 | bytes 1 | tf_op jit(solution)/shard_map/feed_forward/pallas_call | solution.py:1131
  329.4 10.7 %row_terms.2 = (bf16[704,2048]{1,0:T(8,128)(2,1)}, bf16[704,2048]{1,0:T(8,128)(2,1)}) custom-call(s32[4]{0:T(128)} %pad_add_fusion.ids_ref.refs_0_, bf16[1024,1408]{1,0:T(8,128)(2,1)} %get-tuple-element.344.refs_0_, bf16[1024,2048]{1,0:T(8,128)(2,1)} %constant_dynamic-update-slice_fusion.d_ref.refs_1_), custom_call_target="tpu_custom_call" | custom-call | flops 1 | bytes 1 | tf_op jit(solution)/shard_map/row_terms/pallas_call | solution.py:1379
  340.1 5.5 collective-permute-done.27
  349.4 20.4 %times_transposed.2 = (bf16[512,1024]{1,0:T(8,128)(2,1)}, bf16[512,1024]{1,0:T(8,128)(2,1)}, bf16[512,1024]{1,0:T(8,128)(2,1)}, bf16[512,1024]{1,0:T(8,128)(2,1)}) custom-call(s32[4]{0:T(128)} %pad_add_fusion.ids_ref.refs_0_, bf16[1024,2816]{1,0:T(8,128)(2,1)} %get-tuple-element.366.refs_0_.ra_ref, bf16[4,4,64,2816]{3,2,1,0:T(8,128)(2,1)} %bitcast.40, ...), custom_call_target="tpu_custom_call" | custom-call | flops 1 | bytes 1 | tf_op jit(solution)/shard_map/times_transposed/pallas_call | solution.py:1270
  371.4 12.4 %times_rows.3 = (bf16[512,1024]{1,0:T(8,128)(2,1)}, bf16[512,1024]{1,0:T(8,128)(2,1)}, bf16[512,1024]{1,0:T(8,128)(2,1)}, bf16[512,1024]{1,0:T(8,128)(2,1)}) custom-call(s32[4]{0:T(128)} %pad_add_fusion.ids_ref.refs_0_, bf16[1024,1408]{1,0:T(8,128)(2,1)} %get-tuple-element.344.refs_0_, bf16[704,2048]{1,0:T(8,128)(2,1)} %refs_1_.1, ...), custom_call_target="tpu_custom_call" | custom-call | flops 1 | bytes 1 | tf_op jit(solution)/shard_map/times_rows/pallas_call | solution.py:1207
  388.9 6.1 collective-permute-done.30.b_ref.refs_1_
  401.0 22.2 %column_terms.3 = (bf16[352,2048]{1,0:T(8,128)(2,1)}, bf16[352,2048]{1,0:T(8,128)(2,1)}, bf16[352,2048]{1,0:T(8,128)(2,1)}, bf16[352,2048]{1,0:T(8,128)(2,1)}) custom-call(s32[4]{0:T(128)} %pad_add_fusion.ids_ref.refs_0_, bf16[1024,2048]{1,0:T(8,128)(2,1)} %constant_dynamic-update-slice_fusion.4.x_ref.a_ref, ...), custom_call_target="tpu_custom_call" | custom-call | flops 1 | bytes 1 | tf_op jit(solution)/shard_map/column_terms/pallas_call | solution.py:1333
  428.1 6.4 middle_back.1
  439.3 18.9 %collective-permute-done.37 = bf16[256,2048]{1,0:T(8,128)(2,1)S(1)} collective-permute-done((bf16[256,2048]{1,0:T(8,128)(2,1)}, bf16[256,2048]{1,0:T(8,128)(2,1)S(1)}, u32[]{:S(2)}, u32[]{:S(2)}) %collective-permute-start.37) | collective-permute-done | bytes 1048608 | tf_op jit(solution)/shard_map/ppermute | solution.py:1401
  473.3 3.8 collective-permute-start.44
  484.4 3.8 fusion.2.refs_11_
  488.2 26.0 %mixer_backward.2 = (bf16[1024,1536]{1,0:T(8,128)(2,1)}, f32[1024,128]{1,0:T(8,128)}, f32[8,1024]{1,0:T(8,128)}, f32[8,256]{1,0:T(8,128)}) custom-call(s32[4]{0:T(128)} %pad_add_fusion.ids_ref.refs_0_, f32[1024,1536]{1,0:T(8,128)} %project.3.refs_1_, f32[1024,1664]{1,0:T(8,128)} %project.2.refs_1_.refs_2_, f32[8,1024]{1,0:T(8,128)} %get-tuple-element.310.refs_3_, ...), custom_call_target="tpu_custom_call" | custom-call | flops 1 | bytes 1 | tf_op jit(solution)/shard_map/mixer_backward/pallas_call | solution.py:489
  521.9 8.6 row_terms.3
  530.6 12.6 %column_terms.4 = bf16[4,192,2048]{2,1,0:T(8,128)(2,1)} custom-call(s32[4]{0:T(128)} %pad_add_fusion.ids_ref.refs_0_, bf16[1024,2048]{1,0:T(8,128)(2,1)} %norm_rows.1.x_ref.a_ref, bf16[1024,2048]{1,0:T(8,128)(2,1)} %collective-permute-done.29.b_ref, bf16[1024,1536]{1,0:T(8,128)(2,1)} %get-tuple-element.443.ra_ref.refs_3_, ...), custom_call_target="tpu_custom_call" | custom-call | flops 1 | bytes 1 | tf_op jit(solution)/shard_map/column_terms/pallas_call | solution.py:1333
  543.1 5.4 collective-permute-done.46.refs_1_
  549.7 3.7 all-to-all-start.2
  553.4 6.3 collective-permute-start.48
  567.3 5.3 fusion.refs_11_
  572.6 26.6 %mixer_backward.3 = (bf16[1024,1664]{1,0:T(8,128)(2,1)}, f32[1024,128]{1,0:T(8,128)}, f32[8,1024]{1,0:T(8,128)}, f32[8,256]{1,0:T(8,128)}) custom-call(s32[4]{0:T(128)} %pad_add_fusion.ids_ref.refs_0_, f32[1024,1664]{1,0:T(8,128)} %project.2.refs_1_.refs_2_, f32[1024,1664]{1,0:T(8,128)} %project.2.refs_1_.refs_2_, f32[8,1024]{1,0:T(8,128)} %get-tuple-element.305.refs_3_, ...), custom_call_target="tpu_custom_call" | custom-call | flops 1 | bytes 1 | tf_op jit(solution)/shard_map/mixer_backward/pallas_call | solution.py:489
  600.4 4.2 maximum_add_fusion
  615.2 14.0 %column_terms.5 = bf16[4,208,2048]{2,1,0:T(8,128)(2,1)} custom-call(s32[4]{0:T(128)} %pad_add_fusion.ids_ref.refs_0_, bf16[1024,2048]{1,0:T(8,128)(2,1)} %norm_rows.1.x_ref.a_ref, bf16[1024,2048]{1,0:T(8,128)(2,1)} %collective-permute-done.29.b_ref, bf16[1024,1664]{1,0:T(8,128)(2,1)} %get-tuple-element.442.ra_ref.refs_0_, ...), custom_call_target="tpu_custom_call" | custom-call | flops 1 | bytes 1 | tf_op jit(solution)/shard_map/column_terms/pallas_call | solution.py:1333
  632.4 10.0 %collective-permute-done.52.refs_1_.last_ref = bf16[352,2048]{1,0:T(8,128)(2,1)} collective-permute-done((bf16[352,2048]{1,0:T(8,128)(2,1)}, bf16[352,2048]{1,0:T(8,128)(2,1)}, u32[]{:S(2)}, u32[]{:S(2)}) %collective-permute-start.52) | collective-permute-done | bytes 1441824 | tf_op jit(solution)/shard_map/ppermute | solution.py:1417
  642.8 4.1 all-to-all-start.3
  656.6 23.3 %times_transposed.3 = (bf16[512,1024]{1,0:T(8,128)(2,1)}, bf16[512,1024]{1,0:T(8,128)(2,1)}, bf16[512,1024]{1,0:T(8,128)(2,1)}, bf16[512,1024]{1,0:T(8,128)(2,1)}) custom-call(s32[4]{0:T(128)} %pad_add_fusion.ids_ref.refs_0_, bf16[1024,1664]{1,0:T(8,128)(2,1)} %get-tuple-element.442.ra_ref.refs_0_, bf16[4,4,64,1664]{3,2,1,0:T(8,128)(2,1)} %bitcast.43, ...), custom_call_target="tpu_custom_call" | custom-call | flops 1 | bytes 1 | tf_op jit(solution)/shard_map/times_transposed/pallas_call | solution.py:1270
  679.8 7.6 collective-permute-start.56
  712.6 4.8 collective-permute-done.56.refs_1_.last_ref
  737.8 4.1 collective-permute-done.63.refs_2_
  743.4 5.1 collective-permute-done.61.refs_1_
  748.5 5.1 all-to-all-start.4
  753.6 6.4 collective-permute-start.67
  767.7 5.9 tokens_back.1
  775.3 14.2 %collective-permute-done.67.refs_1_.last_ref = bf16[352,2048]{1,0:T(8,128)(2,1)S(1)} collective-permute-done((bf16[352,2048]{1,0:T(8,128)(2,1)S(1)}, bf16[352,2048]{1,0:T(8,128)(2,1)S(1)}, u32[]{:S(2)}, u32[]{:S(2)}) %collective-permute-start.67) | collective-permute-done | bytes 1441824 | tf_op jit(solution)/shard_map/ppermute | solution.py:1417
  798.7 4.9 finish_projection.5.refs_0_
  803.6 15.7 %collective-permute-done.69.refs_1_.last_ref = bf16[352,2048]{1,0:T(8,128)(2,1)} collective-permute-done((bf16[352,2048]{1,0:T(8,128)(2,1)}, bf16[352,2048]{1,0:T(8,128)(2,1)}, u32[]{:S(2)}, u32[]{:S(2)}) %collective-permute-start.69) | collective-permute-done | bytes 1441824 | tf_op jit(solution)/shard_map/ppermute | solution.py:1417
  835.3 10.7 %finish_feed_forward.1 = f32[256,11264]{1,0:T(8,128)} custom-call(bf16[4,256,2816]{2,1,0:T(8,128)(2,1)} %all-to-all-done.4.x_ref), custom_call_target="tpu_custom_call" | custom-call | flops 1 | bytes 1 | tf_op jit(solution)/shard_map/finish_feed_forward/pallas_call | solution.py:1033
  846.0 5.3 collective-permute-done.73.last_ref
  867.3 6.9 finish_projection.6.refs_0_
  874.2 7.1 finish_projection.7.refs_0_
  889.0 3.4 all-to-all-start.5
  895.0 6.2 finish_projection.8.refs_0_
  901.3 18.8 %all-gather.2 = f32[32,1024]{1,0:T(8,128)S(1)} all-gather(f32[8,1024]{1,0:T(8,128)S(1)} %reduce_sum.28), channel_id=4, replica_groups=mesh['rep'=4,'fsdp'=8] {'rep'}, dimensions={0}, use_global_device_ids=true | all-gather | bytes 163840 | tf_op jit(solution)/shard_map/all_gather | solution.py:2005
  923.9 6.3 finish_projection.9
  (352 shorter events, 282.5 us)
Async XLA Ops:
  7.2 92.8 %all-gather.6.cloned.1.call-start = ((), (), s32[]{:S(2)}) async-start(), calls=%async_computation.6 | async-start | bytes 4259840 | tf_op jit(solution)/shard_map/all_gather | solution.py:1804
  42.2 25.0 %collective-permute-start.5 = (bf16[256,2048]{1,0:T(8,128)(2,1)}, bf16[256,2048]{1,0:T(8,128)(2,1)S(1)}, u32[]{:S(2)}, u32[]{:S(2)}) collective-permute-start(bf16[256,2048]{1,0:T(8,128)(2,1)} %t_ref.3), channel_id=1, source_target_pairs={{0,2},{1,3},{2,0},{3,1},{4,6},{5,7},{6,4},{7,5},{8,10},{9,11},{10,... | collective-permute-start | bytes 3145736 | tf_op jit(solution)/shard_map/ppermute | solution.py:1401
  42.8 24.8 %collective-permute-start.6 = (bf16[256,2048]{1,0:T(8,128)(2,1)}, bf16[256,2048]{1,0:T(8,128)(2,1)S(1)}, u32[]{:S(2)}, u32[]{:S(2)}) collective-permute-start(bf16[256,2048]{1,0:T(8,128)(2,1)} %t_ref.3), channel_id=1, source_target_pairs={{0,4},{1,5},{2,6},{3,7},{4,0},{5,1},{6,2},{7,3},{8,12},{9,13},{10,... | collective-permute-start | bytes 3145736 | tf_op jit(solution)/shard_map/ppermute | solution.py:1401
  69.6 30.4 %collective-permute-start.9 = (bf16[256,1536]{1,0:T(8,128)(2,1)}, bf16[256,1536]{1,0:T(8,128)(2,1)S(1)}, u32[]{:S(2)}, u32[]{:S(2)}) collective-permute-start(bf16[256,1536]{1,0:T(8,128)(2,1)} %get-tuple-element.293), channel_id=1, source_target_pairs={{0,2},{1,3},{2,0},{3,1},{4,6},{5,7},{6,4},{7,5},{8,10},{9,11},{10,... | collective-permute-start | bytes 2359304 | tf_op jit(solution)/shard_map/ppermute | solution.py:1401
  70.3 29.7 %collective-permute-start.10 = (bf16[256,1536]{1,0:T(8,128)(2,1)}, bf16[256,1536]{1,0:T(8,128)(2,1)}, u32[]{:S(2)}, u32[]{:S(2)}) collective-permute-start(bf16[256,1536]{1,0:T(8,128)(2,1)} %get-tuple-element.294), channel_id=1, source_target_pairs={{0,4},{1,5},{2,6},{3,7},{4,0},{5,1},{6,2},{7,3},{8,12},{9,13},{10,... | collective-permute-start | bytes 2359304 | tf_op jit(solution)/shard_map/ppermute | solution.py:1401
  83.1 32.1 %collective-permute-start.11 = (bf16[256,1536]{1,0:T(8,128)(2,1)}, bf16[256,1536]{1,0:T(8,128)(2,1)}, u32[]{:S(2)}, u32[]{:S(2)}) collective-permute-start(bf16[256,1536]{1,0:T(8,128)(2,1)} %get-tuple-element.296), channel_id=1, source_target_pairs={{0,6},{1,7},{2,4},{3,5},{4,2},{5,3},{6,0},{7,1},{8,14},{9,15},{10,... | collective-permute-start | bytes 2359304 | tf_op jit(solution)/shard_map/ppermute | solution.py:1401
  100.8 22.1 %collective-permute-start.12 = (bf16[4,4,64,1664]{3,2,1,0:T(8,128)(2,1)}, bf16[4,4,64,1664]{3,2,1,0:T(8,128)(2,1)S(1)}, u32[]{:S(2)}, u32[]{:S(2)}) collective-permute-start(bf16[4,4,64,1664]{3,2,1,0:T(8,128)(2,1)} %bitcast.41), channel_id=1, source_target_pairs={{0,1},{1,0},{2,3},{3,2},{4,5},{5,4},{6,7},{7,6},{8,9},{9,8},{10,11... | collective-permute-start | bytes 10223624 | tf_op jit(solution)/shard_map/ppermute | solution.py:1405
  118.3 19.7 %collective-permute-start.13 = (bf16[1,4,256,1536]{3,2,1,0:T(8,128)(2,1)}, bf16[1,4,256,1536]{3,2,1,0:T(8,128)(2,1)}, u32[]{:S(2)}, u32[]{:S(2)}) collective-permute-start(bf16[1,4,256,1536]{3,2,1,0:T(8,128)(2,1)} %stack_blocks.1.own_ref.refs_4_), channel_id=1, source_target_pairs={{0,1},{1,0},{2,3},{3,2},{4,5},{5,4},{6,7},{7,6},{8,9},{9,8},{10,11... | collective-permute-start | bytes 9437192 | tf_op jit(solution)/shard_map/ppermute | solution.py:1405
  118.3 40.1 %all-to-all-start.1 = ((bf16[4,64,2816]{2,1,0:T(8,128)(2,1)}), bf16[4,64,2816]{2,1,0:T(8,128)(2,1)}, u32[]{:S(2)}, u32[]{:S(2)}) async-start(bf16[4,64,2816]{2,1,0:T(8,128)(2,1)} %pack_columns.1), calls=%async_computation.1 | async-start | bytes 2883584 | tf_op jit(solution)/shard_map/all_to_all | solution.py:1626
  122.7 154.8 %all-gather.8.cloned.1.call-start = ((), (), s32[]{:S(2)}) async-start(), calls=%async_computation.7 | async-start | bytes 7208960 | tf_op jit(solution)/shard_map/all_gather | solution.py:1828
  158.5 61.0 %collective-permute-start.16 = (bf16[256,2048]{1,0:T(8,128)(2,1)S(1)}, bf16[256,2048]{1,0:T(8,128)(2,1)S(1)}, u32[]{:S(2)}, u32[]{:S(2)}) collective-permute-start(bf16[256,2048]{1,0:T(8,128)(2,1)S(1)} %copy-done.28), channel_id=1, source_target_pairs={{0,2},{1,3},{2,0},{3,1},{4,6},{5,7},{6,4},{7,5},{8,10},{9,11},{10,... | collective-permute-start | bytes 3145736 | tf_op jit(solution)/shard_map/ppermute | solution.py:1401
  160.5 59.0 %collective-permute-start.17 = (bf16[256,2048]{1,0:T(8,128)(2,1)S(1)}, bf16[256,2048]{1,0:T(8,128)(2,1)S(1)}, u32[]{:S(2)}, u32[]{:S(2)}) collective-permute-start(bf16[256,2048]{1,0:T(8,128)(2,1)S(1)} %copy-done.28), channel_id=1, source_target_pairs={{0,4},{1,5},{2,6},{3,7},{4,0},{5,1},{6,2},{7,3},{8,12},{9,13},{10,... | collective-permute-start | bytes 3145736 | tf_op jit(solution)/shard_map/ppermute | solution.py:1401
  162.0 57.6 %collective-permute-start.18 = (bf16[256,2048]{1,0:T(8,128)(2,1)S(1)}, bf16[256,2048]{1,0:T(8,128)(2,1)}, u32[]{:S(2)}, u32[]{:S(2)}) collective-permute-start(bf16[256,2048]{1,0:T(8,128)(2,1)S(1)} %copy-done.28), channel_id=1, source_target_pairs={{0,6},{1,7},{2,4},{3,5},{4,2},{5,3},{6,0},{7,1},{8,14},{9,15},{10,... | collective-permute-start | bytes 3145736 | tf_op jit(solution)/shard_map/ppermute | solution.py:1401
  205.3 24.9 %collective-permute-start.14 = (bf16[512,1024]{1,0:T(8,128)(2,1)}, bf16[512,1024]{1,0:T(8,128)(2,1)S(1)}, u32[]{:S(2)}, u32[]{:S(2)}) collective-permute-start(bf16[512,1024]{1,0:T(8,128)(2,1)} %get-tuple-element.313), channel_id=1, source_target_pairs={{0,2},{1,3},{2,0},{3,1},{4,6},{5,7},{6,4},{7,5},{8,10},{9,11},{10,... | collective-permute-start | bytes 3145736 | tf_op jit(solution)/shard_map/ppermute | solution.py:1401
  207.3 24.3 %collective-permute-start.15 = (bf16[512,1024]{1,0:T(8,128)(2,1)}, bf16[512,1024]{1,0:T(8,128)(2,1)S(1)}, u32[]{:S(2)}, u32[]{:S(2)}) collective-permute-start(bf16[512,1024]{1,0:T(8,128)(2,1)} %get-tuple-element.315), channel_id=1, source_target_pairs={{0,4},{1,5},{2,6},{3,7},{4,0},{5,1},{6,2},{7,3},{8,12},{9,13},{10,... | collective-permute-start | bytes 3145736 | tf_op jit(solution)/shard_map/ppermute | solution.py:1401
  254.0 22.5 %collective-permute-start.21 = (bf16[256,2048]{1,0:T(8,128)(2,1)}, bf16[256,2048]{1,0:T(8,128)(2,1)}, u32[]{:S(2)}, u32[]{:S(2)}) collective-permute-start(bf16[256,2048]{1,0:T(8,128)(2,1)} %get-tuple-element.331), channel_id=1, source_target_pairs={{0,2},{1,3},{2,0},{3,1},{4,6},{5,7},{6,4},{7,5},{8,10},{9,11},{10,... | collective-permute-start | bytes 3145736 | tf_op jit(solution)/shard_map/ppermute | solution.py:1401
  254.9 22.5 %collective-permute-start.22 = (bf16[256,2048]{1,0:T(8,128)(2,1)}, bf16[256,2048]{1,0:T(8,128)(2,1)}, u32[]{:S(2)}, u32[]{:S(2)}) collective-permute-start(bf16[256,2048]{1,0:T(8,128)(2,1)} %get-tuple-element.331), channel_id=1, source_target_pairs={{0,4},{1,5},{2,6},{3,7},{4,0},{5,1},{6,2},{7,3},{8,12},{9,13},{10,... | collective-permute-start | bytes 3145736 | tf_op jit(solution)/shard_map/ppermute | solution.py:1401
  277.5 20.9 %collective-permute-start.25 = (bf16[4,4,64,2816]{3,2,1,0:T(8,128)(2,1)}, bf16[4,4,64,2816]{3,2,1,0:T(8,128)(2,1)S(1)}, u32[]{:S(2)}, u32[]{:S(2)}) collective-permute-start(bf16[4,4,64,2816]{3,2,1,0:T(8,128)(2,1)} %bitcast.38), channel_id=1, source_target_pairs={{0,1},{1,0},{2,3},{3,2},{4,5},{5,4},{6,7},{7,6},{8,9},{9,8},{10,11... | collective-permute-start | bytes 17301512 | tf_op jit(solution)/shard_map/ppermute | solution.py:1405
  298.4 31.0 %collective-permute-start.26 = (bf16[1024,2048]{1,0:T(8,128)(2,1)}, bf16[1024,2048]{1,0:T(8,128)(2,1)}, u32[]{:S(2)}, u32[]{:S(2)}) collective-permute-start(bf16[1024,2048]{1,0:T(8,128)(2,1)} %constant_dynamic-update-slice_fusion.4.x_ref.a_ref), channel_id=1, source_target_pairs={{0,1},{1,0},{2,3},{3,2},{4,5},{5,4},{6,7},{7,6},{8,9},{9,8},{10,11... | collective-permute-start | bytes 12582920 | tf_op jit(solution)/shard_map/ppermute | solution.py:1405
  328.9 20.5 %collective-permute-start.28 = (bf16[1024,2816]{1,0:T(8,128)(2,1)}, bf16[1024,2816]{1,0:T(8,128)(2,1)}, u32[]{:S(2)}, u32[]{:S(2)}) collective-permute-start(bf16[1024,2816]{1,0:T(8,128)(2,1)} %get-tuple-element.366.refs_0_.ra_ref), channel_id=1, source_target_pairs={{0,1},{1,0},{2,3},{3,2},{4,5},{5,4},{6,7},{7,6},{8,9},{9,8},{10,11... | collective-permute-start | bytes 17301512 | tf_op jit(solution)/shard_map/ppermute | solution.py:1405
  347.8 36.0 %collective-permute-start.32 = (bf16[352,2048]{1,0:T(8,128)(2,1)S(1)}, bf16[352,2048]{1,0:T(8,128)(2,1)}, u32[]{:S(2)}, u32[]{:S(2)}) collective-permute-start(bf16[352,2048]{1,0:T(8,128)(2,1)S(1)} %get-tuple-element.355.refs_0_), channel_id=1, source_target_pairs={{0,8},{8,0},{16,24},{24,16},{1,9},{9,1},{17,25},{25,17},{2,10},{10... | collective-permute-start | bytes 4325384 | tf_op jit(solution)/shard_map/ppermute | solution.py:1417
  369.8 25.2 %collective-permute-start.30 = (bf16[512,1024]{1,0:T(8,128)(2,1)}, bf16[512,1024]{1,0:T(8,128)(2,1)S(1)}, u32[]{:S(2)}, u32[]{:S(2)}) collective-permute-start(bf16[512,1024]{1,0:T(8,128)(2,1)} %get-tuple-element.340), channel_id=1, source_target_pairs={{0,2},{1,3},{2,0},{3,1},{4,6},{5,7},{6,4},{7,5},{8,10},{9,11},{10,... | collective-permute-start | bytes 3145736 | tf_op jit(solution)/shard_map/ppermute | solution.py:1401
  370.7 24.8 %collective-permute-start.31 = (bf16[512,1024]{1,0:T(8,128)(2,1)}, bf16[512,1024]{1,0:T(8,128)(2,1)S(1)}, u32[]{:S(2)}, u32[]{:S(2)}) collective-permute-start(bf16[512,1024]{1,0:T(8,128)(2,1)} %get-tuple-element.342), channel_id=1, source_target_pairs={{0,4},{1,5},{2,6},{3,7},{4,0},{5,1},{6,2},{7,3},{8,12},{9,13},{10,... | collective-permute-start | bytes 3145736 | tf_op jit(solution)/shard_map/ppermute | solution.py:1401
  383.8 39.4 %collective-permute-start.35 = (bf16[352,2048]{1,0:T(8,128)(2,1)S(1)}, bf16[352,2048]{1,0:T(8,128)(2,1)S(1)}, u32[]{:S(2)}, u32[]{:S(2)}) collective-permute-start(bf16[352,2048]{1,0:T(8,128)(2,1)S(1)} %get-tuple-element.368.refs_0_), channel_id=1, source_target_pairs={{0,8},{8,0},{16,24},{24,16},{1,9},{9,1},{17,25},{25,17},{2,10},{10... | collective-permute-start | bytes 4325384 | tf_op jit(solution)/shard_map/ppermute | solution.py:1417
  387.1 40.0 %collective-permute-start.36 = (bf16[352,2048]{1,0:T(8,128)(2,1)}, bf16[352,2048]{1,0:T(8,128)(2,1)}, u32[]{:S(2)}, u32[]{:S(2)}) collective-permute-start(bf16[352,2048]{1,0:T(8,128)(2,1)} %line_values.24.refs_0_), channel_id=1, source_target_pairs={{8,16},{16,8},{9,17},{17,9},{10,18},{18,10},{11,19},{19,11},{12,20... | collective-permute-start | bytes 4325384 | tf_op jit(solution)/shard_map/ppermute | solution.py:1417
  399.5 27.6 %collective-permute-start.33 = (bf16[256,1024]{1,0:T(8,128)(2,1)}, bf16[256,1024]{1,0:T(8,128)(2,1)S(1)}, u32[]{:S(2)}, u32[]{:S(2)}) collective-permute-start(bf16[256,1024]{1,0:T(8,128)(2,1)} %get-tuple-element.361), channel_id=1, source_target_pairs={{0,4},{1,5},{2,6},{3,7},{4,0},{5,1},{6,2},{7,3},{8,12},{9,13},{10,... | collective-permute-start | bytes 1572872 | tf_op jit(solution)/shard_map/ppermute | solution.py:1401
  400.2 26.9 %collective-permute-start.34 = (bf16[256,1024]{1,0:T(8,128)(2,1)}, bf16[256,1024]{1,0:T(8,128)(2,1)S(1)}, u32[]{:S(2)}, u32[]{:S(2)}) collective-permute-start(bf16[256,1024]{1,0:T(8,128)(2,1)} %get-tuple-element.362), channel_id=1, source_target_pairs={{0,2},{1,3},{2,0},{3,1},{4,6},{5,7},{6,4},{7,5},{8,10},{9,11},{10,... | collective-permute-start | bytes 1572872 | tf_op jit(solution)/shard_map/ppermute | solution.py:1401
  434.5 23.7 %collective-permute-start.37 = (bf16[256,2048]{1,0:T(8,128)(2,1)}, bf16[256,2048]{1,0:T(8,128)(2,1)S(1)}, u32[]{:S(2)}, u32[]{:S(2)}) collective-permute-start(bf16[256,2048]{1,0:T(8,128)(2,1)} %get-tuple-element.391), channel_id=1, source_target_pairs={{0,2},{1,3},{2,0},{3,1},{4,6},{5,7},{6,4},{7,5},{8,10},{9,11},{10,... | collective-permute-start | bytes 3145736 | tf_op jit(solution)/shard_map/ppermute | solution.py:1401
  435.7 23.4 %collective-permute-start.38 = (bf16[256,2048]{1,0:T(8,128)(2,1)}, bf16[256,2048]{1,0:T(8,128)(2,1)S(1)}, u32[]{:S(2)}, u32[]{:S(2)}) collective-permute-start(bf16[256,2048]{1,0:T(8,128)(2,1)} %get-tuple-element.391), channel_id=1, source_target_pairs={{0,4},{1,5},{2,6},{3,7},{4,0},{5,1},{6,2},{7,3},{8,12},{9,13},{10,... | collective-permute-start | bytes 3145736 | tf_op jit(solution)/shard_map/ppermute | solution.py:1401
  437.1 31.7 %collective-permute-start.42 = (bf16[352,2048]{1,0:T(8,128)(2,1)}, bf16[352,2048]{1,0:T(8,128)(2,1)}, u32[]{:S(2)}, u32[]{:S(2)}) collective-permute-start(bf16[352,2048]{1,0:T(8,128)(2,1)} %get-tuple-element.386.refs_0_), channel_id=1, source_target_pairs={{0,8},{8,0},{16,24},{24,16},{1,9},{9,1},{17,25},{25,17},{2,10},{10... | collective-permute-start | bytes 4325384 | tf_op jit(solution)/shard_map/ppermute | solution.py:1417
  437.6 35.7 %collective-permute-start.41 = (bf16[352,2048]{1,0:T(8,128)(2,1)S(1)}, bf16[352,2048]{1,0:T(8,128)(2,1)}, u32[]{:S(2)}, u32[]{:S(2)}) collective-permute-start(bf16[352,2048]{1,0:T(8,128)(2,1)S(1)} %copy-done.19), channel_id=1, source_target_pairs={{8,16},{16,8},{9,17},{17,9},{10,18},{18,10},{11,19},{19,11},{12,20... | collective-permute-start | bytes 4325384 | tf_op jit(solution)/shard_map/ppermute | solution.py:1417
  460.0 20.4 %collective-permute-start.39 = (bf16[128,2048]{1,0:T(8,128)(2,1)}, bf16[128,2048]{1,0:T(8,128)(2,1)S(1)}, u32[]{:S(2)}, u32[]{:S(2)}) collective-permute-start(bf16[128,2048]{1,0:T(8,128)(2,1)} %slice.162), channel_id=1, source_target_pairs={{0,4},{1,5},{2,6},{3,7},{4,0},{5,1},{6,2},{7,3},{8,12},{9,13},{10,... | collective-permute-start | bytes 1572872 | tf_op jit(solution)/shard_map/ppermute | solution.py:1401
  462.5 68.1 %collective-permute-start.29 = (bf16[1024,2048]{1,0:T(8,128)(2,1)S(1)}, bf16[1024,2048]{1,0:T(8,128)(2,1)}, u32[]{:S(2)}, u32[]{:S(2)}) collective-permute-start(bf16[1024,2048]{1,0:T(8,128)(2,1)S(1)} %copy-done), channel_id=1, source_target_pairs={{0,1},{1,0},{2,3},{3,2},{4,5},{5,4},{6,7},{7,6},{8,9},{9,8},{10,11... | collective-permute-start | bytes 12582920 | tf_op jit(solution)/shard_map/ppermute | solution.py:1405
  471.4 42.7 %collective-permute-start.43 = (bf16[352,2048]{1,0:T(8,128)(2,1)}, bf16[352,2048]{1,0:T(8,128)(2,1)}, u32[]{:S(2)}, u32[]{:S(2)}) collective-permute-start(bf16[352,2048]{1,0:T(8,128)(2,1)} %line_values.27.refs_0_), channel_id=1, source_target_pairs={{8,16},{16,8},{9,17},{17,9},{10,18},{18,10},{11,19},{19,11},{12,20... | collective-permute-start | bytes 4325384 | tf_op jit(solution)/shard_map/ppermute | solution.py:1417
  473.3 40.9 %collective-permute-start.44 = (bf16[352,2048]{1,0:T(8,128)(2,1)}, bf16[352,2048]{1,0:T(8,128)(2,1)S(1)}, u32[]{:S(2)}, u32[]{:S(2)}) collective-permute-start(bf16[352,2048]{1,0:T(8,128)(2,1)} %line_values.26), channel_id=1, source_target_pairs={{0,8},{8,0},{16,24},{24,16},{1,9},{9,1},{17,25},{25,17},{2,10},{10... | collective-permute-start | bytes 4325384 | tf_op jit(solution)/shard_map/ppermute | solution.py:1417
  514.2 34.3 %collective-permute-start.46 = (bf16[352,2048]{1,0:T(8,128)(2,1)}, bf16[352,2048]{1,0:T(8,128)(2,1)}, u32[]{:S(2)}, u32[]{:S(2)}) collective-permute-start(bf16[352,2048]{1,0:T(8,128)(2,1)} %line_values.28), channel_id=1, source_target_pairs={{0,8},{8,0},{16,24},{24,16},{1,9},{9,1},{17,25},{25,17},{2,10},{10... | collective-permute-start | bytes 4325384 | tf_op jit(solution)/shard_map/ppermute | solution.py:1417
  518.0 30.6 %collective-permute-start.47 = (bf16[352,2048]{1,0:T(8,128)(2,1)}, bf16[352,2048]{1,0:T(8,128)(2,1)S(1)}, u32[]{:S(2)}, u32[]{:S(2)}) collective-permute-start(bf16[352,2048]{1,0:T(8,128)(2,1)} %line_values.29.refs_0_), channel_id=1, source_target_pairs={{8,16},{16,8},{9,17},{17,9},{10,18},{18,10},{11,19},{19,11},{12,20... | collective-permute-start | bytes 4325384 | tf_op jit(solution)/shard_map/ppermute | solution.py:1417
  549.7 50.7 %all-to-all-start.2 = ((bf16[4,192,2048]{2,1,0:T(8,128)(2,1)}), bf16[4,192,2048]{2,1,0:T(8,128)(2,1)S(1)}, u32[]{:S(2)}, u32[]{:S(2)}) async-start(bf16[4,192,2048]{2,1,0:T(8,128)(2,1)} %column_terms.4), calls=%async_computation.2 | async-start | bytes 6291456 | tf_op jit(solution)/shard_map/all_to_all | solution.py:1626
  553.4 45.8 %collective-permute-start.48 = (bf16[352,2048]{1,0:T(8,128)(2,1)}, bf16[352,2048]{1,0:T(8,128)(2,1)S(1)}, u32[]{:S(2)}, u32[]{:S(2)}) collective-permute-start(bf16[352,2048]{1,0:T(8,128)(2,1)} %line_values.30.t_ref), channel_id=1, source_target_pairs={{0,8},{8,0},{16,24},{24,16},{1,9},{9,1},{17,25},{25,17},{2,10},{10... | collective-permute-start | bytes 4325384 | tf_op jit(solution)/shard_map/ppermute | solution.py:1417
  562.4 37.9 %collective-permute-start.53 = (bf16[352,2048]{1,0:T(8,128)(2,1)}, bf16[352,2048]{1,0:T(8,128)(2,1)}, u32[]{:S(2)}, u32[]{:S(2)}) collective-permute-start(bf16[352,2048]{1,0:T(8,128)(2,1)} %line_values.31.refs_0_), channel_id=1, source_target_pairs={{8,16},{16,8},{9,17},{17,9},{10,18},{18,10},{11,19},{19,11},{12,20... | collective-permute-start | bytes 4325384 | tf_op jit(solution)/shard_map/ppermute | solution.py:1417
  609.0 33.4 %collective-permute-start.52 = (bf16[352,2048]{1,0:T(8,128)(2,1)}, bf16[352,2048]{1,0:T(8,128)(2,1)}, u32[]{:S(2)}, u32[]{:S(2)}) collective-permute-start(bf16[352,2048]{1,0:T(8,128)(2,1)} %line_values.32.t_ref), channel_id=1, source_target_pairs={{0,8},{8,0},{16,24},{24,16},{1,9},{9,1},{17,25},{25,17},{2,10},{10... | collective-permute-start | bytes 4325384 | tf_op jit(solution)/shard_map/ppermute | solution.py:1417
  612.2 30.7 %collective-permute-start.51 = (bf16[352,2048]{1,0:T(8,128)(2,1)}, bf16[352,2048]{1,0:T(8,128)(2,1)}, u32[]{:S(2)}, u32[]{:S(2)}) collective-permute-start(bf16[352,2048]{1,0:T(8,128)(2,1)} %line_values.33.refs_0_), channel_id=1, source_target_pairs={{8,16},{16,8},{9,17},{17,9},{10,18},{18,10},{11,19},{19,11},{12,20... | collective-permute-start | bytes 4325384 | tf_op jit(solution)/shard_map/ppermute | solution.py:1417
  642.5 37.4 %collective-permute-start.55 = (bf16[352,2048]{1,0:T(8,128)(2,1)}, bf16[352,2048]{1,0:T(8,128)(2,1)}, u32[]{:S(2)}, u32[]{:S(2)}) collective-permute-start(bf16[352,2048]{1,0:T(8,128)(2,1)} %line_values.34.t_ref), channel_id=1, source_target_pairs={{0,8},{8,0},{16,24},{24,16},{1,9},{9,1},{17,25},{25,17},{2,10},{10... | collective-permute-start | bytes 4325384 | tf_op jit(solution)/shard_map/ppermute | solution.py:1417
  642.8 64.2 %all-to-all-start.3 = ((bf16[4,208,2048]{2,1,0:T(8,128)(2,1)}), bf16[4,208,2048]{2,1,0:T(8,128)(2,1)S(1)}, u32[]{:S(2)}, u32[]{:S(2)}) async-start(bf16[4,208,2048]{2,1,0:T(8,128)(2,1)} %column_terms.5), calls=%async_computation.3 | async-start | bytes 6815744 | tf_op jit(solution)/shard_map/all_to_all | solution.py:1626
  649.6 44.5 %collective-permute-start.58 = (bf16[352,2048]{1,0:T(8,128)(2,1)}, bf16[352,2048]{1,0:T(8,128)(2,1)S(1)}, u32[]{:S(2)}, u32[]{:S(2)}) collective-permute-start(bf16[352,2048]{1,0:T(8,128)(2,1)} %line_values.35.refs_0_), channel_id=1, source_target_pairs={{8,16},{16,8},{9,17},{17,9},{10,18},{18,10},{11,19},{19,11},{12,20... | collective-permute-start | bytes 4325384 | tf_op jit(solution)/shard_map/ppermute | solution.py:1417
  679.8 37.6 %collective-permute-start.56 = (bf16[352,2048]{1,0:T(8,128)(2,1)}, bf16[352,2048]{1,0:T(8,128)(2,1)}, u32[]{:S(2)}, u32[]{:S(2)}) collective-permute-start(bf16[352,2048]{1,0:T(8,128)(2,1)} %line_values.36.t_ref), channel_id=1, source_target_pairs={{0,8},{8,0},{16,24},{24,16},{1,9},{9,1},{17,25},{25,17},{2,10},{10... | collective-permute-start | bytes 4325384 | tf_op jit(solution)/shard_map/ppermute | solution.py:1417
  690.1 35.3 %collective-permute-start.57 = (bf16[352,2048]{1,0:T(8,128)(2,1)}, bf16[352,2048]{1,0:T(8,128)(2,1)}, u32[]{:S(2)}, u32[]{:S(2)}) collective-permute-start(bf16[352,2048]{1,0:T(8,128)(2,1)} %line_values.37.refs_0_), channel_id=1, source_target_pairs={{8,16},{16,8},{9,17},{17,9},{10,18},{18,10},{11,19},{19,11},{12,20... | collective-permute-start | bytes 4325384 | tf_op jit(solution)/shard_map/ppermute | solution.py:1417
  694.2 34.5 %collective-permute-start.59 = (bf16[512,1024]{1,0:T(8,128)(2,1)}, bf16[512,1024]{1,0:T(8,128)(2,1)}, u32[]{:S(2)}, u32[]{:S(2)}) collective-permute-start(bf16[512,1024]{1,0:T(8,128)(2,1)} %get-tuple-element.466), channel_id=1, source_target_pairs={{0,2},{1,3},{2,0},{3,1},{4,6},{5,7},{6,4},{7,5},{8,10},{9,11},{10,... | collective-permute-start | bytes 3145736 | tf_op jit(solution)/shard_map/ppermute | solution.py:1401
  696.2 32.5 %collective-permute-start.60 = (bf16[512,1024]{1,0:T(8,128)(2,1)}, bf16[512,1024]{1,0:T(8,128)(2,1)}, u32[]{:S(2)}, u32[]{:S(2)}) collective-permute-start(bf16[512,1024]{1,0:T(8,128)(2,1)} %get-tuple-element.467), channel_id=1, source_target_pairs={{0,4},{1,5},{2,6},{3,7},{4,0},{5,1},{6,2},{7,3},{8,12},{9,13},{10,... | collective-permute-start | bytes 3145736 | tf_op jit(solution)/shard_map/ppermute | solution.py:1401
  717.4 31.1 %collective-permute-start.61 = (bf16[352,2048]{1,0:T(8,128)(2,1)}, bf16[352,2048]{1,0:T(8,128)(2,1)}, u32[]{:S(2)}, u32[]{:S(2)}) collective-permute-start(bf16[352,2048]{1,0:T(8,128)(2,1)} %line_values.38), channel_id=1, source_target_pairs={{0,8},{8,0},{16,24},{24,16},{1,9},{9,1},{17,25},{25,17},{2,10},{10... | collective-permute-start | bytes 4325384 | tf_op jit(solution)/shard_map/ppermute | solution.py:1417
  721.9 26.6 %collective-permute-start.62 = (bf16[352,2048]{1,0:T(8,128)(2,1)}, bf16[352,2048]{1,0:T(8,128)(2,1)}, u32[]{:S(2)}, u32[]{:S(2)}) collective-permute-start(bf16[352,2048]{1,0:T(8,128)(2,1)} %line_values.39.refs_0_), channel_id=1, source_target_pairs={{8,16},{16,8},{9,17},{17,9},{10,18},{18,10},{11,19},{19,11},{12,20... | collective-permute-start | bytes 4325384 | tf_op jit(solution)/shard_map/ppermute | solution.py:1417
  748.5 72.1 %all-to-all-start.4 = ((bf16[4,256,2816]{2,1,0:T(8,128)(2,1)}), bf16[4,256,2816]{2,1,0:T(8,128)(2,1)}, u32[]{:S(2)}, u32[]{:S(2)}) async-start(bf16[4,256,2816]{2,1,0:T(8,128)(2,1)} %place_blocks.7), calls=%async_computation.4 | async-start | bytes 11534336 | tf_op jit(solution)/shard_map/all_to_all | solution.py:1626
  753.6 35.8 %collective-permute-start.67 = (bf16[352,2048]{1,0:T(8,128)(2,1)S(1)}, bf16[352,2048]{1,0:T(8,128)(2,1)S(1)}, u32[]{:S(2)}, u32[]{:S(2)}) collective-permute-start(bf16[352,2048]{1,0:T(8,128)(2,1)S(1)} %copy-done.7), channel_id=1, source_target_pairs={{0,8},{8,0},{16,24},{24,16},{1,9},{9,1},{17,25},{25,17},{2,10},{10... | collective-permute-start | bytes 4325384 | tf_op jit(solution)/shard_map/ppermute | solution.py:1417
  762.7 33.2 %collective-permute-start.70 = (bf16[352,2048]{1,0:T(8,128)(2,1)}, bf16[352,2048]{1,0:T(8,128)(2,1)}, u32[]{:S(2)}, u32[]{:S(2)}) collective-permute-start(bf16[352,2048]{1,0:T(8,128)(2,1)} %line_values.41.refs_0_), channel_id=1, source_target_pairs={{8,16},{16,8},{9,17},{17,9},{10,18},{18,10},{11,19},{19,11},{12,20... | collective-permute-start | bytes 4325384 | tf_op jit(solution)/shard_map/ppermute | solution.py:1417
  789.5 29.9 %collective-permute-start.69 = (bf16[352,2048]{1,0:T(8,128)(2,1)}, bf16[352,2048]{1,0:T(8,128)(2,1)}, u32[]{:S(2)}, u32[]{:S(2)}) collective-permute-start(bf16[352,2048]{1,0:T(8,128)(2,1)} %line_values.42.t_ref), channel_id=1, source_target_pairs={{0,8},{8,0},{16,24},{24,16},{1,9},{9,1},{17,25},{25,17},{2,10},{10... | collective-permute-start | bytes 4325384 | tf_op jit(solution)/shard_map/ppermute | solution.py:1417
  794.2 38.3 %collective-permute-start.68 = (bf16[352,2048]{1,0:T(8,128)(2,1)}, bf16[352,2048]{1,0:T(8,128)(2,1)}, u32[]{:S(2)}, u32[]{:S(2)}) collective-permute-start(bf16[352,2048]{1,0:T(8,128)(2,1)} %line_values.43.refs_0_), channel_id=1, source_target_pairs={{8,16},{16,8},{9,17},{17,9},{10,18},{18,10},{11,19},{19,11},{12,20... | collective-permute-start | bytes 4325384 | tf_op jit(solution)/shard_map/ppermute | solution.py:1417
  819.3 32.0 %collective-permute-start.73 = (bf16[352,2048]{1,0:T(8,128)(2,1)}, bf16[352,2048]{1,0:T(8,128)(2,1)}, u32[]{:S(2)}, u32[]{:S(2)}) collective-permute-start(bf16[352,2048]{1,0:T(8,128)(2,1)} %line_values.44.t_ref), channel_id=1, source_target_pairs={{8,0},{16,24},{9,1},{17,25},{10,2},{18,26},{11,3},{19,27},{12,4},{... | collective-permute-start | bytes 4325384 | tf_op jit(solution)/shard_map/ppermute | solution.py:1417
  820.6 32.0 %collective-permute-start.65 = (bf16[512,1024]{1,0:T(8,128)(2,1)}, bf16[512,1024]{1,0:T(8,128)(2,1)S(1)}, u32[]{:S(2)}, u32[]{:S(2)}) collective-permute-start(bf16[512,1024]{1,0:T(8,128)(2,1)} %get-tuple-element.478), channel_id=1, source_target_pairs={{0,2},{1,3},{2,0},{3,1},{4,6},{5,7},{6,4},{7,5},{8,10},{9,11},{10,... | collective-permute-start | bytes 3145736 | tf_op jit(solution)/shard_map/ppermute | solution.py:1401
  822.6 30.0 %collective-permute-start.66 = (bf16[512,1024]{1,0:T(8,128)(2,1)}, bf16[512,1024]{1,0:T(8,128)(2,1)}, u32[]{:S(2)}, u32[]{:S(2)}) collective-permute-start(bf16[512,1024]{1,0:T(8,128)(2,1)} %get-tuple-element.479), channel_id=1, source_target_pairs={{0,4},{1,5},{2,6},{3,7},{4,0},{5,1},{6,2},{7,3},{8,12},{9,13},{10,... | collective-permute-start | bytes 3145736 | tf_op jit(solution)/shard_map/ppermute | solution.py:1401
  827.0 36.5 %collective-permute-start.74 = (bf16[352,2048]{1,0:T(8,128)(2,1)}, bf16[352,2048]{1,0:T(8,128)(2,1)S(1)}, u32[]{:S(2)}, u32[]{:S(2)}) collective-permute-start(bf16[352,2048]{1,0:T(8,128)(2,1)} %line_values.45.refs_0_), channel_id=1, source_target_pairs={{8,16},{16,8},{9,17},{17,9},{10,18},{18,10},{11,19},{19,11},{12,20... | collective-permute-start | bytes 4325384 | tf_op jit(solution)/shard_map/ppermute | solution.py:1417
  851.3 33.3 %collective-permute-start.75 = (bf16[352,2048]{1,0:T(8,128)(2,1)S(1)}, bf16[352,2048]{1,0:T(8,128)(2,1)}, u32[]{:S(2)}, u32[]{:S(2)}) collective-permute-start(bf16[352,2048]{1,0:T(8,128)(2,1)S(1)} %copy-done.3), channel_id=1, source_target_pairs={{8,0},{16,24},{9,1},{17,25},{10,2},{18,26},{11,3},{19,27},{12,4},{... | collective-permute-start | bytes 4325384 | tf_op jit(solution)/shard_map/ppermute | solution.py:1417
  856.1 25.2 %collective-permute-start.71 = (bf16[256,1024]{1,0:T(8,128)(2,1)}, bf16[256,1024]{1,0:T(8,128)(2,1)S(1)}, u32[]{:S(2)}, u32[]{:S(2)}) collective-permute-start(bf16[256,1024]{1,0:T(8,128)(2,1)} %get-tuple-element.515), channel_id=1, source_target_pairs={{0,4},{1,5},{2,6},{3,7},{4,0},{5,1},{6,2},{7,3},{8,12},{9,13},{10,... | collective-permute-start | bytes 1572872 | tf_op jit(solution)/shard_map/ppermute | solution.py:1401
  858.0 23.4 %collective-permute-start.72 = (bf16[256,1024]{1,0:T(8,128)(2,1)}, bf16[256,1024]{1,0:T(8,128)(2,1)}, u32[]{:S(2)}, u32[]{:S(2)}) collective-permute-start(bf16[256,1024]{1,0:T(8,128)(2,1)} %get-tuple-element.516), channel_id=1, source_target_pairs={{0,2},{1,3},{2,0},{3,1},{4,6},{5,7},{6,4},{7,5},{8,10},{9,11},{10,... | collective-permute-start | bytes 1572872 | tf_op jit(solution)/shard_map/ppermute | solution.py:1401
  885.1 37.2 %collective-permute-start.76 = (bf16[352,2048]{1,0:T(8,128)(2,1)S(1)}, bf16[352,2048]{1,0:T(8,128)(2,1)}, u32[]{:S(2)}, u32[]{:S(2)}) collective-permute-start(bf16[352,2048]{1,0:T(8,128)(2,1)S(1)} %copy-done.4), channel_id=1, source_target_pairs={{8,0},{16,24},{9,1},{17,25},{10,2},{18,26},{11,3},{19,27},{12,4},{... | collective-permute-start | bytes 4325384 | tf_op jit(solution)/shard_map/ppermute | solution.py:1417
  (77 other events, 721.9 us)
Sparse Core Ops, SparseCore 0:
  30.0 68.1 all-gather.5
  158.6 108.6 all-gather.7

commit v5 on v4

--- a/solution.py
+++ b/solution.py
@@ -1898,11 +1898,10 @@
     line.prepare(("up3", grad_up[3]))
     d_x1_other = swap_core(after(d_x1, arriving), nf)
     mine, theirs = row_terms(gated, after(d_branch, line.sent), ids)
-    half = mine.shape[0] // 2
-    theirs = [swap_core(theirs[:half], nf), swap_core(theirs[half:], nf)]
+    theirs = swap_core(theirs, nf)
     cols1 = column_terms([normed_in, in_other], [after(d_x1, mine), d_x1_other], ids, False)
     cols1_all = exchange(after(cols1, line.arriving), nf)
-    grad_out = mine + jnp.concatenate(after(theirs, cols1), axis=0)
+    grad_out = mine + after(theirs, cols1)
     line.step(cols1)
     d_x0, dec, g_conv0, g_heads0 = backward(0, line.sent, theirs, more=d_dec)
     arriving = line.arriving

time: 947 us -> 949 us (level)
    unnamed x127 -> x123, local copies, waits for them, and re-layouts: 31.8 us -> 31.3 us
  transfers between devices with their start and end apart: 84 -> 83, of which waited for: 30 -> 29; matrix products, arithmetic and copies ran while one was open for 8% -> 8% of each run, Pallas kernels for 48% -> 48%
where the time goes in v5:
time: 949 us; the launch traced here: 941 us
  Pallas kernels  470 us (50%)
  waiting for transfers between devices  205 us (22%)
  starting transfers between devices  123 us (13%)
  local copies, waits for them, and re-layouts  51.8 us (5%)
  other arithmetic  36.8 us (4%)
  blocking collectives  28.6 us (3%)
  between operations  15.3 us (2%)
  matrix products  10.4 us (1%)
    ppermute x37, waiting for transfers between devices, to_chip(): return lax.ppermute(a, 'fsdp', [(i, i ^ 2 * j) for i in range(nf)])  134 us
    pallas_call x24, Pallas kernels, line_values(): pl.pallas_call(body, grid=(steps,), in_specs=[SMEM] + [block] * len(args)...  69.6 us
    ppermute x27, waiting for transfers between devices, along(): return lax.ppermute(a, 'rep', pairs)  65.1 us
    ppermute x27, starting transfers between devices, along(): return lax.ppermute(a, 'rep', pairs)  54.1 us
    pallas_call x2, Pallas kernels, mixer_backward(): pl.pallas_call(body, grid=(slots,), in_specs=[pl.BlockSpec(memory_space=p...  52.3 us
    pallas_call x3, Pallas kernels, column_terms(): pl.pallas_call(body, grid_spec=pltpu.PrefetchScalarGridSpec(num_scalar_pr...  48.8 us
    ppermute x37, starting transfers between devices, to_chip(): return lax.ppermute(a, 'fsdp', [(i, i ^ 2 * j) for i in range(nf)])  46.6 us
    pallas_call x2, Pallas kernels, times_transposed(): pl.pallas_call(body, grid_spec=pltpu.PrefetchScalarGridSpec(num_scalar_pr...  43.6 us
  transfers between devices with their start and end apart: 83, of which 29 were waited for; matrix products, arithmetic and copies ran while one was open for 8% of the time, Pallas kernels for 48%

profile of v5, /device:TPU:0, one launch (start us, length us, event | category | flops | bytes accessed | tf_op | source)
XLA Modules:
  0.0 940.6 jit_solution(6444291284865561712)
XLA Ops:
  18.8 5.8 pack_relative.3
  24.6 4.2 collective-permute-done.1
  34.0 8.1 all_to_all.30
  45.7 21.4 %collective-permute-done.5.refs_1_ = bf16[256,2048]{1,0:T(8,128)(2,1)S(1)} collective-permute-done((bf16[256,2048]{1,0:T(8,128)(2,1)}, bf16[256,2048]{1,0:T(8,128)(2,1)S(1)}, u32[]{:S(2)}, u32[]{:S(2)}) %collective-permute-start.5) | collective-permute-done | bytes 1048608 | tf_op jit(solution)/shard_map/ppermute | solution.py:1401
  71.7 10.8 %collective-permute-done.7.refs_3_ = bf16[128,2048]{1,0:T(8,128)(2,1)S(1)} collective-permute-done((bf16[128,2048]{1,0:T(8,128)(2,1)S(1)}, bf16[128,2048]{1,0:T(8,128)(2,1)S(1)}, u32[]{:S(2)}, u32[]{:S(2)}) %collective-permute-start.7) | collective-permute-done | bytes 524320 | tf_op jit(solution)/shard_map/ppermute | solution.py:1401
  86.0 3.5 pack_columns.1
  90.8 5.8 norm_rows.1.x_ref.a_ref
  100.8 14.3 %collective-permute-done.11.refs_3_ = bf16[256,1536]{1,0:T(8,128)(2,1)} collective-permute-done((bf16[256,1536]{1,0:T(8,128)(2,1)}, bf16[256,1536]{1,0:T(8,128)(2,1)}, u32[]{:S(2)}, u32[]{:S(2)}) %collective-permute-start.11) | collective-permute-done | bytes 786464 | tf_op jit(solution)/shard_map/ppermute | solution.py:1401
  118.3 4.3 all-to-all-start.1
  124.6 13.3 %project.2.refs_1_.refs_2_ = f32[1024,1664]{1,0:T(8,128)} custom-call(s32[4]{0:T(128)} %pad_add_fusion.ids_ref.refs_0_, bf16[1024,2048]{1,0:T(8,128)(2,1)} %norm_rows.1.x_ref.a_ref, bf16[4,4,64,1664]{3,2,1,0:T(8,128)(2,1)} %bitcast.42, bf16[4,4,64,1664]{3,2,1,0:T(8,128)(2,1)} %copy-done.2), custom_call_target="tpu_custom_call" | custom-call | flops 1 | bytes 1 | tf_op jit(solution)/shard_map/project/pallas_call | solution.py:1064
  138.0 20.4 %mixer_forward.2 = (bf16[1024,512]{1,0:T(8,128)(2,1)}, f32[1024,512]{1,0:T(8,128)}, bf16[1024,512]{1,0:T(8,128)(2,1)}, bf16[1024,256]{1,0:T(8,128)(2,1)}, bf16[4...) custom-call(s32[4]{0:T(128)} %pad_add_fusion.ids_ref.refs_0_, f32[1024,1664]{1,0:T(8,128)} %project.2.refs_1_.refs_2_, ...), custom_call_target="tpu_custom_call" | custom-call | flops 1 | bytes 1 | tf_op jit(solution)/shard_map/mixer_forward/pallas_call | solution.py:227
  162.0 12.4 %project.3.refs_1_ = f32[1024,1536]{1,0:T(8,128)} custom-call(s32[4]{0:T(128)} %pad_add_fusion.ids_ref.refs_0_, bf16[1024,2048]{1,0:T(8,128)(2,1)} %norm_rows.1.x_ref.a_ref, bf16[1,4,256,1536]{3,2,1,0:T(8,128)(2,1)} %stack_blocks.1.own_ref.refs_4_, bf16[1,4,256,1536]{3,2,1,0:T(8,128)(2,1)} %collective-permute-done.13.other_ref.refs_5_), custom_call_target="tpu_custom_call" | custom-call | flops 1 | bytes 1 | tf_op jit(solution)/shard_map/project/pallas_call | solution.py:1064
  174.3 20.3 %mixer_forward.3 = (bf16[1024,512]{1,0:T(8,128)(2,1)}, f32[1024,512]{1,0:T(8,128)}, bf16[1024,512]{1,0:T(8,128)(2,1)}, bf16[1024,256]{1,0:T(8,128)(2,1)}, bf16[4...) custom-call(s32[4]{0:T(128)} %pad_add_fusion.ids_ref.refs_0_, f32[1024,1536]{1,0:T(8,128)} %project.3.refs_1_, ...), custom_call_target="tpu_custom_call" | custom-call | flops 1 | bytes 1 | tf_op jit(solution)/shard_map/mixer_forward/pallas_call | solution.py:227
  194.7 10.6 %times_rows.2 = (bf16[512,1024]{1,0:T(8,128)(2,1)}, bf16[512,1024]{1,0:T(8,128)(2,1)}, bf16[512,1024]{1,0:T(8,128)(2,1)}, bf16[512,1024]{1,0:T(8,128)(2,1)}) custom-call(s32[4]{0:T(128)} %pad_add_fusion.ids_ref.refs_0_, bf16[1024,512]{1,0:T(8,128)(2,1)} %get-tuple-element.307.refs_0_, bf16[1024,512]{1,0:T(8,128)(2,1)} %get-tuple-element.310.refs_1_, ...), custom_call_target="tpu_custom_call" | custom-call | flops 1 | bytes 1 | tf_op jit(solution)/shard_map/times_rows/pallas_call | solution.py:1207
  208.7 5.7 join_cores.2.down_ref
  214.4 5.0 join_cores.3
  224.9 5.2 collective-permute-done.14.b_ref.refs_1_
  237.2 10.2 %collective-permute-done.19.refs_2_ = bf16[256,1024]{1,0:T(8,128)(2,1)S(1)} collective-permute-done((bf16[256,1024]{1,0:T(8,128)(2,1)}, bf16[256,1024]{1,0:T(8,128)(2,1)S(1)}, u32[]{:S(2)}, u32[]{:S(2)}) %collective-permute-start.19) | collective-permute-done | bytes 524320 | tf_op jit(solution)/shard_map/ppermute | solution.py:1401
  249.3 4.6 middle_rows.1
  255.9 20.5 %collective-permute-done.21 = bf16[256,2048]{1,0:T(8,128)(2,1)} collective-permute-done((bf16[256,2048]{1,0:T(8,128)(2,1)}, bf16[256,2048]{1,0:T(8,128)(2,1)}, u32[]{:S(2)}, u32[]{:S(2)}) %collective-permute-start.21) | collective-permute-done | bytes 1048608 | tf_op jit(solution)/shard_map/ppermute | solution.py:1401
  288.8 4.0 collective-permute-done.23
  293.7 3.7 collective-permute-done.24
  300.8 28.0 %feed_forward.1 = (bf16[1024,1408]{1,0:T(8,128)(2,1)}, bf16[1024,2816]{1,0:T(8,128)(2,1)}) custom-call(s32[4]{0:T(128)} %pad_add_fusion.ids_ref.refs_0_, bf16[1024,2048]{1,0:T(8,128)(2,1)} %constant_dynamic-update-slice_fusion.4.x_ref.a_ref, bf16[4,4,64,2816]{3,2,1,0:T(8,128)(2,1)} %bitcast.39, bf16[4,4,64,2816]{3,2,1,0:T(8,128)(2,1)} %copy-done.1, ...), custom_call_target="tpu_custom_call" | custom-call | flops 1 | bytes 1 | tf_op jit(solution)/shard_map/feed_forward/pallas_call | solution.py:1131
  329.3 10.7 %row_terms.2 = (bf16[704,2048]{1,0:T(8,128)(2,1)}, bf16[704,2048]{1,0:T(8,128)(2,1)}) custom-call(s32[4]{0:T(128)} %pad_add_fusion.ids_ref.refs_0_, bf16[1024,1408]{1,0:T(8,128)(2,1)} %get-tuple-element.343.refs_0_, bf16[1024,2048]{1,0:T(8,128)(2,1)} %constant_dynamic-update-slice_fusion.d_ref.refs_1_), custom_call_target="tpu_custom_call" | custom-call | flops 1 | bytes 1 | tf_op jit(solution)/shard_map/row_terms/pallas_call | solution.py:1379
  340.0 5.5 collective-permute-done.27
  349.3 20.4 %times_transposed.2 = (bf16[512,1024]{1,0:T(8,128)(2,1)}, bf16[512,1024]{1,0:T(8,128)(2,1)}, bf16[512,1024]{1,0:T(8,128)(2,1)}, bf16[512,1024]{1,0:T(8,128)(2,1)}) custom-call(s32[4]{0:T(128)} %pad_add_fusion.ids_ref.refs_0_, bf16[1024,2816]{1,0:T(8,128)(2,1)} %get-tuple-element.365.refs_0_.ra_ref, bf16[4,4,64,2816]{3,2,1,0:T(8,128)(2,1)} %bitcast.40, ...), custom_call_target="tpu_custom_call" | custom-call | flops 1 | bytes 1 | tf_op jit(solution)/shard_map/times_transposed/pallas_call | solution.py:1270
  371.2 12.4 %times_rows.3 = (bf16[512,1024]{1,0:T(8,128)(2,1)}, bf16[512,1024]{1,0:T(8,128)(2,1)}, bf16[512,1024]{1,0:T(8,128)(2,1)}, bf16[512,1024]{1,0:T(8,128)(2,1)}) custom-call(s32[4]{0:T(128)} %pad_add_fusion.ids_ref.refs_0_, bf16[1024,1408]{1,0:T(8,128)(2,1)} %get-tuple-element.343.refs_0_, bf16[704,2048]{1,0:T(8,128)(2,1)} %refs_1_.1, ...), custom_call_target="tpu_custom_call" | custom-call | flops 1 | bytes 1 | tf_op jit(solution)/shard_map/times_rows/pallas_call | solution.py:1207
  388.7 6.1 collective-permute-done.30.b_ref.refs_1_
  400.9 22.2 %column_terms.3 = (bf16[352,2048]{1,0:T(8,128)(2,1)}, bf16[352,2048]{1,0:T(8,128)(2,1)}, bf16[352,2048]{1,0:T(8,128)(2,1)}, bf16[352,2048]{1,0:T(8,128)(2,1)}) custom-call(s32[4]{0:T(128)} %pad_add_fusion.ids_ref.refs_0_, bf16[1024,2048]{1,0:T(8,128)(2,1)} %constant_dynamic-update-slice_fusion.4.x_ref.a_ref, ...), custom_call_target="tpu_custom_call" | custom-call | flops 1 | bytes 1 | tf_op jit(solution)/shard_map/column_terms/pallas_call | solution.py:1333
  427.9 6.5 middle_back.1
  439.1 18.9 %collective-permute-done.37 = bf16[256,2048]{1,0:T(8,128)(2,1)S(1)} collective-permute-done((bf16[256,2048]{1,0:T(8,128)(2,1)}, bf16[256,2048]{1,0:T(8,128)(2,1)S(1)}, u32[]{:S(2)}, u32[]{:S(2)}) %collective-permute-start.37) | collective-permute-done | bytes 1048608 | tf_op jit(solution)/shard_map/ppermute | solution.py:1401
  473.0 3.9 collective-permute-start.44
  484.3 3.8 fusion.2.refs_11_
  488.0 26.0 %mixer_backward.2 = (bf16[1024,1536]{1,0:T(8,128)(2,1)}, f32[1024,128]{1,0:T(8,128)}, f32[8,1024]{1,0:T(8,128)}, f32[8,256]{1,0:T(8,128)}) custom-call(s32[4]{0:T(128)} %pad_add_fusion.ids_ref.refs_0_, f32[1024,1536]{1,0:T(8,128)} %project.3.refs_1_, f32[1024,1664]{1,0:T(8,128)} %project.2.refs_1_.refs_2_, f32[8,1024]{1,0:T(8,128)} %get-tuple-element.309.refs_3_, ...), custom_call_target="tpu_custom_call" | custom-call | flops 1 | bytes 1 | tf_op jit(solution)/shard_map/mixer_backward/pallas_call | solution.py:489
  521.9 8.7 row_terms.3
  530.5 12.6 %column_terms.4 = bf16[4,192,2048]{2,1,0:T(8,128)(2,1)} custom-call(s32[4]{0:T(128)} %pad_add_fusion.ids_ref.refs_0_, bf16[1024,2048]{1,0:T(8,128)(2,1)} %norm_rows.1.x_ref.a_ref, bf16[1024,2048]{1,0:T(8,128)(2,1)} %collective-permute-done.29.b_ref, bf16[1024,1536]{1,0:T(8,128)(2,1)} %get-tuple-element.441.ra_ref.refs_3_, ...), custom_call_target="tpu_custom_call" | custom-call | flops 1 | bytes 1 | tf_op jit(solution)/shard_map/column_terms/pallas_call | solution.py:1333
  543.1 5.3 collective-permute-done.46.refs_1_
  549.5 3.7 all-to-all-start.2
  553.3 6.3 collective-permute-start.48
  564.3 6.6 fusion.refs_11_
  571.0 26.3 %mixer_backward.3 = (bf16[1024,1664]{1,0:T(8,128)(2,1)}, f32[1024,128]{1,0:T(8,128)}, f32[8,1024]{1,0:T(8,128)}, f32[8,256]{1,0:T(8,128)}) custom-call(s32[4]{0:T(128)} %pad_add_fusion.ids_ref.refs_0_, f32[1024,1664]{1,0:T(8,128)} %project.2.refs_1_.refs_2_, f32[1024,1664]{1,0:T(8,128)} %project.2.refs_1_.refs_2_, f32[8,1024]{1,0:T(8,128)} %get-tuple-element.304.refs_3_, ...), custom_call_target="tpu_custom_call" | custom-call | flops 1 | bytes 1 | tf_op jit(solution)/shard_map/mixer_backward/pallas_call | solution.py:489
  598.6 4.0 add.61
  613.4 14.0 %column_terms.5 = bf16[4,208,2048]{2,1,0:T(8,128)(2,1)} custom-call(s32[4]{0:T(128)} %pad_add_fusion.ids_ref.refs_0_, bf16[1024,2048]{1,0:T(8,128)(2,1)} %norm_rows.1.x_ref.a_ref, bf16[1024,2048]{1,0:T(8,128)(2,1)} %collective-permute-done.29.b_ref, bf16[1024,1664]{1,0:T(8,128)(2,1)} %get-tuple-element.440.ra_ref.refs_0_, ...), custom_call_target="tpu_custom_call" | custom-call | flops 1 | bytes 1 | tf_op jit(solution)/shard_map/column_terms/pallas_call | solution.py:1333
  630.6 10.5 %collective-permute-done.51.refs_1_.last_ref = bf16[352,2048]{1,0:T(8,128)(2,1)} collective-permute-done((bf16[352,2048]{1,0:T(8,128)(2,1)}, bf16[352,2048]{1,0:T(8,128)(2,1)}, u32[]{:S(2)}, u32[]{:S(2)}) %collective-permute-start.51) | collective-permute-done | bytes 1441824 | tf_op jit(solution)/shard_map/ppermute | solution.py:1417
  641.4 4.1 all-to-all-start.3
  655.0 23.2 %times_transposed.3 = (bf16[512,1024]{1,0:T(8,128)(2,1)}, bf16[512,1024]{1,0:T(8,128)(2,1)}, bf16[512,1024]{1,0:T(8,128)(2,1)}, bf16[512,1024]{1,0:T(8,128)(2,1)}) custom-call(s32[4]{0:T(128)} %pad_add_fusion.ids_ref.refs_0_, bf16[1024,1664]{1,0:T(8,128)(2,1)} %get-tuple-element.440.ra_ref.refs_0_, bf16[4,4,64,1664]{3,2,1,0:T(8,128)(2,1)} %bitcast.43, ...), custom_call_target="tpu_custom_call" | custom-call | flops 1 | bytes 1 | tf_op jit(solution)/shard_map/times_transposed/pallas_call | solution.py:1270
  678.3 7.6 collective-permute-start.55
  711.2 5.4 collective-permute-done.55.refs_1_.last_ref
  736.8 5.1 collective-permute-done.62.refs_2_
  743.3 5.1 collective-permute-done.60.refs_1_
  748.4 5.1 all-to-all-start.4
  753.6 6.4 collective-permute-start.66
  767.6 5.9 tokens_back.1
  775.2 14.2 %collective-permute-done.66.refs_1_.last_ref = bf16[352,2048]{1,0:T(8,128)(2,1)S(1)} collective-permute-done((bf16[352,2048]{1,0:T(8,128)(2,1)S(1)}, bf16[352,2048]{1,0:T(8,128)(2,1)S(1)}, u32[]{:S(2)}, u32[]{:S(2)}) %collective-permute-start.66) | collective-permute-done | bytes 1441824 | tf_op jit(solution)/shard_map/ppermute | solution.py:1417
  798.7 4.9 finish_projection.5.refs_0_
  803.6 16.0 %collective-permute-done.68.refs_1_.last_ref = bf16[352,2048]{1,0:T(8,128)(2,1)} collective-permute-done((bf16[352,2048]{1,0:T(8,128)(2,1)}, bf16[352,2048]{1,0:T(8,128)(2,1)}, u32[]{:S(2)}, u32[]{:S(2)}) %collective-permute-start.68) | collective-permute-done | bytes 1441824 | tf_op jit(solution)/shard_map/ppermute | solution.py:1417
  835.2 10.7 %finish_feed_forward.1 = f32[256,11264]{1,0:T(8,128)} custom-call(bf16[4,256,2816]{2,1,0:T(8,128)(2,1)} %all-to-all-done.4.x_ref), custom_call_target="tpu_custom_call" | custom-call | flops 1 | bytes 1 | tf_op jit(solution)/shard_map/finish_feed_forward/pallas_call | solution.py:1033
  845.9 5.6 collective-permute-done.72.last_ref
  867.3 6.9 finish_projection.6.refs_0_
  874.2 7.1 finish_projection.7.refs_0_
  888.9 3.4 all-to-all-start.5
  895.0 6.2 finish_projection.8.refs_0_
  901.2 20.5 %all-gather.2 = f32[32,1024]{1,0:T(8,128)S(1)} all-gather(f32[8,1024]{1,0:T(8,128)S(1)} %reduce_sum.28), channel_id=4, replica_groups=mesh['rep'=4,'fsdp'=8] {'rep'}, dimensions={0}, use_global_device_ids=true | all-gather | bytes 163840 | tf_op jit(solution)/shard_map/all_gather | solution.py:2004
  925.5 6.3 finish_projection.9
  (345 shorter events, 279.0 us)
Async XLA Ops:
  7.2 92.7 %all-gather.6.cloned.1.call-start = ((), (), s32[]{:S(2)}) async-start(), calls=%async_computation.6 | async-start | bytes 4259840 | tf_op jit(solution)/shard_map/all_gather | solution.py:1804
  42.1 25.0 %collective-permute-start.5 = (bf16[256,2048]{1,0:T(8,128)(2,1)}, bf16[256,2048]{1,0:T(8,128)(2,1)S(1)}, u32[]{:S(2)}, u32[]{:S(2)}) collective-permute-start(bf16[256,2048]{1,0:T(8,128)(2,1)} %t_ref.3), channel_id=1, source_target_pairs={{0,2},{1,3},{2,0},{3,1},{4,6},{5,7},{6,4},{7,5},{8,10},{9,11},{10,... | collective-permute-start | bytes 3145736 | tf_op jit(solution)/shard_map/ppermute | solution.py:1401
  42.8 24.8 %collective-permute-start.6 = (bf16[256,2048]{1,0:T(8,128)(2,1)}, bf16[256,2048]{1,0:T(8,128)(2,1)S(1)}, u32[]{:S(2)}, u32[]{:S(2)}) collective-permute-start(bf16[256,2048]{1,0:T(8,128)(2,1)} %t_ref.3), channel_id=1, source_target_pairs={{0,4},{1,5},{2,6},{3,7},{4,0},{5,1},{6,2},{7,3},{8,12},{9,13},{10,... | collective-permute-start | bytes 3145736 | tf_op jit(solution)/shard_map/ppermute | solution.py:1401
  69.5 30.4 %collective-permute-start.9 = (bf16[256,1536]{1,0:T(8,128)(2,1)}, bf16[256,1536]{1,0:T(8,128)(2,1)S(1)}, u32[]{:S(2)}, u32[]{:S(2)}) collective-permute-start(bf16[256,1536]{1,0:T(8,128)(2,1)} %get-tuple-element.292), channel_id=1, source_target_pairs={{0,2},{1,3},{2,0},{3,1},{4,6},{5,7},{6,4},{7,5},{8,10},{9,11},{10,... | collective-permute-start | bytes 2359304 | tf_op jit(solution)/shard_map/ppermute | solution.py:1401
  70.2 29.7 %collective-permute-start.10 = (bf16[256,1536]{1,0:T(8,128)(2,1)}, bf16[256,1536]{1,0:T(8,128)(2,1)}, u32[]{:S(2)}, u32[]{:S(2)}) collective-permute-start(bf16[256,1536]{1,0:T(8,128)(2,1)} %get-tuple-element.293), channel_id=1, source_target_pairs={{0,4},{1,5},{2,6},{3,7},{4,0},{5,1},{6,2},{7,3},{8,12},{9,13},{10,... | collective-permute-start | bytes 2359304 | tf_op jit(solution)/shard_map/ppermute | solution.py:1401
  83.0 32.1 %collective-permute-start.11 = (bf16[256,1536]{1,0:T(8,128)(2,1)}, bf16[256,1536]{1,0:T(8,128)(2,1)}, u32[]{:S(2)}, u32[]{:S(2)}) collective-permute-start(bf16[256,1536]{1,0:T(8,128)(2,1)} %get-tuple-element.295), channel_id=1, source_target_pairs={{0,6},{1,7},{2,4},{3,5},{4,2},{5,3},{6,0},{7,1},{8,14},{9,15},{10,... | collective-permute-start | bytes 2359304 | tf_op jit(solution)/shard_map/ppermute | solution.py:1401
  100.8 22.1 %collective-permute-start.12 = (bf16[4,4,64,1664]{3,2,1,0:T(8,128)(2,1)}, bf16[4,4,64,1664]{3,2,1,0:T(8,128)(2,1)S(1)}, u32[]{:S(2)}, u32[]{:S(2)}) collective-permute-start(bf16[4,4,64,1664]{3,2,1,0:T(8,128)(2,1)} %bitcast.41), channel_id=1, source_target_pairs={{0,1},{1,0},{2,3},{3,2},{4,5},{5,4},{6,7},{7,6},{8,9},{9,8},{10,11... | collective-permute-start | bytes 10223624 | tf_op jit(solution)/shard_map/ppermute | solution.py:1405
  118.3 19.7 %collective-permute-start.13 = (bf16[1,4,256,1536]{3,2,1,0:T(8,128)(2,1)}, bf16[1,4,256,1536]{3,2,1,0:T(8,128)(2,1)}, u32[]{:S(2)}, u32[]{:S(2)}) collective-permute-start(bf16[1,4,256,1536]{3,2,1,0:T(8,128)(2,1)} %stack_blocks.1.own_ref.refs_4_), channel_id=1, source_target_pairs={{0,1},{1,0},{2,3},{3,2},{4,5},{5,4},{6,7},{7,6},{8,9},{9,8},{10,11... | collective-permute-start | bytes 9437192 | tf_op jit(solution)/shard_map/ppermute | solution.py:1405
  118.3 40.1 %all-to-all-start.1 = ((bf16[4,64,2816]{2,1,0:T(8,128)(2,1)}), bf16[4,64,2816]{2,1,0:T(8,128)(2,1)}, u32[]{:S(2)}, u32[]{:S(2)}) async-start(bf16[4,64,2816]{2,1,0:T(8,128)(2,1)} %pack_columns.1), calls=%async_computation.1 | async-start | bytes 2883584 | tf_op jit(solution)/shard_map/all_to_all | solution.py:1626
  122.6 154.7 %all-gather.8.cloned.1.call-start = ((), (), s32[]{:S(2)}) async-start(), calls=%async_computation.7 | async-start | bytes 7208960 | tf_op jit(solution)/shard_map/all_gather | solution.py:1828
  158.4 61.0 %collective-permute-start.16 = (bf16[256,2048]{1,0:T(8,128)(2,1)S(1)}, bf16[256,2048]{1,0:T(8,128)(2,1)S(1)}, u32[]{:S(2)}, u32[]{:S(2)}) collective-permute-start(bf16[256,2048]{1,0:T(8,128)(2,1)S(1)} %copy-done.27), channel_id=1, source_target_pairs={{0,2},{1,3},{2,0},{3,1},{4,6},{5,7},{6,4},{7,5},{8,10},{9,11},{10,... | collective-permute-start | bytes 3145736 | tf_op jit(solution)/shard_map/ppermute | solution.py:1401
  160.4 59.0 %collective-permute-start.17 = (bf16[256,2048]{1,0:T(8,128)(2,1)S(1)}, bf16[256,2048]{1,0:T(8,128)(2,1)S(1)}, u32[]{:S(2)}, u32[]{:S(2)}) collective-permute-start(bf16[256,2048]{1,0:T(8,128)(2,1)S(1)} %copy-done.27), channel_id=1, source_target_pairs={{0,4},{1,5},{2,6},{3,7},{4,0},{5,1},{6,2},{7,3},{8,12},{9,13},{10,... | collective-permute-start | bytes 3145736 | tf_op jit(solution)/shard_map/ppermute | solution.py:1401
  161.9 57.6 %collective-permute-start.18 = (bf16[256,2048]{1,0:T(8,128)(2,1)S(1)}, bf16[256,2048]{1,0:T(8,128)(2,1)}, u32[]{:S(2)}, u32[]{:S(2)}) collective-permute-start(bf16[256,2048]{1,0:T(8,128)(2,1)S(1)} %copy-done.27), channel_id=1, source_target_pairs={{0,6},{1,7},{2,4},{3,5},{4,2},{5,3},{6,0},{7,1},{8,14},{9,15},{10,... | collective-permute-start | bytes 3145736 | tf_op jit(solution)/shard_map/ppermute | solution.py:1401
  205.3 24.9 %collective-permute-start.14 = (bf16[512,1024]{1,0:T(8,128)(2,1)}, bf16[512,1024]{1,0:T(8,128)(2,1)S(1)}, u32[]{:S(2)}, u32[]{:S(2)}) collective-permute-start(bf16[512,1024]{1,0:T(8,128)(2,1)} %get-tuple-element.312), channel_id=1, source_target_pairs={{0,2},{1,3},{2,0},{3,1},{4,6},{5,7},{6,4},{7,5},{8,10},{9,11},{10,... | collective-permute-start | bytes 3145736 | tf_op jit(solution)/shard_map/ppermute | solution.py:1401
  207.2 24.3 %collective-permute-start.15 = (bf16[512,1024]{1,0:T(8,128)(2,1)}, bf16[512,1024]{1,0:T(8,128)(2,1)S(1)}, u32[]{:S(2)}, u32[]{:S(2)}) collective-permute-start(bf16[512,1024]{1,0:T(8,128)(2,1)} %get-tuple-element.314), channel_id=1, source_target_pairs={{0,4},{1,5},{2,6},{3,7},{4,0},{5,1},{6,2},{7,3},{8,12},{9,13},{10,... | collective-permute-start | bytes 3145736 | tf_op jit(solution)/shard_map/ppermute | solution.py:1401
  253.9 22.5 %collective-permute-start.21 = (bf16[256,2048]{1,0:T(8,128)(2,1)}, bf16[256,2048]{1,0:T(8,128)(2,1)}, u32[]{:S(2)}, u32[]{:S(2)}) collective-permute-start(bf16[256,2048]{1,0:T(8,128)(2,1)} %get-tuple-element.330), channel_id=1, source_target_pairs={{0,2},{1,3},{2,0},{3,1},{4,6},{5,7},{6,4},{7,5},{8,10},{9,11},{10,... | collective-permute-start | bytes 3145736 | tf_op jit(solution)/shard_map/ppermute | solution.py:1401
  254.8 22.5 %collective-permute-start.22 = (bf16[256,2048]{1,0:T(8,128)(2,1)}, bf16[256,2048]{1,0:T(8,128)(2,1)}, u32[]{:S(2)}, u32[]{:S(2)}) collective-permute-start(bf16[256,2048]{1,0:T(8,128)(2,1)} %get-tuple-element.330), channel_id=1, source_target_pairs={{0,4},{1,5},{2,6},{3,7},{4,0},{5,1},{6,2},{7,3},{8,12},{9,13},{10,... | collective-permute-start | bytes 3145736 | tf_op jit(solution)/shard_map/ppermute | solution.py:1401
  277.3 20.9 %collective-permute-start.25 = (bf16[4,4,64,2816]{3,2,1,0:T(8,128)(2,1)}, bf16[4,4,64,2816]{3,2,1,0:T(8,128)(2,1)S(1)}, u32[]{:S(2)}, u32[]{:S(2)}) collective-permute-start(bf16[4,4,64,2816]{3,2,1,0:T(8,128)(2,1)} %bitcast.38), channel_id=1, source_target_pairs={{0,1},{1,0},{2,3},{3,2},{4,5},{5,4},{6,7},{7,6},{8,9},{9,8},{10,11... | collective-permute-start | bytes 17301512 | tf_op jit(solution)/shard_map/ppermute | solution.py:1405
  298.2 31.1 %collective-permute-start.26 = (bf16[1024,2048]{1,0:T(8,128)(2,1)}, bf16[1024,2048]{1,0:T(8,128)(2,1)}, u32[]{:S(2)}, u32[]{:S(2)}) collective-permute-start(bf16[1024,2048]{1,0:T(8,128)(2,1)} %constant_dynamic-update-slice_fusion.4.x_ref.a_ref), channel_id=1, source_target_pairs={{0,1},{1,0},{2,3},{3,2},{4,5},{5,4},{6,7},{7,6},{8,9},{9,8},{10,11... | collective-permute-start | bytes 12582920 | tf_op jit(solution)/shard_map/ppermute | solution.py:1405
  328.8 20.5 %collective-permute-start.28 = (bf16[1024,2816]{1,0:T(8,128)(2,1)}, bf16[1024,2816]{1,0:T(8,128)(2,1)}, u32[]{:S(2)}, u32[]{:S(2)}) collective-permute-start(bf16[1024,2816]{1,0:T(8,128)(2,1)} %get-tuple-element.365.refs_0_.ra_ref), channel_id=1, source_target_pairs={{0,1},{1,0},{2,3},{3,2},{4,5},{5,4},{6,7},{7,6},{8,9},{9,8},{10,11... | collective-permute-start | bytes 17301512 | tf_op jit(solution)/shard_map/ppermute | solution.py:1405
  347.6 36.0 %collective-permute-start.32 = (bf16[352,2048]{1,0:T(8,128)(2,1)S(1)}, bf16[352,2048]{1,0:T(8,128)(2,1)}, u32[]{:S(2)}, u32[]{:S(2)}) collective-permute-start(bf16[352,2048]{1,0:T(8,128)(2,1)S(1)} %get-tuple-element.354.refs_0_), channel_id=1, source_target_pairs={{0,8},{8,0},{16,24},{24,16},{1,9},{9,1},{17,25},{25,17},{2,10},{10... | collective-permute-start | bytes 4325384 | tf_op jit(solution)/shard_map/ppermute | solution.py:1417
  369.7 25.2 %collective-permute-start.30 = (bf16[512,1024]{1,0:T(8,128)(2,1)}, bf16[512,1024]{1,0:T(8,128)(2,1)S(1)}, u32[]{:S(2)}, u32[]{:S(2)}) collective-permute-start(bf16[512,1024]{1,0:T(8,128)(2,1)} %get-tuple-element.339), channel_id=1, source_target_pairs={{0,2},{1,3},{2,0},{3,1},{4,6},{5,7},{6,4},{7,5},{8,10},{9,11},{10,... | collective-permute-start | bytes 3145736 | tf_op jit(solution)/shard_map/ppermute | solution.py:1401
  370.6 24.9 %collective-permute-start.31 = (bf16[512,1024]{1,0:T(8,128)(2,1)}, bf16[512,1024]{1,0:T(8,128)(2,1)S(1)}, u32[]{:S(2)}, u32[]{:S(2)}) collective-permute-start(bf16[512,1024]{1,0:T(8,128)(2,1)} %get-tuple-element.341), channel_id=1, source_target_pairs={{0,4},{1,5},{2,6},{3,7},{4,0},{5,1},{6,2},{7,3},{8,12},{9,13},{10,... | collective-permute-start | bytes 3145736 | tf_op jit(solution)/shard_map/ppermute | solution.py:1401
  383.7 39.4 %collective-permute-start.35 = (bf16[352,2048]{1,0:T(8,128)(2,1)S(1)}, bf16[352,2048]{1,0:T(8,128)(2,1)S(1)}, u32[]{:S(2)}, u32[]{:S(2)}) collective-permute-start(bf16[352,2048]{1,0:T(8,128)(2,1)S(1)} %get-tuple-element.367.refs_0_), channel_id=1, source_target_pairs={{0,8},{8,0},{16,24},{24,16},{1,9},{9,1},{17,25},{25,17},{2,10},{10... | collective-permute-start | bytes 4325384 | tf_op jit(solution)/shard_map/ppermute | solution.py:1417
  386.9 40.0 %collective-permute-start.36 = (bf16[352,2048]{1,0:T(8,128)(2,1)}, bf16[352,2048]{1,0:T(8,128)(2,1)}, u32[]{:S(2)}, u32[]{:S(2)}) collective-permute-start(bf16[352,2048]{1,0:T(8,128)(2,1)} %line_values.24.refs_0_), channel_id=1, source_target_pairs={{8,16},{16,8},{9,17},{17,9},{10,18},{18,10},{11,19},{19,11},{12,20... | collective-permute-start | bytes 4325384 | tf_op jit(solution)/shard_map/ppermute | solution.py:1417
  399.4 27.5 %collective-permute-start.33 = (bf16[256,1024]{1,0:T(8,128)(2,1)}, bf16[256,1024]{1,0:T(8,128)(2,1)S(1)}, u32[]{:S(2)}, u32[]{:S(2)}) collective-permute-start(bf16[256,1024]{1,0:T(8,128)(2,1)} %get-tuple-element.360), channel_id=1, source_target_pairs={{0,4},{1,5},{2,6},{3,7},{4,0},{5,1},{6,2},{7,3},{8,12},{9,13},{10,... | collective-permute-start | bytes 1572872 | tf_op jit(solution)/shard_map/ppermute | solution.py:1401
  400.0 26.9 %collective-permute-start.34 = (bf16[256,1024]{1,0:T(8,128)(2,1)}, bf16[256,1024]{1,0:T(8,128)(2,1)S(1)}, u32[]{:S(2)}, u32[]{:S(2)}) collective-permute-start(bf16[256,1024]{1,0:T(8,128)(2,1)} %get-tuple-element.361), channel_id=1, source_target_pairs={{0,2},{1,3},{2,0},{3,1},{4,6},{5,7},{6,4},{7,5},{8,10},{9,11},{10,... | collective-permute-start | bytes 1572872 | tf_op jit(solution)/shard_map/ppermute | solution.py:1401
  434.3 23.7 %collective-permute-start.37 = (bf16[256,2048]{1,0:T(8,128)(2,1)}, bf16[256,2048]{1,0:T(8,128)(2,1)S(1)}, u32[]{:S(2)}, u32[]{:S(2)}) collective-permute-start(bf16[256,2048]{1,0:T(8,128)(2,1)} %get-tuple-element.390), channel_id=1, source_target_pairs={{0,2},{1,3},{2,0},{3,1},{4,6},{5,7},{6,4},{7,5},{8,10},{9,11},{10,... | collective-permute-start | bytes 3145736 | tf_op jit(solution)/shard_map/ppermute | solution.py:1401
  435.5 23.5 %collective-permute-start.38 = (bf16[256,2048]{1,0:T(8,128)(2,1)}, bf16[256,2048]{1,0:T(8,128)(2,1)S(1)}, u32[]{:S(2)}, u32[]{:S(2)}) collective-permute-start(bf16[256,2048]{1,0:T(8,128)(2,1)} %get-tuple-element.390), channel_id=1, source_target_pairs={{0,4},{1,5},{2,6},{3,7},{4,0},{5,1},{6,2},{7,3},{8,12},{9,13},{10,... | collective-permute-start | bytes 3145736 | tf_op jit(solution)/shard_map/ppermute | solution.py:1401
  436.9 31.6 %collective-permute-start.42 = (bf16[352,2048]{1,0:T(8,128)(2,1)}, bf16[352,2048]{1,0:T(8,128)(2,1)}, u32[]{:S(2)}, u32[]{:S(2)}) collective-permute-start(bf16[352,2048]{1,0:T(8,128)(2,1)} %get-tuple-element.385.refs_0_), channel_id=1, source_target_pairs={{0,8},{8,0},{16,24},{24,16},{1,9},{9,1},{17,25},{25,17},{2,10},{10... | collective-permute-start | bytes 4325384 | tf_op jit(solution)/shard_map/ppermute | solution.py:1417
  437.4 35.7 %collective-permute-start.41 = (bf16[352,2048]{1,0:T(8,128)(2,1)S(1)}, bf16[352,2048]{1,0:T(8,128)(2,1)}, u32[]{:S(2)}, u32[]{:S(2)}) collective-permute-start(bf16[352,2048]{1,0:T(8,128)(2,1)S(1)} %copy-done.18), channel_id=1, source_target_pairs={{8,16},{16,8},{9,17},{17,9},{10,18},{18,10},{11,19},{19,11},{12,20... | collective-permute-start | bytes 4325384 | tf_op jit(solution)/shard_map/ppermute | solution.py:1417
  459.9 20.4 %collective-permute-start.39 = (bf16[128,2048]{1,0:T(8,128)(2,1)}, bf16[128,2048]{1,0:T(8,128)(2,1)S(1)}, u32[]{:S(2)}, u32[]{:S(2)}) collective-permute-start(bf16[128,2048]{1,0:T(8,128)(2,1)} %slice.154), channel_id=1, source_target_pairs={{0,4},{1,5},{2,6},{3,7},{4,0},{5,1},{6,2},{7,3},{8,12},{9,13},{10,... | collective-permute-start | bytes 1572872 | tf_op jit(solution)/shard_map/ppermute | solution.py:1401
  462.4 68.1 %collective-permute-start.29 = (bf16[1024,2048]{1,0:T(8,128)(2,1)S(1)}, bf16[1024,2048]{1,0:T(8,128)(2,1)}, u32[]{:S(2)}, u32[]{:S(2)}) collective-permute-start(bf16[1024,2048]{1,0:T(8,128)(2,1)S(1)} %copy-done), channel_id=1, source_target_pairs={{0,1},{1,0},{2,3},{3,2},{4,5},{5,4},{6,7},{7,6},{8,9},{9,8},{10,11... | collective-permute-start | bytes 12582920 | tf_op jit(solution)/shard_map/ppermute | solution.py:1405
  471.3 42.8 %collective-permute-start.43 = (bf16[352,2048]{1,0:T(8,128)(2,1)}, bf16[352,2048]{1,0:T(8,128)(2,1)}, u32[]{:S(2)}, u32[]{:S(2)}) collective-permute-start(bf16[352,2048]{1,0:T(8,128)(2,1)} %line_values.27.refs_0_), channel_id=1, source_target_pairs={{8,16},{16,8},{9,17},{17,9},{10,18},{18,10},{11,19},{19,11},{12,20... | collective-permute-start | bytes 4325384 | tf_op jit(solution)/shard_map/ppermute | solution.py:1417
  473.0 41.0 %collective-permute-start.44 = (bf16[352,2048]{1,0:T(8,128)(2,1)}, bf16[352,2048]{1,0:T(8,128)(2,1)S(1)}, u32[]{:S(2)}, u32[]{:S(2)}) collective-permute-start(bf16[352,2048]{1,0:T(8,128)(2,1)} %line_values.26), channel_id=1, source_target_pairs={{0,8},{8,0},{16,24},{24,16},{1,9},{9,1},{17,25},{25,17},{2,10},{10... | collective-permute-start | bytes 4325384 | tf_op jit(solution)/shard_map/ppermute | solution.py:1417
  514.1 34.3 %collective-permute-start.46 = (bf16[352,2048]{1,0:T(8,128)(2,1)}, bf16[352,2048]{1,0:T(8,128)(2,1)}, u32[]{:S(2)}, u32[]{:S(2)}) collective-permute-start(bf16[352,2048]{1,0:T(8,128)(2,1)} %line_values.28), channel_id=1, source_target_pairs={{0,8},{8,0},{16,24},{24,16},{1,9},{9,1},{17,25},{25,17},{2,10},{10... | collective-permute-start | bytes 4325384 | tf_op jit(solution)/shard_map/ppermute | solution.py:1417
  517.8 30.6 %collective-permute-start.47 = (bf16[352,2048]{1,0:T(8,128)(2,1)}, bf16[352,2048]{1,0:T(8,128)(2,1)S(1)}, u32[]{:S(2)}, u32[]{:S(2)}) collective-permute-start(bf16[352,2048]{1,0:T(8,128)(2,1)} %line_values.29.refs_0_), channel_id=1, source_target_pairs={{8,16},{16,8},{9,17},{17,9},{10,18},{18,10},{11,19},{19,11},{12,20... | collective-permute-start | bytes 4325384 | tf_op jit(solution)/shard_map/ppermute | solution.py:1417
  549.5 48.8 %all-to-all-start.2 = ((bf16[4,192,2048]{2,1,0:T(8,128)(2,1)}), bf16[4,192,2048]{2,1,0:T(8,128)(2,1)S(1)}, u32[]{:S(2)}, u32[]{:S(2)}) async-start(bf16[4,192,2048]{2,1,0:T(8,128)(2,1)} %column_terms.4), calls=%async_computation.2 | async-start | bytes 6291456 | tf_op jit(solution)/shard_map/all_to_all | solution.py:1626
  553.3 43.9 %collective-permute-start.48 = (bf16[352,2048]{1,0:T(8,128)(2,1)}, bf16[352,2048]{1,0:T(8,128)(2,1)S(1)}, u32[]{:S(2)}, u32[]{:S(2)}) collective-permute-start(bf16[352,2048]{1,0:T(8,128)(2,1)} %line_values.30.t_ref), channel_id=1, source_target_pairs={{0,8},{8,0},{16,24},{24,16},{1,9},{9,1},{17,25},{25,17},{2,10},{10... | collective-permute-start | bytes 4325384 | tf_op jit(solution)/shard_map/ppermute | solution.py:1417
  562.3 36.0 %collective-permute-start.52 = (bf16[352,2048]{1,0:T(8,128)(2,1)}, bf16[352,2048]{1,0:T(8,128)(2,1)}, u32[]{:S(2)}, u32[]{:S(2)}) collective-permute-start(bf16[352,2048]{1,0:T(8,128)(2,1)} %line_values.31.refs_0_), channel_id=1, source_target_pairs={{8,16},{16,8},{9,17},{17,9},{10,18},{18,10},{11,19},{19,11},{12,20... | collective-permute-start | bytes 4325384 | tf_op jit(solution)/shard_map/ppermute | solution.py:1417
  607.1 34.0 %collective-permute-start.51 = (bf16[352,2048]{1,0:T(8,128)(2,1)}, bf16[352,2048]{1,0:T(8,128)(2,1)}, u32[]{:S(2)}, u32[]{:S(2)}) collective-permute-start(bf16[352,2048]{1,0:T(8,128)(2,1)} %line_values.32.t_ref), channel_id=1, source_target_pairs={{0,8},{8,0},{16,24},{24,16},{1,9},{9,1},{17,25},{25,17},{2,10},{10... | collective-permute-start | bytes 4325384 | tf_op jit(solution)/shard_map/ppermute | solution.py:1417
  610.2 31.2 %collective-permute-start.50 = (bf16[352,2048]{1,0:T(8,128)(2,1)}, bf16[352,2048]{1,0:T(8,128)(2,1)}, u32[]{:S(2)}, u32[]{:S(2)}) collective-permute-start(bf16[352,2048]{1,0:T(8,128)(2,1)} %line_values.33.refs_0_), channel_id=1, source_target_pairs={{8,16},{16,8},{9,17},{17,9},{10,18},{18,10},{11,19},{19,11},{12,20... | collective-permute-start | bytes 4325384 | tf_op jit(solution)/shard_map/ppermute | solution.py:1417
  641.0 37.2 %collective-permute-start.54 = (bf16[352,2048]{1,0:T(8,128)(2,1)}, bf16[352,2048]{1,0:T(8,128)(2,1)}, u32[]{:S(2)}, u32[]{:S(2)}) collective-permute-start(bf16[352,2048]{1,0:T(8,128)(2,1)} %line_values.34.t_ref), channel_id=1, source_target_pairs={{0,8},{8,0},{16,24},{24,16},{1,9},{9,1},{17,25},{25,17},{2,10},{10... | collective-permute-start | bytes 4325384 | tf_op jit(solution)/shard_map/ppermute | solution.py:1417
  641.4 64.1 %all-to-all-start.3 = ((bf16[4,208,2048]{2,1,0:T(8,128)(2,1)}), bf16[4,208,2048]{2,1,0:T(8,128)(2,1)S(1)}, u32[]{:S(2)}, u32[]{:S(2)}) async-start(bf16[4,208,2048]{2,1,0:T(8,128)(2,1)} %column_terms.5), calls=%async_computation.3 | async-start | bytes 6815744 | tf_op jit(solution)/shard_map/all_to_all | solution.py:1626
  648.2 44.4 %collective-permute-start.57 = (bf16[352,2048]{1,0:T(8,128)(2,1)}, bf16[352,2048]{1,0:T(8,128)(2,1)S(1)}, u32[]{:S(2)}, u32[]{:S(2)}) collective-permute-start(bf16[352,2048]{1,0:T(8,128)(2,1)} %line_values.35.refs_0_), channel_id=1, source_target_pairs={{8,16},{16,8},{9,17},{17,9},{10,18},{18,10},{11,19},{19,11},{12,20... | collective-permute-start | bytes 4325384 | tf_op jit(solution)/shard_map/ppermute | solution.py:1417
  678.3 38.3 %collective-permute-start.55 = (bf16[352,2048]{1,0:T(8,128)(2,1)}, bf16[352,2048]{1,0:T(8,128)(2,1)}, u32[]{:S(2)}, u32[]{:S(2)}) collective-permute-start(bf16[352,2048]{1,0:T(8,128)(2,1)} %line_values.36.t_ref), channel_id=1, source_target_pairs={{0,8},{8,0},{16,24},{24,16},{1,9},{9,1},{17,25},{25,17},{2,10},{10... | collective-permute-start | bytes 4325384 | tf_op jit(solution)/shard_map/ppermute | solution.py:1417
  688.6 36.0 %collective-permute-start.56 = (bf16[352,2048]{1,0:T(8,128)(2,1)}, bf16[352,2048]{1,0:T(8,128)(2,1)}, u32[]{:S(2)}, u32[]{:S(2)}) collective-permute-start(bf16[352,2048]{1,0:T(8,128)(2,1)} %line_values.37.refs_0_), channel_id=1, source_target_pairs={{8,16},{16,8},{9,17},{17,9},{10,18},{18,10},{11,19},{19,11},{12,20... | collective-permute-start | bytes 4325384 | tf_op jit(solution)/shard_map/ppermute | solution.py:1417
  692.7 35.1 %collective-permute-start.58 = (bf16[512,1024]{1,0:T(8,128)(2,1)}, bf16[512,1024]{1,0:T(8,128)(2,1)}, u32[]{:S(2)}, u32[]{:S(2)}) collective-permute-start(bf16[512,1024]{1,0:T(8,128)(2,1)} %get-tuple-element.464), channel_id=1, source_target_pairs={{0,2},{1,3},{2,0},{3,1},{4,6},{5,7},{6,4},{7,5},{8,10},{9,11},{10,... | collective-permute-start | bytes 3145736 | tf_op jit(solution)/shard_map/ppermute | solution.py:1401
  694.7 33.1 %collective-permute-start.59 = (bf16[512,1024]{1,0:T(8,128)(2,1)}, bf16[512,1024]{1,0:T(8,128)(2,1)}, u32[]{:S(2)}, u32[]{:S(2)}) collective-permute-start(bf16[512,1024]{1,0:T(8,128)(2,1)} %get-tuple-element.465), channel_id=1, source_target_pairs={{0,4},{1,5},{2,6},{3,7},{4,0},{5,1},{6,2},{7,3},{8,12},{9,13},{10,... | collective-permute-start | bytes 3145736 | tf_op jit(solution)/shard_map/ppermute | solution.py:1401
  716.6 31.8 %collective-permute-start.60 = (bf16[352,2048]{1,0:T(8,128)(2,1)}, bf16[352,2048]{1,0:T(8,128)(2,1)}, u32[]{:S(2)}, u32[]{:S(2)}) collective-permute-start(bf16[352,2048]{1,0:T(8,128)(2,1)} %line_values.38), channel_id=1, source_target_pairs={{0,8},{8,0},{16,24},{24,16},{1,9},{9,1},{17,25},{25,17},{2,10},{10... | collective-permute-start | bytes 4325384 | tf_op jit(solution)/shard_map/ppermute | solution.py:1417
  721.0 27.4 %collective-permute-start.61 = (bf16[352,2048]{1,0:T(8,128)(2,1)}, bf16[352,2048]{1,0:T(8,128)(2,1)}, u32[]{:S(2)}, u32[]{:S(2)}) collective-permute-start(bf16[352,2048]{1,0:T(8,128)(2,1)} %line_values.39.refs_0_), channel_id=1, source_target_pairs={{8,16},{16,8},{9,17},{17,9},{10,18},{18,10},{11,19},{19,11},{12,20... | collective-permute-start | bytes 4325384 | tf_op jit(solution)/shard_map/ppermute | solution.py:1417
  748.4 72.4 %all-to-all-start.4 = ((bf16[4,256,2816]{2,1,0:T(8,128)(2,1)}), bf16[4,256,2816]{2,1,0:T(8,128)(2,1)}, u32[]{:S(2)}, u32[]{:S(2)}) async-start(bf16[4,256,2816]{2,1,0:T(8,128)(2,1)} %place_blocks.7), calls=%async_computation.4 | async-start | bytes 11534336 | tf_op jit(solution)/shard_map/all_to_all | solution.py:1626
  753.6 35.8 %collective-permute-start.66 = (bf16[352,2048]{1,0:T(8,128)(2,1)S(1)}, bf16[352,2048]{1,0:T(8,128)(2,1)S(1)}, u32[]{:S(2)}, u32[]{:S(2)}) collective-permute-start(bf16[352,2048]{1,0:T(8,128)(2,1)S(1)} %copy-done.7), channel_id=1, source_target_pairs={{0,8},{8,0},{16,24},{24,16},{1,9},{9,1},{17,25},{25,17},{2,10},{10... | collective-permute-start | bytes 4325384 | tf_op jit(solution)/shard_map/ppermute | solution.py:1417
  762.7 33.2 %collective-permute-start.69 = (bf16[352,2048]{1,0:T(8,128)(2,1)}, bf16[352,2048]{1,0:T(8,128)(2,1)}, u32[]{:S(2)}, u32[]{:S(2)}) collective-permute-start(bf16[352,2048]{1,0:T(8,128)(2,1)} %line_values.41.refs_0_), channel_id=1, source_target_pairs={{8,16},{16,8},{9,17},{17,9},{10,18},{18,10},{11,19},{19,11},{12,20... | collective-permute-start | bytes 4325384 | tf_op jit(solution)/shard_map/ppermute | solution.py:1417
  789.4 30.2 %collective-permute-start.68 = (bf16[352,2048]{1,0:T(8,128)(2,1)}, bf16[352,2048]{1,0:T(8,128)(2,1)}, u32[]{:S(2)}, u32[]{:S(2)}) collective-permute-start(bf16[352,2048]{1,0:T(8,128)(2,1)} %line_values.42.t_ref), channel_id=1, source_target_pairs={{0,8},{8,0},{16,24},{24,16},{1,9},{9,1},{17,25},{25,17},{2,10},{10... | collective-permute-start | bytes 4325384 | tf_op jit(solution)/shard_map/ppermute | solution.py:1417
  794.1 38.4 %collective-permute-start.67 = (bf16[352,2048]{1,0:T(8,128)(2,1)}, bf16[352,2048]{1,0:T(8,128)(2,1)}, u32[]{:S(2)}, u32[]{:S(2)}) collective-permute-start(bf16[352,2048]{1,0:T(8,128)(2,1)} %line_values.43.refs_0_), channel_id=1, source_target_pairs={{8,16},{16,8},{9,17},{17,9},{10,18},{18,10},{11,19},{19,11},{12,20... | collective-permute-start | bytes 4325384 | tf_op jit(solution)/shard_map/ppermute | solution.py:1417
  819.6 32.0 %collective-permute-start.72 = (bf16[352,2048]{1,0:T(8,128)(2,1)}, bf16[352,2048]{1,0:T(8,128)(2,1)}, u32[]{:S(2)}, u32[]{:S(2)}) collective-permute-start(bf16[352,2048]{1,0:T(8,128)(2,1)} %line_values.44.t_ref), channel_id=1, source_target_pairs={{8,0},{16,24},{9,1},{17,25},{10,2},{18,26},{11,3},{19,27},{12,4},{... | collective-permute-start | bytes 4325384 | tf_op jit(solution)/shard_map/ppermute | solution.py:1417
  820.9 32.0 %collective-permute-start.64 = (bf16[512,1024]{1,0:T(8,128)(2,1)}, bf16[512,1024]{1,0:T(8,128)(2,1)S(1)}, u32[]{:S(2)}, u32[]{:S(2)}) collective-permute-start(bf16[512,1024]{1,0:T(8,128)(2,1)} %get-tuple-element.476), channel_id=1, source_target_pairs={{0,2},{1,3},{2,0},{3,1},{4,6},{5,7},{6,4},{7,5},{8,10},{9,11},{10,... | collective-permute-start | bytes 3145736 | tf_op jit(solution)/shard_map/ppermute | solution.py:1401
  822.5 30.3 %collective-permute-start.65 = (bf16[512,1024]{1,0:T(8,128)(2,1)}, bf16[512,1024]{1,0:T(8,128)(2,1)}, u32[]{:S(2)}, u32[]{:S(2)}) collective-permute-start(bf16[512,1024]{1,0:T(8,128)(2,1)} %get-tuple-element.477), channel_id=1, source_target_pairs={{0,4},{1,5},{2,6},{3,7},{4,0},{5,1},{6,2},{7,3},{8,12},{9,13},{10,... | collective-permute-start | bytes 3145736 | tf_op jit(solution)/shard_map/ppermute | solution.py:1401
  826.9 36.6 %collective-permute-start.73 = (bf16[352,2048]{1,0:T(8,128)(2,1)}, bf16[352,2048]{1,0:T(8,128)(2,1)S(1)}, u32[]{:S(2)}, u32[]{:S(2)}) collective-permute-start(bf16[352,2048]{1,0:T(8,128)(2,1)} %line_values.45.refs_0_), channel_id=1, source_target_pairs={{8,16},{16,8},{9,17},{17,9},{10,18},{18,10},{11,19},{19,11},{12,20... | collective-permute-start | bytes 4325384 | tf_op jit(solution)/shard_map/ppermute | solution.py:1417
  851.5 33.1 %collective-permute-start.74 = (bf16[352,2048]{1,0:T(8,128)(2,1)S(1)}, bf16[352,2048]{1,0:T(8,128)(2,1)}, u32[]{:S(2)}, u32[]{:S(2)}) collective-permute-start(bf16[352,2048]{1,0:T(8,128)(2,1)S(1)} %copy-done.3), channel_id=1, source_target_pairs={{8,0},{16,24},{9,1},{17,25},{10,2},{18,26},{11,3},{19,27},{12,4},{... | collective-permute-start | bytes 4325384 | tf_op jit(solution)/shard_map/ppermute | solution.py:1417
  856.3 25.0 %collective-permute-start.70 = (bf16[256,1024]{1,0:T(8,128)(2,1)}, bf16[256,1024]{1,0:T(8,128)(2,1)S(1)}, u32[]{:S(2)}, u32[]{:S(2)}) collective-permute-start(bf16[256,1024]{1,0:T(8,128)(2,1)} %get-tuple-element.513), channel_id=1, source_target_pairs={{0,4},{1,5},{2,6},{3,7},{4,0},{5,1},{6,2},{7,3},{8,12},{9,13},{10,... | collective-permute-start | bytes 1572872 | tf_op jit(solution)/shard_map/ppermute | solution.py:1401
  858.0 23.4 %collective-permute-start.71 = (bf16[256,1024]{1,0:T(8,128)(2,1)}, bf16[256,1024]{1,0:T(8,128)(2,1)}, u32[]{:S(2)}, u32[]{:S(2)}) collective-permute-start(bf16[256,1024]{1,0:T(8,128)(2,1)} %get-tuple-element.514), channel_id=1, source_target_pairs={{0,2},{1,3},{2,0},{3,1},{4,6},{5,7},{6,4},{7,5},{8,10},{9,11},{10,... | collective-permute-start | bytes 1572872 | tf_op jit(solution)/shard_map/ppermute | solution.py:1401
  885.1 38.9 %collective-permute-start.75 = (bf16[352,2048]{1,0:T(8,128)(2,1)S(1)}, bf16[352,2048]{1,0:T(8,128)(2,1)}, u32[]{:S(2)}, u32[]{:S(2)}) collective-permute-start(bf16[352,2048]{1,0:T(8,128)(2,1)S(1)} %copy-done.4), channel_id=1, source_target_pairs={{8,0},{16,24},{9,1},{17,25},{10,2},{18,26},{11,3},{19,27},{12,4},{... | collective-permute-start | bytes 4325384 | tf_op jit(solution)/shard_map/ppermute | solution.py:1417
  (74 other events, 700.8 us)
Sparse Core Ops, SparseCore 0:
  29.9 68.1 all-gather.5
  158.5 108.6 all-gather.7
